TPU v7x, 256 devices: a whole 4x4x8 slice. The times are simulated.
256 devices in a mesh: ctx: 128 (over z, y_lo, x, core), tp: 2 (over y_hi).
Axes of the slice: x: 4, y: 4 (y_hi: 2, y_lo: 2; y = y_hi * 2 + y_lo), z: 8, core: 2. Of those that a mesh axis runs over, the one named last changes fastest.
Arguments:
- queries: bfloat16 [24576, 2048], P('ctx', 'tp'), may hold values from -9 to 9
- keys: bfloat16 [24576, 2048], P('ctx', 'tp'), may hold values from -9 to 9
- values: bfloat16 [24576, 2048], P('ctx', 'tp'), may hold values from -6 to 6
- stream_grad: bfloat16 [24576, 2048], P('ctx', 'tp'), may hold values from -6 to 6
- conv_input: bfloat16 [24576, 2048], P('ctx', 'tp'), may hold values from -6 to 6
- conv_weight: bfloat16 [31, 2048], P(None, 'tp'), may hold values from -1 to 1
- out_weight: bfloat16 [2048, 2048], P('tp'), may hold values from -0.125 to 0.125
Outputs:
- query_grad: bfloat16 [24576, 2048], P('ctx', 'tp')
- key_grad: bfloat16 [24576, 2048], P('ctx', 'tp')
- value_grad: bfloat16 [24576, 2048], P('ctx', 'tp')
- grad_stream: bfloat16 [24576, 2048], P('ctx', 'tp')
- kernel_grad: float32 [31, 2048], P(None, 'tp')
All inputs are finite; a program needn't handle non-finite values.
Results may differ from a plain program's by a relative error of at most 0.012.
The roundings to bfloat16 on the way count: a program that leaves them out, or rounds other values in their place, can miss the bound.
Values may be sent and summed in bfloat16 or wider, within the bound.
No kernel may reach another device: no remote copies, remote signals or barrier semaphores. Data moves between devices by JAX's collectives and lax.ppermute only.
A program may use at most 64 MiB of HBM per device.

v0:
```python
import math

import jax
import jax.numpy as jnp
from jax import lax
from jax.sharding import PartitionSpec as P

HEAD = 128


def with_halo(block, sides, width):
    for axis, dim in sides:
        count = lax.axis_size(axis)
        forward = [(i, i + 1) for i in range(count - 1)]
        backward = [(target, source) for source, target in forward]
        low = lax.ppermute(
            lax.slice_in_dim(block, block.shape[dim] - width, None, axis=dim), axis, forward
        )
        high = lax.ppermute(lax.slice_in_dim(block, 0, width, axis=dim), axis, backward)
        block = jnp.concatenate([low, block, high], axis=dim)
    return block


def shifted(shard, axis, by):
    count = lax.axis_size(axis)
    pairs = [(i, i + by) for i in range(count) if 0 <= i + by < count]
    return lax.ppermute(shard, axis, pairs)


def head_grads(qh, kh, vh, doh, valid, scale):
    contract_last = (((1,), (1,)), ((), ()))
    contract_first = (((0,), (0,)), ((), ()))
    scores = lax.dot_general(qh, kh, contract_last, preferred_element_type=jnp.float32) * scale
    scores = jnp.where(valid, scores, -jnp.inf)
    top = jnp.max(scores, axis=1, keepdims=True)
    expo = jnp.exp(scores - top)
    probs = expo / jnp.sum(expo, axis=1, keepdims=True)
    probs_low = probs.astype(jnp.bfloat16)
    attn_out = jnp.dot(probs_low, vh, preferred_element_type=jnp.float32)
    delta = jnp.sum(doh.astype(jnp.float32) * attn_out, axis=1, keepdims=True)
    prob_grad = lax.dot_general(doh, vh, contract_last, preferred_element_type=jnp.float32)
    score_grad = (probs * (prob_grad - delta)).astype(jnp.bfloat16)
    query_part = jnp.dot(score_grad, kh, preferred_element_type=jnp.float32) * scale
    key_part = (
        lax.dot_general(score_grad, qh, contract_first, preferred_element_type=jnp.float32) * scale
    )
    value_part = lax.dot_general(probs_low, doh, contract_first, preferred_element_type=jnp.float32)
    return (query_part, key_part, value_part)


def per_device(queries, keys, values, stream_grad, conv_input, conv_weight, out_weight):
    block = queries.shape[0]
    width = queries.shape[1]
    taps_count = conv_weight.shape[0]
    reach = taps_count // 2
    device = lax.axis_index("ctx")
    stacked = jnp.stack([conv_input, stream_grad])
    padded = with_halo(stacked, (("ctx", 1),), reach)
    input_pad = padded[0].astype(jnp.float32)
    grad_pad = padded[1].astype(jnp.float32)
    grad_f = stream_grad.astype(jnp.float32)
    taps = conv_weight.astype(jnp.float32)
    conv_back = jnp.zeros_like(grad_f)
    tap_rows = []
    for tap in range(taps_count):
        conv_back = conv_back + taps[tap] * grad_pad[2 * reach - tap : 2 * reach - tap + block]
        tap_rows.append(jnp.sum(grad_f * input_pad[tap : tap + block], axis=0))
    total_frames = block * lax.axis_size("ctx")
    kernel_grad = lax.psum(jnp.stack(tap_rows), "ctx") / math.sqrt(total_frames)
    grad_stream = (grad_f + conv_back).astype(jnp.bfloat16)
    full_stream = lax.all_gather(grad_stream, "tp", axis=1, tiled=True)
    out_grad = lax.dot_general(
        full_stream, out_weight, (((1,), (1,)), ((), ())), preferred_element_type=jnp.float32
    ).astype(jnp.bfloat16)
    pair = jnp.stack([keys, values])
    earlier = [pair]
    moving = pair
    for hop in range(3):
        moving = shifted(moving, "ctx", 1)
        earlier.append(moving)
    window = jnp.concatenate(earlier[::-1], axis=1)
    rows = jnp.arange(block, dtype=jnp.int32)[:, None]
    cols = jnp.arange(4 * block, dtype=jnp.int32)[None, :]
    valid = (cols <= 3 * block + rows) & (cols >= (3 - device) * block)
    scale = 1.0 / math.sqrt(HEAD)
    query_parts, key_parts, value_parts = ([], [], [])
    for head in range(width // HEAD):
        lo, hi = (head * HEAD, (head + 1) * HEAD)
        qp, kp, vp = head_grads(
            queries[:, lo:hi],
            window[0][:, lo:hi],
            window[1][:, lo:hi],
            out_grad[:, lo:hi],
            valid,
            scale,
        )
        query_parts.append(qp)
        key_parts.append(kp)
        value_parts.append(vp)
    query_grad = jnp.concatenate(query_parts, axis=1).astype(jnp.bfloat16)
    terms = jnp.stack(
        [jnp.concatenate(key_parts, axis=1), jnp.concatenate(value_parts, axis=1)]
    ).astype(jnp.bfloat16)
    total = terms[:, 3 * block :].astype(jnp.float32)
    bundle = terms[:, : 3 * block]
    for hop in range(3):
        arrived = shifted(bundle, "ctx", -1)
        total = total + arrived[:, arrived.shape[1] - block :].astype(jnp.float32)
        bundle = arrived[:, : arrived.shape[1] - block]
    key_grad = total[0].astype(jnp.bfloat16)
    value_grad = total[1].astype(jnp.bfloat16)
    return (query_grad, key_grad, value_grad, grad_stream, kernel_grad)


def solution(mesh):
    return jax.shard_map(
        per_device,
        mesh=mesh,
        in_specs=(
            P("ctx", "tp"),
            P("ctx", "tp"),
            P("ctx", "tp"),
            P("ctx", "tp"),
            P("ctx", "tp"),
            P(None, "tp"),
            P("tp", None),
        ),
        out_specs=(P("ctx", "tp"), P("ctx", "tp"), P("ctx", "tp"), P("ctx", "tp"), P(None, "tp")),
        check_vma=False,
    )
```

profile of v0, /device:TPU:1, one launch (start us, length us, event | category | flops | bytes accessed | tf_op | source)
XLA Modules:
  0.0 1104.0 jit_solution(2023817818111889792)
XLA Ops:
  7.2 1.3 pad_maximum_fusion.2
  8.5 4.5 collective-permute-start
  13.1 1.9 collective-permute-start.3
  15.0 2.4 collective-permute-start.4
  17.5 4.5 collective-permute-done
  21.9 4.4 collective-permute-start.1
  26.8 8.4 collective-permute-done.1
  35.2 4.4 collective-permute-start.2
  39.6 3.1 fusion.80
  42.8 20.0 %all_gather.3 = bf16[192,2048]{1,0:T(8,128)(2,1)S(1)} all-gather(bf16[192,1024]{1,0:T(8,128)(2,1)S(1)} %fusion.80), channel_id=1, replica_groups=mesh['ctx'=128,'tp'=2] {'tp'}, dimensions={1}, use_global_device_ids=true | all-gather | bytes 1179648 | tf_op jit(solution)/shard_map/all_gather | solution.py:71
  62.8 1.6 convolution_convert_fusion
  83.3 2.7 copy.14
  85.9 1.9 collective-permute-start.5
  87.9 3.0 fusion.111
  90.9 25.4 %collective-permute-done.5 = bf16[2,576,1024]{2,1,0:T(8,128)(2,1)S(1)} collective-permute-done((bf16[2,576,1024]{2,1,0:T(8,128)(2,1)}, bf16[2,576,1024]{2,1,0:T(8,128)(2,1)S(1)}, u32[]{:S(2)}, u32[]{:S(2)}) %collective-permute-start.5) | collective-permute-done | bytes 2359328 | tf_op jit(solution)/shard_map/ppermute | solution.py:27
  116.3 1.4 copy-done.7
  117.8 1.6 copy.22
  119.5 1.9 collective-permute-start.6
  122.6 2.7 stack.166
  125.3 943.1 %all-reduce.2.cloned.1.call-done = f32[31,1024]{1,0:T(8,128)} async-done(((f32[31,1024]{1,0:T(8,128)}), f32[31,1024]{1,0:T(8,128)}) %all-reduce.2.cloned.1.call-update) | async-done | bytes 126992 | tf_op jit(solution)/shard_map/psum | solution.py:69
  1068.4 1.6 broadcast_multiply_fusion
  1070.0 1.2 fusion.57
  1071.2 1.3 fusion.59
  1074.9 1.3 copy.17
  1076.2 3.8 collective-permute-start.7
  1080.1 1.3 fusion.65
  1081.3 1.3 fusion.67
  1082.6 1.3 fusion.69
  1085.0 2.3 slice.909
  1087.3 2.4 copy.21
  1090.0 2.2 copy.18
  1092.2 2.9 add_convert_fusion
  (129 shorter events, 26.2 us)
Async XLA Ops:
  7.2 5.9 copy-start
  7.2 5.9 copy-start.8
  7.2 10.2 copy-start.13
  7.2 1061.2 %all-reduce.2.cloned.1.call-start = ((), (), s32[]{:S(2)}) async-start(), calls=%async_computation | async-start | bytes 262144 | tf_op jit(solution)/shard_map/psum | solution.py:69
  8.5 13.4 %collective-permute-start = (bf16[2,192,1024]{2,1,0:T(8,128)(2,1)S(1)}, bf16[2,192,1024]{2,1,0:T(8,128)(2,1)S(1)}, u32[]{:S(2)}, u32[]{:S(2)}) collective-permute-start(bf16[2,192,1024]{2,1,0:T(8,128)(2,1)S(1)} %pad_maximum_fusion.2), channel_id=1, source_target_pairs={{0,2},{2,4},{4,6},{6,8},{8,10},{10,12},{12,14},{14,16},{16,18},{18... | collective-permute-start | bytes 2359304 | tf_op jit(solution)/shard_map/ppermute | solution.py:27
  13.1 13.3 %collective-permute-start.3 = (bf16[2,15,1024]{2,1,0:T(8,128)(2,1)S(1)}, bf16[2,15,1024]{2,1,0:T(8,128)(2,1)S(1)}, u32[]{:S(2)}, u32[]{:S(2)}) collective-permute-start(bf16[2,15,1024]{2,1,0:T(8,128)(2,1)S(1)} %get-tuple-element.52), channel_id=1, source_target_pairs={{0,2},{2,4},{4,6},{6,8},{8,10},{10,12},{12,14},{14,16},{16,18},{18... | collective-permute-start | bytes 184328 | tf_op jit(solution)/shard_map/ppermute | solution.py:16
  15.0 11.4 %collective-permute-start.4 = (bf16[2,15,1024]{2,1,0:T(8,128)(2,1)S(1)}, bf16[2,15,1024]{2,1,0:T(8,128)(2,1)S(1)}, u32[]{:S(2)}, u32[]{:S(2)}) collective-permute-start(bf16[2,15,1024]{2,1,0:T(8,128)(2,1)S(1)} %get-tuple-element.53), channel_id=1, source_target_pairs={{2,0},{4,2},{6,4},{8,6},{10,8},{12,10},{14,12},{16,14},{18,16},{20... | collective-permute-start | bytes 184328 | tf_op jit(solution)/shard_map/ppermute | solution.py:19
  21.9 13.3 %collective-permute-start.1 = (bf16[2,192,1024]{2,1,0:T(8,128)(2,1)S(1)}, bf16[2,192,1024]{2,1,0:T(8,128)(2,1)S(1)}, u32[]{:S(2)}, u32[]{:S(2)}) collective-permute-start(bf16[2,192,1024]{2,1,0:T(8,128)(2,1)S(1)} %collective-permute-done), channel_id=1, source_target_pairs={{0,2},{2,4},{4,6},{6,8},{8,10},{10,12},{12,14},{14,16},{16,18},{18... | collective-permute-start | bytes 2359304 | tf_op jit(solution)/shard_map/ppermute | solution.py:27
  35.2 29.1 %collective-permute-start.2 = (bf16[2,192,1024]{2,1,0:T(8,128)(2,1)S(1)}, bf16[2,192,1024]{2,1,0:T(8,128)(2,1)S(1)}, u32[]{:S(2)}, u32[]{:S(2)}) collective-permute-start(bf16[2,192,1024]{2,1,0:T(8,128)(2,1)S(1)} %collective-permute-done.1), channel_id=1, source_target_pairs={{0,2},{2,4},{4,6},{6,8},{8,10},{10,12},{12,14},{14,16},{16,18},{18... | collective-permute-start | bytes 2359304 | tf_op jit(solution)/shard_map/ppermute | solution.py:27
  39.6 23.2 %copy-start.14 = (bf16[1024,2048]{1,0:T(8,128)(2,1)S(1)}, bf16[1024,2048]{1,0:T(8,128)(2,1)}, u32[]{:S(2)}) copy-start(bf16[1024,2048]{1,0:T(8,128)(2,1)} %param.13) | copy-start | bytes 12582916
  42.8 21.6 %copy-start.12 = (bf16[192,1024]{1,0:T(8,128)(2,1)}, bf16[192,1024]{1,0:T(8,128)(2,1)S(1)}, u32[]{:S(2)}) copy-start(bf16[192,1024]{1,0:T(8,128)(2,1)S(1)} %fusion.80) | copy-start | bytes 1179652
  62.8 1.6 copy-start.10
  65.3 3.3 copy-start.11
  75.4 6.3 copy-start.17
  75.6 5.7 copy-start.19
  75.9 5.2 copy-start.20
  76.2 4.7 copy-start.21
  76.5 4.1 copy-start.22
  76.7 3.6 copy-start.24
  77.0 3.0 copy-start.26
  77.3 2.5 copy-start.27
  79.8 2.1 copy-start.2
  85.9 30.4 %collective-permute-start.5 = (bf16[2,576,1024]{2,1,0:T(8,128)(2,1)}, bf16[2,576,1024]{2,1,0:T(8,128)(2,1)S(1)}, u32[]{:S(2)}, u32[]{:S(2)}) collective-permute-start(bf16[2,576,1024]{2,1,0:T(8,128)(2,1)} %copy.14), channel_id=1, source_target_pairs={{2,0},{4,2},{6,4},{8,6},{10,8},{12,10},{14,12},{16,14},{18,16},{20... | collective-permute-start | bytes 7077896 | tf_op jit(solution)/shard_map/ppermute | solution.py:27
  117.8 3.6 copy-start.1
  119.5 955.3 %collective-permute-start.6 = (bf16[2,384,1024]{1,2,0:T(8,128)(2,1)}, bf16[2,384,1024]{1,2,0:T(8,128)(2,1)S(1)}, u32[]{:S(2)}, u32[]{:S(2)}) collective-permute-start(bf16[2,384,1024]{1,2,0:T(8,128)(2,1)} %copy.22), channel_id=1, source_target_pairs={{2,0},{4,2},{6,4},{8,6},{10,8},{12,10},{14,12},{16,14},{18,16},{20... | collective-permute-start | bytes 4718600 | tf_op jit(solution)/shard_map/ppermute | solution.py:27
  122.5 949.9 %copy-start.25 = (bf16[192,768]{1,0:T(8,128)(2,1)S(1)}, bf16[192,768]{1,0:T(8,128)(2,1)}, u32[]{:S(2)}) copy-start(bf16[192,768]{1,0:T(8,128)(2,1)} %copy-done.24) | copy-start | bytes 884740
  122.6 951.1 %copy-start.23 = (bf16[192,768]{1,0:T(8,128)(2,1)S(1)}, bf16[192,768]{1,0:T(8,128)(2,1)}, u32[]{:S(2)}) copy-start(bf16[192,768]{1,0:T(8,128)(2,1)} %copy-done.22) | copy-start | bytes 884740
  1076.2 7.6 copy-start.18
  1076.2 13.7 %collective-permute-start.7 = (bf16[2,192,1024]{2,1,0:T(8,128)(2,1)}, bf16[2,192,1024]{2,1,0:T(8,128)(2,1)}, u32[]{:S(2)}, u32[]{:S(2)}) collective-permute-start(bf16[2,192,1024]{2,1,0:T(8,128)(2,1)} %copy.17), channel_id=1, source_target_pairs={{2,0},{4,2},{6,4},{8,6},{10,8},{12,10},{14,12},{16,14},{18,16},{20... | collective-permute-start | bytes 2359304 | tf_op jit(solution)/shard_map/ppermute | solution.py:27
  1085.0 4.6 copy-start.16
  1087.3 4.9 copy-start.3
  1087.3 4.9 copy-start.5
  (5 other events, 6.6 us)
Sparse Core Ops, SparseCore 0:
  125.4 942.9 all-reduce.1
where the time goes:
time: 1100 us
  waiting for transfers between devices  982 us (89%)
  starting transfers between devices  25.2 us (2%)
  matrix products  24.8 us (2%)
  local copies, waits for them, and re-layouts  21 us (2%)
  blocking collectives  20 us (2%)
  other arithmetic  16.3 us (1%)
  between operations  14.8 us (1%)
    psum x1, waiting for transfers between devices, per_device(): kernel_grad = lax.psum(jnp.stack(tap_rows), 'ctx') / math.sqrt(total_frames)  943 us
    ppermute x6, waiting for transfers between devices, shifted(): return lax.ppermute(shard, axis, pairs)  38.6 us
  transfers between devices with their start and end apart: 9, of which 5 were waited for; matrix products, arithmetic and copies ran while one was open for 3% of the time, Pallas kernels for 0%

commit v1 on v0

--- a/solution.py
+++ b/solution.py
@@ -25,6 +25,19 @@
     count = lax.axis_size(axis)
     pairs = [(i, i + by) for i in range(count) if 0 <= i + by < count]
     return lax.ppermute(shard, axis, pairs)
+
+
+def exchanged(part, by):
+    count = lax.axis_size("ctx")
+    return lax.ppermute(part, "ctx", [(i, i ^ by) for i in range(count)])
+
+
+def summed(part):
+    part = part + exchanged(part, 1)
+    for low in (2, 8, 32):
+        one, two, three = (exchanged(part, low * k) for k in (1, 2, 3))
+        part = (part + one) + (two + three)
+    return part
 
 
 def head_grads(qh, kh, vh, doh, valid, scale):
@@ -66,7 +79,7 @@
         conv_back = conv_back + taps[tap] * grad_pad[2 * reach - tap : 2 * reach - tap + block]
         tap_rows.append(jnp.sum(grad_f * input_pad[tap : tap + block], axis=0))
     total_frames = block * lax.axis_size("ctx")
-    kernel_grad = lax.psum(jnp.stack(tap_rows), "ctx") / math.sqrt(total_frames)
+    kernel_grad = summed(jnp.stack(tap_rows)) / math.sqrt(total_frames)
     grad_stream = (grad_f + conv_back).astype(jnp.bfloat16)
     full_stream = lax.all_gather(grad_stream, "tp", axis=1, tiled=True)
     out_grad = lax.dot_general(

time: 1100 us -> 191 us (0.17)
  the two profiles are of different devices: /device:TPU:1 before, /device:TPU:15 now
where the time goes in v1:
time: 191 us; the launch traced here: 190 us
  starting transfers between devices  69.8 us (37%)
  waiting for transfers between devices  51.1 us (27%)
  matrix products  23.8 us (12%)
  local copies, waits for them, and re-layouts  18.8 us (10%)
  other arithmetic  16.3 us (9%)
  blocking collectives  8.81 us (5%)
    ppermute x10, starting transfers between devices, exchanged(): return lax.ppermute(part, 'ctx', [(i, i ^ by) for i in range(count)])  38.8 us
    ppermute x6, waiting for transfers between devices, shifted(): return lax.ppermute(shard, axis, pairs)  29.2 us
    ppermute x6, starting transfers between devices, shifted(): return lax.ppermute(shard, axis, pairs)  26.7 us
    ppermute x10, waiting for transfers between devices, exchanged(): return lax.ppermute(part, 'ctx', [(i, i ^ by) for i in range(count)])  22 us
    all_gather x1, blocking collectives, per_device(): full_stream = lax.all_gather(grad_stream, 'tp', axis=1, tiled=True)  8.81 us
    dot_general x8, matrix products, head_grads(): jnp.dot(score_grad, kh, preferred_element_type=jnp.float32) * scale  8.68 us
    unnamed x62, local copies, waits for them, and re-layouts  8.2 us
    reduce_sum x2, other arithmetic, per_device(): tap_rows.append(jnp.sum(grad_f * input_pad[tap:tap + block], axis=0))  4.08 us
  transfers between devices with their start and end apart: 18, of which 12 were waited for; matrix products, arithmetic and copies ran while one was open for 14% of the time, Pallas kernels for 0%

profile of v1, /device:TPU:15, one launch (start us, length us, event | category | flops | bytes accessed | tf_op | source)
XLA Modules:
  0.0 190.2 jit_solution(12047146593493905280)
XLA Ops:
  0.7 1.3 pad_maximum_fusion.2
  1.9 3.9 %collective-permute-start = (bf16[2,192,1024]{2,1,0:T(8,128)(2,1)S(1)}, bf16[2,192,1024]{2,1,0:T(8,128)(2,1)S(1)}, u32[]{:S(2)}, u32[]{:S(2)}) collective-permute-start(bf16[2,192,1024]{2,1,0:T(8,128)(2,1)S(1)} %pad_maximum_fusion.2), channel_id=1, source_target_pairs={{0,2},{2,4},{4,6},{6,8},{8,10},{10,12},{12,14},{14,16},{16,18},{18... | collective-permute-start | bytes 2359304 | tf_op jit(solution)/shard_map/ppermute | solution.py:27
  5.9 1.9 %collective-permute-start.3 = (bf16[2,15,1024]{2,1,0:T(8,128)(2,1)S(1)}, bf16[2,15,1024]{2,1,0:T(8,128)(2,1)S(1)}, u32[]{:S(2)}, u32[]{:S(2)}) collective-permute-start(bf16[2,15,1024]{2,1,0:T(8,128)(2,1)S(1)} %get-tuple-element.52), channel_id=1, source_target_pairs={{0,2},{2,4},{4,6},{6,8},{8,10},{10,12},{12,14},{14,16},{16,18},{18... | collective-permute-start | bytes 184328 | tf_op jit(solution)/shard_map/ppermute | solution.py:16
  7.8 2.4 %collective-permute-start.4 = (bf16[2,15,1024]{2,1,0:T(8,128)(2,1)S(1)}, bf16[2,15,1024]{2,1,0:T(8,128)(2,1)S(1)}, u32[]{:S(2)}, u32[]{:S(2)}) collective-permute-start(bf16[2,15,1024]{2,1,0:T(8,128)(2,1)S(1)} %get-tuple-element.53), channel_id=1, source_target_pairs={{2,0},{4,2},{6,4},{8,6},{10,8},{12,10},{14,12},{16,14},{18,16},{20... | collective-permute-start | bytes 184328 | tf_op jit(solution)/shard_map/ppermute | solution.py:19
  10.3 4.5 %collective-permute-done = bf16[2,192,1024]{2,1,0:T(8,128)(2,1)S(1)} collective-permute-done((bf16[2,192,1024]{2,1,0:T(8,128)(2,1)S(1)}, bf16[2,192,1024]{2,1,0:T(8,128)(2,1)S(1)}, u32[]{:S(2)}, u32[]{:S(2)}) %collective-permute-start) | collective-permute-done | bytes 786464 | tf_op jit(solution)/shard_map/ppermute | solution.py:27
  14.8 7.4 %collective-permute-start.1 = (bf16[2,192,1024]{2,1,0:T(8,128)(2,1)S(1)}, bf16[2,192,1024]{2,1,0:T(8,128)(2,1)S(1)}, u32[]{:S(2)}, u32[]{:S(2)}) collective-permute-start(bf16[2,192,1024]{2,1,0:T(8,128)(2,1)S(1)} %collective-permute-done), channel_id=1, source_target_pairs={{0,2},{2,4},{4,6},{6,8},{8,10},{10,12},{12,14},{14,16},{16,18},{18... | collective-permute-start | bytes 2359304 | tf_op jit(solution)/shard_map/ppermute | solution.py:27
  22.6 8.4 %collective-permute-done.1 = bf16[2,192,1024]{2,1,0:T(8,128)(2,1)S(1)} collective-permute-done((bf16[2,192,1024]{2,1,0:T(8,128)(2,1)S(1)}, bf16[2,192,1024]{2,1,0:T(8,128)(2,1)S(1)}, u32[]{:S(2)}, u32[]{:S(2)}) %collective-permute-start.1) | collective-permute-done | bytes 786464 | tf_op jit(solution)/shard_map/ppermute | solution.py:27
  31.1 7.4 %collective-permute-start.2 = (bf16[2,192,1024]{2,1,0:T(8,128)(2,1)S(1)}, bf16[2,192,1024]{2,1,0:T(8,128)(2,1)S(1)}, u32[]{:S(2)}, u32[]{:S(2)}) collective-permute-start(bf16[2,192,1024]{2,1,0:T(8,128)(2,1)S(1)} %collective-permute-done.1), channel_id=1, source_target_pairs={{0,2},{2,4},{4,6},{6,8},{8,10},{10,12},{12,14},{14,16},{16,18},{18... | collective-permute-start | bytes 2359304 | tf_op jit(solution)/shard_map/ppermute | solution.py:27
  38.5 3.1 %fusion.80 = bf16[192,1024]{1,0:T(8,128)(2,1)S(1)} fusion(bf16[192,1024]{1,0:T(8,128)(2,1)S(1)} %copy-done, f32[1,222,1024]{2,1,0:T(8,128)S(1)} %get-tuple-element.51, f32[1024]{0:T(1024)S(1)} %bitcast.550, f32[1024]{0:T(1024)S(1)} %bitcast.549, f32[1024]{0:T(1024)S(1)} %bitcast.548, f32[1024]{0:T(1024)S(1)} %bitcast.547, f32[1024]{0:T(1024)S(1)} %bitcast.546, ...), kind=kLoop, calls=%fused_computation.167 | loop fusion | flops 12582912 | bytes 25292800 | tf_op jit(solution)/shard_map/convert_element_type | solution.py:83
  41.6 8.8 %all_gather.3 = bf16[192,2048]{1,0:T(8,128)(2,1)S(1)} all-gather(bf16[192,1024]{1,0:T(8,128)(2,1)S(1)} %fusion.80), channel_id=1, replica_groups=mesh['ctx'=128,'tp'=2] {'tp'}, dimensions={1}, use_global_device_ids=true | all-gather | bytes 1179648 | tf_op jit(solution)/shard_map/all_gather | solution.py:84
  50.4 1.6 convolution_convert_fusion
  70.9 2.6 %copy.14 = bf16[2,576,1024]{2,1,0:T(8,128)(2,1)} copy(bf16[2,576,1024]{1,2,0:T(8,128)(2,1)S(1)} %pad_maximum_fusion) | data formatting | bytes 4718592 | tf_op jit(solution)/shard_map/slice | solution.py:118
  73.5 2.1 %collective-permute-start.5 = (bf16[2,576,1024]{2,1,0:T(8,128)(2,1)}, bf16[2,576,1024]{2,1,0:T(8,128)(2,1)}, u32[]{:S(2)}, u32[]{:S(2)}) collective-permute-start(bf16[2,576,1024]{2,1,0:T(8,128)(2,1)} %copy.14), channel_id=1, source_target_pairs={{2,0},{4,2},{6,4},{8,6},{10,8},{12,10},{14,12},{16,14},{18,16},{20... | collective-permute-start | bytes 7077896 | tf_op jit(solution)/shard_map/ppermute | solution.py:27
  75.7 2.2 %fusion.110 = (f32[1024]{0:T(1024)S(1)}, f32[1024]{0:T(1024)S(1)}, f32[1024]{0:T(1024)S(1)}, f32[1024]{0:T(1024)S(1)}, f32[1024]{0:T(1024)S(1)}, /*index=5*/f32[...) fusion(bf16[192,1024]{1,0:T(8,128)(2,1)} %param.10, ...), kind=kLoop, calls=%fused_computation.197 | loop fusion | flops 5295104 | bytes 10670080 | tf_op jit(solution)/shard_map/reduce_sum | solution.py:80
  77.9 1.9 fusion.111
  80.1 1.3 collective-permute-done.8
  82.7 2.1 %collective-permute-start.9 = (f32[31,1024]{1,0:T(8,128)S(1)}, f32[31,1024]{1,0:T(8,128)S(1)}, u32[]{:S(2)}, u32[]{:S(2)}) collective-permute-start(f32[31,1024]{1,0:T(8,128)S(1)} %add.179), channel_id=1, source_target_pairs={{0,4},{2,6},{4,0},{6,2},{8,12},{10,14},{12,8},{14,10},{16,20},{18,... | collective-permute-start | bytes 380936 | tf_op jit(solution)/shard_map/ppermute | solution.py:32
  84.8 4.6 %collective-permute-done.11 = f32[31,1024]{1,0:T(8,128)S(1)} collective-permute-done((f32[31,1024]{1,0:T(8,128)S(1)}, f32[31,1024]{1,0:T(8,128)S(1)}, u32[]{:S(2)}, u32[]{:S(2)}) %collective-permute-start.11) | collective-permute-done | bytes 127008 | tf_op jit(solution)/shard_map/ppermute | solution.py:32
  89.5 1.3 collective-permute-done.9
  90.9 27.4 %collective-permute-start.14 = (f32[31,1024]{1,0:T(8,128)S(1)}, f32[31,1024]{1,0:T(8,128)S(1)}, u32[]{:S(2)}, u32[]{:S(2)}) collective-permute-start(f32[31,1024]{1,0:T(8,128)S(1)} %add_add_fusion.1), channel_id=1, source_target_pairs={{0,48},{2,50},{4,52},{6,54},{8,56},{10,58},{12,60},{14,62},{16,32}... | collective-permute-start | bytes 380936 | tf_op jit(solution)/shard_map/ppermute | solution.py:32
  118.6 1.5 slice.910
  121.0 3.0 %collective-permute-start.6 = (bf16[2,384,1024]{1,2,0:T(8,128)(2,1)S(1)}, bf16[2,384,1024]{1,2,0:T(8,128)(2,1)S(1)}, u32[]{:S(2)}, u32[]{:S(2)}) collective-permute-start(bf16[2,384,1024]{1,2,0:T(8,128)(2,1)S(1)} %copy.22), channel_id=1, source_target_pairs={{2,0},{4,2},{6,4},{8,6},{10,8},{12,10},{14,12},{16,14},{18,16},{20... | collective-permute-start | bytes 4718600 | tf_op jit(solution)/shard_map/ppermute | solution.py:27
  125.9 5.3 %collective-permute-start.17 = (f32[31,1024]{1,0:T(8,128)S(1)}, f32[31,1024]{1,0:T(8,128)S(1)}, u32[]{:S(2)}, u32[]{:S(2)}) collective-permute-start(f32[31,1024]{1,0:T(8,128)S(1)} %add_add_fusion), channel_id=1, source_target_pairs={{0,192},{2,194},{4,196},{6,198},{8,200},{10,202},{12,204},{14,206}... | collective-permute-start | bytes 380936 | tf_op jit(solution)/shard_map/ppermute | solution.py:32
  131.2 2.4 %collective-permute-start.16 = (f32[31,1024]{1,0:T(8,128)S(1)}, f32[31,1024]{1,0:T(8,128)S(1)}, u32[]{:S(2)}, u32[]{:S(2)}) collective-permute-start(f32[31,1024]{1,0:T(8,128)S(1)} %add_add_fusion), channel_id=1, source_target_pairs={{0,128},{2,130},{4,132},{6,134},{8,136},{10,138},{12,140},{14,142}... | collective-permute-start | bytes 380936 | tf_op jit(solution)/shard_map/ppermute | solution.py:32
  134.6 8.7 %collective-permute-done.16 = f32[31,1024]{1,0:T(8,128)S(1)} collective-permute-done((f32[31,1024]{1,0:T(8,128)S(1)}, f32[31,1024]{1,0:T(8,128)S(1)}, u32[]{:S(2)}, u32[]{:S(2)}) %collective-permute-start.16) | collective-permute-done | bytes 127008 | tf_op jit(solution)/shard_map/ppermute | solution.py:32
  143.4 3.9 %collective-permute-done.15 = f32[31,1024]{1,0:T(8,128)S(1)} collective-permute-done((f32[31,1024]{1,0:T(8,128)S(1)}, f32[31,1024]{1,0:T(8,128)S(1)}, u32[]{:S(2)}, u32[]{:S(2)}) %collective-permute-start.15) | collective-permute-done | bytes 127008 | tf_op jit(solution)/shard_map/ppermute | solution.py:32
  155.3 2.9 %collective-permute-start.7 = (bf16[2,192,1024]{2,1,0:T(8,128)(2,1)}, bf16[2,192,1024]{2,1,0:T(8,128)(2,1)}, u32[]{:S(2)}, u32[]{:S(2)}) collective-permute-start(bf16[2,192,1024]{2,1,0:T(8,128)(2,1)} %copy.17), channel_id=1, source_target_pairs={{2,0},{4,2},{6,4},{8,6},{10,8},{12,10},{14,12},{16,14},{18,16},{20... | collective-permute-start | bytes 2359304 | tf_op jit(solution)/shard_map/ppermute | solution.py:27
  162.1 2.3 %slice.909 = bf16[2,192,1024]{2,1,0:T(8,128)(2,1)} slice(bf16[2,576,1024]{2,1,0:T(8,128)(2,1)} %collective-permute-done.5), slice={[0:2], [384:576], [0:1024]} | slice | bytes 1572864 | tf_op jit(solution)/shard_map/slice | solution.py:121
  164.4 2.4 %copy.21 = bf16[2,192,1024]{1,2,0:T(8,128)(2,1)} copy(bf16[2,192,1024]{2,1,0:T(8,128)(2,1)} %slice.909) | data formatting | bytes 1572864
  166.8 16.3 %collective-permute-done.7 = bf16[2,192,1024]{2,1,0:T(8,128)(2,1)} collective-permute-done((bf16[2,192,1024]{2,1,0:T(8,128)(2,1)}, bf16[2,192,1024]{2,1,0:T(8,128)(2,1)}, u32[]{:S(2)}, u32[]{:S(2)}) %collective-permute-start.7) | collective-permute-done | bytes 786464 | tf_op jit(solution)/shard_map/ppermute | solution.py:27
  183.1 2.2 %copy.18 = bf16[2,192,1024]{1,2,0:T(8,128)(2,1)} copy(bf16[2,192,1024]{2,1,0:T(8,128)(2,1)} %collective-permute-done.7) | data formatting | bytes 1572864 | tf_op jit(solution)/shard_map/ppermute | solution.py:27
  185.3 2.9 %add_convert_fusion = bf16[2,192,1024]{1,2,0:T(8,128)(2,1)S(1)} fusion(bf16[2,192,1024]{1,2,0:T(8,128)(2,1)} %copy.18, bf16[2,192,1024]{1,2,0:T(8,128)(2,1)} %copy.21, bf16[2,384,1024]{1,2,0:T(8,128)(2,1)} %copy-done.6, bf16[1,768,1024]{1,2,0:T(8,128)(2,1)S(1)} %bitcast.499, bf16[1,768,1024]{1,2,0:T(8,128)(2,1)S(1)} %bitcast.501), kind=kLoop, calls=%fused_computation.34 | loop fusion | flops 4325376 | bytes 6291456 | tf_op jit(solution)/shard_map/convert.1
  (151 shorter events, 38.8 us)
Async XLA Ops:
  0.6 5.2 %copy-start = (bf16[192,1024]{1,0:T(8,128)(2,1)S(1)}, bf16[192,1024]{1,0:T(8,128)(2,1)}, u32[]{:S(2)}) copy-start(bf16[192,1024]{1,0:T(8,128)(2,1)} %param.10) | copy-start | bytes 1179652
  0.6 5.2 %copy-start.7 = (bf16[192,1024]{1,0:T(8,128)(2,1)S(1)}, bf16[192,1024]{1,0:T(8,128)(2,1)}, u32[]{:S(2)}) copy-start(bf16[192,1024]{1,0:T(8,128)(2,1)} %param.11) | copy-start | bytes 1179652
  0.7 9.6 %copy-start.13 = (bf16[31,1024]{1,0:T(8,128)(2,1)S(1)}, bf16[31,1024]{1,0:T(8,128)(2,1)}, u32[]{:S(2)}) copy-start(bf16[31,1024]{1,0:T(8,128)(2,1)} %param.12) | copy-start | bytes 190468
  1.9 12.8 %collective-permute-start = (bf16[2,192,1024]{2,1,0:T(8,128)(2,1)S(1)}, bf16[2,192,1024]{2,1,0:T(8,128)(2,1)S(1)}, u32[]{:S(2)}, u32[]{:S(2)}) collective-permute-start(bf16[2,192,1024]{2,1,0:T(8,128)(2,1)S(1)} %pad_maximum_fusion.2), channel_id=1, source_target_pairs={{0,2},{2,4},{4,6},{6,8},{8,10},{10,12},{12,14},{14,16},{16,18},{18... | collective-permute-start | bytes 2359304 | tf_op jit(solution)/shard_map/ppermute | solution.py:27
  5.9 16.4 %collective-permute-start.3 = (bf16[2,15,1024]{2,1,0:T(8,128)(2,1)S(1)}, bf16[2,15,1024]{2,1,0:T(8,128)(2,1)S(1)}, u32[]{:S(2)}, u32[]{:S(2)}) collective-permute-start(bf16[2,15,1024]{2,1,0:T(8,128)(2,1)S(1)} %get-tuple-element.52), channel_id=1, source_target_pairs={{0,2},{2,4},{4,6},{6,8},{8,10},{10,12},{12,14},{14,16},{16,18},{18... | collective-permute-start | bytes 184328 | tf_op jit(solution)/shard_map/ppermute | solution.py:16
  7.8 14.4 %collective-permute-start.4 = (bf16[2,15,1024]{2,1,0:T(8,128)(2,1)S(1)}, bf16[2,15,1024]{2,1,0:T(8,128)(2,1)S(1)}, u32[]{:S(2)}, u32[]{:S(2)}) collective-permute-start(bf16[2,15,1024]{2,1,0:T(8,128)(2,1)S(1)} %get-tuple-element.53), channel_id=1, source_target_pairs={{2,0},{4,2},{6,4},{8,6},{10,8},{12,10},{14,12},{16,14},{18,16},{20... | collective-permute-start | bytes 184328 | tf_op jit(solution)/shard_map/ppermute | solution.py:19
  14.8 16.3 %collective-permute-start.1 = (bf16[2,192,1024]{2,1,0:T(8,128)(2,1)S(1)}, bf16[2,192,1024]{2,1,0:T(8,128)(2,1)S(1)}, u32[]{:S(2)}, u32[]{:S(2)}) collective-permute-start(bf16[2,192,1024]{2,1,0:T(8,128)(2,1)S(1)} %collective-permute-done), channel_id=1, source_target_pairs={{0,2},{2,4},{4,6},{6,8},{8,10},{10,12},{12,14},{14,16},{16,18},{18... | collective-permute-start | bytes 2359304 | tf_op jit(solution)/shard_map/ppermute | solution.py:27
  31.1 21.0 %collective-permute-start.2 = (bf16[2,192,1024]{2,1,0:T(8,128)(2,1)S(1)}, bf16[2,192,1024]{2,1,0:T(8,128)(2,1)S(1)}, u32[]{:S(2)}, u32[]{:S(2)}) collective-permute-start(bf16[2,192,1024]{2,1,0:T(8,128)(2,1)S(1)} %collective-permute-done.1), channel_id=1, source_target_pairs={{0,2},{2,4},{4,6},{6,8},{8,10},{10,12},{12,14},{14,16},{16,18},{18... | collective-permute-start | bytes 2359304 | tf_op jit(solution)/shard_map/ppermute | solution.py:27
  38.5 12.0 %copy-start.14 = (bf16[1024,2048]{1,0:T(8,128)(2,1)S(1)}, bf16[1024,2048]{1,0:T(8,128)(2,1)}, u32[]{:S(2)}) copy-start(bf16[1024,2048]{1,0:T(8,128)(2,1)} %param.13) | copy-start | bytes 12582916
  41.6 10.4 %copy-start.12 = (bf16[192,1024]{1,0:T(8,128)(2,1)}, bf16[192,1024]{1,0:T(8,128)(2,1)S(1)}, u32[]{:S(2)}) copy-start(bf16[192,1024]{1,0:T(8,128)(2,1)S(1)} %fusion.80) | copy-start | bytes 1179652
  63.0 6.3 %copy-start.17 = (bf16[192,768]{1,0:T(8,128)(2,1)}, bf16[192,768]{1,0:T(8,128)(2,1)S(1)}, u32[]{:S(2)}) copy-start(bf16[192,768]{1,0:T(8,128)(2,1)S(1)} %fusion.24) | copy-start | bytes 884740
  63.3 5.7 %copy-start.19 = (bf16[192,768]{1,0:T(8,128)(2,1)}, bf16[192,768]{1,0:T(8,128)(2,1)S(1)}, u32[]{:S(2)}) copy-start(bf16[192,768]{1,0:T(8,128)(2,1)S(1)} %fusion.25) | copy-start | bytes 884740
  63.6 5.2 %copy-start.20 = (bf16[192,768]{1,0:T(8,128)(2,1)}, bf16[192,768]{1,0:T(8,128)(2,1)S(1)}, u32[]{:S(2)}) copy-start(bf16[192,768]{1,0:T(8,128)(2,1)S(1)} %fusion.26) | copy-start | bytes 884740
  73.5 45.1 %collective-permute-start.5 = (bf16[2,576,1024]{2,1,0:T(8,128)(2,1)}, bf16[2,576,1024]{2,1,0:T(8,128)(2,1)}, u32[]{:S(2)}, u32[]{:S(2)}) collective-permute-start(bf16[2,576,1024]{2,1,0:T(8,128)(2,1)} %copy.14), channel_id=1, source_target_pairs={{2,0},{4,2},{6,4},{8,6},{10,8},{12,10},{14,12},{16,14},{18,16},{20... | collective-permute-start | bytes 7077896 | tf_op jit(solution)/shard_map/ppermute | solution.py:27
  80.0 1.4 collective-permute-start.8
  81.5 7.9 %collective-permute-start.11 = (f32[31,1024]{1,0:T(8,128)S(1)}, f32[31,1024]{1,0:T(8,128)S(1)}, u32[]{:S(2)}, u32[]{:S(2)}) collective-permute-start(f32[31,1024]{1,0:T(8,128)S(1)} %add.179), channel_id=1, source_target_pairs={{0,12},{2,14},{4,8},{6,10},{8,4},{10,6},{12,0},{14,2},{16,28},{18,... | collective-permute-start | bytes 380936 | tf_op jit(solution)/shard_map/ppermute | solution.py:32
  82.7 6.8 %collective-permute-start.10 = (f32[31,1024]{1,0:T(8,128)S(1)}, f32[31,1024]{1,0:T(8,128)S(1)}, u32[]{:S(2)}, u32[]{:S(2)}) collective-permute-start(f32[31,1024]{1,0:T(8,128)S(1)} %add.179), channel_id=1, source_target_pairs={{0,8},{2,10},{4,12},{6,14},{8,0},{10,2},{12,4},{14,6},{16,24},{18,... | collective-permute-start | bytes 380936 | tf_op jit(solution)/shard_map/ppermute | solution.py:32
  82.7 8.1 %collective-permute-start.9 = (f32[31,1024]{1,0:T(8,128)S(1)}, f32[31,1024]{1,0:T(8,128)S(1)}, u32[]{:S(2)}, u32[]{:S(2)}) collective-permute-start(f32[31,1024]{1,0:T(8,128)S(1)} %add.179), channel_id=1, source_target_pairs={{0,4},{2,6},{4,0},{6,2},{8,12},{10,14},{12,8},{14,10},{16,20},{18,... | collective-permute-start | bytes 380936 | tf_op jit(solution)/shard_map/ppermute | solution.py:32
  90.9 33.2 %collective-permute-start.14 = (f32[31,1024]{1,0:T(8,128)S(1)}, f32[31,1024]{1,0:T(8,128)S(1)}, u32[]{:S(2)}, u32[]{:S(2)}) collective-permute-start(f32[31,1024]{1,0:T(8,128)S(1)} %add_add_fusion.1), channel_id=1, source_target_pairs={{0,48},{2,50},{4,52},{6,54},{8,56},{10,58},{12,60},{14,62},{16,32}... | collective-permute-start | bytes 380936 | tf_op jit(solution)/shard_map/ppermute | solution.py:32
  118.2 5.9 %collective-permute-start.13 = (f32[31,1024]{1,0:T(8,128)S(1)}, f32[31,1024]{1,0:T(8,128)S(1)}, u32[]{:S(2)}, u32[]{:S(2)}) collective-permute-start(f32[31,1024]{1,0:T(8,128)S(1)} %add_add_fusion.1), channel_id=1, source_target_pairs={{0,32},{2,34},{4,36},{6,38},{8,40},{10,42},{12,44},{14,46},{16,48}... | collective-permute-start | bytes 380936 | tf_op jit(solution)/shard_map/ppermute | solution.py:32
  118.2 6.7 %collective-permute-start.12 = (f32[31,1024]{1,0:T(8,128)S(1)}, f32[31,1024]{1,0:T(8,128)}, u32[]{:S(2)}, u32[]{:S(2)}) collective-permute-start(f32[31,1024]{1,0:T(8,128)S(1)} %add_add_fusion.1), channel_id=1, source_target_pairs={{0,16},{2,18},{4,20},{6,22},{8,24},{10,26},{12,28},{14,30},{16,0},... | collective-permute-start | bytes 380936 | tf_op jit(solution)/shard_map/ppermute | solution.py:32
  121.0 28.2 %copy-start.27 = (bf16[192,768]{1,0:T(8,128)(2,1)S(1)}, bf16[192,768]{1,0:T(8,128)(2,1)}, u32[]{:S(2)}) copy-start(bf16[192,768]{1,0:T(8,128)(2,1)} %copy-done.26) | copy-start | bytes 884740
  121.0 29.4 %copy-start.25 = (bf16[192,768]{1,0:T(8,128)(2,1)S(1)}, bf16[192,768]{1,0:T(8,128)(2,1)}, u32[]{:S(2)}) copy-start(bf16[192,768]{1,0:T(8,128)(2,1)} %copy-done.24) | copy-start | bytes 884740
  121.0 30.5 %copy-start.23 = (bf16[192,768]{1,0:T(8,128)(2,1)S(1)}, bf16[192,768]{1,0:T(8,128)(2,1)}, u32[]{:S(2)}) copy-start(bf16[192,768]{1,0:T(8,128)(2,1)} %copy-done.22) | copy-start | bytes 884740
  121.0 31.7 %collective-permute-start.6 = (bf16[2,384,1024]{1,2,0:T(8,128)(2,1)S(1)}, bf16[2,384,1024]{1,2,0:T(8,128)(2,1)S(1)}, u32[]{:S(2)}, u32[]{:S(2)}) collective-permute-start(bf16[2,384,1024]{1,2,0:T(8,128)(2,1)S(1)} %copy.22), channel_id=1, source_target_pairs={{2,0},{4,2},{6,4},{8,6},{10,8},{12,10},{14,12},{16,14},{18,16},{20... | collective-permute-start | bytes 4718600 | tf_op jit(solution)/shard_map/ppermute | solution.py:27
  125.9 8.7 %collective-permute-start.17 = (f32[31,1024]{1,0:T(8,128)S(1)}, f32[31,1024]{1,0:T(8,128)S(1)}, u32[]{:S(2)}, u32[]{:S(2)}) collective-permute-start(f32[31,1024]{1,0:T(8,128)S(1)} %add_add_fusion), channel_id=1, source_target_pairs={{0,192},{2,194},{4,196},{6,198},{8,200},{10,202},{12,204},{14,206}... | collective-permute-start | bytes 380936 | tf_op jit(solution)/shard_map/ppermute | solution.py:32
  131.2 12.2 %collective-permute-start.16 = (f32[31,1024]{1,0:T(8,128)S(1)}, f32[31,1024]{1,0:T(8,128)S(1)}, u32[]{:S(2)}, u32[]{:S(2)}) collective-permute-start(f32[31,1024]{1,0:T(8,128)S(1)} %add_add_fusion), channel_id=1, source_target_pairs={{0,128},{2,130},{4,132},{6,134},{8,136},{10,138},{12,140},{14,142}... | collective-permute-start | bytes 380936 | tf_op jit(solution)/shard_map/ppermute | solution.py:32
  133.5 13.7 %collective-permute-start.15 = (f32[31,1024]{1,0:T(8,128)S(1)}, f32[31,1024]{1,0:T(8,128)S(1)}, u32[]{:S(2)}, u32[]{:S(2)}) collective-permute-start(f32[31,1024]{1,0:T(8,128)S(1)} %add_add_fusion), channel_id=1, source_target_pairs={{0,64},{2,66},{4,68},{6,70},{8,72},{10,74},{12,76},{14,78},{16,80}... | collective-permute-start | bytes 380936 | tf_op jit(solution)/shard_map/ppermute | solution.py:32
  154.0 7.8 %copy-start.18 = (bf16[192,768]{1,0:T(8,128)(2,1)S(1)}, bf16[192,768]{1,0:T(8,128)(2,1)}, u32[]{:S(2)}) copy-start(bf16[192,768]{1,0:T(8,128)(2,1)} %copy-done.17) | copy-start | bytes 884740
  155.3 27.8 %collective-permute-start.7 = (bf16[2,192,1024]{2,1,0:T(8,128)(2,1)}, bf16[2,192,1024]{2,1,0:T(8,128)(2,1)}, u32[]{:S(2)}, u32[]{:S(2)}) collective-permute-start(bf16[2,192,1024]{2,1,0:T(8,128)(2,1)} %copy.17), channel_id=1, source_target_pairs={{2,0},{4,2},{6,4},{8,6},{10,8},{12,10},{14,12},{16,14},{18,16},{20... | collective-permute-start | bytes 2359304 | tf_op jit(solution)/shard_map/ppermute | solution.py:27
  164.4 20.9 %copy-start.3 = (bf16[768,1024]{0,1:T(8,128)(2,1)S(1)}, bf16[768,1024]{0,1:T(8,128)(2,1)}, u32[]{:S(2)}) copy-start(bf16[768,1024]{0,1:T(8,128)(2,1)} %copy-done.2) | copy-start | bytes 4718596
  164.4 20.9 %copy-start.5 = (bf16[768,1024]{0,1:T(8,128)(2,1)S(1)}, bf16[768,1024]{0,1:T(8,128)(2,1)}, u32[]{:S(2)}) copy-start(bf16[768,1024]{0,1:T(8,128)(2,1)} %copy-done.4) | copy-start | bytes 4718596
  (15 other events, 40.9 us)

commit v2 on v1

v2 whole, which is shorter than its diff:
```python
import functools
import math

import jax
import jax.numpy as jnp
from jax import lax
from jax.experimental import pallas as pl
from jax.experimental.pallas import tpu as pltpu
from jax.sharding import PartitionSpec as P

HEAD = 128
EDGE = 16
NT = (((1,), (1,)), ((), ()))
BIG = 1e30


def rotated(part, by):
    count = lax.axis_size("ctx")
    return lax.ppermute(part, "ctx", [(i, (i + by) % count) for i in range(count)])


def exchanged(part, by):
    count = lax.axis_size("ctx")
    return lax.ppermute(part, "ctx", [(i, i ^ by) for i in range(count)])


def summed(part):
    part = part + exchanged(part, 1)
    for low in (2, 8, 32):
        one, two, three = (exchanged(part, low * k) for k in (1, 2, 3))
        part = (part + one) + (two + three)
    return part


def conv_kernel(last, idx_ref, grad_ref, input_ref, low_ref, high_ref, taps_ref, out_ref, rows_ref, gpad, cpad):
    block = grad_ref.shape[0]
    taps_count = taps_ref.shape[0]
    reach = taps_count // 2
    device = idx_ref[0]
    f32 = jnp.float32
    low = jnp.where(device > 0, low_ref[...].astype(f32), 0.0)
    high = jnp.where(device < last, high_ref[...].astype(f32), 0.0)
    grad = grad_ref[...].astype(f32)
    cpad[:EDGE] = low[:EDGE]
    gpad[:EDGE] = low[EDGE:]
    cpad[EDGE : EDGE + block] = input_ref[...].astype(f32)
    gpad[EDGE : EDGE + block] = grad
    cpad[EDGE + block :] = high[:EDGE]
    gpad[EDGE + block :] = high[EDGE:]
    taps = taps_ref[...].astype(f32)
    total = jnp.zeros_like(grad)
    for tap in range(taps_count):
        total = total + taps[tap : tap + 1] * gpad[pl.ds(EDGE + reach - tap, block), :]
    out_ref[...] = (grad + total).astype(out_ref.dtype)
    for tap in range(taps_count):
        prod = grad * cpad[pl.ds(EDGE - reach + tap, block), :]
        rows_ref[tap : tap + 1, :] = jnp.sum(prod, axis=0, keepdims=True)


def conv(device, grad, inputs, low, high, taps, last):
    block, width = grad.shape
    count = taps.shape[0]
    lanes = 128
    column = lambda rows: pl.BlockSpec((rows, lanes), lambda c: (0, c))
    return pl.pallas_call(
        functools.partial(conv_kernel, last),
        grid=(width // lanes,),
        in_specs=[
            pl.BlockSpec(memory_space=pltpu.SMEM),
            column(block),
            column(block),
            column(2 * EDGE),
            column(2 * EDGE),
            column(count),
        ],
        out_specs=[column(block), column(count)],
        out_shape=[
            jax.ShapeDtypeStruct((block, width), jnp.bfloat16),
            jax.ShapeDtypeStruct((count, width), jnp.float32),
        ],
        scratch_shapes=[
            pltpu.VMEM((block + 2 * EDGE, lanes), jnp.float32),
            pltpu.VMEM((block + 2 * EDGE, lanes), jnp.float32),
        ],
        compiler_params=pltpu.CompilerParams(vmem_limit_bytes=8 * 2**20),
        cost_estimate=pl.CostEstimate(flops=8 * block * width * count, bytes_accessed=4 * block * width, transcendentals=0),
    )(device, grad, inputs, low, high, taps)


def project_kernel(idx_ref, own_ref, other_ref, weight_ref, out_ref):
    half = own_ref.shape[1]
    tp = idx_ref[0]
    first = weight_ref[:, pl.ds(pl.multiple_of(tp * half, half), half)]
    second = weight_ref[:, pl.ds(pl.multiple_of((1 - tp) * half, half), half)]
    total = lax.dot_general(own_ref[...], first, NT, preferred_element_type=jnp.float32)
    total = total + lax.dot_general(other_ref[...], second, NT, preferred_element_type=jnp.float32)
    out_ref[...] = total.astype(out_ref.dtype)


def project(tp, own, other, weight):
    block, half = own.shape
    rows, full = weight.shape
    step = 256
    return pl.pallas_call(
        project_kernel,
        grid=(rows // step,),
        in_specs=[
            pl.BlockSpec(memory_space=pltpu.SMEM),
            pl.BlockSpec((block, half), lambda n: (0, 0)),
            pl.BlockSpec((block, half), lambda n: (0, 0)),
            pl.BlockSpec((step, full), lambda n: (n, 0)),
        ],
        out_specs=pl.BlockSpec((block, step), lambda n: (0, n)),
        out_shape=jax.ShapeDtypeStruct((block, rows), jnp.bfloat16),
        compiler_params=pltpu.CompilerParams(vmem_limit_bytes=16 * 2**20),
        cost_estimate=pl.CostEstimate(flops=2 * block * rows * full, bytes_accessed=2 * rows * full, transcendentals=0),
    )(tp, own, other, weight)


def query_kernel(scale, idx_ref, q_ref, do_ref, k3, k2, k1, k0, v3, v2, v1, v0, out_ref, stats_ref, bias, columns):
    head = pl.program_id(0)
    heads = pl.num_programs(0)
    block = q_ref.shape[0]
    f32 = jnp.float32

    @pl.when(head == 0)
    def _():
        rows = lax.broadcasted_iota(jnp.int32, bias.shape, 0)
        cols = lax.broadcasted_iota(jnp.int32, bias.shape, 1)
        valid = (cols <= 3 * block + rows) & (cols >= (3 - idx_ref[0]) * block)
        bias[...] = jnp.where(valid, 0.0, -jnp.inf)
        columns[...] = jnp.zeros_like(columns)

    keys = jnp.concatenate([k3[...], k2[...], k1[...], k0[...]], axis=0)
    values = jnp.concatenate([v3[...], v2[...], v1[...], v0[...]], axis=0)
    do = do_ref[...]
    scores = lax.dot_general(q_ref[...], keys, NT, preferred_element_type=f32) * scale + bias[...]
    top = jnp.max(scores, axis=1, keepdims=True)
    expo = jnp.exp(scores - top)
    denom = jnp.sum(expo, axis=1, keepdims=True)
    probs = expo * (1.0 / denom)
    prob_grad = lax.dot_general(do, values, NT, preferred_element_type=f32)
    delta = jnp.sum(probs.astype(jnp.bfloat16).astype(f32) * prob_grad, axis=1, keepdims=True)
    score_grad = (probs * (prob_grad - delta)).astype(jnp.bfloat16)
    out = jnp.dot(score_grad, keys, preferred_element_type=f32) * scale
    out_ref[...] = out.astype(out_ref.dtype)
    lane = lax.broadcasted_iota(jnp.int32, columns.shape, 1)
    both = jnp.where(lane == head, top + jnp.log(denom), columns[...])
    columns[...] = jnp.where(lane == heads + head, delta, both)

    @pl.when(head == heads - 1)
    def _():
        stats_ref[...] = columns[...].T[: stats_ref.shape[0]]


def query_side(device, queries, out_grad, keys, values, scale):
    block, width = queries.shape
    heads = width // HEAD
    column = pl.BlockSpec((block, HEAD), lambda h: (0, h))
    return pl.pallas_call(
        functools.partial(query_kernel, scale),
        grid=(heads,),
        in_specs=[pl.BlockSpec(memory_space=pltpu.SMEM)] + [column] * 10,
        out_specs=[column, pl.BlockSpec((2 * heads, block), lambda h: (0, 0))],
        out_shape=[
            jax.ShapeDtypeStruct((block, width), jnp.bfloat16),
            jax.ShapeDtypeStruct((2 * heads, block), jnp.float32),
        ],
        scratch_shapes=[
            pltpu.VMEM((block, 4 * block), jnp.float32),
            pltpu.VMEM((block, HEAD), jnp.float32),
        ],
        compiler_params=pltpu.CompilerParams(vmem_limit_bytes=24 * 2**20),
        cost_estimate=pl.CostEstimate(
            flops=40 * block * block * width, bytes_accessed=24 * block * width, transcendentals=4 * block * block * heads
        ),
    )(device, queries, out_grad, *keys, *values)


def key_kernel(scale, last, idx_ref, k_ref, v_ref, q0, q1, q2, q3, d0, d1, d2, d3, s0, s1, s2, s3, dk_ref, dv_ref, bias, lse, delta):
    head = pl.program_id(0)
    heads = pl.num_programs(0)
    block = k_ref.shape[0]
    f32 = jnp.float32
    device = idx_ref[0]

    @pl.when(head == 0)
    def _():
        rows = lax.broadcasted_iota(jnp.int32, bias.shape, 0)
        cols = lax.broadcasted_iota(jnp.int32, bias.shape, 1)
        bias[...] = jnp.where(cols >= rows, 0.0, -jnp.inf)
        parts = [s0[...]]
        for hop, ref in enumerate((s1, s2, s3), 1):
            part = ref[...]
            row = lax.broadcasted_iota(jnp.int32, part.shape, 0)
            parts.append(jnp.where((device + hop > last) & (row < heads), BIG, part))
        stats = jnp.concatenate(parts, axis=1)
        for one in range(lse.shape[0]):
            lse[one] = stats[one : one + 1]
            delta[one] = stats[lse.shape[0] + one : lse.shape[0] + one + 1]

    queries = jnp.concatenate([q0[...], q1[...], q2[...], q3[...]], axis=0)
    dos = jnp.concatenate([d0[...], d1[...], d2[...], d3[...]], axis=0)
    scores = lax.dot_general(k_ref[...], queries, NT, preferred_element_type=f32) * scale - lse[head]
    edge = bias.shape[1]
    scores = jnp.concatenate([scores[:, :edge] + bias[...], scores[:, edge:]], axis=1)
    probs = jnp.exp(scores)
    prob_grad = lax.dot_general(v_ref[...], dos, NT, preferred_element_type=f32)
    score_grad = (probs * (prob_grad - delta[head])).astype(jnp.bfloat16)
    dk_ref[...] = (jnp.dot(score_grad, queries, preferred_element_type=f32) * scale).astype(dk_ref.dtype)
    dv_ref[...] = jnp.dot(probs.astype(jnp.bfloat16), dos, preferred_element_type=f32).astype(dv_ref.dtype)


def key_side(device, keys, values, queries, out_grads, stats, scale, last):
    block, width = keys.shape
    heads = width // HEAD
    column = pl.BlockSpec((block, HEAD), lambda h: (0, h))
    whole = pl.BlockSpec((2 * heads, block), lambda h: (0, 0))
    shape = jax.ShapeDtypeStruct((block, width), jnp.bfloat16)
    return pl.pallas_call(
        functools.partial(key_kernel, scale, last),
        grid=(heads,),
        in_specs=[pl.BlockSpec(memory_space=pltpu.SMEM)] + [column] * 10 + [whole] * 4,
        out_specs=[column, column],
        out_shape=[shape, shape],
        scratch_shapes=[
            pltpu.VMEM((block, 256), jnp.float32),
            pltpu.VMEM((heads, 1, 4 * block), jnp.float32),
            pltpu.VMEM((heads, 1, 4 * block), jnp.float32),
        ],
        compiler_params=pltpu.CompilerParams(vmem_limit_bytes=24 * 2**20),
        cost_estimate=pl.CostEstimate(
            flops=40 * block * block * width, bytes_accessed=24 * block * width, transcendentals=4 * block * block * heads
        ),
    )(device, keys, values, *queries, *out_grads, *stats)


def per_device(queries, keys, values, stream_grad, conv_input, conv_weight, out_weight):
    block = queries.shape[0]
    last = lax.axis_size("ctx") - 1
    scale = 1.0 / math.sqrt(HEAD)
    device = lax.axis_index("ctx").astype(jnp.int32).reshape(1)
    tp = lax.axis_index("tp").astype(jnp.int32).reshape(1)

    low = rotated(jnp.concatenate([conv_input[block - EDGE :], stream_grad[block - EDGE :]], axis=0), 1)
    high = rotated(jnp.concatenate([conv_input[:EDGE], stream_grad[:EDGE]], axis=0), -1)
    key_blocks, value_blocks, query_blocks = [keys], [values], [queries]
    for hop in range(3):
        key_blocks.append(rotated(key_blocks[-1], 1))
        value_blocks.append(rotated(value_blocks[-1], 1))
        query_blocks.append(rotated(query_blocks[-1], -1))

    grad_stream, tap_rows = conv(device, stream_grad, conv_input, low, high, conv_weight, last)
    other = lax.ppermute(grad_stream, "tp", [(0, 1), (1, 0)])
    kernel_grad = summed(tap_rows) / math.sqrt(block * (last + 1))
    out_grad = project(tp, grad_stream, other, out_weight)
    out_grads = [out_grad]
    for hop in range(3):
        out_grads.append(rotated(out_grads[-1], -1))

    query_grad, stats = query_side(device, queries, out_grad, key_blocks[::-1], value_blocks[::-1], scale)
    all_stats = [stats] + [rotated(stats, -hop) for hop in (1, 2, 3)]
    key_grad, value_grad = key_side(device, keys, values, query_blocks, out_grads, all_stats, scale, last)
    return (query_grad, key_grad, value_grad, grad_stream, kernel_grad)


def solution(mesh):
    return jax.shard_map(
        per_device,
        mesh=mesh,
        in_specs=(
            P("ctx", "tp"),
            P("ctx", "tp"),
            P("ctx", "tp"),
            P("ctx", "tp"),
            P("ctx", "tp"),
            P(None, "tp"),
            P("tp", None),
        ),
        out_specs=(P("ctx", "tp"), P("ctx", "tp"), P("ctx", "tp"), P("ctx", "tp"), P(None, "tp")),
        check_vma=False,
    )
```

time: 191 us -> 131 us (0.69)
  the two profiles are of different devices: /device:TPU:15 before, /device:TPU:57 now
where the time goes in v2:
time: 131 us
  starting transfers between devices  65.7 us (50%)
  waiting for transfers between devices  34.7 us (26%)
  Pallas kernels  22.1 us (17%)
  local copies, waits for them, and re-layouts  6.9 us (5%)
    ppermute x17, starting transfers between devices, rotated(): lax.ppermute(part, 'ctx', [(i, (i + by) % count) for i in range(count)])  39.7 us
    ppermute x10, waiting for transfers between devices, exchanged(): return lax.ppermute(part, 'ctx', [(i, i ^ by) for i in range(count)])  27 us
    ppermute x10, starting transfers between devices, exchanged(): return lax.ppermute(part, 'ctx', [(i, i ^ by) for i in range(count)])  25.1 us
    pallas_call x1, Pallas kernels, query_side(): pl.pallas_call(functools.partial(query_kernel, scale), grid=(heads,), in_...  8.83 us
    pallas_call x1, Pallas kernels, key_side(): pl.pallas_call(functools.partial(key_kernel, scale, last), grid=(heads,),...  6.71 us
    unnamed x16, local copies, waits for them, and re-layouts  6.03 us
    ppermute x17, waiting for transfers between devices, rotated(): lax.ppermute(part, 'ctx', [(i, (i + by) % count) for i in range(count)])  5.93 us
    pallas_call x1, Pallas kernels, conv(): pl.pallas_call(functools.partial(conv_kernel, last), grid=(width // lanes...  4.45 us
  transfers between devices with their start and end apart: 28, of which 10 were waited for; matrix products, arithmetic and copies ran while one was open for 1% of the time, Pallas kernels for 8%

profile of v2, /device:TPU:57, one launch (start us, length us, event | category | flops | bytes accessed | tf_op | source)
XLA Modules:
  0.0 130.9 jit_solution(16619775540393190653)
XLA Ops:
  0.6 0.9 fusion
  2.3 1.2 collective-permute-start
  3.5 1.8 %collective-permute-done.1.high_ref = bf16[32,1024]{1,0:T(8,128)(2,1)S(1)} collective-permute-done((bf16[32,1024]{1,0:T(8,128)(2,1)S(1)}, bf16[32,1024]{1,0:T(8,128)(2,1)S(1)}, u32[]{:S(2)}, u32[]{:S(2)}) %collective-permute-start.1) | collective-permute-done | bytes 65568 | tf_op jit(solution)/shard_map/ppermute | solution.py:19
  5.4 1.0 copy-done.1
  6.4 1.0 copy-done.2
  7.4 0.8 copy-done.4
  8.3 4.4 %shard_map.110 = (bf16[192,1024]{1,0:T(8,128)(2,1)}, f32[31,1024]{1,0:T(8,128)S(1)}) custom-call(s32[1]{0:T(128)} %bitcast.idx_ref, bf16[192,1024]{1,0:T(8,128)(2,1)S(1)} %copy-done.1, bf16[192,1024]{1,0:T(8,128)(2,1)S(1)} %copy-done.2, bf16[32,1024]{1,0:T(8,128)(2,1)S(1)} %collective-permute-done.low_ref, ...), custom_call_target="tpu_custom_call" | custom-call | flops 48758784 | bytes 786432 | tf_op jit(solution)/shard_map/pallas_call | solution.py:65
  12.7 0.9 collective-permute-start.2
  13.6 5.1 %collective-permute-start.18 = (f32[31,1024]{1,0:T(8,128)S(1)}, f32[31,1024]{1,0:T(8,128)S(1)}, u32[]{:S(2)}, u32[]{:S(2)}) collective-permute-start(f32[31,1024]{1,0:T(8,128)S(1)} %get-tuple-element.16), channel_id=1, source_target_pairs={{0,2},{2,0},{4,6},{6,4},{8,10},{10,8},{12,14},{14,12},{16,18},{18,... | collective-permute-start | bytes 380936 | tf_op jit(solution)/shard_map/ppermute | solution.py:24
  19.2 1.8 %collective-permute-done.2.other_ref = bf16[192,1024]{1,0:T(8,128)(2,1)S(1)} collective-permute-done((bf16[192,1024]{1,0:T(8,128)(2,1)}, bf16[192,1024]{1,0:T(8,128)(2,1)S(1)}, u32[]{:S(2)}, u32[]{:S(2)}) %collective-permute-start.2) | collective-permute-done | bytes 393248 | tf_op jit(solution)/shard_map/ppermute | solution.py:254
  21.0 2.2 %copy-done = bf16[1024,2048]{1,0:T(8,128)(2,1)S(1)} copy-done((bf16[1024,2048]{1,0:T(8,128)(2,1)S(1)}, bf16[1024,2048]{1,0:T(8,128)(2,1)}, u32[]{:S(2)}) %copy-start) | copy-done | bytes 4194328
  23.2 1.0 copy-done.3
  24.2 2.1 %shard_map.111.do_ref.d0 = bf16[192,1024]{1,0:T(8,128)(2,1)S(1)} custom-call(s32[1]{0:T(128)} %bitcast.1.idx_ref, bf16[192,1024]{1,0:T(8,128)(2,1)S(1)} %copy-done.3, bf16[192,1024]{1,0:T(8,128)(2,1)S(1)} %collective-permute-done.2.other_ref, bf16[1024,2048]{1,0:T(8,128)(2,1)S(1)} %copy-done), custom_call_target="tpu_custom_call" | custom-call | flops 805306368 | bytes 4194304 | tf_op jit(solution)/shard_map/pallas_call | solution.py:104
  26.3 11.8 %collective-permute-start.12 = (bf16[192,1024]{1,0:T(8,128)(2,1)S(1)}, bf16[192,1024]{1,0:T(8,128)(2,1)S(1)}, u32[]{:S(2)}, u32[]{:S(2)}) collective-permute-start(bf16[192,1024]{1,0:T(8,128)(2,1)S(1)} %shard_map.111.do_ref.d0), channel_id=1, source_target_pairs={{0,254},{2,0},{4,2},{6,4},{8,6},{10,8},{12,10},{14,12},{16,14},{18... | collective-permute-start | bytes 1179656 | tf_op jit(solution)/shard_map/ppermute | solution.py:19
  38.3 5.1 %collective-permute-done.19 = f32[31,1024]{1,0:T(8,128)S(1)} collective-permute-done((f32[31,1024]{1,0:T(8,128)S(1)}, f32[31,1024]{1,0:T(8,128)S(1)}, u32[]{:S(2)}, u32[]{:S(2)}) %collective-permute-start.19) | collective-permute-done | bytes 127008 | tf_op jit(solution)/shard_map/ppermute | solution.py:24
  43.3 5.7 %collective-permute-done.20 = f32[31,1024]{1,0:T(8,128)S(1)} collective-permute-done((f32[31,1024]{1,0:T(8,128)S(1)}, f32[31,1024]{1,0:T(8,128)S(1)}, u32[]{:S(2)}, u32[]{:S(2)}) %collective-permute-start.20) | collective-permute-done | bytes 127008 | tf_op jit(solution)/shard_map/ppermute | solution.py:24
  49.3 1.6 %collective-permute-start.4 = (bf16[192,1024]{1,0:T(8,128)(2,1)S(1)}, bf16[192,1024]{1,0:T(8,128)(2,1)S(1)}, u32[]{:S(2)}, u32[]{:S(2)}) collective-permute-start(bf16[192,1024]{1,0:T(8,128)(2,1)S(1)} %collective-permute-done.3.k1), channel_id=1, source_target_pairs={{0,2},{2,4},{4,6},{6,8},{8,10},{10,12},{12,14},{14,16},{16,18},{18... | collective-permute-start | bytes 1179656 | tf_op jit(solution)/shard_map/ppermute | solution.py:19
  51.4 5.0 %collective-permute-start.13 = (bf16[192,1024]{1,0:T(8,128)(2,1)S(1)}, bf16[192,1024]{1,0:T(8,128)(2,1)S(1)}, u32[]{:S(2)}, u32[]{:S(2)}) collective-permute-start(bf16[192,1024]{1,0:T(8,128)(2,1)S(1)} %collective-permute-done.12.d1), channel_id=1, source_target_pairs={{0,254},{2,0},{4,2},{6,4},{8,6},{10,8},{12,10},{14,12},{16,14},{18... | collective-permute-start | bytes 1179656 | tf_op jit(solution)/shard_map/ppermute | solution.py:19
  56.4 4.2 %collective-permute-start.22 = (f32[31,1024]{1,0:T(8,128)S(1)}, f32[31,1024]{1,0:T(8,128)S(1)}, u32[]{:S(2)}, u32[]{:S(2)}) collective-permute-start(f32[31,1024]{1,0:T(8,128)S(1)} %add_add_fusion.1), channel_id=1, source_target_pairs={{0,16},{2,18},{4,20},{6,22},{8,24},{10,26},{12,28},{14,30},{16,0},... | collective-permute-start | bytes 380936 | tf_op jit(solution)/shard_map/ppermute | solution.py:24
  60.6 10.2 %collective-permute-done.22 = f32[31,1024]{1,0:T(8,128)S(1)} collective-permute-done((f32[31,1024]{1,0:T(8,128)S(1)}, f32[31,1024]{1,0:T(8,128)S(1)}, u32[]{:S(2)}, u32[]{:S(2)}) %collective-permute-start.22) | collective-permute-done | bytes 127008 | tf_op jit(solution)/shard_map/ppermute | solution.py:24
  70.8 6.8 %collective-permute-start.23 = (f32[31,1024]{1,0:T(8,128)S(1)}, f32[31,1024]{1,0:T(8,128)S(1)}, u32[]{:S(2)}, u32[]{:S(2)}) collective-permute-start(f32[31,1024]{1,0:T(8,128)S(1)} %add_add_fusion.1), channel_id=1, source_target_pairs={{0,32},{2,34},{4,36},{6,38},{8,40},{10,42},{12,44},{14,46},{16,48}... | collective-permute-start | bytes 380936 | tf_op jit(solution)/shard_map/ppermute | solution.py:24
  77.6 3.3 %collective-permute-done.23 = f32[31,1024]{1,0:T(8,128)S(1)} collective-permute-done((f32[31,1024]{1,0:T(8,128)S(1)}, f32[31,1024]{1,0:T(8,128)S(1)}, u32[]{:S(2)}, u32[]{:S(2)}) %collective-permute-start.23) | collective-permute-done | bytes 127008 | tf_op jit(solution)/shard_map/ppermute | solution.py:24
  81.0 3.1 %collective-permute-start.24 = (f32[31,1024]{1,0:T(8,128)S(1)}, f32[31,1024]{1,0:T(8,128)S(1)}, u32[]{:S(2)}, u32[]{:S(2)}) collective-permute-start(f32[31,1024]{1,0:T(8,128)S(1)} %add_add_fusion.1), channel_id=1, source_target_pairs={{0,48},{2,50},{4,52},{6,54},{8,56},{10,58},{12,60},{14,62},{16,32}... | collective-permute-start | bytes 380936 | tf_op jit(solution)/shard_map/ppermute | solution.py:24
  84.0 1.6 %collective-permute-start.11 = (bf16[192,1024]{1,0:T(8,128)(2,1)S(1)}, bf16[192,1024]{1,0:T(8,128)(2,1)S(1)}, u32[]{:S(2)}, u32[]{:S(2)}) collective-permute-start(bf16[192,1024]{1,0:T(8,128)(2,1)S(1)} %collective-permute-done.10.q2), channel_id=1, source_target_pairs={{0,254},{2,0},{4,2},{6,4},{8,6},{10,8},{12,10},{14,12},{16,14},{18... | collective-permute-start | bytes 1179656 | tf_op jit(solution)/shard_map/ppermute | solution.py:19
  85.7 2.7 %collective-permute-done.24 = f32[31,1024]{1,0:T(8,128)S(1)} collective-permute-done((f32[31,1024]{1,0:T(8,128)S(1)}, f32[31,1024]{1,0:T(8,128)S(1)}, u32[]{:S(2)}, u32[]{:S(2)}) %collective-permute-start.24) | collective-permute-done | bytes 127008 | tf_op jit(solution)/shard_map/ppermute | solution.py:24
  88.5 1.4 %collective-permute-start.26 = (f32[31,1024]{1,0:T(8,128)S(1)}, f32[31,1024]{1,0:T(8,128)S(1)}, u32[]{:S(2)}, u32[]{:S(2)}) collective-permute-start(f32[31,1024]{1,0:T(8,128)S(1)} %add_add_fusion), channel_id=1, source_target_pairs={{0,128},{2,130},{4,132},{6,134},{8,136},{10,138},{12,140},{14,142}... | collective-permute-start | bytes 380936 | tf_op jit(solution)/shard_map/ppermute | solution.py:24
  89.9 4.3 %collective-permute-start.27 = (f32[31,1024]{1,0:T(8,128)S(1)}, f32[31,1024]{1,0:T(8,128)S(1)}, u32[]{:S(2)}, u32[]{:S(2)}) collective-permute-start(f32[31,1024]{1,0:T(8,128)S(1)} %add_add_fusion), channel_id=1, source_target_pairs={{0,192},{2,194},{4,196},{6,198},{8,200},{10,202},{12,204},{14,206}... | collective-permute-start | bytes 380936 | tf_op jit(solution)/shard_map/ppermute | solution.py:24
  94.2 8.8 %shard_map.112 = (bf16[192,1024]{1,0:T(8,128)(2,1)}, f32[16,192]{1,0:T(8,128)S(1)}) custom-call(s32[1]{0:T(128)} %bitcast.idx_ref, bf16[192,1024]{1,0:T(8,128)(2,1)S(1)} %copy-done.5, bf16[192,1024]{1,0:T(8,128)(2,1)S(1)} %shard_map.111.do_ref.d0, bf16[192,1024]{1,0:T(8,128)(2,1)S(1)} %collective-permute-done.5.k3, ...), custom_call_target="tpu_custom_call" | custom-call | flops 1509949440 | bytes 4718592 | tf_op jit(solution)/shard_map/pallas_call | solution.py:160
  103.0 4.8 %collective-permute-start.15 = (f32[16,192]{1,0:T(8,128)S(1)}, f32[16,192]{1,0:T(8,128)S(1)}, u32[]{:S(2)}, u32[]{:S(2)}) collective-permute-start(f32[16,192]{1,0:T(8,128)S(1)} %get-tuple-element.13.s0), channel_id=1, source_target_pairs={{0,254},{2,0},{4,2},{6,4},{8,6},{10,8},{12,10},{14,12},{16,14},{18... | collective-permute-start | bytes 36872 | tf_op jit(solution)/shard_map/ppermute | solution.py:19
  107.8 11.6 %collective-permute-start.16 = (f32[16,192]{1,0:T(8,128)S(1)}, f32[16,192]{1,0:T(8,128)S(1)}, u32[]{:S(2)}, u32[]{:S(2)}) collective-permute-start(f32[16,192]{1,0:T(8,128)S(1)} %get-tuple-element.13.s0), channel_id=1, source_target_pairs={{0,252},{2,254},{4,0},{6,2},{8,4},{10,6},{12,8},{14,10},{16,12},{1... | collective-permute-start | bytes 36872 | tf_op jit(solution)/shard_map/ppermute | solution.py:19
  120.4 3.8 %collective-permute-done.17.s3 = f32[16,192]{1,0:T(8,128)S(1)} collective-permute-done((f32[16,192]{1,0:T(8,128)S(1)}, f32[16,192]{1,0:T(8,128)S(1)}, u32[]{:S(2)}, u32[]{:S(2)}) %collective-permute-start.17) | collective-permute-done | bytes 12320 | tf_op jit(solution)/shard_map/ppermute | solution.py:19
  124.2 6.7 %shard_map.113 = (bf16[192,1024]{1,0:T(8,128)(2,1)}, bf16[192,1024]{1,0:T(8,128)(2,1)}) custom-call(s32[1]{0:T(128)} %bitcast.idx_ref, bf16[192,1024]{1,0:T(8,128)(2,1)S(1)} %copy-done.6, bf16[192,1024]{1,0:T(8,128)(2,1)S(1)} %copy-done.7, bf16[192,1024]{1,0:T(8,128)(2,1)S(1)} %copy-done.5, bf16[192,1024]{1,0:T(8,128)(2,1)S(1)} %collective-permute-done.9.q1, ...), custom_call_target="tpu_custom_call" | custom-call | flops 1509949440 | bytes 4718592 | tf_op jit(solution)/shard_map/pallas_call | solution.py:220
  (51 shorter events, 3.4 us)
Async XLA Ops:
  0.6 93.5 %copy-start.5 = (bf16[192,1024]{1,0:T(8,128)(2,1)S(1)}, bf16[192,1024]{1,0:T(8,128)(2,1)}, u32[]{:S(2)}) copy-start(bf16[192,1024]{1,0:T(8,128)(2,1)} %q0.1) | copy-start | bytes 1179652
  1.5 3.8 %collective-permute-start.1 = (bf16[32,1024]{1,0:T(8,128)(2,1)S(1)}, bf16[32,1024]{1,0:T(8,128)(2,1)S(1)}, u32[]{:S(2)}, u32[]{:S(2)}) collective-permute-start(bf16[32,1024]{1,0:T(8,128)(2,1)S(1)} %pad_maximum_fusion.1), channel_id=1, source_target_pairs={{0,254},{2,0},{4,2},{6,4},{8,6},{10,8},{12,10},{14,12},{16,14},{18... | collective-permute-start | bytes 196616 | tf_op jit(solution)/shard_map/ppermute | solution.py:19
  2.3 3.1 %collective-permute-start = (bf16[32,1024]{1,0:T(8,128)(2,1)S(1)}, bf16[32,1024]{1,0:T(8,128)(2,1)S(1)}, u32[]{:S(2)}, u32[]{:S(2)}) collective-permute-start(bf16[32,1024]{1,0:T(8,128)(2,1)S(1)} %pad_maximum_fusion), channel_id=1, source_target_pairs={{0,2},{2,4},{4,6},{6,8},{8,10},{10,12},{12,14},{14,16},{16,18},{18... | collective-permute-start | bytes 196616 | tf_op jit(solution)/shard_map/ppermute | solution.py:19
  8.2 85.9 %copy-start.6 = (bf16[192,1024]{1,0:T(8,128)(2,1)S(1)}, bf16[192,1024]{1,0:T(8,128)(2,1)}, u32[]{:S(2)}) copy-start(bf16[192,1024]{1,0:T(8,128)(2,1)} %k_ref.1) | copy-start | bytes 1179652
  8.2 85.9 %copy-start.7 = (bf16[192,1024]{1,0:T(8,128)(2,1)S(1)}, bf16[192,1024]{1,0:T(8,128)(2,1)}, u32[]{:S(2)}) copy-start(bf16[192,1024]{1,0:T(8,128)(2,1)} %v_ref.1) | copy-start | bytes 1179652
  12.7 8.3 %collective-permute-start.2 = (bf16[192,1024]{1,0:T(8,128)(2,1)}, bf16[192,1024]{1,0:T(8,128)(2,1)S(1)}, u32[]{:S(2)}, u32[]{:S(2)}) collective-permute-start(bf16[192,1024]{1,0:T(8,128)(2,1)} %get-tuple-element.9.own_ref), channel_id=1, source_target_pairs={{0,1},{1,0},{2,3},{3,2},{4,5},{5,4},{6,7},{7,6},{8,9},{9,8},{10,11... | collective-permute-start | bytes 1179656 | tf_op jit(solution)/shard_map/ppermute | solution.py:254
  13.6 24.6 %collective-permute-start.18 = (f32[31,1024]{1,0:T(8,128)S(1)}, f32[31,1024]{1,0:T(8,128)S(1)}, u32[]{:S(2)}, u32[]{:S(2)}) collective-permute-start(f32[31,1024]{1,0:T(8,128)S(1)} %get-tuple-element.16), channel_id=1, source_target_pairs={{0,2},{2,0},{4,6},{6,4},{8,10},{10,8},{12,14},{14,12},{16,18},{18,... | collective-permute-start | bytes 380936 | tf_op jit(solution)/shard_map/ppermute | solution.py:24
  18.7 30.6 %collective-permute-start.3 = (bf16[192,1024]{1,0:T(8,128)(2,1)}, bf16[192,1024]{1,0:T(8,128)(2,1)S(1)}, u32[]{:S(2)}, u32[]{:S(2)}) collective-permute-start(bf16[192,1024]{1,0:T(8,128)(2,1)} %k_ref.1), channel_id=1, source_target_pairs={{0,2},{2,4},{4,6},{6,8},{8,10},{10,12},{12,14},{14,16},{16,18},{18... | collective-permute-start | bytes 1179656 | tf_op jit(solution)/shard_map/ppermute | solution.py:19
  18.7 32.2 %collective-permute-start.6 = (bf16[192,1024]{1,0:T(8,128)(2,1)}, bf16[192,1024]{1,0:T(8,128)(2,1)S(1)}, u32[]{:S(2)}, u32[]{:S(2)}) collective-permute-start(bf16[192,1024]{1,0:T(8,128)(2,1)} %v_ref.1), channel_id=1, source_target_pairs={{0,2},{2,4},{4,6},{6,8},{8,10},{10,12},{12,14},{14,16},{16,18},{18... | collective-permute-start | bytes 1179656 | tf_op jit(solution)/shard_map/ppermute | solution.py:19
  18.7 32.3 %collective-permute-start.9 = (bf16[192,1024]{1,0:T(8,128)(2,1)}, bf16[192,1024]{1,0:T(8,128)(2,1)S(1)}, u32[]{:S(2)}, u32[]{:S(2)}) collective-permute-start(bf16[192,1024]{1,0:T(8,128)(2,1)} %q0.1), channel_id=1, source_target_pairs={{0,254},{2,0},{4,2},{6,4},{8,6},{10,8},{12,10},{14,12},{16,14},{18... | collective-permute-start | bytes 1179656 | tf_op jit(solution)/shard_map/ppermute | solution.py:19
  21.0 2.2 %copy-start = (bf16[1024,2048]{1,0:T(8,128)(2,1)S(1)}, bf16[1024,2048]{1,0:T(8,128)(2,1)}, u32[]{:S(2)}) copy-start(bf16[1024,2048]{1,0:T(8,128)(2,1)} %weight_ref.1) | copy-start | bytes 12582916
  26.3 25.1 %collective-permute-start.12 = (bf16[192,1024]{1,0:T(8,128)(2,1)S(1)}, bf16[192,1024]{1,0:T(8,128)(2,1)S(1)}, u32[]{:S(2)}, u32[]{:S(2)}) collective-permute-start(bf16[192,1024]{1,0:T(8,128)(2,1)S(1)} %shard_map.111.do_ref.d0), channel_id=1, source_target_pairs={{0,254},{2,0},{4,2},{6,4},{8,6},{10,8},{12,10},{14,12},{16,14},{18... | collective-permute-start | bytes 1179656 | tf_op jit(solution)/shard_map/ppermute | solution.py:19
  38.2 5.2 %collective-permute-start.19 = (f32[31,1024]{1,0:T(8,128)S(1)}, f32[31,1024]{1,0:T(8,128)S(1)}, u32[]{:S(2)}, u32[]{:S(2)}) collective-permute-start(f32[31,1024]{1,0:T(8,128)S(1)} %add.30), channel_id=1, source_target_pairs={{0,4},{2,6},{4,0},{6,2},{8,12},{10,14},{12,8},{14,10},{16,20},{18,... | collective-permute-start | bytes 380936 | tf_op jit(solution)/shard_map/ppermute | solution.py:24
  43.3 5.7 %collective-permute-start.20 = (f32[31,1024]{1,0:T(8,128)S(1)}, f32[31,1024]{1,0:T(8,128)S(1)}, u32[]{:S(2)}, u32[]{:S(2)}) collective-permute-start(f32[31,1024]{1,0:T(8,128)S(1)} %add.30), channel_id=1, source_target_pairs={{0,8},{2,10},{4,12},{6,14},{8,0},{10,2},{12,4},{14,6},{16,24},{18,... | collective-permute-start | bytes 380936 | tf_op jit(solution)/shard_map/ppermute | solution.py:24
  49.1 7.3 %collective-permute-start.21 = (f32[31,1024]{1,0:T(8,128)S(1)}, f32[31,1024]{1,0:T(8,128)S(1)}, u32[]{:S(2)}, u32[]{:S(2)}) collective-permute-start(f32[31,1024]{1,0:T(8,128)S(1)} %add.30), channel_id=1, source_target_pairs={{0,12},{2,14},{4,8},{6,10},{8,4},{10,6},{12,0},{14,2},{16,28},{18,... | collective-permute-start | bytes 380936 | tf_op jit(solution)/shard_map/ppermute | solution.py:24
  49.3 28.3 %collective-permute-start.4 = (bf16[192,1024]{1,0:T(8,128)(2,1)S(1)}, bf16[192,1024]{1,0:T(8,128)(2,1)S(1)}, u32[]{:S(2)}, u32[]{:S(2)}) collective-permute-start(bf16[192,1024]{1,0:T(8,128)(2,1)S(1)} %collective-permute-done.3.k1), channel_id=1, source_target_pairs={{0,2},{2,4},{4,6},{6,8},{8,10},{10,12},{12,14},{14,16},{16,18},{18... | collective-permute-start | bytes 1179656 | tf_op jit(solution)/shard_map/ppermute | solution.py:19
  50.9 26.7 %collective-permute-start.7 = (bf16[192,1024]{1,0:T(8,128)(2,1)S(1)}, bf16[192,1024]{1,0:T(8,128)(2,1)S(1)}, u32[]{:S(2)}, u32[]{:S(2)}) collective-permute-start(bf16[192,1024]{1,0:T(8,128)(2,1)S(1)} %collective-permute-done.6.v1), channel_id=1, source_target_pairs={{0,2},{2,4},{4,6},{6,8},{8,10},{10,12},{12,14},{14,16},{16,18},{18... | collective-permute-start | bytes 1179656 | tf_op jit(solution)/shard_map/ppermute | solution.py:19
  51.0 33.1 %collective-permute-start.10 = (bf16[192,1024]{1,0:T(8,128)(2,1)S(1)}, bf16[192,1024]{1,0:T(8,128)(2,1)S(1)}, u32[]{:S(2)}, u32[]{:S(2)}) collective-permute-start(bf16[192,1024]{1,0:T(8,128)(2,1)S(1)} %collective-permute-done.9.q1), channel_id=1, source_target_pairs={{0,254},{2,0},{4,2},{6,4},{8,6},{10,8},{12,10},{14,12},{16,14},{18... | collective-permute-start | bytes 1179656 | tf_op jit(solution)/shard_map/ppermute | solution.py:19
  51.4 34.3 %collective-permute-start.13 = (bf16[192,1024]{1,0:T(8,128)(2,1)S(1)}, bf16[192,1024]{1,0:T(8,128)(2,1)S(1)}, u32[]{:S(2)}, u32[]{:S(2)}) collective-permute-start(bf16[192,1024]{1,0:T(8,128)(2,1)S(1)} %collective-permute-done.12.d1), channel_id=1, source_target_pairs={{0,254},{2,0},{4,2},{6,4},{8,6},{10,8},{12,10},{14,12},{16,14},{18... | collective-permute-start | bytes 1179656 | tf_op jit(solution)/shard_map/ppermute | solution.py:19
  56.4 14.3 %collective-permute-start.22 = (f32[31,1024]{1,0:T(8,128)S(1)}, f32[31,1024]{1,0:T(8,128)S(1)}, u32[]{:S(2)}, u32[]{:S(2)}) collective-permute-start(f32[31,1024]{1,0:T(8,128)S(1)} %add_add_fusion.1), channel_id=1, source_target_pairs={{0,16},{2,18},{4,20},{6,22},{8,24},{10,26},{12,28},{14,30},{16,0},... | collective-permute-start | bytes 380936 | tf_op jit(solution)/shard_map/ppermute | solution.py:24
  70.8 10.2 %collective-permute-start.23 = (f32[31,1024]{1,0:T(8,128)S(1)}, f32[31,1024]{1,0:T(8,128)S(1)}, u32[]{:S(2)}, u32[]{:S(2)}) collective-permute-start(f32[31,1024]{1,0:T(8,128)S(1)} %add_add_fusion.1), channel_id=1, source_target_pairs={{0,32},{2,34},{4,36},{6,38},{8,40},{10,42},{12,44},{14,46},{16,48}... | collective-permute-start | bytes 380936 | tf_op jit(solution)/shard_map/ppermute | solution.py:24
  77.5 11.0 %collective-permute-start.5 = (bf16[192,1024]{1,0:T(8,128)(2,1)S(1)}, bf16[192,1024]{1,0:T(8,128)(2,1)S(1)}, u32[]{:S(2)}, u32[]{:S(2)}) collective-permute-start(bf16[192,1024]{1,0:T(8,128)(2,1)S(1)} %collective-permute-done.4.k2), channel_id=1, source_target_pairs={{0,2},{2,4},{4,6},{6,8},{8,10},{10,12},{12,14},{14,16},{16,18},{18... | collective-permute-start | bytes 1179656 | tf_op jit(solution)/shard_map/ppermute | solution.py:19
  77.5 12.4 %collective-permute-start.8 = (bf16[192,1024]{1,0:T(8,128)(2,1)S(1)}, bf16[192,1024]{1,0:T(8,128)(2,1)S(1)}, u32[]{:S(2)}, u32[]{:S(2)}) collective-permute-start(bf16[192,1024]{1,0:T(8,128)(2,1)S(1)} %collective-permute-done.7.v2), channel_id=1, source_target_pairs={{0,2},{2,4},{4,6},{6,8},{8,10},{10,12},{12,14},{14,16},{16,18},{18... | collective-permute-start | bytes 1179656 | tf_op jit(solution)/shard_map/ppermute | solution.py:19
  81.0 7.4 %collective-permute-start.24 = (f32[31,1024]{1,0:T(8,128)S(1)}, f32[31,1024]{1,0:T(8,128)S(1)}, u32[]{:S(2)}, u32[]{:S(2)}) collective-permute-start(f32[31,1024]{1,0:T(8,128)S(1)} %add_add_fusion.1), channel_id=1, source_target_pairs={{0,48},{2,50},{4,52},{6,54},{8,56},{10,58},{12,60},{14,62},{16,32}... | collective-permute-start | bytes 380936 | tf_op jit(solution)/shard_map/ppermute | solution.py:24
  84.0 36.2 %collective-permute-start.11 = (bf16[192,1024]{1,0:T(8,128)(2,1)S(1)}, bf16[192,1024]{1,0:T(8,128)(2,1)S(1)}, u32[]{:S(2)}, u32[]{:S(2)}) collective-permute-start(bf16[192,1024]{1,0:T(8,128)(2,1)S(1)} %collective-permute-done.10.q2), channel_id=1, source_target_pairs={{0,254},{2,0},{4,2},{6,4},{8,6},{10,8},{12,10},{14,12},{16,14},{18... | collective-permute-start | bytes 1179656 | tf_op jit(solution)/shard_map/ppermute | solution.py:19
  85.6 38.5 %collective-permute-start.14 = (bf16[192,1024]{1,0:T(8,128)(2,1)S(1)}, bf16[192,1024]{1,0:T(8,128)(2,1)S(1)}, u32[]{:S(2)}, u32[]{:S(2)}) collective-permute-start(bf16[192,1024]{1,0:T(8,128)(2,1)S(1)} %collective-permute-done.13.d2), channel_id=1, source_target_pairs={{0,254},{2,0},{4,2},{6,4},{8,6},{10,8},{12,10},{14,12},{16,14},{18... | collective-permute-start | bytes 1179656 | tf_op jit(solution)/shard_map/ppermute | solution.py:19
  88.4 14.6 %collective-permute-start.25 = (f32[31,1024]{1,0:T(8,128)S(1)}, f32[31,1024]{1,0:T(8,128)S(1)}, u32[]{:S(2)}, u32[]{:S(2)}) collective-permute-start(f32[31,1024]{1,0:T(8,128)S(1)} %add_add_fusion), channel_id=1, source_target_pairs={{0,64},{2,66},{4,68},{6,70},{8,72},{10,74},{12,76},{14,78},{16,80}... | collective-permute-start | bytes 380936 | tf_op jit(solution)/shard_map/ppermute | solution.py:24
  88.5 19.3 %collective-permute-start.26 = (f32[31,1024]{1,0:T(8,128)S(1)}, f32[31,1024]{1,0:T(8,128)S(1)}, u32[]{:S(2)}, u32[]{:S(2)}) collective-permute-start(f32[31,1024]{1,0:T(8,128)S(1)} %add_add_fusion), channel_id=1, source_target_pairs={{0,128},{2,130},{4,132},{6,134},{8,136},{10,138},{12,140},{14,142}... | collective-permute-start | bytes 380936 | tf_op jit(solution)/shard_map/ppermute | solution.py:24
  89.9 29.6 %collective-permute-start.27 = (f32[31,1024]{1,0:T(8,128)S(1)}, f32[31,1024]{1,0:T(8,128)S(1)}, u32[]{:S(2)}, u32[]{:S(2)}) collective-permute-start(f32[31,1024]{1,0:T(8,128)S(1)} %add_add_fusion), channel_id=1, source_target_pairs={{0,192},{2,194},{4,196},{6,198},{8,200},{10,202},{12,204},{14,206}... | collective-permute-start | bytes 380936 | tf_op jit(solution)/shard_map/ppermute | solution.py:24
  103.0 17.2 %collective-permute-start.15 = (f32[16,192]{1,0:T(8,128)S(1)}, f32[16,192]{1,0:T(8,128)S(1)}, u32[]{:S(2)}, u32[]{:S(2)}) collective-permute-start(f32[16,192]{1,0:T(8,128)S(1)} %get-tuple-element.13.s0), channel_id=1, source_target_pairs={{0,254},{2,0},{4,2},{6,4},{8,6},{10,8},{12,10},{14,12},{16,14},{18... | collective-permute-start | bytes 36872 | tf_op jit(solution)/shard_map/ppermute | solution.py:19
  107.8 12.5 %collective-permute-start.16 = (f32[16,192]{1,0:T(8,128)S(1)}, f32[16,192]{1,0:T(8,128)S(1)}, u32[]{:S(2)}, u32[]{:S(2)}) collective-permute-start(f32[16,192]{1,0:T(8,128)S(1)} %get-tuple-element.13.s0), channel_id=1, source_target_pairs={{0,252},{2,254},{4,0},{6,2},{8,4},{10,6},{12,8},{14,10},{16,12},{1... | collective-permute-start | bytes 36872 | tf_op jit(solution)/shard_map/ppermute | solution.py:19
  119.5 4.7 %collective-permute-start.17 = (f32[16,192]{1,0:T(8,128)S(1)}, f32[16,192]{1,0:T(8,128)S(1)}, u32[]{:S(2)}, u32[]{:S(2)}) collective-permute-start(f32[16,192]{1,0:T(8,128)S(1)} %get-tuple-element.13.s0), channel_id=1, source_target_pairs={{0,250},{2,252},{4,254},{6,0},{8,2},{10,4},{12,6},{14,8},{16,10},{... | collective-permute-start | bytes 36872 | tf_op jit(solution)/shard_map/ppermute | solution.py:19
  (4 other events, 3.8 us)

commit v3 on v2

--- a/solution.py
+++ b/solution.py
@@ -6,30 +6,31 @@
 from jax import lax
 from jax.experimental import pallas as pl
 from jax.experimental.pallas import tpu as pltpu
+from jax.sharding import Mesh
 from jax.sharding import PartitionSpec as P
 
 HEAD = 128
 EDGE = 16
 NT = (((1,), (1,)), ((), ()))
 BIG = 1e30
+CTX = ("far", "near")
 
 
 def rotated(part, by):
-    count = lax.axis_size("ctx")
-    return lax.ppermute(part, "ctx", [(i, (i + by) % count) for i in range(count)])
-
-
-def exchanged(part, by):
-    count = lax.axis_size("ctx")
-    return lax.ppermute(part, "ctx", [(i, i ^ by) for i in range(count)])
+    count = lax.axis_size(CTX)
+    return lax.ppermute(part, CTX, [(i, (i + by) % count) for i in range(count)])
+
+
+def after(parts, done):
+    return lax.optimization_barrier(tuple(parts) + tuple(done))[: len(parts)]
 
 
 def summed(part):
-    part = part + exchanged(part, 1)
-    for low in (2, 8, 32):
-        one, two, three = (exchanged(part, low * k) for k in (1, 2, 3))
-        part = (part + one) + (two + three)
-    return part
+    part = jnp.sum(lax.all_to_all(part, "far", 0, 0, tiled=True), axis=0)
+    copies = jnp.broadcast_to(part, (lax.axis_size("near"),) + part.shape)
+    part = jnp.sum(lax.all_to_all(copies, "near", 0, 0, tiled=True), axis=0)
+    copies = jnp.broadcast_to(part, (lax.axis_size("far"),) + part.shape)
+    return lax.all_to_all(copies, "far", 0, 0, tiled=True)
 
 
 def conv_kernel(last, idx_ref, grad_ref, input_ref, low_ref, high_ref, taps_ref, out_ref, rows_ref, gpad, cpad):
@@ -54,13 +55,15 @@
     out_ref[...] = (grad + total).astype(out_ref.dtype)
     for tap in range(taps_count):
         prod = grad * cpad[pl.ds(EDGE - reach + tap, block), :]
-        rows_ref[tap : tap + 1, :] = jnp.sum(prod, axis=0, keepdims=True)
+        rows_ref[0, tap : tap + 1, :] = jnp.sum(prod, axis=0, keepdims=True)
+    rows_ref[0, taps_count:, :] = jnp.zeros_like(rows_ref[0, taps_count:, :])
 
 
 def conv(device, grad, inputs, low, high, taps, last):
     block, width = grad.shape
     count = taps.shape[0]
     lanes = 128
+    rows = 8 * pl.cdiv(count, 8)
     column = lambda rows: pl.BlockSpec((rows, lanes), lambda c: (0, c))
     return pl.pallas_call(
         functools.partial(conv_kernel, last),
@@ -73,16 +76,16 @@
             column(2 * EDGE),
             column(count),
         ],
-        out_specs=[column(block), column(count)],
+        out_specs=[column(block), pl.BlockSpec((1, rows, lanes), lambda c: (c, 0, 0))],
         out_shape=[
             jax.ShapeDtypeStruct((block, width), jnp.bfloat16),
-            jax.ShapeDtypeStruct((count, width), jnp.float32),
+            jax.ShapeDtypeStruct((width // lanes, rows, lanes), jnp.float32),
         ],
         scratch_shapes=[
             pltpu.VMEM((block + 2 * EDGE, lanes), jnp.float32),
             pltpu.VMEM((block + 2 * EDGE, lanes), jnp.float32),
         ],
-        compiler_params=pltpu.CompilerParams(vmem_limit_bytes=8 * 2**20),
+        compiler_params=pltpu.CompilerParams(vmem_limit_bytes=56 * 2**20),
         cost_estimate=pl.CostEstimate(flops=8 * block * width * count, bytes_accessed=4 * block * width, transcendentals=0),
     )(device, grad, inputs, low, high, taps)
 
@@ -112,7 +115,7 @@
         ],
         out_specs=pl.BlockSpec((block, step), lambda n: (0, n)),
         out_shape=jax.ShapeDtypeStruct((block, rows), jnp.bfloat16),
-        compiler_params=pltpu.CompilerParams(vmem_limit_bytes=16 * 2**20),
+        compiler_params=pltpu.CompilerParams(vmem_limit_bytes=56 * 2**20),
         cost_estimate=pl.CostEstimate(flops=2 * block * rows * full, bytes_accessed=2 * rows * full, transcendentals=0),
     )(tp, own, other, weight)
 
@@ -177,7 +180,10 @@
     )(device, queries, out_grad, *keys, *values)
 
 
-def key_kernel(scale, last, idx_ref, k_ref, v_ref, q0, q1, q2, q3, d0, d1, d2, d3, s0, s1, s2, s3, dk_ref, dv_ref, bias, lse, delta):
+def key_kernel(
+    scale, norm, last, idx_ref, k_ref, v_ref, q0, q1, q2, q3, d0, d1, d2, d3, s0, s1, s2, s3, taps_ref,
+    dk_ref, dv_ref, kernel_ref, bias, lse, delta,
+):
     head = pl.program_id(0)
     heads = pl.num_programs(0)
     block = k_ref.shape[0]
@@ -199,6 +205,7 @@
             lse[one] = stats[one : one + 1]
             delta[one] = stats[lse.shape[0] + one : lse.shape[0] + one + 1]
 
+    kernel_ref[...] = taps_ref[0, : kernel_ref.shape[0]] * norm
     queries = jnp.concatenate([q0[...], q1[...], q2[...], q3[...]], axis=0)
     dos = jnp.concatenate([d0[...], d1[...], d2[...], d3[...]], axis=0)
     scores = lax.dot_general(k_ref[...], queries, NT, preferred_element_type=f32) * scale - lse[head]
@@ -211,18 +218,19 @@
     dv_ref[...] = jnp.dot(probs.astype(jnp.bfloat16), dos, preferred_element_type=f32).astype(dv_ref.dtype)
 
 
-def key_side(device, keys, values, queries, out_grads, stats, scale, last):
+def key_side(device, keys, values, queries, out_grads, stats, tap_sums, taps_count, scale, norm, last):
     block, width = keys.shape
     heads = width // HEAD
     column = pl.BlockSpec((block, HEAD), lambda h: (0, h))
     whole = pl.BlockSpec((2 * heads, block), lambda h: (0, 0))
     shape = jax.ShapeDtypeStruct((block, width), jnp.bfloat16)
     return pl.pallas_call(
-        functools.partial(key_kernel, scale, last),
+        functools.partial(key_kernel, scale, norm, last),
         grid=(heads,),
-        in_specs=[pl.BlockSpec(memory_space=pltpu.SMEM)] + [column] * 10 + [whole] * 4,
-        out_specs=[column, column],
-        out_shape=[shape, shape],
+        in_specs=[pl.BlockSpec(memory_space=pltpu.SMEM)] + [column] * 10 + [whole] * 4
+        + [pl.BlockSpec((1,) + tap_sums.shape[1:], lambda h: (h, 0, 0))],
+        out_specs=[column, column, pl.BlockSpec((taps_count, HEAD), lambda h: (0, h))],
+        out_shape=[shape, shape, jax.ShapeDtypeStruct((taps_count, width), jnp.float32)],
         scratch_shapes=[
             pltpu.VMEM((block, 256), jnp.float32),
             pltpu.VMEM((heads, 1, 4 * block), jnp.float32),
@@ -232,14 +240,14 @@
         cost_estimate=pl.CostEstimate(
             flops=40 * block * block * width, bytes_accessed=24 * block * width, transcendentals=4 * block * block * heads
         ),
-    )(device, keys, values, *queries, *out_grads, *stats)
+    )(device, keys, values, *queries, *out_grads, *stats, tap_sums)
 
 
 def per_device(queries, keys, values, stream_grad, conv_input, conv_weight, out_weight):
     block = queries.shape[0]
-    last = lax.axis_size("ctx") - 1
+    last = lax.axis_size(CTX) - 1
     scale = 1.0 / math.sqrt(HEAD)
-    device = lax.axis_index("ctx").astype(jnp.int32).reshape(1)
+    device = lax.axis_index(CTX).astype(jnp.int32).reshape(1)
     tp = lax.axis_index("tp").astype(jnp.int32).reshape(1)
 
     low = rotated(jnp.concatenate([conv_input[block - EDGE :], stream_grad[block - EDGE :]], axis=0), 1)
@@ -250,33 +258,36 @@
         value_blocks.append(rotated(value_blocks[-1], 1))
         query_blocks.append(rotated(query_blocks[-1], -1))
 
+    low, high = after((low, high), (key_blocks[1], query_blocks[1]))
     grad_stream, tap_rows = conv(device, stream_grad, conv_input, low, high, conv_weight, last)
-    other = lax.ppermute(grad_stream, "tp", [(0, 1), (1, 0)])
-    kernel_grad = summed(tap_rows) / math.sqrt(block * (last + 1))
+    (own,) = after((grad_stream,), (value_blocks[1],))
+    other = lax.ppermute(own, "tp", [(0, 1), (1, 0)])
+    tap_sums = summed(tap_rows)
+    (other,) = after((other,), (key_blocks[2], query_blocks[2]))
     out_grad = project(tp, grad_stream, other, out_weight)
-    out_grads = [out_grad]
-    for hop in range(3):
+    (sent,) = after((out_grad,), (value_blocks[2],))
+    out_grads = [out_grad, rotated(sent, -1)]
+    for hop in range(2):
         out_grads.append(rotated(out_grads[-1], -1))
 
     query_grad, stats = query_side(device, queries, out_grad, key_blocks[::-1], value_blocks[::-1], scale)
     all_stats = [stats] + [rotated(stats, -hop) for hop in (1, 2, 3)]
-    key_grad, value_grad = key_side(device, keys, values, query_blocks, out_grads, all_stats, scale, last)
+    norm = 1.0 / math.sqrt(block * (last + 1))
+    key_grad, value_grad, kernel_grad = key_side(
+        device, keys, values, query_blocks, out_grads, all_stats, tap_sums, conv_weight.shape[0], scale, norm, last
+    )
     return (query_grad, key_grad, value_grad, grad_stream, kernel_grad)
 
 
 def solution(mesh):
+    count, pair = mesh.devices.shape
+    far = 8
+    split = Mesh(mesh.devices.reshape(far, count // far, pair), CTX + ("tp",))
+    frames = P(CTX, "tp")
     return jax.shard_map(
         per_device,
-        mesh=mesh,
-        in_specs=(
-            P("ctx", "tp"),
-            P("ctx", "tp"),
-            P("ctx", "tp"),
-            P("ctx", "tp"),
-            P("ctx", "tp"),
-            P(None, "tp"),
-            P("tp", None),
-        ),
-        out_specs=(P("ctx", "tp"), P("ctx", "tp"), P("ctx", "tp"), P("ctx", "tp"), P(None, "tp")),
+        mesh=split,
+        in_specs=(frames,) * 5 + (P(None, "tp"), P("tp", None)),
+        out_specs=(frames,) * 4 + (P(None, "tp"),),
         check_vma=False,
     )

time: 131 us -> 126 us (0.962)
  the two profiles are of different devices: /device:TPU:57 before, /device:TPU:1 now
where the time goes in v3:
time: 126 us; the launch traced here: 125 us
  starting transfers between devices  71.6 us (57%)
  Pallas kernels  28.3 us (22%)
  waiting for transfers between devices  20.1 us (16%)
  local copies, waits for them, and re-layouts  3.86 us (3%)
    ppermute x17, starting transfers between devices, rotated(): lax.ppermute(part, CTX, [(i, (i + by) % count) for i in range(count)])  47.1 us
    all_to_all x1, starting transfers between devices, summed(): part = jnp.sum(lax.all_to_all(copies, 'near', 0, 0, tiled=True), axis=0)  10.9 us
    pallas_call x1, Pallas kernels, query_side(): pl.pallas_call(functools.partial(query_kernel, scale), grid=(heads,), in_...  9.16 us
    ppermute x17, waiting for transfers between devices, rotated(): lax.ppermute(part, CTX, [(i, (i + by) % count) for i in range(count)])  8.34 us
    all_to_all x1, waiting for transfers between devices, summed(): part = jnp.sum(lax.all_to_all(part, 'far', 0, 0, tiled=True), axis=0)  7.83 us
    pallas_call x1, Pallas kernels, key_side(): pl.pallas_call(functools.partial(key_kernel, scale, norm, last), grid=(he...  7.59 us
    pallas_call x1, Pallas kernels, conv(): pl.pallas_call(functools.partial(conv_kernel, last), grid=(width // lanes...  6.51 us
    all_to_all x1, starting transfers between devices, summed(): part = jnp.sum(lax.all_to_all(part, 'far', 0, 0, tiled=True), axis=0)  5.86 us
  transfers between devices with their start and end apart: 21, of which 7 were waited for; matrix products, arithmetic and copies ran while one was open for 2% of the time, Pallas kernels for 17%

profile of v3, /device:TPU:1, one launch (start us, length us, event | category | flops | bytes accessed | tf_op | source)
XLA Modules:
  0.0 124.8 jit_solution(6507539270254517408)
XLA Ops:
  0.6 2.7 %collective-permute-start.2 = (bf16[192,1024]{1,0:T(8,128)(2,1)}, bf16[192,1024]{1,0:T(8,128)(2,1)S(1)}, u32[]{:S(2)}, u32[]{:S(2)}) collective-permute-start(bf16[192,1024]{1,0:T(8,128)(2,1)} %k_ref.1), channel_id=1, source_target_pairs={{0,2},{2,4},{4,6},{6,8},{8,10},{10,12},{12,14},{14,16},{16,18},{18... | collective-permute-start | bytes 1179656 | tf_op jit(solution)/shard_map/ppermute | solution.py:21
  3.3 0.7 collective-permute-start.3
  4.0 1.0 collective-permute-start.4
  5.1 0.8 fusion
  6.0 5.8 %collective-permute-start.1 = (bf16[32,1024]{1,0:T(8,128)(2,1)S(1)}, bf16[32,1024]{1,0:T(8,128)(2,1)S(1)}, u32[]{:S(2)}, u32[]{:S(2)}) collective-permute-start(bf16[32,1024]{1,0:T(8,128)(2,1)S(1)} %pad_maximum_fusion.1), channel_id=1, source_target_pairs={{0,254},{2,0},{4,2},{6,4},{8,6},{10,8},{12,10},{14,12},{16,14},{18... | collective-permute-start | bytes 196616 | tf_op jit(solution)/shard_map/ppermute | solution.py:21
  11.9 1.3 %collective-permute-done.low_ref = bf16[32,1024]{1,0:T(8,128)(2,1)S(1)} collective-permute-done((bf16[32,1024]{1,0:T(8,128)(2,1)S(1)}, bf16[32,1024]{1,0:T(8,128)(2,1)S(1)}, u32[]{:S(2)}, u32[]{:S(2)}) %collective-permute-start) | collective-permute-done | bytes 65568 | tf_op jit(solution)/shard_map/ppermute | solution.py:21
  13.2 0.6 copy-done.6
  13.8 6.5 %shard_map.110 = (bf16[192,1024]{1,0:T(8,128)(2,1)}, f32[8,32,128]{2,1,0:T(8,128)}) custom-call(s32[1]{0:T(128)} %bitcast.idx_ref, bf16[192,1024]{1,0:T(8,128)(2,1)} %grad_ref.1, bf16[192,1024]{1,0:T(8,128)(2,1)} %input_ref.1, bf16[32,1024]{1,0:T(8,128)(2,1)} %copy-done.6, bf16[32,1024]{1,0:T(8,128)(2,1)} %copy-done.7, bf16[31,1024]{1,0:T(8,128)(2,1)} %taps_ref.1), custom_call_target="tpu_custom_call" | custom-call | flops 48758784 | bytes 786432 | tf_op jit(solution)/shard_map/pallas_call | solution.py:68
  20.3 3.0 %collective-permute-start.5 = (bf16[192,1024]{1,0:T(8,128)(2,1)}, bf16[192,1024]{1,0:T(8,128)(2,1)S(1)}, u32[]{:S(2)}, u32[]{:S(2)}) collective-permute-start(bf16[192,1024]{1,0:T(8,128)(2,1)} %get-tuple-element.20.own_ref), channel_id=1, source_target_pairs={{0,1},{1,0},{2,3},{3,2},{4,5},{5,4},{6,7},{7,6},{8,9},{9,8},{10,11... | collective-permute-start | bytes 1179656 | tf_op jit(solution)/shard_map/ppermute | solution.py:264
  23.3 2.8 %collective-permute-start.6 = (bf16[192,1024]{1,0:T(8,128)(2,1)S(1)}, bf16[192,1024]{1,0:T(8,128)(2,1)}, u32[]{:S(2)}, u32[]{:S(2)}) collective-permute-start(bf16[192,1024]{1,0:T(8,128)(2,1)S(1)} %collective-permute-done.2.k1), channel_id=1, source_target_pairs={{0,2},{2,4},{4,6},{6,8},{8,10},{10,12},{12,14},{14,16},{16,18},{18... | collective-permute-start | bytes 1179656 | tf_op jit(solution)/shard_map/ppermute | solution.py:21
  26.1 7.2 %collective-permute-start.7 = (bf16[192,1024]{1,0:T(8,128)(2,1)S(1)}, bf16[192,1024]{1,0:T(8,128)(2,1)S(1)}, u32[]{:S(2)}, u32[]{:S(2)}) collective-permute-start(bf16[192,1024]{1,0:T(8,128)(2,1)S(1)} %collective-permute-done.3.q1), channel_id=1, source_target_pairs={{0,254},{2,0},{4,2},{6,4},{8,6},{10,8},{12,10},{14,12},{16,14},{18... | collective-permute-start | bytes 1179656 | tf_op jit(solution)/shard_map/ppermute | solution.py:21
  33.3 1.3 %collective-permute-done.6.k2 = bf16[192,1024]{1,0:T(8,128)(2,1)} collective-permute-done((bf16[192,1024]{1,0:T(8,128)(2,1)S(1)}, bf16[192,1024]{1,0:T(8,128)(2,1)}, u32[]{:S(2)}, u32[]{:S(2)}) %collective-permute-start.6) | collective-permute-done | bytes 393248 | tf_op jit(solution)/shard_map/ppermute | solution.py:21
  34.6 5.1 %shard_map.111.do_ref.d0 = bf16[192,1024]{1,0:T(8,128)(2,1)} custom-call(s32[1]{0:T(128)} %bitcast.1.idx_ref, bf16[192,1024]{1,0:T(8,128)(2,1)} %get-tuple-element.20.own_ref, bf16[192,1024]{1,0:T(8,128)(2,1)} %copy-done.5, bf16[1024,2048]{1,0:T(8,128)(2,1)} %weight_ref.1), custom_call_target="tpu_custom_call" | custom-call | flops 805306368 | bytes 4194304 | tf_op jit(solution)/shard_map/pallas_call | solution.py:107
  39.7 0.9 collective-permute-done.9.v2
  40.6 10.6 %collective-permute-start.12 = (bf16[192,1024]{1,0:T(8,128)(2,1)}, bf16[192,1024]{1,0:T(8,128)(2,1)}, u32[]{:S(2)}, u32[]{:S(2)}) collective-permute-start(bf16[192,1024]{1,0:T(8,128)(2,1)} %shard_map.111.do_ref.d0), channel_id=1, source_target_pairs={{0,254},{2,0},{4,2},{6,4},{8,6},{10,8},{12,10},{14,12},{16,14},{18... | collective-permute-start | bytes 1179656 | tf_op jit(solution)/shard_map/ppermute | solution.py:21
  51.2 1.7 %collective-permute-done.12.d1 = bf16[192,1024]{1,0:T(8,128)(2,1)} collective-permute-done((bf16[192,1024]{1,0:T(8,128)(2,1)}, bf16[192,1024]{1,0:T(8,128)(2,1)}, u32[]{:S(2)}, u32[]{:S(2)}) %collective-permute-start.12) | collective-permute-done | bytes 393248 | tf_op jit(solution)/shard_map/ppermute | solution.py:21
  52.9 8.5 %collective-permute-start.13 = (bf16[192,1024]{1,0:T(8,128)(2,1)}, bf16[192,1024]{1,0:T(8,128)(2,1)}, u32[]{:S(2)}, u32[]{:S(2)}) collective-permute-start(bf16[192,1024]{1,0:T(8,128)(2,1)} %collective-permute-done.12.d1), channel_id=1, source_target_pairs={{0,254},{2,0},{4,2},{6,4},{8,6},{10,8},{12,10},{14,12},{16,14},{18... | collective-permute-start | bytes 1179656 | tf_op jit(solution)/shard_map/ppermute | solution.py:21
  61.4 5.9 %all-to-all-start = ((f32[8,32,128]{2,1,0:T(8,128)}), f32[8,32,128]{2,1,0:T(8,128)S(1)}, u32[]{:S(2)}, u32[]{:S(2)}) async-start(f32[8,32,128]{2,1,0:T(8,128)} %get-tuple-element.25), calls=%async_computation | async-start | bytes 262144 | tf_op jit(solution)/shard_map/all_to_all | solution.py:29
  67.4 7.8 %all-to-all-done = f32[8,32,128]{2,1,0:T(8,128)S(1)} async-done(((f32[8,32,128]{2,1,0:T(8,128)}), f32[8,32,128]{2,1,0:T(8,128)S(1)}, u32[]{:S(2)}, u32[]{:S(2)}) %all-to-all-start) | async-done | bytes 131104 | tf_op jit(solution)/shard_map/all_to_all | solution.py:29
  75.2 0.7 broadcast_in_dim.6
  76.0 10.9 %all-to-all-start.1 = ((f32[16,32,128]{2,1,0:T(8,128)}), f32[16,32,128]{2,1,0:T(8,128)S(1)}, u32[]{:S(2)}, u32[]{:S(2)}) async-start(f32[16,32,128]{2,1,0:T(8,128)} %broadcast_in_dim.6), calls=%async_computation.1 | async-start | bytes 524288 | tf_op jit(solution)/shard_map/all_to_all | solution.py:31
  87.2 3.0 %collective-permute-start.14 = (bf16[192,1024]{1,0:T(8,128)(2,1)}, bf16[192,1024]{1,0:T(8,128)(2,1)}, u32[]{:S(2)}, u32[]{:S(2)}) collective-permute-start(bf16[192,1024]{1,0:T(8,128)(2,1)} %collective-permute-done.13.d2), channel_id=1, source_target_pairs={{0,254},{2,0},{4,2},{6,4},{8,6},{10,8},{12,10},{14,12},{16,14},{18... | collective-permute-start | bytes 1179656 | tf_op jit(solution)/shard_map/ppermute | solution.py:21
  90.1 4.0 %all-to-all-done.1 = f32[16,32,128]{2,1,0:T(8,128)S(1)} async-done(((f32[16,32,128]{2,1,0:T(8,128)}), f32[16,32,128]{2,1,0:T(8,128)S(1)}, u32[]{:S(2)}, u32[]{:S(2)}) %all-to-all-start.1) | async-done | bytes 262176 | tf_op jit(solution)/shard_map/all_to_all | solution.py:31
  94.1 0.7 broadcast_in_dim.7
  94.8 4.7 %all-to-all-start.2 = ((f32[8,32,128]{2,1,0:T(8,128)}), f32[8,32,128]{2,1,0:T(8,128)S(1)}, u32[]{:S(2)}, u32[]{:S(2)}) async-start(f32[8,32,128]{2,1,0:T(8,128)} %broadcast_in_dim.7), calls=%async_computation.2 | async-start | bytes 262144 | tf_op jit(solution)/shard_map/all_to_all | solution.py:33
  99.6 1.0 copy-done
  100.6 9.2 %shard_map.112 = (bf16[192,1024]{1,0:T(8,128)(2,1)}, f32[16,192]{1,0:T(8,128)S(1)}) custom-call(s32[1]{0:T(128)} %bitcast.idx_ref, bf16[192,1024]{1,0:T(8,128)(2,1)S(1)} %copy-done.2, bf16[192,1024]{1,0:T(8,128)(2,1)S(1)} %copy-done, bf16[192,1024]{1,0:T(8,128)(2,1)} %collective-permute-done.8.k3, bf16[192,1024]{1,0:T(8,128)(2,1)} %collective-permute-done.6.k2, ...), custom_call_target="tpu_custom_call" | custom-call | flops 1509949440 | bytes 4718592 | tf_op jit(solution)/shard_map/pallas_call | solution.py:163
  109.7 0.7 collective-permute-start.15
  110.5 2.1 %collective-permute-start.16 = (f32[16,192]{1,0:T(8,128)S(1)}, f32[16,192]{1,0:T(8,128)S(1)}, u32[]{:S(2)}, u32[]{:S(2)}) collective-permute-start(f32[16,192]{1,0:T(8,128)S(1)} %get-tuple-element.24.s0), channel_id=1, source_target_pairs={{0,252},{2,254},{4,0},{6,2},{8,4},{10,6},{12,8},{14,10},{16,12},{1... | collective-permute-start | bytes 36872 | tf_op jit(solution)/shard_map/ppermute | solution.py:21
  112.5 1.5 %collective-permute-start.17 = (f32[16,192]{1,0:T(8,128)S(1)}, f32[16,192]{1,0:T(8,128)S(1)}, u32[]{:S(2)}, u32[]{:S(2)}) collective-permute-start(f32[16,192]{1,0:T(8,128)S(1)} %get-tuple-element.24.s0), channel_id=1, source_target_pairs={{0,250},{2,252},{4,254},{6,0},{8,2},{10,4},{12,6},{14,8},{16,10},{... | collective-permute-start | bytes 36872 | tf_op jit(solution)/shard_map/ppermute | solution.py:21
  114.1 3.1 %collective-permute-done.17.s3 = f32[16,192]{1,0:T(8,128)S(1)} collective-permute-done((f32[16,192]{1,0:T(8,128)S(1)}, f32[16,192]{1,0:T(8,128)S(1)}, u32[]{:S(2)}, u32[]{:S(2)}) %collective-permute-start.17) | collective-permute-done | bytes 12320 | tf_op jit(solution)/shard_map/ppermute | solution.py:21
  117.2 7.6 %shard_map.113 = (bf16[192,1024]{1,0:T(8,128)(2,1)}, bf16[192,1024]{1,0:T(8,128)(2,1)}, f32[31,1024]{1,0:T(8,128)}) custom-call(s32[1]{0:T(128)} %bitcast.idx_ref, bf16[192,1024]{1,0:T(8,128)(2,1)S(1)} %copy-done.3, bf16[192,1024]{1,0:T(8,128)(2,1)S(1)} %copy-done.4, bf16[192,1024]{1,0:T(8,128)(2,1)S(1)} %copy-done.2, ...), custom_call_target="tpu_custom_call" | custom-call | flops 1509949440 | bytes 4718592 | tf_op jit(solution)/shard_map/pallas_call | solution.py:227
  (37 shorter events, 0.6 us)
Async XLA Ops:
  0.6 12.5 %collective-permute-start.2 = (bf16[192,1024]{1,0:T(8,128)(2,1)}, bf16[192,1024]{1,0:T(8,128)(2,1)S(1)}, u32[]{:S(2)}, u32[]{:S(2)}) collective-permute-start(bf16[192,1024]{1,0:T(8,128)(2,1)} %k_ref.1), channel_id=1, source_target_pairs={{0,2},{2,4},{4,6},{6,8},{8,10},{10,12},{12,14},{14,16},{16,18},{18... | collective-permute-start | bytes 1179656 | tf_op jit(solution)/shard_map/ppermute | solution.py:21
  3.3 9.9 %collective-permute-start.3 = (bf16[192,1024]{1,0:T(8,128)(2,1)}, bf16[192,1024]{1,0:T(8,128)(2,1)S(1)}, u32[]{:S(2)}, u32[]{:S(2)}) collective-permute-start(bf16[192,1024]{1,0:T(8,128)(2,1)} %q0.1), channel_id=1, source_target_pairs={{0,254},{2,0},{4,2},{6,4},{8,6},{10,8},{12,10},{14,12},{16,14},{18... | collective-permute-start | bytes 1179656 | tf_op jit(solution)/shard_map/ppermute | solution.py:21
  4.0 16.3 %collective-permute-start.4 = (bf16[192,1024]{1,0:T(8,128)(2,1)}, bf16[192,1024]{1,0:T(8,128)(2,1)S(1)}, u32[]{:S(2)}, u32[]{:S(2)}) collective-permute-start(bf16[192,1024]{1,0:T(8,128)(2,1)} %v_ref.1), channel_id=1, source_target_pairs={{0,2},{2,4},{4,6},{6,8},{8,10},{10,12},{12,14},{14,16},{16,18},{18... | collective-permute-start | bytes 1179656 | tf_op jit(solution)/shard_map/ppermute | solution.py:21
  5.9 7.3 %collective-permute-start = (bf16[32,1024]{1,0:T(8,128)(2,1)S(1)}, bf16[32,1024]{1,0:T(8,128)(2,1)S(1)}, u32[]{:S(2)}, u32[]{:S(2)}) collective-permute-start(bf16[32,1024]{1,0:T(8,128)(2,1)S(1)} %pad_maximum_fusion), channel_id=1, source_target_pairs={{0,2},{2,4},{4,6},{6,8},{8,10},{10,12},{12,14},{14,16},{16,18},{18... | collective-permute-start | bytes 196616 | tf_op jit(solution)/shard_map/ppermute | solution.py:21
  6.0 93.6 %copy-start.2 = (bf16[192,1024]{1,0:T(8,128)(2,1)S(1)}, bf16[192,1024]{1,0:T(8,128)(2,1)}, u32[]{:S(2)}) copy-start(bf16[192,1024]{1,0:T(8,128)(2,1)} %q0.1) | copy-start | bytes 1179652
  6.0 93.6 %copy-start.3 = (bf16[192,1024]{1,0:T(8,128)(2,1)S(1)}, bf16[192,1024]{1,0:T(8,128)(2,1)}, u32[]{:S(2)}) copy-start(bf16[192,1024]{1,0:T(8,128)(2,1)} %k_ref.1) | copy-start | bytes 1179652
  6.0 93.6 %copy-start.4 = (bf16[192,1024]{1,0:T(8,128)(2,1)S(1)}, bf16[192,1024]{1,0:T(8,128)(2,1)}, u32[]{:S(2)}) copy-start(bf16[192,1024]{1,0:T(8,128)(2,1)} %v_ref.1) | copy-start | bytes 1179652
  6.0 7.1 %collective-permute-start.1 = (bf16[32,1024]{1,0:T(8,128)(2,1)S(1)}, bf16[32,1024]{1,0:T(8,128)(2,1)S(1)}, u32[]{:S(2)}, u32[]{:S(2)}) collective-permute-start(bf16[32,1024]{1,0:T(8,128)(2,1)S(1)} %pad_maximum_fusion.1), channel_id=1, source_target_pairs={{0,254},{2,0},{4,2},{6,4},{8,6},{10,8},{12,10},{14,12},{16,14},{18... | collective-permute-start | bytes 196616 | tf_op jit(solution)/shard_map/ppermute | solution.py:21
  13.2 0.6 copy-start.6
  13.2 0.6 copy-start.7
  20.3 13.0 %collective-permute-start.5 = (bf16[192,1024]{1,0:T(8,128)(2,1)}, bf16[192,1024]{1,0:T(8,128)(2,1)S(1)}, u32[]{:S(2)}, u32[]{:S(2)}) collective-permute-start(bf16[192,1024]{1,0:T(8,128)(2,1)} %get-tuple-element.20.own_ref), channel_id=1, source_target_pairs={{0,1},{1,0},{2,3},{3,2},{4,5},{5,4},{6,7},{7,6},{8,9},{9,8},{10,11... | collective-permute-start | bytes 1179656 | tf_op jit(solution)/shard_map/ppermute | solution.py:264
  23.3 11.3 %collective-permute-start.6 = (bf16[192,1024]{1,0:T(8,128)(2,1)S(1)}, bf16[192,1024]{1,0:T(8,128)(2,1)}, u32[]{:S(2)}, u32[]{:S(2)}) collective-permute-start(bf16[192,1024]{1,0:T(8,128)(2,1)S(1)} %collective-permute-done.2.k1), channel_id=1, source_target_pairs={{0,2},{2,4},{4,6},{6,8},{8,10},{10,12},{12,14},{14,16},{16,18},{18... | collective-permute-start | bytes 1179656 | tf_op jit(solution)/shard_map/ppermute | solution.py:21
  26.1 8.6 %collective-permute-start.7 = (bf16[192,1024]{1,0:T(8,128)(2,1)S(1)}, bf16[192,1024]{1,0:T(8,128)(2,1)S(1)}, u32[]{:S(2)}, u32[]{:S(2)}) collective-permute-start(bf16[192,1024]{1,0:T(8,128)(2,1)S(1)} %collective-permute-done.3.q1), channel_id=1, source_target_pairs={{0,254},{2,0},{4,2},{6,4},{8,6},{10,8},{12,10},{14,12},{16,14},{18... | collective-permute-start | bytes 1179656 | tf_op jit(solution)/shard_map/ppermute | solution.py:21
  33.3 7.3 %collective-permute-start.9 = (bf16[192,1024]{1,0:T(8,128)(2,1)S(1)}, bf16[192,1024]{1,0:T(8,128)(2,1)}, u32[]{:S(2)}, u32[]{:S(2)}) collective-permute-start(bf16[192,1024]{1,0:T(8,128)(2,1)S(1)} %collective-permute-done.4.v1), channel_id=1, source_target_pairs={{0,2},{2,4},{4,6},{6,8},{8,10},{10,12},{12,14},{14,16},{16,18},{18... | collective-permute-start | bytes 1179656 | tf_op jit(solution)/shard_map/ppermute | solution.py:21
  33.3 1.3 %copy-start.5 = (bf16[192,1024]{1,0:T(8,128)(2,1)}, bf16[192,1024]{1,0:T(8,128)(2,1)S(1)}, u32[]{:S(2)}) copy-start(bf16[192,1024]{1,0:T(8,128)(2,1)S(1)} %collective-permute-done.5.other_ref) | copy-start | bytes 1179652
  39.7 77.5 %copy-start.1 = (bf16[192,1024]{1,0:T(8,128)(2,1)S(1)}, bf16[192,1024]{1,0:T(8,128)(2,1)}, u32[]{:S(2)}) copy-start(bf16[192,1024]{1,0:T(8,128)(2,1)} %shard_map.111.do_ref.d0) | copy-start | bytes 1179652
  40.6 12.3 %collective-permute-start.12 = (bf16[192,1024]{1,0:T(8,128)(2,1)}, bf16[192,1024]{1,0:T(8,128)(2,1)}, u32[]{:S(2)}, u32[]{:S(2)}) collective-permute-start(bf16[192,1024]{1,0:T(8,128)(2,1)} %shard_map.111.do_ref.d0), channel_id=1, source_target_pairs={{0,254},{2,0},{4,2},{6,4},{8,6},{10,8},{12,10},{14,12},{16,14},{18... | collective-permute-start | bytes 1179656 | tf_op jit(solution)/shard_map/ppermute | solution.py:21
  52.9 34.2 %collective-permute-start.13 = (bf16[192,1024]{1,0:T(8,128)(2,1)}, bf16[192,1024]{1,0:T(8,128)(2,1)}, u32[]{:S(2)}, u32[]{:S(2)}) collective-permute-start(bf16[192,1024]{1,0:T(8,128)(2,1)} %collective-permute-done.12.d1), channel_id=1, source_target_pairs={{0,254},{2,0},{4,2},{6,4},{8,6},{10,8},{12,10},{14,12},{16,14},{18... | collective-permute-start | bytes 1179656 | tf_op jit(solution)/shard_map/ppermute | solution.py:21
  61.4 13.8 %all-to-all-start = ((f32[8,32,128]{2,1,0:T(8,128)}), f32[8,32,128]{2,1,0:T(8,128)S(1)}, u32[]{:S(2)}, u32[]{:S(2)}) async-start(f32[8,32,128]{2,1,0:T(8,128)} %get-tuple-element.25), calls=%async_computation | async-start | bytes 262144 | tf_op jit(solution)/shard_map/all_to_all | solution.py:29
  67.3 32.2 %collective-permute-start.8 = (bf16[192,1024]{1,0:T(8,128)(2,1)}, bf16[192,1024]{1,0:T(8,128)(2,1)}, u32[]{:S(2)}, u32[]{:S(2)}) collective-permute-start(bf16[192,1024]{1,0:T(8,128)(2,1)} %collective-permute-done.6.k2), channel_id=1, source_target_pairs={{0,2},{2,4},{4,6},{6,8},{8,10},{10,12},{12,14},{14,16},{16,18},{18... | collective-permute-start | bytes 1179656 | tf_op jit(solution)/shard_map/ppermute | solution.py:21
  67.3 32.2 %collective-permute-start.10 = (bf16[192,1024]{1,0:T(8,128)(2,1)}, bf16[192,1024]{1,0:T(8,128)(2,1)}, u32[]{:S(2)}, u32[]{:S(2)}) collective-permute-start(bf16[192,1024]{1,0:T(8,128)(2,1)} %collective-permute-done.9.v2), channel_id=1, source_target_pairs={{0,2},{2,4},{4,6},{6,8},{8,10},{10,12},{12,14},{14,16},{16,18},{18... | collective-permute-start | bytes 1179656 | tf_op jit(solution)/shard_map/ppermute | solution.py:21
  76.0 18.1 %all-to-all-start.1 = ((f32[16,32,128]{2,1,0:T(8,128)}), f32[16,32,128]{2,1,0:T(8,128)S(1)}, u32[]{:S(2)}, u32[]{:S(2)}) async-start(f32[16,32,128]{2,1,0:T(8,128)} %broadcast_in_dim.6), calls=%async_computation.1 | async-start | bytes 524288 | tf_op jit(solution)/shard_map/all_to_all | solution.py:31
  86.9 27.2 %collective-permute-start.11 = (bf16[192,1024]{1,0:T(8,128)(2,1)S(1)}, bf16[192,1024]{1,0:T(8,128)(2,1)}, u32[]{:S(2)}, u32[]{:S(2)}) collective-permute-start(bf16[192,1024]{1,0:T(8,128)(2,1)S(1)} %collective-permute-done.7.q2), channel_id=1, source_target_pairs={{0,254},{2,0},{4,2},{6,4},{8,6},{10,8},{12,10},{14,12},{16,14},{18... | collective-permute-start | bytes 1179656 | tf_op jit(solution)/shard_map/ppermute | solution.py:21
  87.2 30.0 %collective-permute-start.14 = (bf16[192,1024]{1,0:T(8,128)(2,1)}, bf16[192,1024]{1,0:T(8,128)(2,1)}, u32[]{:S(2)}, u32[]{:S(2)}) collective-permute-start(bf16[192,1024]{1,0:T(8,128)(2,1)} %collective-permute-done.13.d2), channel_id=1, source_target_pairs={{0,254},{2,0},{4,2},{6,4},{8,6},{10,8},{12,10},{14,12},{16,14},{18... | collective-permute-start | bytes 1179656 | tf_op jit(solution)/shard_map/ppermute | solution.py:21
  94.8 19.3 %all-to-all-start.2 = ((f32[8,32,128]{2,1,0:T(8,128)}), f32[8,32,128]{2,1,0:T(8,128)S(1)}, u32[]{:S(2)}, u32[]{:S(2)}) async-start(f32[8,32,128]{2,1,0:T(8,128)} %broadcast_in_dim.7), calls=%async_computation.2 | async-start | bytes 262144 | tf_op jit(solution)/shard_map/all_to_all | solution.py:33
  99.6 1.0 copy-start
  109.7 4.3 %collective-permute-start.15 = (f32[16,192]{1,0:T(8,128)S(1)}, f32[16,192]{1,0:T(8,128)S(1)}, u32[]{:S(2)}, u32[]{:S(2)}) collective-permute-start(f32[16,192]{1,0:T(8,128)S(1)} %get-tuple-element.24.s0), channel_id=1, source_target_pairs={{0,254},{2,0},{4,2},{6,4},{8,6},{10,8},{12,10},{14,12},{16,14},{18... | collective-permute-start | bytes 36872 | tf_op jit(solution)/shard_map/ppermute | solution.py:21
  110.5 3.6 %collective-permute-start.16 = (f32[16,192]{1,0:T(8,128)S(1)}, f32[16,192]{1,0:T(8,128)S(1)}, u32[]{:S(2)}, u32[]{:S(2)}) collective-permute-start(f32[16,192]{1,0:T(8,128)S(1)} %get-tuple-element.24.s0), channel_id=1, source_target_pairs={{0,252},{2,254},{4,0},{6,2},{8,4},{10,6},{12,8},{14,10},{16,12},{1... | collective-permute-start | bytes 36872 | tf_op jit(solution)/shard_map/ppermute | solution.py:21
  112.5 4.7 %collective-permute-start.17 = (f32[16,192]{1,0:T(8,128)S(1)}, f32[16,192]{1,0:T(8,128)S(1)}, u32[]{:S(2)}, u32[]{:S(2)}) collective-permute-start(f32[16,192]{1,0:T(8,128)S(1)} %get-tuple-element.24.s0), channel_id=1, source_target_pairs={{0,250},{2,252},{4,254},{6,0},{8,2},{10,4},{12,6},{14,8},{16,10},{... | collective-permute-start | bytes 36872 | tf_op jit(solution)/shard_map/ppermute | solution.py:21

commit v4 on v3

v4 whole, which is shorter than its diff:
```python
import functools
import math

import jax
import jax.numpy as jnp
from jax import lax
from jax.experimental import pallas as pl
from jax.experimental.pallas import tpu as pltpu
from jax.sharding import Mesh
from jax.sharding import PartitionSpec as P

HEAD = 128
EDGE = 16
NT = (((1,), (1,)), ((), ()))
BIG = 1e30
GROUP = 2
CTX = ("far", "near")


def rotated(part, by):
    count = lax.axis_size(CTX)
    return lax.ppermute(part, CTX, [(i, (i + by) % count) for i in range(count)])


def after(parts, done):
    return lax.optimization_barrier(tuple(parts) + tuple(done))[: len(parts)]


def conv_kernel(last, idx_ref, grad_ref, input_ref, low_ref, high_ref, taps_ref, out_ref, rows_ref, gpad, cpad):
    block = grad_ref.shape[0]
    taps_count = taps_ref.shape[0]
    reach = taps_count // 2
    device = idx_ref[0]
    f32 = jnp.float32
    rows_ref[:, taps_count:, :] = jnp.zeros_like(rows_ref[:, taps_count:, :])
    for group in range(rows_ref.shape[0]):
        lanes = slice(group * HEAD, (group + 1) * HEAD)
        low = jnp.where(device > 0, low_ref[block:, lanes].astype(f32), 0.0)
        high = jnp.where(device < last, high_ref[block:, lanes].astype(f32), 0.0)
        grad = grad_ref[:, lanes].astype(f32)
        cpad[:EDGE, lanes] = low[:EDGE]
        gpad[:EDGE, lanes] = low[EDGE:]
        cpad[EDGE : EDGE + block, lanes] = input_ref[:, lanes].astype(f32)
        gpad[EDGE : EDGE + block, lanes] = grad
        cpad[EDGE + block :, lanes] = high[:EDGE]
        gpad[EDGE + block :, lanes] = high[EDGE:]
        taps = taps_ref[:, lanes].astype(f32)
        total = jnp.zeros_like(grad)
        for tap in range(taps_count):
            total = total + taps[tap : tap + 1] * gpad[pl.ds(EDGE + reach - tap, block), lanes]
        out_ref[:, lanes] = (grad + total).astype(out_ref.dtype)
        for tap in range(taps_count):
            prod = grad * cpad[pl.ds(EDGE - reach + tap, block), lanes]
            rows_ref[group, tap : tap + 1, :] = jnp.sum(prod, axis=0, keepdims=True)


def conv(device, grad, inputs, low, high, taps, last):
    block, width = grad.shape
    count = taps.shape[0]
    lanes = GROUP * HEAD
    rows = 8 * pl.cdiv(count, 8)
    column = lambda rows: pl.BlockSpec((rows, lanes), lambda c: (0, c))
    return pl.pallas_call(
        functools.partial(conv_kernel, last),
        grid=(width // lanes,),
        in_specs=[
            pl.BlockSpec(memory_space=pltpu.SMEM),
            column(block),
            column(block),
            column(block + 2 * EDGE),
            column(block + 2 * EDGE),
            column(count),
        ],
        out_specs=[column(block), pl.BlockSpec((GROUP, rows, HEAD), lambda c: (c, 0, 0))],
        out_shape=[
            jax.ShapeDtypeStruct((block, width), jnp.bfloat16),
            jax.ShapeDtypeStruct((width // HEAD, rows, HEAD), jnp.float32),
        ],
        scratch_shapes=[
            pltpu.VMEM((block + 2 * EDGE, lanes), jnp.float32),
            pltpu.VMEM((block + 2 * EDGE, lanes), jnp.float32),
        ],
        compiler_params=pltpu.CompilerParams(vmem_limit_bytes=16 * 2**20),
        cost_estimate=pl.CostEstimate(flops=8 * block * width * count, bytes_accessed=4 * block * width, transcendentals=0),
    )(device, grad, inputs, low, high, taps)


def own_kernel(idx_ref, part_ref, weight_ref, out_ref):
    out_ref[...] = lax.dot_general(part_ref[...], weight_ref[...], NT, preferred_element_type=jnp.float32)


def other_kernel(idx_ref, part_ref, weight_ref, before_ref, out_ref):
    total = lax.dot_general(part_ref[...], weight_ref[...], NT, preferred_element_type=jnp.float32)
    out_ref[...] = (before_ref[...] + total).astype(out_ref.dtype)


def project(place, part, weight, before=None):
    block, half = part.shape
    rows = weight.shape[0]
    step = 256
    columns = pl.BlockSpec((block, step), lambda n, place: (0, n))
    return pl.pallas_call(
        own_kernel if before is None else other_kernel,
        grid_spec=pltpu.PrefetchScalarGridSpec(
            num_scalar_prefetch=1,
            grid=(rows // step,),
            in_specs=[
                pl.BlockSpec((block, half), lambda n, place: (0, 0)),
                pl.BlockSpec((step, half), lambda n, place: (n, place[0])),
            ]
            + [columns] * (before is not None),
            out_specs=columns,
        ),
        out_shape=jax.ShapeDtypeStruct((block, rows), jnp.float32 if before is None else jnp.bfloat16),
        compiler_params=pltpu.CompilerParams(vmem_limit_bytes=56 * 2**20),
        cost_estimate=pl.CostEstimate(flops=2 * block * rows * half, bytes_accessed=2 * rows * half, transcendentals=0),
    )(place, part, weight, *(() if before is None else (before,)))


def query_kernel(scale, idx_ref, q_ref, do_ref, k3, k2, k1, k0, v3, v2, v1, v0, out_ref, stats_ref, bias, columns):
    step = pl.program_id(0)
    steps = pl.num_programs(0)
    block = q_ref.shape[0]
    f32 = jnp.float32

    @pl.when(step == 0)
    def _():
        rows = lax.broadcasted_iota(jnp.int32, bias.shape, 0)
        cols = lax.broadcasted_iota(jnp.int32, bias.shape, 1)
        valid = (cols <= 3 * block + rows) & (cols >= (3 - idx_ref[0]) * block)
        bias[...] = jnp.where(valid, 0.0, -jnp.inf)
        columns[...] = jnp.zeros_like(columns)

    lane = lax.broadcasted_iota(jnp.int32, columns.shape, 1)
    both = columns[...]
    for group in range(GROUP):
        lanes = slice(group * HEAD, (group + 1) * HEAD)
        keys = jnp.concatenate([ref[:block, lanes] for ref in (k3, k2, k1, k0)], axis=0)
        values = jnp.concatenate([ref[:, lanes] for ref in (v3, v2, v1, v0)], axis=0)
        scores = lax.dot_general(q_ref[:, lanes], keys, NT, preferred_element_type=f32) * scale + bias[...]
        top = jnp.max(scores, axis=1, keepdims=True)
        expo = jnp.exp(scores - top)
        denom = jnp.sum(expo, axis=1, keepdims=True)
        probs = expo * (1.0 / denom)
        prob_grad = lax.dot_general(do_ref[:, lanes], values, NT, preferred_element_type=f32)
        delta = jnp.sum(probs.astype(jnp.bfloat16).astype(f32) * prob_grad, axis=1, keepdims=True)
        score_grad = (probs * (prob_grad - delta)).astype(jnp.bfloat16)
        out = jnp.dot(score_grad, keys, preferred_element_type=f32) * scale
        out_ref[:, lanes] = out.astype(out_ref.dtype)
        both = jnp.where(lane == GROUP * step + group, top + jnp.log(denom), both)
        both = jnp.where(lane == GROUP * (steps + step) + group, delta, both)
    columns[...] = both

    @pl.when(step == steps - 1)
    def _():
        stats_ref[...] = columns[...].T[: stats_ref.shape[0]]


def head_columns(array):
    return pl.BlockSpec((array.shape[0], GROUP * HEAD), lambda h: (0, h))


def query_side(device, queries, out_grad, keys, values, scale):
    block, width = queries.shape
    heads = width // HEAD
    operands = (queries, out_grad, *keys, *values)
    return pl.pallas_call(
        functools.partial(query_kernel, scale),
        grid=(heads // GROUP,),
        in_specs=[pl.BlockSpec(memory_space=pltpu.SMEM)] + [head_columns(array) for array in operands],
        out_specs=[head_columns(queries), pl.BlockSpec((2 * heads, block), lambda h: (0, 0))],
        out_shape=[
            jax.ShapeDtypeStruct((block, width), jnp.bfloat16),
            jax.ShapeDtypeStruct((2 * heads, block), jnp.float32),
        ],
        scratch_shapes=[
            pltpu.VMEM((block, 4 * block), jnp.float32),
            pltpu.VMEM((block, HEAD), jnp.float32),
        ],
        compiler_params=pltpu.CompilerParams(vmem_limit_bytes=32 * 2**20),
        cost_estimate=pl.CostEstimate(
            flops=40 * block * block * width, bytes_accessed=24 * block * width, transcendentals=4 * block * block * heads
        ),
    )(device, *operands)


def key_kernel(scale, last, idx_ref, k_ref, v_ref, q0, q1, q2, q3, d0, d1, d2, d3, s0, s1, s2, s3, dk_ref, dv_ref, bias, lse, delta):
    step = pl.program_id(0)
    block = k_ref.shape[0]
    heads = lse.shape[0]
    f32 = jnp.float32

    @pl.when(step == 0)
    def _():
        rows = lax.broadcasted_iota(jnp.int32, bias.shape, 0)
        cols = lax.broadcasted_iota(jnp.int32, bias.shape, 1)
        bias[...] = jnp.where(cols >= rows, 0.0, -jnp.inf)
        parts = [s0[...]]
        for hop, ref in enumerate((s1, s2, s3), 1):
            part = ref[...]
            row = lax.broadcasted_iota(jnp.int32, part.shape, 0)
            parts.append(jnp.where((idx_ref[0] + hop > last) & (row < heads), BIG, part))
        stats = jnp.concatenate(parts, axis=1)
        for one in range(heads):
            lse[one] = stats[one : one + 1]
            delta[one] = stats[heads + one : heads + one + 1]

    edge = bias.shape[1]
    for group in range(GROUP):
        lanes = slice(group * HEAD, (group + 1) * HEAD)
        head = GROUP * step + group
        queries = jnp.concatenate([ref[:block, lanes] for ref in (q0, q1, q2, q3)], axis=0)
        dos = jnp.concatenate([ref[:, lanes] for ref in (d0, d1, d2, d3)], axis=0)
        scores = lax.dot_general(k_ref[:, lanes], queries, NT, preferred_element_type=f32) * scale - lse[head]
        scores = jnp.concatenate([scores[:, :edge] + bias[...], scores[:, edge:]], axis=1)
        probs = jnp.exp(scores)
        prob_grad = lax.dot_general(v_ref[:, lanes], dos, NT, preferred_element_type=f32)
        score_grad = (probs * (prob_grad - delta[head])).astype(jnp.bfloat16)
        dk_ref[:, lanes] = (jnp.dot(score_grad, queries, preferred_element_type=f32) * scale).astype(dk_ref.dtype)
        dv_ref[:, lanes] = jnp.dot(probs.astype(jnp.bfloat16), dos, preferred_element_type=f32).astype(dv_ref.dtype)


def key_side(device, keys, values, queries, out_grads, stats, scale, last):
    block, width = keys.shape
    heads = width // HEAD
    whole = pl.BlockSpec((2 * heads, block), lambda h: (0, 0))
    shape = jax.ShapeDtypeStruct((block, width), jnp.bfloat16)
    operands = (keys, values, *queries, *out_grads)
    return pl.pallas_call(
        functools.partial(key_kernel, scale, last),
        grid=(heads // GROUP,),
        in_specs=[pl.BlockSpec(memory_space=pltpu.SMEM)] + [head_columns(array) for array in operands] + [whole] * 4,
        out_specs=[head_columns(keys)] * 2,
        out_shape=[shape, shape],
        scratch_shapes=[
            pltpu.VMEM((block, 256), jnp.float32),
            pltpu.VMEM((heads, 1, 4 * block), jnp.float32),
            pltpu.VMEM((heads, 1, 4 * block), jnp.float32),
        ],
        compiler_params=pltpu.CompilerParams(vmem_limit_bytes=32 * 2**20),
        cost_estimate=pl.CostEstimate(
            flops=40 * block * block * width, bytes_accessed=24 * block * width, transcendentals=4 * block * block * heads
        ),
    )(device, *operands, *stats)


def per_device(queries, keys, values, stream_grad, conv_input, conv_weight, out_weight):
    block = queries.shape[0]
    last = lax.axis_size(CTX) - 1
    scale = 1.0 / math.sqrt(HEAD)
    device = lax.axis_index(CTX).astype(jnp.int32).reshape(1)
    tp = lax.axis_index("tp").astype(jnp.int32).reshape(1)

    k1 = rotated(jnp.concatenate([keys, conv_input[block - EDGE :], stream_grad[block - EDGE :]], axis=0), 1)
    q1 = rotated(jnp.concatenate([queries, conv_input[:EDGE], stream_grad[:EDGE]], axis=0), -1)
    (first,) = after((values,), (q1,))
    v1 = rotated(first, 1)
    k2, q2 = rotated(k1, 1), rotated(q1, -1)
    v2 = rotated(v1, 1)

    grad_stream, tap_rows = conv(device, stream_grad, conv_input, k1, q1, conv_weight, last)
    other = lax.ppermute(grad_stream, "tp", [(0, 1), (1, 0)])
    before = project(tp, grad_stream, out_weight)
    (tap_rows,) = after((tap_rows,), (k2,))
    tap_sums = jnp.sum(lax.all_to_all(tap_rows, "far", 0, 0, tiled=True), axis=0)
    (other,) = after((other,), (k2, q2, tap_sums))
    out_grad = project(1 - tp, other, out_weight, before)
    k3, q3 = rotated(k2, 1), rotated(q2, -1)
    v3 = rotated(v2, 1)

    (sent,) = after((out_grad,), (v2,))
    d1 = rotated(sent, -1)
    (sent,) = after((d1,), (k3, q3))
    d2 = rotated(sent, -1)
    (sent,) = after((d2,), (v3,))
    d3 = rotated(sent, -1)

    copies = jnp.broadcast_to(tap_sums, (lax.axis_size("near"),) + tap_sums.shape)
    (copies,) = after((copies,), (v2, out_grad))
    tap_sums = jnp.sum(lax.all_to_all(copies, "near", 0, 0, tiled=True), axis=0)
    (inner,) = after((queries,), (tap_sums,))
    query_grad, stats = query_side(device, inner, out_grad, (k3, k2, k1, keys), (v3, v2, v1, values), scale)
    all_stats = [stats] + [rotated(stats, -hop) for hop in (1, 2, 3)]
    copies = jnp.broadcast_to(tap_sums, (lax.axis_size("far"),) + tap_sums.shape)
    (copies,) = after((copies,), (stats,))
    tap_sums = lax.all_to_all(copies, "far", 0, 0, tiled=True)
    (inner,) = after((keys,), (tap_sums,))
    key_grad, value_grad = key_side(
        device, inner, values, (queries, q1, q2, q3), (out_grad, d1, d2, d3), all_stats, scale, last
    )
    rows = jnp.transpose(tap_sums, (1, 0, 2)).reshape(tap_sums.shape[1], -1)[: conv_weight.shape[0]]
    kernel_grad = rows / math.sqrt(block * (last + 1))
    return (query_grad, key_grad, value_grad, grad_stream, kernel_grad)


def solution(mesh):
    count, pair = mesh.devices.shape
    far = 8
    split = Mesh(mesh.devices.reshape(far, count // far, pair), CTX + ("tp",))
    frames = P(CTX, "tp")
    return jax.shard_map(
        per_device,
        mesh=split,
        in_specs=(frames,) * 5 + (P(None, "tp"), P("tp", None)),
        out_specs=(frames,) * 4 + (P(None, "tp"),),
        check_vma=False,
    )
```

time: 126 us -> 113 us (0.90)
  starting transfers between devices: 71.6 us -> 49.4 us
  local copies, waits for them, and re-layouts: 3.86 us -> 8.8 us
  other arithmetic: 0.05 us -> 3.06 us
    ppermute x17 -> x15, starting transfers between devices: 47.1 us -> 31 us  [rotated(): lax.ppermute(part, CTX, [(i, (i + by) % count) for i in range(count)])]
    all_to_all x3, starting transfers between devices: 21.5 us -> 15.8 us  [the longest x1 7.22 us: per_device(): tap_sums = jnp.sum(lax.all_to_all(copies, 'near', 0, 0, tiled=True), axis=0)]
    unnamed x16 -> x20, local copies, waits for them, and re-layouts: 1.65 us -> 6.51 us
    all_to_all x3, waiting for transfers between devices: 11.8 us -> 9.26 us  [the longest x1 6.84 us: per_device(): tap_sums = jnp.sum(lax.all_to_all(copies, 'near', 0, 0, tiled=True), axis=0)]
    concatenate x2, other arithmetic: 0.01 us -> 2.05 us  [the longest x1 1.03 us: per_device(): jnp.concatenate([queries, conv_input[:EDGE], stream_grad[:EDGE]], axis=0)]
    ppermute x1, waiting for transfers between devices: 0.01 us -> 2.03 us  [per_device(): other = lax.ppermute(grad_stream, 'tp', [(0, 1), (1, 0)])]
    ppermute x17 -> x15, waiting for transfers between devices: 8.34 us -> 8.1 us  [rotated(): lax.ppermute(part, CTX, [(i, (i + by) % count) for i in range(count)])]
    pallas_call x3 -> x4, Pallas kernels: 21.8 us -> 21.9 us  [the longest x2 8.6 us: project(): pl.pallas_call(own_kernel if before is None else other_kernel, grid_spec=...]
  transfers between devices with their start and end apart: 21 -> 19, of which waited for: 7 -> 5; matrix products, arithmetic and copies ran while one was open for 2% -> 4% of each run, Pallas kernels for 17% -> 21%
where the time goes in v4:
time: 113 us; the launch traced here: 111 us
  starting transfers between devices  49.4 us (44%)
  Pallas kernels  29.4 us (26%)
  waiting for transfers between devices  19.4 us (17%)
  local copies, waits for them, and re-layouts  8.8 us (8%)
  other arithmetic  3.06 us (3%)
    ppermute x15, starting transfers between devices, rotated(): lax.ppermute(part, CTX, [(i, (i + by) % count) for i in range(count)])  31 us
    pallas_call x2, Pallas kernels, project(): pl.pallas_call(own_kernel if before is None else other_kernel, grid_spec=...  8.6 us
    ppermute x15, waiting for transfers between devices, rotated(): lax.ppermute(part, CTX, [(i, (i + by) % count) for i in range(count)])  8.1 us
    pallas_call x1, Pallas kernels, conv(): pl.pallas_call(functools.partial(conv_kernel, last), grid=(width // lanes...  7.53 us
    pallas_call x1, Pallas kernels, query_side(): pl.pallas_call(functools.partial(query_kernel, scale), grid=(heads // GRO...  7.44 us
    all_to_all x1, starting transfers between devices, per_device(): tap_sums = jnp.sum(lax.all_to_all(copies, 'near', 0, 0, tiled=True), axis=0)  7.22 us
    all_to_all x1, waiting for transfers between devices, per_device(): tap_sums = jnp.sum(lax.all_to_all(copies, 'near', 0, 0, tiled=True), axis=0)  6.84 us
    unnamed x20, local copies, waits for them, and re-layouts  6.51 us
  transfers between devices with their start and end apart: 19, of which 5 were waited for; matrix products, arithmetic and copies ran while one was open for 4% of the time, Pallas kernels for 21%

profile of v4, /device:TPU:1, one launch (start us, length us, event | category | flops | bytes accessed | tf_op | source)
XLA Modules:
  0.0 110.8 jit_solution(3001838474285951135)
XLA Ops:
  0.6 0.8 fusion
  1.5 1.0 pad_maximum_fusion.1
  2.5 3.3 %collective-permute-start.1 = (bf16[224,1024]{1,0:T(8,128)(2,1)S(1)}, bf16[224,1024]{1,0:T(8,128)(2,1)S(1)}, u32[]{:S(2)}, u32[]{:S(2)}) collective-permute-start(bf16[224,1024]{1,0:T(8,128)(2,1)S(1)} %pad_maximum_fusion.1), channel_id=1, source_target_pairs={{0,254},{2,0},{4,2},{6,4},{8,6},{10,8},{12,10},{14,12},{16,14},{18... | collective-permute-start | bytes 1376264 | tf_op jit(solution)/shard_map/ppermute | solution.py:22
  5.8 1.0 pad_maximum_fusion
  6.9 4.4 %collective-permute-done.1.high_ref.q1 = bf16[224,1024]{1,0:T(8,128)(2,1)S(1)} collective-permute-done((bf16[224,1024]{1,0:T(8,128)(2,1)S(1)}, bf16[224,1024]{1,0:T(8,128)(2,1)S(1)}, u32[]{:S(2)}, u32[]{:S(2)}) %collective-permute-start.1) | collective-permute-done | bytes 458784 | tf_op jit(solution)/shard_map/ppermute | solution.py:22
  11.3 3.7 %collective-permute-done.low_ref.k1 = bf16[224,1024]{1,0:T(8,128)(2,1)S(1)} collective-permute-done((bf16[224,1024]{1,0:T(8,128)(2,1)S(1)}, bf16[224,1024]{1,0:T(8,128)(2,1)S(1)}, u32[]{:S(2)}, u32[]{:S(2)}) %collective-permute-start) | collective-permute-done | bytes 458784 | tf_op jit(solution)/shard_map/ppermute | solution.py:22
  15.0 10.8 %collective-permute-start.6 = (bf16[224,1024]{1,0:T(8,128)(2,1)S(1)}, bf16[224,1024]{1,0:T(8,128)(2,1)S(1)}, u32[]{:S(2)}, u32[]{:S(2)}) collective-permute-start(bf16[224,1024]{1,0:T(8,128)(2,1)S(1)} %collective-permute-done.1.high_ref.q1), channel_id=1, source_target_pairs={{0,254},{2,0},{4,2},{6,4},{8,6},{10,8},{12,10},{14,12},{16,14},{18... | collective-permute-start | bytes 1376264 | tf_op jit(solution)/shard_map/ppermute | solution.py:22
  25.8 1.0 copy-done
  26.8 1.0 copy-done.1
  27.8 0.8 copy-done.6
  28.6 7.5 %shard_map.110 = (bf16[192,1024]{1,0:T(8,128)(2,1)}, f32[8,32,128]{2,1,0:T(8,128)}) custom-call(s32[1]{0:T(128)} %bitcast.idx_ref, bf16[192,1024]{1,0:T(8,128)(2,1)S(1)} %copy-done, bf16[192,1024]{1,0:T(8,128)(2,1)S(1)} %copy-done.1, bf16[224,1024]{1,0:T(8,128)(2,1)S(1)} %collective-permute-done.low_ref.k1, ...), custom_call_target="tpu_custom_call" | custom-call | flops 48758784 | bytes 786432 | tf_op jit(solution)/shard_map/pallas_call | solution.py:63
  36.2 2.6 %collective-permute-start.5 = (bf16[192,1024]{1,0:T(8,128)(2,1)}, bf16[192,1024]{1,0:T(8,128)(2,1)}, u32[]{:S(2)}, u32[]{:S(2)}) collective-permute-start(bf16[192,1024]{1,0:T(8,128)(2,1)} %get-tuple-element.19.part_ref), channel_id=1, source_target_pairs={{0,1},{1,0},{2,3},{3,2},{4,5},{5,4},{6,7},{7,6},{8,9},{9,8},{10,11... | collective-permute-start | bytes 1179656 | tf_op jit(solution)/shard_map/ppermute | solution.py:262
  38.8 3.4 %all-to-all-start = ((f32[8,32,128]{2,1,0:T(8,128)}), f32[8,32,128]{2,1,0:T(8,128)S(1)}, u32[]{:S(2)}, u32[]{:S(2)}) async-start(f32[8,32,128]{2,1,0:T(8,128)} %get-tuple-element.22), calls=%async_computation | async-start | bytes 262144 | tf_op jit(solution)/shard_map/all_to_all | solution.py:265
  42.3 6.3 %collective-permute-start.9 = (bf16[224,1024]{1,0:T(8,128)(2,1)S(1)}, bf16[224,1024]{1,0:T(8,128)(2,1)S(1)}, u32[]{:S(2)}, u32[]{:S(2)}) collective-permute-start(bf16[224,1024]{1,0:T(8,128)(2,1)S(1)} %collective-permute-done.6.q2), channel_id=1, source_target_pairs={{0,254},{2,0},{4,2},{6,4},{8,6},{10,8},{12,10},{14,12},{16,14},{18... | collective-permute-start | bytes 1376264 | tf_op jit(solution)/shard_map/ppermute | solution.py:22
  48.6 4.3 %shard_map.111.before_ref = f32[192,1024]{1,0:T(8,128)} custom-call(s32[1]{0:T(128)} %bitcast.1.idx_ref, bf16[192,1024]{1,0:T(8,128)(2,1)} %get-tuple-element.19.part_ref, bf16[1024,2048]{1,0:T(8,128)(2,1)} %weight_ref.3), custom_call_target="tpu_custom_call" | custom-call | flops 402653184 | bytes 2097152 | tf_op jit(solution)/shard_map/pallas_call | solution.py:102
  53.0 2.0 %collective-permute-done.5.part_ref = bf16[192,1024]{1,0:T(8,128)(2,1)} collective-permute-done((bf16[192,1024]{1,0:T(8,128)(2,1)}, bf16[192,1024]{1,0:T(8,128)(2,1)}, u32[]{:S(2)}, u32[]{:S(2)}) %collective-permute-start.5) | collective-permute-done | bytes 393248 | tf_op jit(solution)/shard_map/ppermute | solution.py:262
  55.0 4.3 %shard_map.112.do_ref.d0 = bf16[192,1024]{1,0:T(8,128)(2,1)} custom-call(s32[1]{0:T(128)S(6)} %sub.3.idx_ref, bf16[192,1024]{1,0:T(8,128)(2,1)} %collective-permute-done.5.part_ref, bf16[1024,2048]{1,0:T(8,128)(2,1)} %weight_ref.3, f32[192,1024]{1,0:T(8,128)} %shard_map.111.before_ref), custom_call_target="tpu_custom_call" | custom-call | flops 402653184 | bytes 2097152 | tf_op jit(solution)/shard_map/pallas_call | solution.py:102
  59.3 4.6 %collective-permute-start.10 = (bf16[192,1024]{1,0:T(8,128)(2,1)}, bf16[192,1024]{1,0:T(8,128)(2,1)}, u32[]{:S(2)}, u32[]{:S(2)}) collective-permute-start(bf16[192,1024]{1,0:T(8,128)(2,1)} %shard_map.112.do_ref.d0), channel_id=1, source_target_pairs={{0,254},{2,0},{4,2},{6,4},{8,6},{10,8},{12,10},{14,12},{16,14},{18... | collective-permute-start | bytes 1179656 | tf_op jit(solution)/shard_map/ppermute | solution.py:22
  63.9 0.7 broadcast_in_dim.6
  64.6 7.2 %all-to-all-start.1 = ((f32[16,32,128]{2,1,0:T(8,128)}), f32[16,32,128]{2,1,0:T(8,128)}, u32[]{:S(2)}, u32[]{:S(2)}) async-start(f32[16,32,128]{2,1,0:T(8,128)} %broadcast_in_dim.6), calls=%async_computation.1 | async-start | bytes 524288 | tf_op jit(solution)/shard_map/all_to_all | solution.py:280
  72.2 6.8 %all-to-all-done.1 = f32[16,32,128]{2,1,0:T(8,128)} async-done(((f32[16,32,128]{2,1,0:T(8,128)}), f32[16,32,128]{2,1,0:T(8,128)}, u32[]{:S(2)}, u32[]{:S(2)}) %all-to-all-start.1) | async-done | bytes 262176 | tf_op jit(solution)/shard_map/all_to_all | solution.py:280
  79.1 1.0 reduce_sum.19
  80.1 1.0 copy-done.4
  81.1 1.0 copy-done.7
  82.1 7.4 %shard_map.113 = (bf16[192,1024]{1,0:T(8,128)(2,1)}, f32[16,192]{1,0:T(8,128)S(1)}) custom-call(s32[1]{0:T(128)} %bitcast.idx_ref, bf16[192,1024]{1,0:T(8,128)(2,1)S(1)} %copy-done.2, bf16[192,1024]{1,0:T(8,128)(2,1)S(1)} %copy-done.4, bf16[224,1024]{1,0:T(8,128)(2,1)} %collective-permute-done.7.k3, bf16[224,1024]{1,0:T(8,128)(2,1)S(1)} %collective-permute-done.2.k2, ...), custom_call_target="tpu_custom_call" | custom-call | flops 1509949440 | bytes 4718592 | tf_op jit(solution)/shard_map/pallas_call | solution.py:167
  90.2 5.2 %all-to-all-start.2 = ((f32[8,32,128]{2,1,0:T(8,128)}), f32[8,32,128]{2,1,0:T(8,128)S(1)}, u32[]{:S(2)}, u32[]{:S(2)}) async-start(f32[8,32,128]{2,1,0:T(8,128)} %broadcast_in_dim.7), calls=%async_computation.2 | async-start | bytes 262144 | tf_op jit(solution)/shard_map/all_to_all | solution.py:286
  95.4 0.8 collective-permute-start.12
  96.2 2.3 %collective-permute-start.13 = (f32[16,192]{1,0:T(8,128)S(1)}, f32[16,192]{1,0:T(8,128)S(1)}, u32[]{:S(2)}, u32[]{:S(2)}) collective-permute-start(f32[16,192]{1,0:T(8,128)S(1)} %get-tuple-element.29.s0), channel_id=1, source_target_pairs={{0,254},{2,0},{4,2},{6,4},{8,6},{10,8},{12,10},{14,12},{16,14},{18... | collective-permute-start | bytes 36872 | tf_op jit(solution)/shard_map/ppermute | solution.py:22
  99.0 1.7 %collective-permute-start.15 = (f32[16,192]{1,0:T(8,128)S(1)}, f32[16,192]{1,0:T(8,128)S(1)}, u32[]{:S(2)}, u32[]{:S(2)}) collective-permute-start(f32[16,192]{1,0:T(8,128)S(1)} %get-tuple-element.29.s0), channel_id=1, source_target_pairs={{0,250},{2,252},{4,254},{6,0},{8,2},{10,4},{12,6},{14,8},{16,10},{... | collective-permute-start | bytes 36872 | tf_op jit(solution)/shard_map/ppermute | solution.py:22
  100.8 2.4 %all-to-all-done.2 = f32[8,32,128]{2,1,0:T(8,128)S(1)} async-done(((f32[8,32,128]{2,1,0:T(8,128)}), f32[8,32,128]{2,1,0:T(8,128)S(1)}, u32[]{:S(2)}, u32[]{:S(2)}) %all-to-all-start.2) | async-done | bytes 131104 | tf_op jit(solution)/shard_map/all_to_all | solution.py:286
  104.0 1.0 copy-done.8
  105.0 5.8 %shard_map.114 = (bf16[192,1024]{1,0:T(8,128)(2,1)}, bf16[192,1024]{1,0:T(8,128)(2,1)}) custom-call(s32[1]{0:T(128)} %bitcast.idx_ref, bf16[192,1024]{1,0:T(8,128)(2,1)S(1)} %copy-done.3, bf16[192,1024]{1,0:T(8,128)(2,1)S(1)} %copy-done.8, bf16[192,1024]{1,0:T(8,128)(2,1)S(1)} %copy-done.2, bf16[224,1024]{1,0:T(8,128)(2,1)S(1)} %collective-permute-done.1.high_ref.q1, ...), custom_call_target="tpu_custom_call" | custom-call | flops 1509949440 | bytes 4718592 | tf_op jit(solution)/shard_map/pallas_call | solution.py:229
  (40 shorter events, 2.6 us)
Async XLA Ops:
  2.5 8.8 %collective-permute-start.1 = (bf16[224,1024]{1,0:T(8,128)(2,1)S(1)}, bf16[224,1024]{1,0:T(8,128)(2,1)S(1)}, u32[]{:S(2)}, u32[]{:S(2)}) collective-permute-start(bf16[224,1024]{1,0:T(8,128)(2,1)S(1)} %pad_maximum_fusion.1), channel_id=1, source_target_pairs={{0,254},{2,0},{4,2},{6,4},{8,6},{10,8},{12,10},{14,12},{16,14},{18... | collective-permute-start | bytes 1376264 | tf_op jit(solution)/shard_map/ppermute | solution.py:22
  6.8 8.2 %collective-permute-start = (bf16[224,1024]{1,0:T(8,128)(2,1)S(1)}, bf16[224,1024]{1,0:T(8,128)(2,1)S(1)}, u32[]{:S(2)}, u32[]{:S(2)}) collective-permute-start(bf16[224,1024]{1,0:T(8,128)(2,1)S(1)} %pad_maximum_fusion), channel_id=1, source_target_pairs={{0,2},{2,4},{4,6},{6,8},{8,10},{10,12},{12,14},{14,16},{16,18},{18... | collective-permute-start | bytes 1376264 | tf_op jit(solution)/shard_map/ppermute | solution.py:22
  11.3 27.5 %collective-permute-start.3 = (bf16[192,1024]{1,0:T(8,128)(2,1)}, bf16[192,1024]{1,0:T(8,128)(2,1)}, u32[]{:S(2)}, u32[]{:S(2)}) collective-permute-start(bf16[192,1024]{1,0:T(8,128)(2,1)} %v_ref.1), channel_id=1, source_target_pairs={{0,2},{2,4},{4,6},{6,8},{8,10},{10,12},{12,14},{14,16},{16,18},{18... | collective-permute-start | bytes 1179656 | tf_op jit(solution)/shard_map/ppermute | solution.py:22
  15.0 23.8 %collective-permute-start.2 = (bf16[224,1024]{1,0:T(8,128)(2,1)S(1)}, bf16[224,1024]{1,0:T(8,128)(2,1)S(1)}, u32[]{:S(2)}, u32[]{:S(2)}) collective-permute-start(bf16[224,1024]{1,0:T(8,128)(2,1)S(1)} %collective-permute-done.low_ref.k1), channel_id=1, source_target_pairs={{0,2},{2,4},{4,6},{6,8},{8,10},{10,12},{12,14},{14,16},{16,18},{18... | collective-permute-start | bytes 1376264 | tf_op jit(solution)/shard_map/ppermute | solution.py:22
  15.0 27.3 %collective-permute-start.6 = (bf16[224,1024]{1,0:T(8,128)(2,1)S(1)}, bf16[224,1024]{1,0:T(8,128)(2,1)S(1)}, u32[]{:S(2)}, u32[]{:S(2)}) collective-permute-start(bf16[224,1024]{1,0:T(8,128)(2,1)S(1)} %collective-permute-done.1.high_ref.q1), channel_id=1, source_target_pairs={{0,254},{2,0},{4,2},{6,4},{8,6},{10,8},{12,10},{14,12},{16,14},{18... | collective-permute-start | bytes 1376264 | tf_op jit(solution)/shard_map/ppermute | solution.py:22
  25.8 1.0 copy-start
  26.8 1.0 copy-start.1
  27.8 0.8 copy-start.6
  36.2 18.8 %collective-permute-start.5 = (bf16[192,1024]{1,0:T(8,128)(2,1)}, bf16[192,1024]{1,0:T(8,128)(2,1)}, u32[]{:S(2)}, u32[]{:S(2)}) collective-permute-start(bf16[192,1024]{1,0:T(8,128)(2,1)} %get-tuple-element.19.part_ref), channel_id=1, source_target_pairs={{0,1},{1,0},{2,3},{3,2},{4,5},{5,4},{6,7},{7,6},{8,9},{9,8},{10,11... | collective-permute-start | bytes 1179656 | tf_op jit(solution)/shard_map/ppermute | solution.py:262
  38.8 20.5 %collective-permute-start.4 = (bf16[192,1024]{1,0:T(8,128)(2,1)}, bf16[192,1024]{1,0:T(8,128)(2,1)}, u32[]{:S(2)}, u32[]{:S(2)}) collective-permute-start(bf16[192,1024]{1,0:T(8,128)(2,1)} %collective-permute-done.3.v1), channel_id=1, source_target_pairs={{0,2},{2,4},{4,6},{6,8},{8,10},{10,12},{12,14},{14,16},{16,18},{18... | collective-permute-start | bytes 1179656 | tf_op jit(solution)/shard_map/ppermute | solution.py:22
  38.8 14.1 %all-to-all-start = ((f32[8,32,128]{2,1,0:T(8,128)}), f32[8,32,128]{2,1,0:T(8,128)S(1)}, u32[]{:S(2)}, u32[]{:S(2)}) async-start(f32[8,32,128]{2,1,0:T(8,128)} %get-tuple-element.22), calls=%async_computation | async-start | bytes 262144 | tf_op jit(solution)/shard_map/all_to_all | solution.py:265
  42.2 29.6 %collective-permute-start.7 = (bf16[224,1024]{1,0:T(8,128)(2,1)S(1)}, bf16[224,1024]{1,0:T(8,128)(2,1)}, u32[]{:S(2)}, u32[]{:S(2)}) collective-permute-start(bf16[224,1024]{1,0:T(8,128)(2,1)S(1)} %collective-permute-done.2.k2), channel_id=1, source_target_pairs={{0,2},{2,4},{4,6},{6,8},{8,10},{10,12},{12,14},{14,16},{16,18},{18... | collective-permute-start | bytes 1376264 | tf_op jit(solution)/shard_map/ppermute | solution.py:22
  42.3 29.5 %collective-permute-start.9 = (bf16[224,1024]{1,0:T(8,128)(2,1)S(1)}, bf16[224,1024]{1,0:T(8,128)(2,1)S(1)}, u32[]{:S(2)}, u32[]{:S(2)}) collective-permute-start(bf16[224,1024]{1,0:T(8,128)(2,1)S(1)} %collective-permute-done.6.q2), channel_id=1, source_target_pairs={{0,254},{2,0},{4,2},{6,4},{8,6},{10,8},{12,10},{14,12},{16,14},{18... | collective-permute-start | bytes 1376264 | tf_op jit(solution)/shard_map/ppermute | solution.py:22
  52.9 27.2 %copy-start.2 = (bf16[192,1024]{1,0:T(8,128)(2,1)S(1)}, bf16[192,1024]{1,0:T(8,128)(2,1)}, u32[]{:S(2)}) copy-start(bf16[192,1024]{1,0:T(8,128)(2,1)} %q0.1) | copy-start | bytes 1179652
  52.9 27.2 %copy-start.3 = (bf16[192,1024]{1,0:T(8,128)(2,1)S(1)}, bf16[192,1024]{1,0:T(8,128)(2,1)}, u32[]{:S(2)}) copy-start(bf16[192,1024]{1,0:T(8,128)(2,1)} %k_ref) | copy-start | bytes 1179652
  59.3 44.7 %copy-start.5 = (bf16[192,1024]{1,0:T(8,128)(2,1)S(1)}, bf16[192,1024]{1,0:T(8,128)(2,1)}, u32[]{:S(2)}) copy-start(bf16[192,1024]{1,0:T(8,128)(2,1)} %shard_map.112.do_ref.d0) | copy-start | bytes 1179652
  59.3 12.5 %collective-permute-start.10 = (bf16[192,1024]{1,0:T(8,128)(2,1)}, bf16[192,1024]{1,0:T(8,128)(2,1)}, u32[]{:S(2)}, u32[]{:S(2)}) collective-permute-start(bf16[192,1024]{1,0:T(8,128)(2,1)} %shard_map.112.do_ref.d0), channel_id=1, source_target_pairs={{0,254},{2,0},{4,2},{6,4},{8,6},{10,8},{12,10},{14,12},{16,14},{18... | collective-permute-start | bytes 1179656 | tf_op jit(solution)/shard_map/ppermute | solution.py:22
  63.9 16.2 %collective-permute-start.8 = (bf16[192,1024]{1,0:T(8,128)(2,1)}, bf16[192,1024]{1,0:T(8,128)(2,1)}, u32[]{:S(2)}, u32[]{:S(2)}) collective-permute-start(bf16[192,1024]{1,0:T(8,128)(2,1)} %collective-permute-done.4.v2), channel_id=1, source_target_pairs={{0,2},{2,4},{4,6},{6,8},{8,10},{10,12},{12,14},{14,16},{16,18},{18... | collective-permute-start | bytes 1179656 | tf_op jit(solution)/shard_map/ppermute | solution.py:22
  64.6 14.5 %all-to-all-start.1 = ((f32[16,32,128]{2,1,0:T(8,128)}), f32[16,32,128]{2,1,0:T(8,128)}, u32[]{:S(2)}, u32[]{:S(2)}) async-start(f32[16,32,128]{2,1,0:T(8,128)} %broadcast_in_dim.6), calls=%async_computation.1 | async-start | bytes 524288 | tf_op jit(solution)/shard_map/all_to_all | solution.py:280
  71.8 23.5 %collective-permute-start.11 = (bf16[192,1024]{1,0:T(8,128)(2,1)}, bf16[192,1024]{1,0:T(8,128)(2,1)}, u32[]{:S(2)}, u32[]{:S(2)}) collective-permute-start(bf16[192,1024]{1,0:T(8,128)(2,1)} %collective-permute-done.10.d1), channel_id=1, source_target_pairs={{0,254},{2,0},{4,2},{6,4},{8,6},{10,8},{12,10},{14,12},{16,14},{18... | collective-permute-start | bytes 1179656 | tf_op jit(solution)/shard_map/ppermute | solution.py:22
  80.1 1.0 copy-start.4
  81.1 1.0 copy-start.7
  90.2 13.0 %all-to-all-start.2 = ((f32[8,32,128]{2,1,0:T(8,128)}), f32[8,32,128]{2,1,0:T(8,128)S(1)}, u32[]{:S(2)}, u32[]{:S(2)}) async-start(f32[8,32,128]{2,1,0:T(8,128)} %broadcast_in_dim.7), calls=%async_computation.2 | async-start | bytes 262144 | tf_op jit(solution)/shard_map/all_to_all | solution.py:286
  95.4 8.6 %collective-permute-start.12 = (bf16[192,1024]{1,0:T(8,128)(2,1)}, bf16[192,1024]{1,0:T(8,128)(2,1)S(1)}, u32[]{:S(2)}, u32[]{:S(2)}) collective-permute-start(bf16[192,1024]{1,0:T(8,128)(2,1)} %collective-permute-done.11.d2), channel_id=1, source_target_pairs={{0,254},{2,0},{4,2},{6,4},{8,6},{10,8},{12,10},{14,12},{16,14},{18... | collective-permute-start | bytes 1179656 | tf_op jit(solution)/shard_map/ppermute | solution.py:22
  96.2 7.8 %collective-permute-start.13 = (f32[16,192]{1,0:T(8,128)S(1)}, f32[16,192]{1,0:T(8,128)S(1)}, u32[]{:S(2)}, u32[]{:S(2)}) collective-permute-start(f32[16,192]{1,0:T(8,128)S(1)} %get-tuple-element.29.s0), channel_id=1, source_target_pairs={{0,254},{2,0},{4,2},{6,4},{8,6},{10,8},{12,10},{14,12},{16,14},{18... | collective-permute-start | bytes 36872 | tf_op jit(solution)/shard_map/ppermute | solution.py:22
  98.5 5.5 %collective-permute-start.14 = (f32[16,192]{1,0:T(8,128)S(1)}, f32[16,192]{1,0:T(8,128)S(1)}, u32[]{:S(2)}, u32[]{:S(2)}) collective-permute-start(f32[16,192]{1,0:T(8,128)S(1)} %get-tuple-element.29.s0), channel_id=1, source_target_pairs={{0,252},{2,254},{4,0},{6,2},{8,4},{10,6},{12,8},{14,10},{16,12},{1... | collective-permute-start | bytes 36872 | tf_op jit(solution)/shard_map/ppermute | solution.py:22
  99.0 5.0 %collective-permute-start.15 = (f32[16,192]{1,0:T(8,128)S(1)}, f32[16,192]{1,0:T(8,128)S(1)}, u32[]{:S(2)}, u32[]{:S(2)}) collective-permute-start(f32[16,192]{1,0:T(8,128)S(1)} %get-tuple-element.29.s0), channel_id=1, source_target_pairs={{0,250},{2,252},{4,254},{6,0},{8,2},{10,4},{12,6},{14,8},{16,10},{... | collective-permute-start | bytes 36872 | tf_op jit(solution)/shard_map/ppermute | solution.py:22
  104.0 1.0 copy-start.8

commit v5 on v4

--- a/solution.py
+++ b/solution.py
@@ -14,6 +14,7 @@
 NT = (((1,), (1,)), ((), ()))
 BIG = 1e30
 GROUP = 2
+PIECES = 4
 CTX = ("far", "near")
 
 
@@ -22,8 +23,44 @@
     return lax.ppermute(part, CTX, [(i, (i + by) % count) for i in range(count)])
 
 
+def exchanged(part, by):
+    count = lax.axis_size(CTX)
+    return part + lax.ppermute(part, CTX, [(i, i ^ by) for i in range(count)])
+
+
 def after(parts, done):
     return lax.optimization_barrier(tuple(parts) + tuple(done))[: len(parts)]
+
+
+def pack_kernel(k_ref, q_ref, input_ref, grad_ref, low_ref, high_ref, sems):
+    block = k_ref.shape[0]
+    half = block // 2
+    pairs = []
+    for source, target in ((k_ref, low_ref), (q_ref, high_ref)):
+        for start in (0, half):
+            pairs.append((source.at[pl.ds(start, half)], target.at[pl.ds(start, half)]))
+    for target, start in ((low_ref, block - EDGE), (high_ref, 0)):
+        pairs.append((input_ref.at[pl.ds(start, EDGE)], target.at[pl.ds(block, EDGE)]))
+        pairs.append((grad_ref.at[pl.ds(start, EDGE)], target.at[pl.ds(block + EDGE, EDGE)]))
+    copies = [pltpu.make_async_copy(source, target, sems.at[i]) for i, (source, target) in enumerate(pairs)]
+    for copy in copies:
+        copy.start()
+    for copy in copies:
+        copy.wait()
+
+
+def pack(keys, queries, inputs, grad):
+    block, width = keys.shape
+    anywhere = pl.BlockSpec(memory_space=pl.ANY)
+    shape = jax.ShapeDtypeStruct((block + 2 * EDGE, width), keys.dtype)
+    return pl.pallas_call(
+        pack_kernel,
+        in_specs=[anywhere] * 4,
+        out_specs=[anywhere] * 2,
+        out_shape=[shape, shape],
+        scratch_shapes=[pltpu.SemaphoreType.DMA((8,))],
+        compiler_params=pltpu.CompilerParams(vmem_limit_bytes=56 * 2**20),
+    )(keys, queries, inputs, grad)
 
 
 def conv_kernel(last, idx_ref, grad_ref, input_ref, low_ref, high_ref, taps_ref, out_ref, rows_ref, gpad, cpad):
@@ -32,8 +69,8 @@
     reach = taps_count // 2
     device = idx_ref[0]
     f32 = jnp.float32
-    rows_ref[:, taps_count:, :] = jnp.zeros_like(rows_ref[:, taps_count:, :])
-    for group in range(rows_ref.shape[0]):
+    rows_ref[taps_count:, :] = jnp.zeros_like(rows_ref[taps_count:, :])
+    for group in range(GROUP):
         lanes = slice(group * HEAD, (group + 1) * HEAD)
         low = jnp.where(device > 0, low_ref[block:, lanes].astype(f32), 0.0)
         high = jnp.where(device < last, high_ref[block:, lanes].astype(f32), 0.0)
@@ -45,13 +82,21 @@
         cpad[EDGE + block :, lanes] = high[:EDGE]
         gpad[EDGE + block :, lanes] = high[EDGE:]
         taps = taps_ref[:, lanes].astype(f32)
-        total = jnp.zeros_like(grad)
-        for tap in range(taps_count):
-            total = total + taps[tap : tap + 1] * gpad[pl.ds(EDGE + reach - tap, block), lanes]
-        out_ref[:, lanes] = (grad + total).astype(out_ref.dtype)
-        for tap in range(taps_count):
-            prod = grad * cpad[pl.ds(EDGE - reach + tap, block), lanes]
-            rows_ref[group, tap : tap + 1, :] = jnp.sum(prod, axis=0, keepdims=True)
+        total = grad
+        for shift in range(8):
+            moved = gpad[pl.ds(shift, block + 24), lanes]
+            for start in range(0, 32, 8):
+                tap = EDGE + reach - (start + shift)
+                if 0 <= tap < taps_count:
+                    total = total + taps[tap : tap + 1] * moved[start : start + block]
+        out_ref[:, lanes] = total.astype(out_ref.dtype)
+        for shift in range(8):
+            moved = cpad[pl.ds(shift, block + 24), lanes]
+            for start in range(0, 32, 8):
+                tap = start + shift - EDGE + reach
+                if 0 <= tap < taps_count:
+                    prod = grad * moved[start : start + block]
+                    rows_ref[tap : tap + 1, lanes] = jnp.sum(prod, axis=0, keepdims=True)
 
 
 def conv(device, grad, inputs, low, high, taps, last):
@@ -71,50 +116,51 @@
             column(block + 2 * EDGE),
             column(count),
         ],
-        out_specs=[column(block), pl.BlockSpec((GROUP, rows, HEAD), lambda c: (c, 0, 0))],
+        out_specs=[column(block), column(rows)],
         out_shape=[
             jax.ShapeDtypeStruct((block, width), jnp.bfloat16),
-            jax.ShapeDtypeStruct((width // HEAD, rows, HEAD), jnp.float32),
+            jax.ShapeDtypeStruct((rows, width), jnp.float32),
         ],
         scratch_shapes=[
             pltpu.VMEM((block + 2 * EDGE, lanes), jnp.float32),
             pltpu.VMEM((block + 2 * EDGE, lanes), jnp.float32),
         ],
-        compiler_params=pltpu.CompilerParams(vmem_limit_bytes=16 * 2**20),
+        compiler_params=pltpu.CompilerParams(vmem_limit_bytes=56 * 2**20),
         cost_estimate=pl.CostEstimate(flops=8 * block * width * count, bytes_accessed=4 * block * width, transcendentals=0),
     )(device, grad, inputs, low, high, taps)
 
 
-def own_kernel(idx_ref, part_ref, weight_ref, out_ref):
-    out_ref[...] = lax.dot_general(part_ref[...], weight_ref[...], NT, preferred_element_type=jnp.float32)
-
-
-def other_kernel(idx_ref, part_ref, weight_ref, before_ref, out_ref):
-    total = lax.dot_general(part_ref[...], weight_ref[...], NT, preferred_element_type=jnp.float32)
-    out_ref[...] = (before_ref[...] + total).astype(out_ref.dtype)
+def project_kernel(idx_ref, part_ref, *refs):
+    weights, before, out_ref = refs[:PIECES], refs[PIECES:-1], refs[-1]
+    part = part_ref[...]
+    for piece, weight in enumerate(weights):
+        lanes = slice(piece * HEAD, (piece + 1) * HEAD)
+        total = lax.dot_general(part, weight[...], NT, preferred_element_type=jnp.float32)
+        for ref in before:
+            total = ref[:, lanes] + total
+        out_ref[:, lanes] = total.astype(out_ref.dtype)
 
 
 def project(place, part, weight, before=None):
     block, half = part.shape
     rows = weight.shape[0]
-    step = 256
+    step = PIECES * HEAD
     columns = pl.BlockSpec((block, step), lambda n, place: (0, n))
-    return pl.pallas_call(
-        own_kernel if before is None else other_kernel,
+    piece = lambda p: pl.BlockSpec((HEAD, half), lambda n, place: (PIECES * n + p, place[0]))
+    return pl.pallas_call(
+        project_kernel,
         grid_spec=pltpu.PrefetchScalarGridSpec(
             num_scalar_prefetch=1,
             grid=(rows // step,),
-            in_specs=[
-                pl.BlockSpec((block, half), lambda n, place: (0, 0)),
-                pl.BlockSpec((step, half), lambda n, place: (n, place[0])),
-            ]
+            in_specs=[pl.BlockSpec((block, half), lambda n, place: (0, 0))]
+            + [piece(p) for p in range(PIECES)]
             + [columns] * (before is not None),
             out_specs=columns,
         ),
         out_shape=jax.ShapeDtypeStruct((block, rows), jnp.float32 if before is None else jnp.bfloat16),
         compiler_params=pltpu.CompilerParams(vmem_limit_bytes=56 * 2**20),
         cost_estimate=pl.CostEstimate(flops=2 * block * rows * half, bytes_accessed=2 * rows * half, transcendentals=0),
-    )(place, part, weight, *(() if before is None else (before,)))
+    )(place, part, *([weight] * PIECES), *(() if before is None else (before,)))
 
 
 def query_kernel(scale, idx_ref, q_ref, do_ref, k3, k2, k1, k0, v3, v2, v1, v0, out_ref, stats_ref, bias, columns):
@@ -177,7 +223,7 @@
             pltpu.VMEM((block, 4 * block), jnp.float32),
             pltpu.VMEM((block, HEAD), jnp.float32),
         ],
-        compiler_params=pltpu.CompilerParams(vmem_limit_bytes=32 * 2**20),
+        compiler_params=pltpu.CompilerParams(vmem_limit_bytes=56 * 2**20),
         cost_estimate=pl.CostEstimate(
             flops=40 * block * block * width, bytes_accessed=24 * block * width, transcendentals=4 * block * block * heads
         ),
@@ -237,7 +283,7 @@
             pltpu.VMEM((heads, 1, 4 * block), jnp.float32),
             pltpu.VMEM((heads, 1, 4 * block), jnp.float32),
         ],
-        compiler_params=pltpu.CompilerParams(vmem_limit_bytes=32 * 2**20),
+        compiler_params=pltpu.CompilerParams(vmem_limit_bytes=56 * 2**20),
         cost_estimate=pl.CostEstimate(
             flops=40 * block * block * width, bytes_accessed=24 * block * width, transcendentals=4 * block * block * heads
         ),
@@ -251,8 +297,8 @@
     device = lax.axis_index(CTX).astype(jnp.int32).reshape(1)
     tp = lax.axis_index("tp").astype(jnp.int32).reshape(1)
 
-    k1 = rotated(jnp.concatenate([keys, conv_input[block - EDGE :], stream_grad[block - EDGE :]], axis=0), 1)
-    q1 = rotated(jnp.concatenate([queries, conv_input[:EDGE], stream_grad[:EDGE]], axis=0), -1)
+    low, high = pack(keys, queries, conv_input, stream_grad)
+    k1, q1 = rotated(low, 1), rotated(high, -1)
     (first,) = after((values,), (q1,))
     v1 = rotated(first, 1)
     k2, q2 = rotated(k1, 1), rotated(q1, -1)
@@ -260,36 +306,36 @@
 
     grad_stream, tap_rows = conv(device, stream_grad, conv_input, k1, q1, conv_weight, last)
     other = lax.ppermute(grad_stream, "tp", [(0, 1), (1, 0)])
-    before = project(tp, grad_stream, out_weight)
-    (tap_rows,) = after((tap_rows,), (k2,))
-    tap_sums = jnp.sum(lax.all_to_all(tap_rows, "far", 0, 0, tiled=True), axis=0)
-    (other,) = after((other,), (k2, q2, tap_sums))
+    tap_rows = exchanged(tap_rows, 1)
+    (own,) = after((grad_stream,), (tap_rows,))
+    before = project(tp, own, out_weight)
+    tap_rows = exchanged(tap_rows, 2)
+    (other,) = after((other,), (k2, q2, tap_rows))
     out_grad = project(1 - tp, other, out_weight, before)
     k3, q3 = rotated(k2, 1), rotated(q2, -1)
     v3 = rotated(v2, 1)
 
     (sent,) = after((out_grad,), (v2,))
     d1 = rotated(sent, -1)
-    (sent,) = after((d1,), (k3, q3))
+    tap_rows = exchanged(tap_rows, 4)
+    (sent,) = after((d1,), (k3, q3, tap_rows))
     d2 = rotated(sent, -1)
+    tap_rows = exchanged(tap_rows, 8)
     (sent,) = after((d2,), (v3,))
     d3 = rotated(sent, -1)
 
-    copies = jnp.broadcast_to(tap_sums, (lax.axis_size("near"),) + tap_sums.shape)
-    (copies,) = after((copies,), (v2, out_grad))
-    tap_sums = jnp.sum(lax.all_to_all(copies, "near", 0, 0, tiled=True), axis=0)
-    (inner,) = after((queries,), (tap_sums,))
+    (inner,) = after((queries,), (tap_rows,))
+    tap_rows = exchanged(tap_rows, 64)
     query_grad, stats = query_side(device, inner, out_grad, (k3, k2, k1, keys), (v3, v2, v1, values), scale)
     all_stats = [stats] + [rotated(stats, -hop) for hop in (1, 2, 3)]
-    copies = jnp.broadcast_to(tap_sums, (lax.axis_size("far"),) + tap_sums.shape)
-    (copies,) = after((copies,), (stats,))
-    tap_sums = lax.all_to_all(copies, "far", 0, 0, tiled=True)
-    (inner,) = after((keys,), (tap_sums,))
+    (tap_rows,) = after((tap_rows,), (stats,))
+    tap_rows = exchanged(tap_rows, 16)
+    (inner,) = after((keys,), (tap_rows,))
+    tap_rows = exchanged(tap_rows, 32)
     key_grad, value_grad = key_side(
         device, inner, values, (queries, q1, q2, q3), (out_grad, d1, d2, d3), all_stats, scale, last
     )
-    rows = jnp.transpose(tap_sums, (1, 0, 2)).reshape(tap_sums.shape[1], -1)[: conv_weight.shape[0]]
-    kernel_grad = rows / math.sqrt(block * (last + 1))
+    kernel_grad = tap_rows[: conv_weight.shape[0]] / math.sqrt(block * (last + 1))
     return (query_grad, key_grad, value_grad, grad_stream, kernel_grad)
 
 

time: 113 us -> 142 us (1.26); the launches traced: 111 us -> 141 us
  Pallas kernels: 29.4 us -> 57.2 us
  waiting for transfers between devices: 19.4 us -> 44.6 us
  starting transfers between devices: 49.4 us -> 33.9 us
  local copies, waits for them, and re-layouts: 8.8 us -> 2.82 us
    ppermute x0 -> x7, waiting for transfers between devices: none -> 30.9 us  [exchanged(): return part + lax.ppermute(part, CTX, [(i, i ^ by) for i in range(count)])]
    pallas_call x2 -> x3, Pallas kernels: 8.6 us -> 36 us  [the longest x1 29 us: pack(): pl.pallas_call(pack_kernel, in_specs=[anywhere] * 4, out_specs=[anywhere]...]
    all_to_all x3 -> x0, starting transfers between devices: 15.8 us -> none  [the longest x1 7.22 us: per_device(): tap_sums = jnp.sum(lax.all_to_all(copies, 'near', 0, 0, tiled=True), axis=0)]
    all_to_all x3 -> x0, waiting for transfers between devices: 9.26 us -> none  [the longest x1 6.84 us: per_device(): tap_sums = jnp.sum(lax.all_to_all(copies, 'near', 0, 0, tiled=True), axis=0)]
    ppermute x0 -> x7, starting transfers between devices: none -> 9.13 us  [exchanged(): return part + lax.ppermute(part, CTX, [(i, i ^ by) for i in range(count)])]
    ppermute x15, starting transfers between devices: 31 us -> 22.2 us  [rotated(): lax.ppermute(part, CTX, [(i, (i + by) % count) for i in range(count)])]
    unnamed x20 -> x32, local copies, waits for them, and re-layouts: 6.51 us -> 2.82 us
    ppermute x1, waiting for transfers between devices: 2.03 us -> 4.28 us  [per_device(): other = lax.ppermute(grad_stream, 'tp', [(0, 1), (1, 0)])]
  transfers between devices with their start and end apart: 19 -> 23, of which waited for: 5 -> 10; matrix products, arithmetic and copies ran while one was open for 4% -> 1% of each run, Pallas kernels for 21% -> 16%
where the time goes in v5:
time: 142 us; the launch traced here: 141 us
  Pallas kernels  57.2 us (40%)
  waiting for transfers between devices  44.6 us (31%)
  starting transfers between devices  33.9 us (24%)
  local copies, waits for them, and re-layouts  2.82 us (2%)
  other arithmetic  1.69 us (1%)
    ppermute x7, waiting for transfers between devices, exchanged(): return part + lax.ppermute(part, CTX, [(i, i ^ by) for i in range(count)])  30.9 us
    pallas_call x1, Pallas kernels, pack(): pl.pallas_call(pack_kernel, in_specs=[anywhere] * 4, out_specs=[anywhere]...  29 us
    ppermute x15, starting transfers between devices, rotated(): lax.ppermute(part, CTX, [(i, (i + by) % count) for i in range(count)])  22.2 us
    ppermute x15, waiting for transfers between devices, rotated(): lax.ppermute(part, CTX, [(i, (i + by) % count) for i in range(count)])  9.45 us
    ppermute x7, starting transfers between devices, exchanged(): return part + lax.ppermute(part, CTX, [(i, i ^ by) for i in range(count)])  9.13 us
    pallas_call x1, Pallas kernels, query_side(): pl.pallas_call(functools.partial(query_kernel, scale), grid=(heads // GRO...  7.52 us
    pallas_call x1, Pallas kernels, conv(): pl.pallas_call(functools.partial(conv_kernel, last), grid=(width // lanes...  7.39 us
    pallas_call x2, Pallas kernels, project(): pl.pallas_call(project_kernel, grid_spec=pltpu.PrefetchScalarGridSpec(num...  7.08 us
  transfers between devices with their start and end apart: 23, of which 10 were waited for; matrix products, arithmetic and copies ran while one was open for 1% of the time, Pallas kernels for 16%

profile of v5, /device:TPU:1, one launch (start us, length us, event | category | flops | bytes accessed | tf_op | source)
XLA Modules:
  0.0 141.3 jit_solution(10722787202853238773)
XLA Ops:
  0.6 29.0 %shard_map.110 = (bf16[224,1024]{1,0:T(8,128)(2,1)}, bf16[224,1024]{1,0:T(8,128)(2,1)}) custom-call(bf16[192,1024]{1,0:T(8,128)(2,1)} %k_ref.2, bf16[192,1024]{1,0:T(8,128)(2,1)} %q0.1, bf16[192,1024]{1,0:T(8,128)(2,1)} %input_ref.3, bf16[192,1024]{1,0:T(8,128)(2,1)} %grad_ref.3), custom_call_target="tpu_custom_call" | custom-call | tf_op jit(solution)/shard_map/pallas_call | solution.py:56
  29.6 3.3 %collective-permute-start.1 = (bf16[224,1024]{1,0:T(8,128)(2,1)}, bf16[224,1024]{1,0:T(8,128)(2,1)S(1)}, u32[]{:S(2)}, u32[]{:S(2)}) collective-permute-start(bf16[224,1024]{1,0:T(8,128)(2,1)} %get-tuple-element.23), channel_id=1, source_target_pairs={{0,254},{2,0},{4,2},{6,4},{8,6},{10,8},{12,10},{14,12},{16,14},{18... | collective-permute-start | bytes 1376264 | tf_op jit(solution)/shard_map/ppermute | solution.py:23
  32.9 5.7 %collective-permute-done.1.high_ref.q1 = bf16[224,1024]{1,0:T(8,128)(2,1)S(1)} collective-permute-done((bf16[224,1024]{1,0:T(8,128)(2,1)}, bf16[224,1024]{1,0:T(8,128)(2,1)S(1)}, u32[]{:S(2)}, u32[]{:S(2)}) %collective-permute-start.1) | collective-permute-done | bytes 458784 | tf_op jit(solution)/shard_map/ppermute | solution.py:23
  38.7 2.5 %collective-permute-done.low_ref.k1 = bf16[224,1024]{1,0:T(8,128)(2,1)S(1)} collective-permute-done((bf16[224,1024]{1,0:T(8,128)(2,1)}, bf16[224,1024]{1,0:T(8,128)(2,1)S(1)}, u32[]{:S(2)}, u32[]{:S(2)}) %collective-permute-start) | collective-permute-done | bytes 458784 | tf_op jit(solution)/shard_map/ppermute | solution.py:23
  41.2 10.8 %collective-permute-start.8 = (bf16[224,1024]{1,0:T(8,128)(2,1)S(1)}, bf16[224,1024]{1,0:T(8,128)(2,1)S(1)}, u32[]{:S(2)}, u32[]{:S(2)}) collective-permute-start(bf16[224,1024]{1,0:T(8,128)(2,1)S(1)} %collective-permute-done.1.high_ref.q1), channel_id=1, source_target_pairs={{0,254},{2,0},{4,2},{6,4},{8,6},{10,8},{12,10},{14,12},{16,14},{18... | collective-permute-start | bytes 1376264 | tf_op jit(solution)/shard_map/ppermute | solution.py:23
  52.0 7.4 %shard_map.111 = (bf16[192,1024]{1,0:T(8,128)(2,1)}, f32[32,1024]{1,0:T(8,128)}) custom-call(s32[1]{0:T(128)} %bitcast.idx_ref, bf16[192,1024]{1,0:T(8,128)(2,1)} %grad_ref.3, bf16[192,1024]{1,0:T(8,128)(2,1)} %input_ref.3, bf16[224,1024]{1,0:T(8,128)(2,1)} %copy-done.1, bf16[224,1024]{1,0:T(8,128)(2,1)} %copy-done, bf16[31,1024]{1,0:T(8,128)(2,1)} %taps_ref.1), custom_call_target="tpu_custom_call" | custom-call | flops 48758784 | bytes 786432 | tf_op jit(solution)/shard_map/pallas_call | solution.py:108
  59.4 2.6 %collective-permute-start.6 = (bf16[192,1024]{1,0:T(8,128)(2,1)}, bf16[192,1024]{1,0:T(8,128)(2,1)S(1)}, u32[]{:S(2)}, u32[]{:S(2)}) collective-permute-start(bf16[192,1024]{1,0:T(8,128)(2,1)} %get-tuple-element.28.part_ref), channel_id=1, source_target_pairs={{0,1},{1,0},{2,3},{3,2},{4,5},{5,4},{6,7},{7,6},{8,9},{9,8},{10,11... | collective-permute-start | bytes 1179656 | tf_op jit(solution)/shard_map/ppermute | solution.py:308
  62.1 6.3 %collective-permute-start.2 = (f32[32,1024]{1,0:T(8,128)}, f32[32,1024]{1,0:T(8,128)S(1)}, u32[]{:S(2)}, u32[]{:S(2)}) collective-permute-start(f32[32,1024]{1,0:T(8,128)} %get-tuple-element.24), channel_id=1, source_target_pairs={{0,2},{2,0},{4,6},{6,4},{8,10},{10,8},{12,14},{14,12},{16,18},{18,... | collective-permute-start | bytes 393224 | tf_op jit(solution)/shard_map/ppermute | solution.py:28
  68.4 1.5 %collective-permute-done.2 = f32[32,1024]{1,0:T(8,128)S(1)} collective-permute-done((f32[32,1024]{1,0:T(8,128)}, f32[32,1024]{1,0:T(8,128)S(1)}, u32[]{:S(2)}, u32[]{:S(2)}) %collective-permute-start.2) | collective-permute-done | bytes 131104 | tf_op jit(solution)/shard_map/ppermute | solution.py:28
  69.9 0.9 add.25
  71.0 1.7 %collective-permute-start.9 = (bf16[224,1024]{1,0:T(8,128)(2,1)S(1)}, bf16[224,1024]{1,0:T(8,128)(2,1)S(1)}, u32[]{:S(2)}, u32[]{:S(2)}) collective-permute-start(bf16[224,1024]{1,0:T(8,128)(2,1)S(1)} %collective-permute-done.7.k2), channel_id=1, source_target_pairs={{0,2},{2,4},{4,6},{6,8},{8,10},{10,12},{12,14},{14,16},{16,18},{18... | collective-permute-start | bytes 1376264 | tf_op jit(solution)/shard_map/ppermute | solution.py:23
  72.7 3.5 %shard_map.112.refs_4_ = f32[192,1024]{1,0:T(8,128)} custom-call(s32[1]{0:T(128)} %bitcast.1.idx_ref, bf16[192,1024]{1,0:T(8,128)(2,1)} %get-tuple-element.28.part_ref, bf16[1024,2048]{1,0:T(8,128)(2,1)} %refs_3_.3, bf16[1024,2048]{1,0:T(8,128)(2,1)} %refs_3_.3, bf16[1024,2048]{1,0:T(8,128)(2,1)} %refs_3_.3, bf16[1024,2048]{1,0:T(8,128)(2,1)} %refs_3_.3), custom_call_target="tpu_custom_call" | custom-call | flops 402653184 | bytes 2097152 | tf_op jit(solution)/shard_map/pallas_call | solution.py:150
  76.3 4.3 %collective-permute-done.6.part_ref = bf16[192,1024]{1,0:T(8,128)(2,1)S(1)} collective-permute-done((bf16[192,1024]{1,0:T(8,128)(2,1)}, bf16[192,1024]{1,0:T(8,128)(2,1)S(1)}, u32[]{:S(2)}, u32[]{:S(2)}) %collective-permute-start.6) | collective-permute-done | bytes 393248 | tf_op jit(solution)/shard_map/ppermute | solution.py:308
  80.6 0.7 copy-done.2
  81.4 3.5 %shard_map.113.do_ref.d0 = bf16[192,1024]{1,0:T(8,128)(2,1)} custom-call(s32[1]{0:T(128)S(6)} %sub.3.idx_ref, bf16[192,1024]{1,0:T(8,128)(2,1)} %copy-done.2, bf16[1024,2048]{1,0:T(8,128)(2,1)} %refs_3_.3, bf16[1024,2048]{1,0:T(8,128)(2,1)} %refs_3_.3, bf16[1024,2048]{1,0:T(8,128)(2,1)} %refs_3_.3, bf16[1024,2048]{1,0:T(8,128)(2,1)} %refs_3_.3, ...), custom_call_target="tpu_custom_call" | custom-call | flops 402653184 | bytes 2097152 | tf_op jit(solution)/shard_map/pallas_call | solution.py:150
  85.5 1.2 collective-permute-start.12
  86.7 4.7 %collective-permute-done.4 = f32[32,1024]{1,0:T(8,128)S(1)} collective-permute-done((f32[32,1024]{1,0:T(8,128)S(1)}, f32[32,1024]{1,0:T(8,128)S(1)}, u32[]{:S(2)}, u32[]{:S(2)}) %collective-permute-start.4) | collective-permute-done | bytes 131104 | tf_op jit(solution)/shard_map/ppermute | solution.py:28
  91.5 1.1 collective-permute-done.16.d1
  92.7 1.2 collective-permute-start.17
  93.9 6.0 %collective-permute-done.5 = f32[32,1024]{1,0:T(8,128)S(1)} collective-permute-done((f32[32,1024]{1,0:T(8,128)S(1)}, f32[32,1024]{1,0:T(8,128)S(1)}, u32[]{:S(2)}, u32[]{:S(2)}) %collective-permute-start.5) | collective-permute-done | bytes 131104 | tf_op jit(solution)/shard_map/ppermute | solution.py:28
  100.0 2.4 %collective-permute-start.13 = (f32[32,1024]{1,0:T(8,128)S(1)}, f32[32,1024]{1,0:T(8,128)S(1)}, u32[]{:S(2)}, u32[]{:S(2)}) collective-permute-start(f32[32,1024]{1,0:T(8,128)S(1)} %add.28), channel_id=1, source_target_pairs={{0,128},{2,130},{4,132},{6,134},{8,136},{10,138},{12,140},{14,142}... | collective-permute-start | bytes 393224 | tf_op jit(solution)/shard_map/ppermute | solution.py:28
  102.4 9.3 %collective-permute-done.13 = f32[32,1024]{1,0:T(8,128)S(1)} collective-permute-done((f32[32,1024]{1,0:T(8,128)S(1)}, f32[32,1024]{1,0:T(8,128)S(1)}, u32[]{:S(2)}, u32[]{:S(2)}) %collective-permute-start.13) | collective-permute-done | bytes 131104 | tf_op jit(solution)/shard_map/ppermute | solution.py:28
  111.8 0.7 copy-done.12
  112.5 7.5 %shard_map.114 = (bf16[192,1024]{1,0:T(8,128)(2,1)}, f32[16,192]{1,0:T(8,128)}) custom-call(s32[1]{0:T(128)} %bitcast.idx_ref, bf16[192,1024]{1,0:T(8,128)(2,1)} %q0.1, bf16[192,1024]{1,0:T(8,128)(2,1)} %shard_map.113.do_ref.d0, bf16[224,1024]{1,0:T(8,128)(2,1)} %copy-done.6, bf16[224,1024]{1,0:T(8,128)(2,1)} %copy-done.4, bf16[224,1024]{1,0:T(8,128)(2,1)} %copy-done.1, ...), custom_call_target="tpu_custom_call" | custom-call | flops 1509949440 | bytes 4718592 | tf_op jit(solution)/shard_map/pallas_call | solution.py:213
  120.2 0.9 collective-permute-start.18
  121.0 3.7 %collective-permute-done.14 = f32[32,1024]{1,0:T(8,128)S(1)} collective-permute-done((f32[32,1024]{1,0:T(8,128)S(1)}, f32[32,1024]{1,0:T(8,128)S(1)}, u32[]{:S(2)}, u32[]{:S(2)}) %collective-permute-start.14) | collective-permute-done | bytes 131104 | tf_op jit(solution)/shard_map/ppermute | solution.py:28
  124.8 1.4 collective-permute-start.19
  126.2 0.9 collective-permute-start.20
  127.2 5.7 %collective-permute-done.22 = f32[32,1024]{1,0:T(8,128)S(1)} collective-permute-done((f32[32,1024]{1,0:T(8,128)S(1)}, f32[32,1024]{1,0:T(8,128)S(1)}, u32[]{:S(2)}, u32[]{:S(2)}) %collective-permute-start.22) | collective-permute-done | bytes 131104 | tf_op jit(solution)/shard_map/ppermute | solution.py:28
  132.9 0.7 fusion
  134.2 0.7 copy-done.11
  134.9 6.2 %shard_map.115 = (bf16[192,1024]{1,0:T(8,128)(2,1)}, bf16[192,1024]{1,0:T(8,128)(2,1)}) custom-call(s32[1]{0:T(128)} %bitcast.idx_ref, bf16[192,1024]{1,0:T(8,128)(2,1)} %k_ref.2, bf16[192,1024]{1,0:T(8,128)(2,1)} %v_ref.1, bf16[192,1024]{1,0:T(8,128)(2,1)} %q0.1, bf16[224,1024]{1,0:T(8,128)(2,1)} %copy-done, bf16[224,1024]{1,0:T(8,128)(2,1)} %copy-done.3, ...), custom_call_target="tpu_custom_call" | custom-call | flops 1509949440 | bytes 4718592 | tf_op jit(solution)/shard_map/pallas_call | solution.py:275
  (59 shorter events, 1.7 us)
Async XLA Ops:
  29.6 9.1 %collective-permute-start.1 = (bf16[224,1024]{1,0:T(8,128)(2,1)}, bf16[224,1024]{1,0:T(8,128)(2,1)S(1)}, u32[]{:S(2)}, u32[]{:S(2)}) collective-permute-start(bf16[224,1024]{1,0:T(8,128)(2,1)} %get-tuple-element.23), channel_id=1, source_target_pairs={{0,254},{2,0},{4,2},{6,4},{8,6},{10,8},{12,10},{14,12},{16,14},{18... | collective-permute-start | bytes 1376264 | tf_op jit(solution)/shard_map/ppermute | solution.py:23
  32.9 8.3 %collective-permute-start = (bf16[224,1024]{1,0:T(8,128)(2,1)}, bf16[224,1024]{1,0:T(8,128)(2,1)S(1)}, u32[]{:S(2)}, u32[]{:S(2)}) collective-permute-start(bf16[224,1024]{1,0:T(8,128)(2,1)} %get-tuple-element.22), channel_id=1, source_target_pairs={{0,2},{2,4},{4,6},{6,8},{8,10},{10,12},{12,14},{14,16},{16,18},{18... | collective-permute-start | bytes 1376264 | tf_op jit(solution)/shard_map/ppermute | solution.py:23
  38.7 13.4 %copy-start = (bf16[224,1024]{1,0:T(8,128)(2,1)}, bf16[224,1024]{1,0:T(8,128)(2,1)S(1)}, u32[]{:S(2)}) copy-start(bf16[224,1024]{1,0:T(8,128)(2,1)S(1)} %collective-permute-done.1.high_ref.q1) | copy-start | bytes 1376260
  38.7 23.4 %collective-permute-start.10 = (bf16[192,1024]{1,0:T(8,128)(2,1)}, bf16[192,1024]{1,0:T(8,128)(2,1)S(1)}, u32[]{:S(2)}, u32[]{:S(2)}) collective-permute-start(bf16[192,1024]{1,0:T(8,128)(2,1)} %v_ref.1), channel_id=1, source_target_pairs={{0,2},{2,4},{4,6},{6,8},{8,10},{10,12},{12,14},{14,16},{16,18},{18... | collective-permute-start | bytes 1179656 | tf_op jit(solution)/shard_map/ppermute | solution.py:23
  41.2 10.8 %copy-start.1 = (bf16[224,1024]{1,0:T(8,128)(2,1)}, bf16[224,1024]{1,0:T(8,128)(2,1)S(1)}, u32[]{:S(2)}) copy-start(bf16[224,1024]{1,0:T(8,128)(2,1)S(1)} %collective-permute-done.low_ref.k1) | copy-start | bytes 1376260
  41.2 29.7 %collective-permute-start.7 = (bf16[224,1024]{1,0:T(8,128)(2,1)S(1)}, bf16[224,1024]{1,0:T(8,128)(2,1)S(1)}, u32[]{:S(2)}, u32[]{:S(2)}) collective-permute-start(bf16[224,1024]{1,0:T(8,128)(2,1)S(1)} %collective-permute-done.low_ref.k1), channel_id=1, source_target_pairs={{0,2},{2,4},{4,6},{6,8},{8,10},{10,12},{12,14},{14,16},{16,18},{18... | collective-permute-start | bytes 1376264 | tf_op jit(solution)/shard_map/ppermute | solution.py:23
  41.2 31.5 %collective-permute-start.8 = (bf16[224,1024]{1,0:T(8,128)(2,1)S(1)}, bf16[224,1024]{1,0:T(8,128)(2,1)S(1)}, u32[]{:S(2)}, u32[]{:S(2)}) collective-permute-start(bf16[224,1024]{1,0:T(8,128)(2,1)S(1)} %collective-permute-done.1.high_ref.q1), channel_id=1, source_target_pairs={{0,254},{2,0},{4,2},{6,4},{8,6},{10,8},{12,10},{14,12},{16,14},{18... | collective-permute-start | bytes 1376264 | tf_op jit(solution)/shard_map/ppermute | solution.py:23
  59.4 21.2 %collective-permute-start.6 = (bf16[192,1024]{1,0:T(8,128)(2,1)}, bf16[192,1024]{1,0:T(8,128)(2,1)S(1)}, u32[]{:S(2)}, u32[]{:S(2)}) collective-permute-start(bf16[192,1024]{1,0:T(8,128)(2,1)} %get-tuple-element.28.part_ref), channel_id=1, source_target_pairs={{0,1},{1,0},{2,3},{3,2},{4,5},{5,4},{6,7},{7,6},{8,9},{9,8},{10,11... | collective-permute-start | bytes 1179656 | tf_op jit(solution)/shard_map/ppermute | solution.py:308
  62.1 14.2 %copy-start.7 = (bf16[192,1024]{1,0:T(8,128)(2,1)}, bf16[192,1024]{1,0:T(8,128)(2,1)S(1)}, u32[]{:S(2)}) copy-start(bf16[192,1024]{1,0:T(8,128)(2,1)S(1)} %collective-permute-done.10.v1) | copy-start | bytes 1179652
  62.1 22.8 %collective-permute-start.11 = (bf16[192,1024]{1,0:T(8,128)(2,1)S(1)}, bf16[192,1024]{1,0:T(8,128)(2,1)S(1)}, u32[]{:S(2)}, u32[]{:S(2)}) collective-permute-start(bf16[192,1024]{1,0:T(8,128)(2,1)S(1)} %collective-permute-done.10.v1), channel_id=1, source_target_pairs={{0,2},{2,4},{4,6},{6,8},{8,10},{10,12},{12,14},{14,16},{16,18},{18... | collective-permute-start | bytes 1179656 | tf_op jit(solution)/shard_map/ppermute | solution.py:23
  62.1 7.9 %collective-permute-start.2 = (f32[32,1024]{1,0:T(8,128)}, f32[32,1024]{1,0:T(8,128)S(1)}, u32[]{:S(2)}, u32[]{:S(2)}) collective-permute-start(f32[32,1024]{1,0:T(8,128)} %get-tuple-element.24), channel_id=1, source_target_pairs={{0,2},{2,0},{4,6},{6,4},{8,10},{10,8},{12,14},{14,12},{16,18},{18,... | collective-permute-start | bytes 393224 | tf_op jit(solution)/shard_map/ppermute | solution.py:28
  70.8 5.5 %collective-permute-start.3 = (f32[32,1024]{1,0:T(8,128)S(1)}, f32[32,1024]{1,0:T(8,128)S(1)}, u32[]{:S(2)}, u32[]{:S(2)}) collective-permute-start(f32[32,1024]{1,0:T(8,128)S(1)} %add.25), channel_id=1, source_target_pairs={{0,4},{2,6},{4,0},{6,2},{8,12},{10,14},{12,8},{14,10},{16,20},{18,... | collective-permute-start | bytes 393224 | tf_op jit(solution)/shard_map/ppermute | solution.py:28
  71.0 5.3 %copy-start.4 = (bf16[224,1024]{1,0:T(8,128)(2,1)}, bf16[224,1024]{1,0:T(8,128)(2,1)S(1)}, u32[]{:S(2)}) copy-start(bf16[224,1024]{1,0:T(8,128)(2,1)S(1)} %collective-permute-done.7.k2) | copy-start | bytes 1376260
  71.0 20.5 %collective-permute-start.9 = (bf16[224,1024]{1,0:T(8,128)(2,1)S(1)}, bf16[224,1024]{1,0:T(8,128)(2,1)S(1)}, u32[]{:S(2)}, u32[]{:S(2)}) collective-permute-start(bf16[224,1024]{1,0:T(8,128)(2,1)S(1)} %collective-permute-done.7.k2), channel_id=1, source_target_pairs={{0,2},{2,4},{4,6},{6,8},{8,10},{10,12},{12,14},{14,16},{16,18},{18... | collective-permute-start | bytes 1376264 | tf_op jit(solution)/shard_map/ppermute | solution.py:23
  72.7 18.8 %collective-permute-start.15 = (bf16[224,1024]{1,0:T(8,128)(2,1)S(1)}, bf16[224,1024]{1,0:T(8,128)(2,1)S(1)}, u32[]{:S(2)}, u32[]{:S(2)}) collective-permute-start(bf16[224,1024]{1,0:T(8,128)(2,1)S(1)} %collective-permute-done.8.q2), channel_id=1, source_target_pairs={{0,254},{2,0},{4,2},{6,4},{8,6},{10,8},{12,10},{14,12},{16,14},{18... | collective-permute-start | bytes 1376264 | tf_op jit(solution)/shard_map/ppermute | solution.py:23
  84.9 26.9 %copy-start.9 = (bf16[192,1024]{1,0:T(8,128)(2,1)}, bf16[192,1024]{1,0:T(8,128)(2,1)S(1)}, u32[]{:S(2)}) copy-start(bf16[192,1024]{1,0:T(8,128)(2,1)S(1)} %collective-permute-done.11.v2) | copy-start | bytes 1179652
  84.9 7.8 %collective-permute-start.16 = (bf16[192,1024]{1,0:T(8,128)(2,1)}, bf16[192,1024]{1,0:T(8,128)(2,1)S(1)}, u32[]{:S(2)}, u32[]{:S(2)}) collective-permute-start(bf16[192,1024]{1,0:T(8,128)(2,1)} %shard_map.113.do_ref.d0), channel_id=1, source_target_pairs={{0,254},{2,0},{4,2},{6,4},{8,6},{10,8},{12,10},{14,12},{16,14},{18... | collective-permute-start | bytes 1179656 | tf_op jit(solution)/shard_map/ppermute | solution.py:23
  85.5 5.9 %collective-permute-start.4 = (f32[32,1024]{1,0:T(8,128)S(1)}, f32[32,1024]{1,0:T(8,128)S(1)}, u32[]{:S(2)}, u32[]{:S(2)}) collective-permute-start(f32[32,1024]{1,0:T(8,128)S(1)} %add.26), channel_id=1, source_target_pairs={{0,8},{2,10},{4,12},{6,14},{8,0},{10,2},{12,4},{14,6},{16,24},{18,... | collective-permute-start | bytes 393224 | tf_op jit(solution)/shard_map/ppermute | solution.py:28
  85.5 26.3 %collective-permute-start.12 = (bf16[192,1024]{1,0:T(8,128)(2,1)S(1)}, bf16[192,1024]{1,0:T(8,128)(2,1)S(1)}, u32[]{:S(2)}, u32[]{:S(2)}) collective-permute-start(bf16[192,1024]{1,0:T(8,128)(2,1)S(1)} %collective-permute-done.11.v2), channel_id=1, source_target_pairs={{0,2},{2,4},{4,6},{6,8},{8,10},{10,12},{12,14},{14,16},{16,18},{18... | collective-permute-start | bytes 1179656 | tf_op jit(solution)/shard_map/ppermute | solution.py:23
  91.4 8.5 %collective-permute-start.5 = (f32[32,1024]{1,0:T(8,128)S(1)}, f32[32,1024]{1,0:T(8,128)S(1)}, u32[]{:S(2)}, u32[]{:S(2)}) collective-permute-start(f32[32,1024]{1,0:T(8,128)S(1)} %add.27), channel_id=1, source_target_pairs={{0,16},{2,18},{4,20},{6,22},{8,24},{10,26},{12,28},{14,30},{16,0},... | collective-permute-start | bytes 393224 | tf_op jit(solution)/shard_map/ppermute | solution.py:28
  91.5 20.2 %copy-start.6 = (bf16[224,1024]{1,0:T(8,128)(2,1)}, bf16[224,1024]{1,0:T(8,128)(2,1)S(1)}, u32[]{:S(2)}) copy-start(bf16[224,1024]{1,0:T(8,128)(2,1)S(1)} %collective-permute-done.9.k3) | copy-start | bytes 1376260
  91.5 42.1 %copy-start.5 = (bf16[224,1024]{1,0:T(8,128)(2,1)}, bf16[224,1024]{1,0:T(8,128)(2,1)S(1)}, u32[]{:S(2)}) copy-start(bf16[224,1024]{1,0:T(8,128)(2,1)S(1)} %collective-permute-done.15.q3) | copy-start | bytes 1376260
  92.7 40.9 %copy-start.8 = (bf16[192,1024]{1,0:T(8,128)(2,1)}, bf16[192,1024]{1,0:T(8,128)(2,1)S(1)}, u32[]{:S(2)}) copy-start(bf16[192,1024]{1,0:T(8,128)(2,1)S(1)} %collective-permute-done.16.d1) | copy-start | bytes 1179652
  92.7 27.4 %collective-permute-start.17 = (bf16[192,1024]{1,0:T(8,128)(2,1)S(1)}, bf16[192,1024]{1,0:T(8,128)(2,1)S(1)}, u32[]{:S(2)}, u32[]{:S(2)}) collective-permute-start(bf16[192,1024]{1,0:T(8,128)(2,1)S(1)} %collective-permute-done.16.d1), channel_id=1, source_target_pairs={{0,254},{2,0},{4,2},{6,4},{8,6},{10,8},{12,10},{14,12},{16,14},{18... | collective-permute-start | bytes 1179656 | tf_op jit(solution)/shard_map/ppermute | solution.py:23
  100.0 11.8 %collective-permute-start.13 = (f32[32,1024]{1,0:T(8,128)S(1)}, f32[32,1024]{1,0:T(8,128)S(1)}, u32[]{:S(2)}, u32[]{:S(2)}) collective-permute-start(f32[32,1024]{1,0:T(8,128)S(1)} %add.28), channel_id=1, source_target_pairs={{0,128},{2,130},{4,132},{6,134},{8,136},{10,138},{12,140},{14,142}... | collective-permute-start | bytes 393224 | tf_op jit(solution)/shard_map/ppermute | solution.py:28
  120.0 4.7 %collective-permute-start.14 = (f32[32,1024]{1,0:T(8,128)S(1)}, f32[32,1024]{1,0:T(8,128)S(1)}, u32[]{:S(2)}, u32[]{:S(2)}) collective-permute-start(f32[32,1024]{1,0:T(8,128)S(1)} %add.29), channel_id=1, source_target_pairs={{0,32},{2,34},{4,36},{6,38},{8,40},{10,42},{12,44},{14,46},{16,48}... | collective-permute-start | bytes 393224 | tf_op jit(solution)/shard_map/ppermute | solution.py:28
  120.1 13.5 %copy-start.10 = (bf16[192,1024]{1,0:T(8,128)(2,1)}, bf16[192,1024]{1,0:T(8,128)(2,1)S(1)}, u32[]{:S(2)}) copy-start(bf16[192,1024]{1,0:T(8,128)(2,1)S(1)} %collective-permute-done.17.d2) | copy-start | bytes 1179652
  120.2 13.4 %collective-permute-start.18 = (bf16[192,1024]{1,0:T(8,128)(2,1)S(1)}, bf16[192,1024]{1,0:T(8,128)(2,1)S(1)}, u32[]{:S(2)}, u32[]{:S(2)}) collective-permute-start(bf16[192,1024]{1,0:T(8,128)(2,1)S(1)} %collective-permute-done.17.d2), channel_id=1, source_target_pairs={{0,254},{2,0},{4,2},{6,4},{8,6},{10,8},{12,10},{14,12},{16,14},{18... | collective-permute-start | bytes 1179656 | tf_op jit(solution)/shard_map/ppermute | solution.py:23
  124.7 8.2 %collective-permute-start.22 = (f32[32,1024]{1,0:T(8,128)S(1)}, f32[32,1024]{1,0:T(8,128)S(1)}, u32[]{:S(2)}, u32[]{:S(2)}) collective-permute-start(f32[32,1024]{1,0:T(8,128)S(1)} %add.30), channel_id=1, source_target_pairs={{0,64},{2,66},{4,68},{6,70},{8,72},{10,74},{12,76},{14,78},{16,80}... | collective-permute-start | bytes 393224 | tf_op jit(solution)/shard_map/ppermute | solution.py:28
  124.8 8.7 %collective-permute-start.19 = (f32[16,192]{1,0:T(8,128)}, f32[16,192]{1,0:T(8,128)S(1)}, u32[]{:S(2)}, u32[]{:S(2)}) collective-permute-start(f32[16,192]{1,0:T(8,128)} %get-tuple-element.31.s0), channel_id=1, source_target_pairs={{0,254},{2,0},{4,2},{6,4},{8,6},{10,8},{12,10},{14,12},{16,14},{18... | collective-permute-start | bytes 36872 | tf_op jit(solution)/shard_map/ppermute | solution.py:23
  126.2 7.3 %collective-permute-start.20 = (f32[16,192]{1,0:T(8,128)}, f32[16,192]{1,0:T(8,128)S(1)}, u32[]{:S(2)}, u32[]{:S(2)}) collective-permute-start(f32[16,192]{1,0:T(8,128)} %get-tuple-element.31.s0), channel_id=1, source_target_pairs={{0,252},{2,254},{4,0},{6,2},{8,4},{10,6},{12,8},{14,10},{16,12},{1... | collective-permute-start | bytes 36872 | tf_op jit(solution)/shard_map/ppermute | solution.py:23
  127.2 6.4 %collective-permute-start.21 = (f32[16,192]{1,0:T(8,128)}, f32[16,192]{1,0:T(8,128)S(1)}, u32[]{:S(2)}, u32[]{:S(2)}) collective-permute-start(f32[16,192]{1,0:T(8,128)} %get-tuple-element.31.s0), channel_id=1, source_target_pairs={{0,250},{2,252},{4,254},{6,0},{8,2},{10,4},{12,6},{14,8},{16,10},{... | collective-permute-start | bytes 36872 | tf_op jit(solution)/shard_map/ppermute | solution.py:23
  (7 other events, 7.6 us)

commit v6 on v5

v6 whole, which is shorter than its diff:
```python
import functools
import math

import jax
import jax.numpy as jnp
from jax import lax
from jax.experimental import pallas as pl
from jax.experimental.pallas import tpu as pltpu
from jax.sharding import Mesh
from jax.sharding import PartitionSpec as P

HEAD = 128
EDGE = 16
NT = (((1,), (1,)), ((), ()))
BIG = 1e30
GROUP = 4
VMEM_BYTES = 24 * 2**20
INSIDE = pl.BlockSpec(memory_space=pltpu.VMEM)
CTX = ("far", "near")


def rotated(part, by):
    count = lax.axis_size(CTX)
    return lax.ppermute(part, CTX, [(i, (i + by) % count) for i in range(count)])


def exchanged(part, low):
    count = lax.axis_size(CTX)
    one, two, three = (lax.ppermute(part, CTX, [(i, i ^ (low * k)) for i in range(count)]) for k in (1, 2, 3))
    return (part + one) + (two + three)


def after(parts, done):
    return lax.optimization_barrier(tuple(parts) + tuple(done))[: len(parts)]


def pack_kernel(k_ref, q_ref, input_ref, grad_ref, low_ref, high_ref, sems):
    block = k_ref.shape[0]
    pairs = [
        (k_ref, low_ref.at[pl.ds(0, block)]),
        (q_ref, high_ref.at[pl.ds(0, block)]),
    ]
    for target, start in ((low_ref, block - EDGE), (high_ref, 0)):
        pairs.append((input_ref.at[pl.ds(start, EDGE)], target.at[pl.ds(block, EDGE)]))
        pairs.append((grad_ref.at[pl.ds(start, EDGE)], target.at[pl.ds(block + EDGE, EDGE)]))
    copies = [pltpu.make_async_copy(source, target, sems.at[i]) for i, (source, target) in enumerate(pairs)]
    for copy in copies:
        copy.start()
    for copy in copies:
        copy.wait()


def pack(keys, queries, inputs, grad):
    block, width = keys.shape
    shape = jax.ShapeDtypeStruct((block + 2 * EDGE, width), keys.dtype)
    return pl.pallas_call(
        pack_kernel,
        in_specs=[pl.BlockSpec(memory_space=pltpu.HBM)] * 4,
        out_specs=[INSIDE] * 2,
        out_shape=[shape, shape],
        scratch_shapes=[pltpu.SemaphoreType.DMA((6,))],
        compiler_params=pltpu.CompilerParams(vmem_limit_bytes=56 * 2**20),
    )(keys, queries, inputs, grad)


def conv_kernel(last, idx_ref, grad_ref, input_ref, low_ref, high_ref, taps_ref, out_ref, rows_ref, gpad, cpad):
    block = grad_ref.shape[0]
    width = grad_ref.shape[1]
    taps_count = taps_ref.shape[0]
    reach = taps_count // 2
    device = idx_ref[0]
    f32 = jnp.float32
    columns = width // HEAD

    @pl.loop(0, columns)
    def _(column):
        lanes = pl.ds(pl.multiple_of(column * HEAD, HEAD), HEAD)
        low = jnp.where(device > 0, low_ref[pl.ds(block, 2 * EDGE), lanes].astype(f32), 0.0)
        high = jnp.where(device < last, high_ref[pl.ds(block, 2 * EDGE), lanes].astype(f32), 0.0)
        grad = grad_ref[:, lanes].astype(f32)
        cpad[:EDGE] = low[:EDGE]
        gpad[:EDGE] = low[EDGE:]
        cpad[EDGE : EDGE + block] = input_ref[:, lanes].astype(f32)
        gpad[EDGE : EDGE + block] = grad
        cpad[EDGE + block :] = high[:EDGE]
        gpad[EDGE + block :] = high[EDGE:]
        taps = taps_ref[:, lanes].astype(f32)
        total = grad
        for tap in range(taps_count):
            total = total + taps[tap : tap + 1] * gpad[pl.ds(EDGE + reach - tap, block), :]
        out_ref[:, lanes] = total.astype(out_ref.dtype)
        grad = gpad[EDGE : EDGE + block]
        for tap in range(taps_count):
            prod = grad * cpad[pl.ds(EDGE - reach + tap, block), :]
            rows_ref[tap : tap + 1, lanes] = jnp.sum(prod, axis=0, keepdims=True)
        rows_ref[taps_count:, lanes] = jnp.zeros_like(rows_ref[taps_count:, lanes])


def conv(device, grad, inputs, low, high, taps, last):
    block, width = grad.shape
    count = taps.shape[0]
    return pl.pallas_call(
        functools.partial(conv_kernel, last),
        in_specs=[pl.BlockSpec(memory_space=pltpu.SMEM)] + [INSIDE] * 5,
        out_specs=[INSIDE] * 2,
        out_shape=[
            jax.ShapeDtypeStruct((block, width), jnp.bfloat16),
            jax.ShapeDtypeStruct((8 * pl.cdiv(count, 8), width), jnp.float32),
        ],
        scratch_shapes=[
            pltpu.VMEM((block + 2 * EDGE, HEAD), jnp.float32),
            pltpu.VMEM((block + 2 * EDGE, HEAD), jnp.float32),
        ],
        compiler_params=pltpu.CompilerParams(vmem_limit_bytes=VMEM_BYTES),
        cost_estimate=pl.CostEstimate(flops=8 * block * width * count, bytes_accessed=4 * block * width, transcendentals=0),
    )(device, grad, inputs, low, high, taps)


def project(tp, own, other, weight):
    full = jnp.where(tp == 0, jnp.concatenate([own, other], axis=1), jnp.concatenate([other, own], axis=1))
    return lax.dot_general(full, weight, NT, preferred_element_type=jnp.float32).astype(jnp.bfloat16)


def query_kernel(scale, idx_ref, q_ref, do_ref, k3, k2, k1, k0, v3, v2, v1, v0, out_ref, stats_ref, bias, columns):
    block = q_ref.shape[0]
    heads = q_ref.shape[1] // HEAD
    f32 = jnp.float32
    rows = lax.broadcasted_iota(jnp.int32, bias.shape, 0)
    cols = lax.broadcasted_iota(jnp.int32, bias.shape, 1)
    valid = (cols <= 3 * block + rows) & (cols >= (3 - idx_ref[0]) * block)
    bias[...] = jnp.where(valid, 0.0, -jnp.inf)
    columns[...] = jnp.zeros_like(columns)

    @pl.loop(0, heads // GROUP)
    def _(step):
        lane = lax.broadcasted_iota(jnp.int32, columns.shape, 1)
        both = columns[...]
        for group in range(GROUP):
            head = step * GROUP + group
            lanes = pl.ds(pl.multiple_of(head * HEAD, HEAD), HEAD)
            keys = jnp.concatenate([ref[pl.ds(0, block), lanes] for ref in (k3, k2, k1, k0)], axis=0)
            values = jnp.concatenate([ref[:, lanes] for ref in (v3, v2, v1, v0)], axis=0)
            scores = lax.dot_general(q_ref[:, lanes], keys, NT, preferred_element_type=f32) * scale + bias[...]
            top = jnp.max(scores, axis=1, keepdims=True)
            expo = jnp.exp(scores - top)
            denom = jnp.sum(expo, axis=1, keepdims=True)
            probs = expo * (1.0 / denom)
            prob_grad = lax.dot_general(do_ref[:, lanes], values, NT, preferred_element_type=f32)
            delta = jnp.sum(probs.astype(jnp.bfloat16).astype(f32) * prob_grad, axis=1, keepdims=True)
            score_grad = (probs * (prob_grad - delta)).astype(jnp.bfloat16)
            out = jnp.dot(score_grad, keys, preferred_element_type=f32) * scale
            out_ref[:, lanes] = out.astype(out_ref.dtype)
            both = jnp.where(lane == head, top + jnp.log(denom), both)
            both = jnp.where(lane == heads + head, delta, both)
        columns[...] = both

    stats_ref[...] = columns[...].T[: stats_ref.shape[0]]


def query_side(device, queries, out_grad, keys, values, scale):
    block, width = queries.shape
    heads = width // HEAD
    return pl.pallas_call(
        functools.partial(query_kernel, scale),
        in_specs=[pl.BlockSpec(memory_space=pltpu.SMEM)] + [INSIDE] * 10,
        out_specs=[INSIDE] * 2,
        out_shape=[
            jax.ShapeDtypeStruct((block, width), jnp.bfloat16),
            jax.ShapeDtypeStruct((2 * heads, block), jnp.float32),
        ],
        scratch_shapes=[
            pltpu.VMEM((block, 4 * block), jnp.float32),
            pltpu.VMEM((block, HEAD), jnp.float32),
        ],
        compiler_params=pltpu.CompilerParams(vmem_limit_bytes=VMEM_BYTES),
        cost_estimate=pl.CostEstimate(
            flops=40 * block * block * width, bytes_accessed=24 * block * width, transcendentals=4 * block * block * heads
        ),
    )(device, queries, out_grad, *keys, *values)


def key_kernel(scale, last, idx_ref, k_ref, v_ref, q0, q1, q2, q3, d0, d1, d2, d3, s0, s1, s2, s3, dk_ref, dv_ref, bias, lse, delta):
    block = k_ref.shape[0]
    heads = lse.shape[0]
    f32 = jnp.float32
    rows = lax.broadcasted_iota(jnp.int32, bias.shape, 0)
    cols = lax.broadcasted_iota(jnp.int32, bias.shape, 1)
    bias[...] = jnp.where(cols >= rows, 0.0, -jnp.inf)
    parts = [s0[...]]
    for hop, ref in enumerate((s1, s2, s3), 1):
        part = ref[...]
        row = lax.broadcasted_iota(jnp.int32, part.shape, 0)
        parts.append(jnp.where((idx_ref[0] + hop > last) & (row < heads), BIG, part))
    stats = jnp.concatenate(parts, axis=1)
    for one in range(heads):
        lse[one] = stats[one : one + 1]
        delta[one] = stats[heads + one : heads + one + 1]
    edge = bias.shape[1]

    @pl.loop(0, heads // GROUP)
    def _(step):
        for group in range(GROUP):
            head = GROUP * step + group
            lanes = pl.ds(pl.multiple_of(head * HEAD, HEAD), HEAD)
            queries = jnp.concatenate([ref[pl.ds(0, block), lanes] for ref in (q0, q1, q2, q3)], axis=0)
            dos = jnp.concatenate([ref[:, lanes] for ref in (d0, d1, d2, d3)], axis=0)
            scores = lax.dot_general(k_ref[:, lanes], queries, NT, preferred_element_type=f32) * scale - lse[head]
            scores = jnp.concatenate([scores[:, :edge] + bias[...], scores[:, edge:]], axis=1)
            probs = jnp.exp(scores)
            prob_grad = lax.dot_general(v_ref[:, lanes], dos, NT, preferred_element_type=f32)
            score_grad = (probs * (prob_grad - delta[head])).astype(jnp.bfloat16)
            dk_ref[:, lanes] = (jnp.dot(score_grad, queries, preferred_element_type=f32) * scale).astype(dk_ref.dtype)
            dv_ref[:, lanes] = jnp.dot(probs.astype(jnp.bfloat16), dos, preferred_element_type=f32).astype(dv_ref.dtype)


def key_side(device, keys, values, queries, out_grads, stats, scale, last):
    block, width = keys.shape
    heads = width // HEAD
    shape = jax.ShapeDtypeStruct((block, width), jnp.bfloat16)
    return pl.pallas_call(
        functools.partial(key_kernel, scale, last),
        in_specs=[pl.BlockSpec(memory_space=pltpu.SMEM)] + [INSIDE] * 14,
        out_specs=[INSIDE] * 2,
        out_shape=[shape, shape],
        scratch_shapes=[
            pltpu.VMEM((block, 256), jnp.float32),
            pltpu.VMEM((heads, 1, 4 * block), jnp.float32),
            pltpu.VMEM((heads, 1, 4 * block), jnp.float32),
        ],
        compiler_params=pltpu.CompilerParams(vmem_limit_bytes=VMEM_BYTES),
        cost_estimate=pl.CostEstimate(
            flops=40 * block * block * width, bytes_accessed=24 * block * width, transcendentals=4 * block * block * heads
        ),
    )(device, keys, values, *queries, *out_grads, *stats)


def per_device(queries, keys, values, stream_grad, conv_input, conv_weight, out_weight):
    block = queries.shape[0]
    last = lax.axis_size(CTX) - 1
    scale = 1.0 / math.sqrt(HEAD)
    device = lax.axis_index(CTX).astype(jnp.int32).reshape(1)
    tp = lax.axis_index("tp")

    low, high = pack(keys, queries, conv_input, stream_grad)
    k1, q1 = rotated(low, 1), rotated(high, -1)
    (first,) = after((values,), (q1,))
    v1 = rotated(first, 1)
    k2, q2 = rotated(k1, 1), rotated(q1, -1)
    v2 = rotated(v1, 1)

    grad_stream, tap_rows = conv(device, stream_grad, conv_input, k1, q1, conv_weight, last)
    other = lax.ppermute(grad_stream, "tp", [(0, 1), (1, 0)])
    tap_rows = tap_rows + lax.ppermute(tap_rows, CTX, [(i, i ^ 1) for i in range(last + 1)])
    tap_rows = exchanged(tap_rows, 2)
    (other,) = after((other,), (k2, q2))
    out_grad = project(tp, grad_stream, other, out_weight)
    k3, q3 = rotated(k2, 1), rotated(q2, -1)
    v3 = rotated(v2, 1)

    (sent,) = after((out_grad,), (v2,))
    d1 = rotated(sent, -1)
    (sent,) = after((d1,), (k3, q3, tap_rows))
    d2 = rotated(sent, -1)
    (sent,) = after((d2,), (v3,))
    d3 = rotated(sent, -1)

    tap_rows = exchanged(tap_rows, 8)
    query_grad, stats = query_side(device, queries, out_grad, (k3, k2, k1, keys), (v3, v2, v1, values), scale)
    (stats,) = after((stats,), (tap_rows,))
    all_stats = [stats] + [rotated(stats, -hop) for hop in (1, 2, 3)]
    (tap_rows,) = after((tap_rows,), (*all_stats[1:], d3))
    tap_rows = exchanged(tap_rows, 32)
    key_grad, value_grad = key_side(
        device, keys, values, (queries, q1, q2, q3), (out_grad, d1, d2, d3), all_stats, scale, last
    )
    kernel_grad = tap_rows[: conv_weight.shape[0]] / math.sqrt(block * (last + 1))
    return (query_grad, key_grad, value_grad, grad_stream, kernel_grad)


def solution(mesh):
    count, pair = mesh.devices.shape
    far = 8
    split = Mesh(mesh.devices.reshape(far, count // far, pair), CTX + ("tp",))
    frames = P(CTX, "tp")
    return jax.shard_map(
        per_device,
        mesh=split,
        in_specs=(frames,) * 5 + (P(None, "tp"), P("tp", None)),
        out_specs=(frames,) * 4 + (P(None, "tp"),),
        check_vma=False,
    )
```

time: 142 us -> 116 us (0.82)
  Pallas kernels: 57.2 us -> 17.7 us
  starting transfers between devices: 33.9 us -> 58.1 us
  waiting for transfers between devices: 44.6 us -> 34.1 us
  matrix products: 0 us -> 4.22 us
  local copies, waits for them, and re-layouts: 2.82 us -> 0.03 us
    pallas_call x6 -> x4, Pallas kernels: 57.2 us -> 17.7 us  [the longest x1 6.72 us: query_side(): pl.pallas_call(functools.partial(query_kernel, scale), in_specs=[pl.Block...]
    ppermute x15, starting transfers between devices: 22.2 us -> 40.6 us  [rotated(): lax.ppermute(part, CTX, [(i, (i + by) % count) for i in range(count)])]
    ppermute x7 -> x10, waiting for transfers between devices: 30.9 us -> 18.5 us  [the longest x9 17.5 us: exchanged(): lax.ppermute(part, CTX, [(i, i ^ low * k) for i in range(count)])]
    ppermute x7 -> x10, starting transfers between devices: 9.13 us -> 14.9 us  [the longest x9 8.58 us: exchanged(): lax.ppermute(part, CTX, [(i, i ^ low * k) for i in range(count)])]
    ppermute x15, waiting for transfers between devices: 9.45 us -> 13.9 us  [rotated(): lax.ppermute(part, CTX, [(i, (i + by) % count) for i in range(count)])]
    dot_general x0 -> x1, matrix products: none -> 4.22 us  [project(): lax.dot_general(full, weight, NT, preferred_element_type=jnp.float32)]
    unnamed x32 -> x12, local copies, waits for them, and re-layouts: 2.82 us -> 0.03 us
    ppermute x1, waiting for transfers between devices: 4.28 us -> 1.7 us  [per_device(): other = lax.ppermute(grad_stream, 'tp', [(0, 1), (1, 0)])]
  transfers between devices with their start and end apart: 23 -> 26, of which waited for: 10 -> 11; matrix products, arithmetic and copies ran while one was open for 1% -> 4% of each run, Pallas kernels for 16% -> 13%
where the time goes in v6:
time: 116 us
  starting transfers between devices  58.1 us (50%)
  waiting for transfers between devices  34.1 us (29%)
  Pallas kernels  17.7 us (15%)
  matrix products  4.22 us (4%)
    ppermute x15, starting transfers between devices, rotated(): lax.ppermute(part, CTX, [(i, (i + by) % count) for i in range(count)])  40.6 us
    ppermute x9, waiting for transfers between devices, exchanged(): lax.ppermute(part, CTX, [(i, i ^ low * k) for i in range(count)])  17.5 us
    ppermute x15, waiting for transfers between devices, rotated(): lax.ppermute(part, CTX, [(i, (i + by) % count) for i in range(count)])  13.9 us
    ppermute x9, starting transfers between devices, exchanged(): lax.ppermute(part, CTX, [(i, i ^ low * k) for i in range(count)])  8.58 us
    pallas_call x1, Pallas kernels, query_side(): pl.pallas_call(functools.partial(query_kernel, scale), in_specs=[pl.Block...  6.72 us
    ppermute x1, starting transfers between devices, per_device(): lax.ppermute(tap_rows, CTX, [(i, i ^ 1) for i in range(last + 1)])  6.3 us
    pallas_call x1, Pallas kernels, conv(): pl.pallas_call(functools.partial(conv_kernel, last), in_specs=[pl.BlockSp...  4.42 us
    pallas_call x1, Pallas kernels, key_side(): pl.pallas_call(functools.partial(key_kernel, scale, last), in_specs=[pl.B...  4.37 us
  transfers between devices with their start and end apart: 26, of which 11 were waited for; matrix products, arithmetic and copies ran while one was open for 4% of the time, Pallas kernels for 13%

profile of v6, /device:TPU:1, one launch (start us, length us, event | category | flops | bytes accessed | tf_op | source)
XLA Modules:
  0.0 115.7 jit_solution(13474061186751240418)
XLA Ops:
  0.7 2.2 %shard_map.110 = (bf16[224,1024]{1,0:T(8,128)(2,1)}, bf16[224,1024]{1,0:T(8,128)(2,1)}) custom-call(bf16[192,1024]{1,0:T(8,128)(2,1)} %k_ref.3, bf16[192,1024]{1,0:T(8,128)(2,1)} %q0.1, bf16[192,1024]{1,0:T(8,128)(2,1)} %input_ref.3, bf16[192,1024]{1,0:T(8,128)(2,1)} %grad_ref.3), custom_call_target="tpu_custom_call" | custom-call | tf_op jit(solution)/shard_map/pallas_call | solution.py:56
  2.9 2.7 %collective-permute-start = (bf16[224,1024]{1,0:T(8,128)(2,1)}, bf16[224,1024]{1,0:T(8,128)(2,1)S(1)}, u32[]{:S(2)}, u32[]{:S(2)}) collective-permute-start(bf16[224,1024]{1,0:T(8,128)(2,1)} %get-tuple-element.20), channel_id=1, source_target_pairs={{0,2},{2,4},{4,6},{6,8},{8,10},{10,12},{12,14},{14,16},{16,18},{18... | collective-permute-start | bytes 1376264 | tf_op jit(solution)/shard_map/ppermute | solution.py:24
  5.6 0.7 collective-permute-start.1
  6.3 5.0 %collective-permute-done.low_ref.k1 = bf16[224,1024]{1,0:T(8,128)(2,1)S(1)} collective-permute-done((bf16[224,1024]{1,0:T(8,128)(2,1)}, bf16[224,1024]{1,0:T(8,128)(2,1)S(1)}, u32[]{:S(2)}, u32[]{:S(2)}) %collective-permute-start) | collective-permute-done | bytes 458784 | tf_op jit(solution)/shard_map/ppermute | solution.py:24
  11.3 2.4 %collective-permute-start.3 = (bf16[224,1024]{1,0:T(8,128)(2,1)S(1)}, bf16[224,1024]{1,0:T(8,128)(2,1)S(1)}, u32[]{:S(2)}, u32[]{:S(2)}) collective-permute-start(bf16[224,1024]{1,0:T(8,128)(2,1)S(1)} %collective-permute-done.low_ref.k1), channel_id=1, source_target_pairs={{0,2},{2,4},{4,6},{6,8},{8,10},{10,12},{12,14},{14,16},{16,18},{18... | collective-permute-start | bytes 1376264 | tf_op jit(solution)/shard_map/ppermute | solution.py:24
  13.7 5.7 %collective-permute-start.4 = (bf16[224,1024]{1,0:T(8,128)(2,1)S(1)}, bf16[224,1024]{1,0:T(8,128)(2,1)S(1)}, u32[]{:S(2)}, u32[]{:S(2)}) collective-permute-start(bf16[224,1024]{1,0:T(8,128)(2,1)S(1)} %collective-permute-done.1.high_ref.q1), channel_id=1, source_target_pairs={{0,254},{2,0},{4,2},{6,4},{8,6},{10,8},{12,10},{14,12},{16,14},{18... | collective-permute-start | bytes 1376264 | tf_op jit(solution)/shard_map/ppermute | solution.py:24
  19.4 4.4 %shard_map.111 = (bf16[192,1024]{1,0:T(8,128)(2,1)}, f32[32,1024]{1,0:T(8,128)S(1)}) custom-call(s32[1]{0:T(128)} %bitcast.idx_ref, bf16[192,1024]{1,0:T(8,128)(2,1)S(1)} %copy-done, bf16[192,1024]{1,0:T(8,128)(2,1)S(1)} %copy-done.1, bf16[224,1024]{1,0:T(8,128)(2,1)S(1)} %collective-permute-done.low_ref.k1, ...), custom_call_target="tpu_custom_call" | custom-call | flops 48758784 | bytes 786432 | tf_op jit(solution)/shard_map/pallas_call | solution.py:102
  23.8 2.6 %collective-permute-start.2 = (bf16[192,1024]{1,0:T(8,128)(2,1)}, bf16[192,1024]{1,0:T(8,128)(2,1)}, u32[]{:S(2)}, u32[]{:S(2)}) collective-permute-start(bf16[192,1024]{1,0:T(8,128)(2,1)} %get-tuple-element.18), channel_id=1, source_target_pairs={{0,1},{1,0},{2,3},{3,2},{4,5},{5,4},{6,7},{7,6},{8,9},{9,8},{10,11... | collective-permute-start | bytes 1179656 | tf_op jit(solution)/shard_map/ppermute | solution.py:252
  26.4 6.3 %collective-permute-start.11 = (f32[32,1024]{1,0:T(8,128)S(1)}, f32[32,1024]{1,0:T(8,128)S(1)}, u32[]{:S(2)}, u32[]{:S(2)}) collective-permute-start(f32[32,1024]{1,0:T(8,128)S(1)} %get-tuple-element.27), channel_id=1, source_target_pairs={{0,2},{2,0},{4,6},{6,4},{8,10},{10,8},{12,14},{14,12},{16,18},{18,... | collective-permute-start | bytes 393224 | tf_op jit(solution)/shard_map/ppermute | solution.py:253
  32.7 1.0 collective-permute-done.11
  34.0 1.7 %collective-permute-done.2 = bf16[192,1024]{1,0:T(8,128)(2,1)} collective-permute-done((bf16[192,1024]{1,0:T(8,128)(2,1)}, bf16[192,1024]{1,0:T(8,128)(2,1)}, u32[]{:S(2)}, u32[]{:S(2)}) %collective-permute-start.2) | collective-permute-done | bytes 393248 | tf_op jit(solution)/shard_map/ppermute | solution.py:252
  35.7 8.5 %collective-permute-start.9 = (bf16[224,1024]{1,0:T(8,128)(2,1)S(1)}, bf16[224,1024]{1,0:T(8,128)(2,1)S(1)}, u32[]{:S(2)}, u32[]{:S(2)}) collective-permute-start(bf16[224,1024]{1,0:T(8,128)(2,1)S(1)} %collective-permute-done.4.q2), channel_id=1, source_target_pairs={{0,254},{2,0},{4,2},{6,4},{8,6},{10,8},{12,10},{14,12},{16,14},{18... | collective-permute-start | bytes 1376264 | tf_op jit(solution)/shard_map/ppermute | solution.py:24
  44.2 4.2 %convolution_convert_fusion.do_ref.d0 = bf16[192,1024]{1,0:T(8,128)(2,1)S(1)} fusion(bf16[1024,2048]{1,0:T(8,128)(2,1)} %param.13, bf16[192,1024]{1,0:T(8,128)(2,1)} %collective-permute-done.2, bf16[192,1024]{1,0:T(8,128)(2,1)} %get-tuple-element.18, pred[]{:T(512)S(6)} %eq.3), kind=kOutput, calls=%fused_computation | convolution fusion | flops 809041920 | bytes 5373953 | tf_op jit(solution)/shard_map/dot_general | solution.py:121
  48.4 6.0 %collective-permute-start.10 = (bf16[192,1024]{1,0:T(8,128)(2,1)S(1)}, bf16[192,1024]{1,0:T(8,128)(2,1)S(1)}, u32[]{:S(2)}, u32[]{:S(2)}) collective-permute-start(bf16[192,1024]{1,0:T(8,128)(2,1)S(1)} %convolution_convert_fusion.do_ref.d0), channel_id=1, source_target_pairs={{0,254},{2,0},{4,2},{6,4},{8,6},{10,8},{12,10},{14,12},{16,14},{18... | collective-permute-start | bytes 1179656 | tf_op jit(solution)/shard_map/ppermute | solution.py:24
  54.4 8.4 %collective-permute-done.14 = f32[32,1024]{1,0:T(8,128)S(1)} collective-permute-done((f32[32,1024]{1,0:T(8,128)S(1)}, f32[32,1024]{1,0:T(8,128)S(1)}, u32[]{:S(2)}, u32[]{:S(2)}) %collective-permute-start.14) | collective-permute-done | bytes 131104 | tf_op jit(solution)/shard_map/ppermute | solution.py:29
  63.7 1.6 %collective-permute-start.18 = (f32[32,1024]{1,0:T(8,128)S(1)}, f32[32,1024]{1,0:T(8,128)S(1)}, u32[]{:S(2)}, u32[]{:S(2)}) collective-permute-start(f32[32,1024]{1,0:T(8,128)S(1)} %add_add_fusion.1), channel_id=1, source_target_pairs={{0,32},{2,34},{4,36},{6,38},{8,40},{10,42},{12,44},{14,46},{16,48}... | collective-permute-start | bytes 393224 | tf_op jit(solution)/shard_map/ppermute | solution.py:29
  65.4 1.2 %collective-permute-start.17 = (f32[32,1024]{1,0:T(8,128)S(1)}, f32[32,1024]{1,0:T(8,128)S(1)}, u32[]{:S(2)}, u32[]{:S(2)}) collective-permute-start(f32[32,1024]{1,0:T(8,128)S(1)} %add_add_fusion.1), channel_id=1, source_target_pairs={{0,16},{2,18},{4,20},{6,22},{8,24},{10,26},{12,28},{14,30},{16,0},... | collective-permute-start | bytes 393224 | tf_op jit(solution)/shard_map/ppermute | solution.py:29
  66.6 1.3 %collective-permute-done.8.v3 = bf16[192,1024]{1,0:T(8,128)(2,1)S(1)} collective-permute-done((bf16[192,1024]{1,0:T(8,128)(2,1)S(1)}, bf16[192,1024]{1,0:T(8,128)(2,1)S(1)}, u32[]{:S(2)}, u32[]{:S(2)}) %collective-permute-start.8) | collective-permute-done | bytes 393248 | tf_op jit(solution)/shard_map/ppermute | solution.py:24
  67.9 2.9 %collective-permute-done.15.d2 = bf16[192,1024]{1,0:T(8,128)(2,1)S(1)} collective-permute-done((bf16[192,1024]{1,0:T(8,128)(2,1)S(1)}, bf16[192,1024]{1,0:T(8,128)(2,1)S(1)}, u32[]{:S(2)}, u32[]{:S(2)}) %collective-permute-start.15) | collective-permute-done | bytes 393248 | tf_op jit(solution)/shard_map/ppermute | solution.py:24
  70.7 4.6 %collective-permute-start.16 = (bf16[192,1024]{1,0:T(8,128)(2,1)S(1)}, bf16[192,1024]{1,0:T(8,128)(2,1)S(1)}, u32[]{:S(2)}, u32[]{:S(2)}) collective-permute-start(bf16[192,1024]{1,0:T(8,128)(2,1)S(1)} %collective-permute-done.15.d2), channel_id=1, source_target_pairs={{0,254},{2,0},{4,2},{6,4},{8,6},{10,8},{12,10},{14,12},{16,14},{18... | collective-permute-start | bytes 1179656 | tf_op jit(solution)/shard_map/ppermute | solution.py:24
  75.3 1.5 %collective-permute-done.17 = f32[32,1024]{1,0:T(8,128)S(1)} collective-permute-done((f32[32,1024]{1,0:T(8,128)S(1)}, f32[32,1024]{1,0:T(8,128)S(1)}, u32[]{:S(2)}, u32[]{:S(2)}) %collective-permute-start.17) | collective-permute-done | bytes 131104 | tf_op jit(solution)/shard_map/ppermute | solution.py:29
  76.9 6.7 %shard_map.112 = (bf16[192,1024]{1,0:T(8,128)(2,1)}, f32[16,192]{1,0:T(8,128)S(1)}) custom-call(s32[1]{0:T(128)} %bitcast.idx_ref, bf16[192,1024]{1,0:T(8,128)(2,1)S(1)} %copy-done.2, bf16[192,1024]{1,0:T(8,128)(2,1)S(1)} %convolution_convert_fusion.do_ref.d0, bf16[224,1024]{1,0:T(8,128)(2,1)S(1)} %collective-permute-done.5.k3, ...), custom_call_target="tpu_custom_call" | custom-call | flops 1509949440 | bytes 4718592 | tf_op jit(solution)/shard_map/pallas_call | solution.py:163
  83.6 6.4 %collective-permute-start.20 = (f32[16,192]{1,0:T(8,128)S(1)}, f32[16,192]{1,0:T(8,128)S(1)}, u32[]{:S(2)}, u32[]{:S(2)}) collective-permute-start(f32[16,192]{1,0:T(8,128)S(1)} %get-tuple-element.31.s0), channel_id=1, source_target_pairs={{0,254},{2,0},{4,2},{6,4},{8,6},{10,8},{12,10},{14,12},{16,14},{18... | collective-permute-start | bytes 36872 | tf_op jit(solution)/shard_map/ppermute | solution.py:24
  90.1 2.8 %collective-permute-start.21 = (f32[16,192]{1,0:T(8,128)S(1)}, f32[16,192]{1,0:T(8,128)S(1)}, u32[]{:S(2)}, u32[]{:S(2)}) collective-permute-start(f32[16,192]{1,0:T(8,128)S(1)} %get-tuple-element.31.s0), channel_id=1, source_target_pairs={{0,252},{2,254},{4,0},{6,2},{8,4},{10,6},{12,8},{14,10},{16,12},{1... | collective-permute-start | bytes 36872 | tf_op jit(solution)/shard_map/ppermute | solution.py:24
  92.8 0.9 collective-permute-done.21.s2
  93.7 3.8 %collective-permute-done.22.s3 = f32[16,192]{1,0:T(8,128)S(1)} collective-permute-done((f32[16,192]{1,0:T(8,128)S(1)}, f32[16,192]{1,0:T(8,128)S(1)}, u32[]{:S(2)}, u32[]{:S(2)}) %collective-permute-start.22) | collective-permute-done | bytes 12320 | tf_op jit(solution)/shard_map/ppermute | solution.py:24
  97.5 1.9 %collective-permute-start.25 = (f32[32,1024]{1,0:T(8,128)S(1)}, f32[32,1024]{1,0:T(8,128)S(1)}, u32[]{:S(2)}, u32[]{:S(2)}) collective-permute-start(f32[32,1024]{1,0:T(8,128)S(1)} %add_add_fusion), channel_id=1, source_target_pairs={{0,192},{2,194},{4,196},{6,198},{8,200},{10,202},{12,204},{14,206}... | collective-permute-start | bytes 393224 | tf_op jit(solution)/shard_map/ppermute | solution.py:29
  99.4 3.3 %collective-permute-start.24 = (f32[32,1024]{1,0:T(8,128)S(1)}, f32[32,1024]{1,0:T(8,128)S(1)}, u32[]{:S(2)}, u32[]{:S(2)}) collective-permute-start(f32[32,1024]{1,0:T(8,128)S(1)} %add_add_fusion), channel_id=1, source_target_pairs={{0,128},{2,130},{4,132},{6,134},{8,136},{10,138},{12,140},{14,142}... | collective-permute-start | bytes 393224 | tf_op jit(solution)/shard_map/ppermute | solution.py:29
  103.2 4.4 %shard_map.113 = (bf16[192,1024]{1,0:T(8,128)(2,1)}, bf16[192,1024]{1,0:T(8,128)(2,1)}) custom-call(s32[1]{0:T(128)} %bitcast.idx_ref, bf16[192,1024]{1,0:T(8,128)(2,1)S(1)} %copy-done.3, bf16[192,1024]{1,0:T(8,128)(2,1)S(1)} %copy-done.5, bf16[192,1024]{1,0:T(8,128)(2,1)S(1)} %copy-done.2, bf16[224,1024]{1,0:T(8,128)(2,1)S(1)} %collective-permute-done.1.high_ref.q1, ...), custom_call_target="tpu_custom_call" | custom-call | flops 1509949440 | bytes 4718592 | tf_op jit(solution)/shard_map/pallas_call | solution.py:220
  107.5 2.8 %collective-permute-done.25 = f32[32,1024]{1,0:T(8,128)S(1)} collective-permute-done((f32[32,1024]{1,0:T(8,128)S(1)}, f32[32,1024]{1,0:T(8,128)S(1)}, u32[]{:S(2)}, u32[]{:S(2)}) %collective-permute-start.25) | collective-permute-done | bytes 131104 | tf_op jit(solution)/shard_map/ppermute | solution.py:29
  110.4 4.7 %collective-permute-done.23 = f32[32,1024]{1,0:T(8,128)S(1)} collective-permute-done((f32[32,1024]{1,0:T(8,128)S(1)}, f32[32,1024]{1,0:T(8,128)S(1)}, u32[]{:S(2)}, u32[]{:S(2)}) %collective-permute-start.23) | collective-permute-done | bytes 131104 | tf_op jit(solution)/shard_map/ppermute | solution.py:29
  115.1 0.7 fusion.7
  (41 shorter events, 1.6 us)
Async XLA Ops:
  0.6 18.8 %copy-start = (bf16[192,1024]{1,0:T(8,128)(2,1)S(1)}, bf16[192,1024]{1,0:T(8,128)(2,1)}, u32[]{:S(2)}) copy-start(bf16[192,1024]{1,0:T(8,128)(2,1)} %grad_ref.3) | copy-start | bytes 1179652
  0.6 18.7 %copy-start.1 = (bf16[192,1024]{1,0:T(8,128)(2,1)S(1)}, bf16[192,1024]{1,0:T(8,128)(2,1)}, u32[]{:S(2)}) copy-start(bf16[192,1024]{1,0:T(8,128)(2,1)} %input_ref.3) | copy-start | bytes 1179652
  0.7 18.7 %copy-start.5 = (bf16[192,1024]{1,0:T(8,128)(2,1)S(1)}, bf16[192,1024]{1,0:T(8,128)(2,1)}, u32[]{:S(2)}) copy-start(bf16[192,1024]{1,0:T(8,128)(2,1)} %v_ref.1) | copy-start | bytes 1179652
  0.7 18.7 %copy-start.4 = (bf16[31,1024]{1,0:T(8,128)(2,1)S(1)}, bf16[31,1024]{1,0:T(8,128)(2,1)}, u32[]{:S(2)}) copy-start(bf16[31,1024]{1,0:T(8,128)(2,1)} %taps_ref.1) | copy-start | bytes 190468
  2.9 8.4 %collective-permute-start = (bf16[224,1024]{1,0:T(8,128)(2,1)}, bf16[224,1024]{1,0:T(8,128)(2,1)S(1)}, u32[]{:S(2)}, u32[]{:S(2)}) collective-permute-start(bf16[224,1024]{1,0:T(8,128)(2,1)} %get-tuple-element.20), channel_id=1, source_target_pairs={{0,2},{2,4},{4,6},{6,8},{8,10},{10,12},{12,14},{14,16},{16,18},{18... | collective-permute-start | bytes 1376264 | tf_op jit(solution)/shard_map/ppermute | solution.py:24
  5.6 8.1 %collective-permute-start.1 = (bf16[224,1024]{1,0:T(8,128)(2,1)}, bf16[224,1024]{1,0:T(8,128)(2,1)S(1)}, u32[]{:S(2)}, u32[]{:S(2)}) collective-permute-start(bf16[224,1024]{1,0:T(8,128)(2,1)} %get-tuple-element.21), channel_id=1, source_target_pairs={{0,254},{2,0},{4,2},{6,4},{8,6},{10,8},{12,10},{14,12},{16,14},{18... | collective-permute-start | bytes 1376264 | tf_op jit(solution)/shard_map/ppermute | solution.py:24
  11.3 24.4 %collective-permute-start.3 = (bf16[224,1024]{1,0:T(8,128)(2,1)S(1)}, bf16[224,1024]{1,0:T(8,128)(2,1)S(1)}, u32[]{:S(2)}, u32[]{:S(2)}) collective-permute-start(bf16[224,1024]{1,0:T(8,128)(2,1)S(1)} %collective-permute-done.low_ref.k1), channel_id=1, source_target_pairs={{0,2},{2,4},{4,6},{6,8},{8,10},{10,12},{12,14},{14,16},{16,18},{18... | collective-permute-start | bytes 1376264 | tf_op jit(solution)/shard_map/ppermute | solution.py:24
  13.7 22.0 %collective-permute-start.4 = (bf16[224,1024]{1,0:T(8,128)(2,1)S(1)}, bf16[224,1024]{1,0:T(8,128)(2,1)S(1)}, u32[]{:S(2)}, u32[]{:S(2)}) collective-permute-start(bf16[224,1024]{1,0:T(8,128)(2,1)S(1)} %collective-permute-done.1.high_ref.q1), channel_id=1, source_target_pairs={{0,254},{2,0},{4,2},{6,4},{8,6},{10,8},{12,10},{14,12},{16,14},{18... | collective-permute-start | bytes 1376264 | tf_op jit(solution)/shard_map/ppermute | solution.py:24
  19.4 14.5 %collective-permute-start.6 = (bf16[192,1024]{1,0:T(8,128)(2,1)S(1)}, bf16[192,1024]{1,0:T(8,128)(2,1)}, u32[]{:S(2)}, u32[]{:S(2)}) collective-permute-start(bf16[192,1024]{1,0:T(8,128)(2,1)S(1)} %copy-done.5), channel_id=1, source_target_pairs={{0,2},{2,4},{4,6},{6,8},{8,10},{10,12},{12,14},{14,16},{16,18},{18... | collective-permute-start | bytes 1179656 | tf_op jit(solution)/shard_map/ppermute | solution.py:24
  23.8 11.9 %collective-permute-start.2 = (bf16[192,1024]{1,0:T(8,128)(2,1)}, bf16[192,1024]{1,0:T(8,128)(2,1)}, u32[]{:S(2)}, u32[]{:S(2)}) collective-permute-start(bf16[192,1024]{1,0:T(8,128)(2,1)} %get-tuple-element.18), channel_id=1, source_target_pairs={{0,1},{1,0},{2,3},{3,2},{4,5},{5,4},{6,7},{7,6},{8,9},{9,8},{10,11... | collective-permute-start | bytes 1179656 | tf_op jit(solution)/shard_map/ppermute | solution.py:252
  26.4 7.3 %collective-permute-start.11 = (f32[32,1024]{1,0:T(8,128)S(1)}, f32[32,1024]{1,0:T(8,128)S(1)}, u32[]{:S(2)}, u32[]{:S(2)}) collective-permute-start(f32[32,1024]{1,0:T(8,128)S(1)} %get-tuple-element.27), channel_id=1, source_target_pairs={{0,2},{2,0},{4,6},{6,4},{8,10},{10,8},{12,14},{14,12},{16,18},{18,... | collective-permute-start | bytes 393224 | tf_op jit(solution)/shard_map/ppermute | solution.py:253
  33.8 43.1 %copy-start.2 = (bf16[192,1024]{1,0:T(8,128)(2,1)S(1)}, bf16[192,1024]{1,0:T(8,128)(2,1)}, u32[]{:S(2)}) copy-start(bf16[192,1024]{1,0:T(8,128)(2,1)} %q0.1) | copy-start | bytes 1179652
  33.8 43.1 %copy-start.3 = (bf16[192,1024]{1,0:T(8,128)(2,1)S(1)}, bf16[192,1024]{1,0:T(8,128)(2,1)}, u32[]{:S(2)}) copy-start(bf16[192,1024]{1,0:T(8,128)(2,1)} %k_ref.3) | copy-start | bytes 1179652
  33.8 20.6 %collective-permute-start.13 = (f32[32,1024]{1,0:T(8,128)S(1)}, f32[32,1024]{1,0:T(8,128)S(1)}, u32[]{:S(2)}, u32[]{:S(2)}) collective-permute-start(f32[32,1024]{1,0:T(8,128)S(1)} %add.34), channel_id=1, source_target_pairs={{0,8},{2,10},{4,12},{6,14},{8,0},{10,2},{12,4},{14,6},{16,24},{18,... | collective-permute-start | bytes 393224 | tf_op jit(solution)/shard_map/ppermute | solution.py:29
  33.9 14.5 %collective-permute-start.7 = (bf16[192,1024]{1,0:T(8,128)(2,1)}, bf16[192,1024]{1,0:T(8,128)(2,1)S(1)}, u32[]{:S(2)}, u32[]{:S(2)}) collective-permute-start(bf16[192,1024]{1,0:T(8,128)(2,1)} %collective-permute-done.6.v1), channel_id=1, source_target_pairs={{0,2},{2,4},{4,6},{6,8},{8,10},{10,12},{12,14},{14,16},{16,18},{18... | collective-permute-start | bytes 1179656 | tf_op jit(solution)/shard_map/ppermute | solution.py:24
  35.7 27.5 %collective-permute-start.5 = (bf16[224,1024]{1,0:T(8,128)(2,1)S(1)}, bf16[224,1024]{1,0:T(8,128)(2,1)S(1)}, u32[]{:S(2)}, u32[]{:S(2)}) collective-permute-start(bf16[224,1024]{1,0:T(8,128)(2,1)S(1)} %collective-permute-done.3.k2), channel_id=1, source_target_pairs={{0,2},{2,4},{4,6},{6,8},{8,10},{10,12},{12,14},{14,16},{16,18},{18... | collective-permute-start | bytes 1376264 | tf_op jit(solution)/shard_map/ppermute | solution.py:24
  35.7 27.5 %collective-permute-start.9 = (bf16[224,1024]{1,0:T(8,128)(2,1)S(1)}, bf16[224,1024]{1,0:T(8,128)(2,1)S(1)}, u32[]{:S(2)}, u32[]{:S(2)}) collective-permute-start(bf16[224,1024]{1,0:T(8,128)(2,1)S(1)} %collective-permute-done.4.q2), channel_id=1, source_target_pairs={{0,254},{2,0},{4,2},{6,4},{8,6},{10,8},{12,10},{14,12},{16,14},{18... | collective-permute-start | bytes 1376264 | tf_op jit(solution)/shard_map/ppermute | solution.py:24
  48.4 14.7 %collective-permute-start.10 = (bf16[192,1024]{1,0:T(8,128)(2,1)S(1)}, bf16[192,1024]{1,0:T(8,128)(2,1)S(1)}, u32[]{:S(2)}, u32[]{:S(2)}) collective-permute-start(bf16[192,1024]{1,0:T(8,128)(2,1)S(1)} %convolution_convert_fusion.do_ref.d0), channel_id=1, source_target_pairs={{0,254},{2,0},{4,2},{6,4},{8,6},{10,8},{12,10},{14,12},{16,14},{18... | collective-permute-start | bytes 1179656 | tf_op jit(solution)/shard_map/ppermute | solution.py:24
  54.4 8.4 %collective-permute-start.14 = (f32[32,1024]{1,0:T(8,128)S(1)}, f32[32,1024]{1,0:T(8,128)S(1)}, u32[]{:S(2)}, u32[]{:S(2)}) collective-permute-start(f32[32,1024]{1,0:T(8,128)S(1)} %add.34), channel_id=1, source_target_pairs={{0,12},{2,14},{4,8},{6,10},{8,4},{10,6},{12,0},{14,2},{16,28},{18,... | collective-permute-start | bytes 393224 | tf_op jit(solution)/shard_map/ppermute | solution.py:29
  54.4 8.4 %collective-permute-start.12 = (f32[32,1024]{1,0:T(8,128)S(1)}, f32[32,1024]{1,0:T(8,128)S(1)}, u32[]{:S(2)}, u32[]{:S(2)}) collective-permute-start(f32[32,1024]{1,0:T(8,128)S(1)} %add.34), channel_id=1, source_target_pairs={{0,4},{2,6},{4,0},{6,2},{8,12},{10,14},{12,8},{14,10},{16,20},{18,... | collective-permute-start | bytes 393224 | tf_op jit(solution)/shard_map/ppermute | solution.py:29
  62.9 5.0 %collective-permute-start.8 = (bf16[192,1024]{1,0:T(8,128)(2,1)S(1)}, bf16[192,1024]{1,0:T(8,128)(2,1)S(1)}, u32[]{:S(2)}, u32[]{:S(2)}) collective-permute-start(bf16[192,1024]{1,0:T(8,128)(2,1)S(1)} %collective-permute-done.7.v2), channel_id=1, source_target_pairs={{0,2},{2,4},{4,6},{6,8},{8,10},{10,12},{12,14},{14,16},{16,18},{18... | collective-permute-start | bytes 1179656 | tf_op jit(solution)/shard_map/ppermute | solution.py:24
  63.2 7.6 %collective-permute-start.15 = (bf16[192,1024]{1,0:T(8,128)(2,1)S(1)}, bf16[192,1024]{1,0:T(8,128)(2,1)S(1)}, u32[]{:S(2)}, u32[]{:S(2)}) collective-permute-start(bf16[192,1024]{1,0:T(8,128)(2,1)S(1)} %collective-permute-done.10.d1), channel_id=1, source_target_pairs={{0,254},{2,0},{4,2},{6,4},{8,6},{10,8},{12,10},{14,12},{16,14},{18... | collective-permute-start | bytes 1179656 | tf_op jit(solution)/shard_map/ppermute | solution.py:24
  63.7 11.6 %collective-permute-start.18 = (f32[32,1024]{1,0:T(8,128)S(1)}, f32[32,1024]{1,0:T(8,128)S(1)}, u32[]{:S(2)}, u32[]{:S(2)}) collective-permute-start(f32[32,1024]{1,0:T(8,128)S(1)} %add_add_fusion.1), channel_id=1, source_target_pairs={{0,32},{2,34},{4,36},{6,38},{8,40},{10,42},{12,44},{14,46},{16,48}... | collective-permute-start | bytes 393224 | tf_op jit(solution)/shard_map/ppermute | solution.py:29
  65.4 9.9 %collective-permute-start.19 = (f32[32,1024]{1,0:T(8,128)S(1)}, f32[32,1024]{1,0:T(8,128)S(1)}, u32[]{:S(2)}, u32[]{:S(2)}) collective-permute-start(f32[32,1024]{1,0:T(8,128)S(1)} %add_add_fusion.1), channel_id=1, source_target_pairs={{0,48},{2,50},{4,52},{6,54},{8,56},{10,58},{12,60},{14,62},{16,32}... | collective-permute-start | bytes 393224 | tf_op jit(solution)/shard_map/ppermute | solution.py:29
  65.4 11.5 %collective-permute-start.17 = (f32[32,1024]{1,0:T(8,128)S(1)}, f32[32,1024]{1,0:T(8,128)S(1)}, u32[]{:S(2)}, u32[]{:S(2)}) collective-permute-start(f32[32,1024]{1,0:T(8,128)S(1)} %add_add_fusion.1), channel_id=1, source_target_pairs={{0,16},{2,18},{4,20},{6,22},{8,24},{10,26},{12,28},{14,30},{16,0},... | collective-permute-start | bytes 393224 | tf_op jit(solution)/shard_map/ppermute | solution.py:29
  70.7 26.8 %collective-permute-start.16 = (bf16[192,1024]{1,0:T(8,128)(2,1)S(1)}, bf16[192,1024]{1,0:T(8,128)(2,1)S(1)}, u32[]{:S(2)}, u32[]{:S(2)}) collective-permute-start(bf16[192,1024]{1,0:T(8,128)(2,1)S(1)} %collective-permute-done.15.d2), channel_id=1, source_target_pairs={{0,254},{2,0},{4,2},{6,4},{8,6},{10,8},{12,10},{14,12},{16,14},{18... | collective-permute-start | bytes 1179656 | tf_op jit(solution)/shard_map/ppermute | solution.py:24
  83.6 9.2 %collective-permute-start.20 = (f32[16,192]{1,0:T(8,128)S(1)}, f32[16,192]{1,0:T(8,128)S(1)}, u32[]{:S(2)}, u32[]{:S(2)}) collective-permute-start(f32[16,192]{1,0:T(8,128)S(1)} %get-tuple-element.31.s0), channel_id=1, source_target_pairs={{0,254},{2,0},{4,2},{6,4},{8,6},{10,8},{12,10},{14,12},{16,14},{18... | collective-permute-start | bytes 36872 | tf_op jit(solution)/shard_map/ppermute | solution.py:24
  90.1 3.6 %collective-permute-start.21 = (f32[16,192]{1,0:T(8,128)S(1)}, f32[16,192]{1,0:T(8,128)S(1)}, u32[]{:S(2)}, u32[]{:S(2)}) collective-permute-start(f32[16,192]{1,0:T(8,128)S(1)} %get-tuple-element.31.s0), channel_id=1, source_target_pairs={{0,252},{2,254},{4,0},{6,2},{8,4},{10,6},{12,8},{14,10},{16,12},{1... | collective-permute-start | bytes 36872 | tf_op jit(solution)/shard_map/ppermute | solution.py:24
  92.8 4.7 %collective-permute-start.22 = (f32[16,192]{1,0:T(8,128)S(1)}, f32[16,192]{1,0:T(8,128)S(1)}, u32[]{:S(2)}, u32[]{:S(2)}) collective-permute-start(f32[16,192]{1,0:T(8,128)S(1)} %get-tuple-element.31.s0), channel_id=1, source_target_pairs={{0,250},{2,252},{4,254},{6,0},{8,2},{10,4},{12,6},{14,8},{16,10},{... | collective-permute-start | bytes 36872 | tf_op jit(solution)/shard_map/ppermute | solution.py:24
  97.5 12.9 %collective-permute-start.25 = (f32[32,1024]{1,0:T(8,128)S(1)}, f32[32,1024]{1,0:T(8,128)S(1)}, u32[]{:S(2)}, u32[]{:S(2)}) collective-permute-start(f32[32,1024]{1,0:T(8,128)S(1)} %add_add_fusion), channel_id=1, source_target_pairs={{0,192},{2,194},{4,196},{6,198},{8,200},{10,202},{12,204},{14,206}... | collective-permute-start | bytes 393224 | tf_op jit(solution)/shard_map/ppermute | solution.py:29
  99.4 11.0 %collective-permute-start.24 = (f32[32,1024]{1,0:T(8,128)S(1)}, f32[32,1024]{1,0:T(8,128)S(1)}, u32[]{:S(2)}, u32[]{:S(2)}) collective-permute-start(f32[32,1024]{1,0:T(8,128)S(1)} %add_add_fusion), channel_id=1, source_target_pairs={{0,128},{2,130},{4,132},{6,134},{8,136},{10,138},{12,140},{14,142}... | collective-permute-start | bytes 393224 | tf_op jit(solution)/shard_map/ppermute | solution.py:29
  102.7 12.3 %collective-permute-start.23 = (f32[32,1024]{1,0:T(8,128)S(1)}, f32[32,1024]{1,0:T(8,128)S(1)}, u32[]{:S(2)}, u32[]{:S(2)}) collective-permute-start(f32[32,1024]{1,0:T(8,128)S(1)} %add_add_fusion), channel_id=1, source_target_pairs={{0,64},{2,66},{4,68},{6,70},{8,72},{10,74},{12,76},{14,78},{16,80}... | collective-permute-start | bytes 393224 | tf_op jit(solution)/shard_map/ppermute | solution.py:29

commit v7 on v6

v7 whole, which is shorter than its diff:
```python
import functools
import math

import jax
import jax.numpy as jnp
from jax import lax
from jax.experimental import pallas as pl
from jax.experimental.pallas import tpu as pltpu
from jax.sharding import Mesh
from jax.sharding import PartitionSpec as P

HEAD = 128
EDGE = 16
NT = (((1,), (1,)), ((), ()))
BIG = 1e30
GROUP = 4
VMEM_BYTES = 24 * 2**20
INSIDE = pl.BlockSpec(memory_space=pltpu.VMEM)
CTX = ("z", "near")


def rotated(part, by):
    count = lax.axis_size(CTX)
    return lax.ppermute(part, CTX, [(i, (i + by) % count) for i in range(count)])


def swapped(part, first):
    count = lax.axis_size(CTX)
    partner = lambda i: ((i - first) ^ 1) + first
    return lax.ppermute(part, CTX, [(i, partner(i) if 0 <= partner(i) < count and i >= first else i) for i in range(count)])


def after(parts, done):
    return lax.optimization_barrier(tuple(parts) + tuple(done))[: len(parts)]


def pack_kernel(idx_ref, k_ref, v_ref, input_ref, grad_ref, both_ref, inside_ref, across_ref, sems):
    block = k_ref.shape[0]
    odd = lax.rem(idx_ref[0], 2)
    pairs = [(k_ref, both_ref.at[pl.ds(0, block)]), (v_ref, both_ref.at[pl.ds(block, block)])]
    for target, start in ((inside_ref, (1 - odd) * (block - EDGE)), (across_ref, odd * (block - EDGE))):
        rows = pl.ds(pl.multiple_of(start, EDGE), EDGE)
        pairs.append((input_ref.at[rows], target.at[pl.ds(0, EDGE)]))
        pairs.append((grad_ref.at[rows], target.at[pl.ds(EDGE, EDGE)]))
    copies = [pltpu.make_async_copy(source, target, sems.at[i]) for i, (source, target) in enumerate(pairs)]
    for copy in copies:
        copy.start()
    for copy in copies:
        copy.wait()


def pack(device, keys, values, inputs, grad):
    block, width = keys.shape
    edge = jax.ShapeDtypeStruct((2 * EDGE, width), keys.dtype)
    return pl.pallas_call(
        pack_kernel,
        in_specs=[pl.BlockSpec(memory_space=pltpu.SMEM)] + [pl.BlockSpec(memory_space=pltpu.HBM)] * 4,
        out_specs=[INSIDE] * 3,
        out_shape=[jax.ShapeDtypeStruct((2 * block, width), keys.dtype), edge, edge],
        scratch_shapes=[pltpu.SemaphoreType.DMA((6,))],
        compiler_params=pltpu.CompilerParams(vmem_limit_bytes=56 * 2**20),
    )(device, keys, values, inputs, grad)


def conv_kernel(last, idx_ref, grad_ref, input_ref, inside_ref, across_ref, taps_ref, out_ref, rows_ref, gpad, cpad):
    block = grad_ref.shape[0]
    width = grad_ref.shape[1]
    taps_count = taps_ref.shape[0]
    reach = taps_count // 2
    device = idx_ref[0]
    f32 = jnp.float32
    columns = width // HEAD

    @pl.loop(0, columns)
    def _(column):
        lanes = pl.ds(pl.multiple_of(column * HEAD, HEAD), HEAD)
        inside = inside_ref[:, lanes].astype(f32)
        across = across_ref[:, lanes].astype(f32)
        even = lax.rem(device, 2) == 0
        low = jnp.where(device > 0, jnp.where(even, across, inside), 0.0)
        high = jnp.where(device < last, jnp.where(even, inside, across), 0.0)
        grad = grad_ref[:, lanes].astype(f32)
        cpad[:EDGE] = low[:EDGE]
        gpad[:EDGE] = low[EDGE:]
        cpad[EDGE : EDGE + block] = input_ref[:, lanes].astype(f32)
        gpad[EDGE : EDGE + block] = grad
        cpad[EDGE + block :] = high[:EDGE]
        gpad[EDGE + block :] = high[EDGE:]
        taps = taps_ref[:, lanes].astype(f32)
        total = grad
        for tap in range(taps_count):
            total = total + taps[tap : tap + 1] * gpad[pl.ds(EDGE + reach - tap, block), :]
        out_ref[:, lanes] = total.astype(out_ref.dtype)
        grad = gpad[EDGE : EDGE + block]
        for tap in range(taps_count):
            prod = grad * cpad[pl.ds(EDGE - reach + tap, block), :]
            rows_ref[tap : tap + 1, lanes] = jnp.sum(prod, axis=0, keepdims=True)
        rows_ref[taps_count:, lanes] = jnp.zeros_like(rows_ref[taps_count:, lanes])


def conv(device, grad, inputs, inside, across, taps, last):
    block, width = grad.shape
    count = taps.shape[0]
    return pl.pallas_call(
        functools.partial(conv_kernel, last),
        in_specs=[pl.BlockSpec(memory_space=pltpu.SMEM)] + [INSIDE] * 5,
        out_specs=[INSIDE] * 2,
        out_shape=[
            jax.ShapeDtypeStruct((block, width), jnp.bfloat16),
            jax.ShapeDtypeStruct((8 * pl.cdiv(count, 8), width), jnp.float32),
        ],
        scratch_shapes=[
            pltpu.VMEM((block + 2 * EDGE, HEAD), jnp.float32),
            pltpu.VMEM((block + 2 * EDGE, HEAD), jnp.float32),
        ],
        compiler_params=pltpu.CompilerParams(vmem_limit_bytes=VMEM_BYTES),
        cost_estimate=pl.CostEstimate(flops=block * width, bytes_accessed=block * width // 16, transcendentals=0),
    )(device, grad, inputs, inside, across, taps)


def project(tp, own, other, weight):
    full = jnp.where(tp == 0, jnp.concatenate([own, other], axis=1), jnp.concatenate([other, own], axis=1))
    return lax.dot_general(full, weight, NT, preferred_element_type=jnp.float32).astype(jnp.bfloat16)


def query_kernel(scale, idx_ref, q_ref, do_ref, both3, both2, both1, both0, out_ref, stats_ref, bias, columns):
    block = q_ref.shape[0]
    heads = q_ref.shape[1] // HEAD
    f32 = jnp.float32
    rows = lax.broadcasted_iota(jnp.int32, bias.shape, 0)
    cols = lax.broadcasted_iota(jnp.int32, bias.shape, 1)
    valid = (cols <= 3 * block + rows) & (cols >= (3 - idx_ref[0]) * block)
    bias[...] = jnp.where(valid, 0.0, -jnp.inf)
    columns[...] = jnp.zeros_like(columns)

    @pl.loop(0, heads // GROUP)
    def _(step):
        lane = lax.broadcasted_iota(jnp.int32, columns.shape, 1)
        both = columns[...]
        for group in range(GROUP):
            head = step * GROUP + group
            lanes = pl.ds(pl.multiple_of(head * HEAD, HEAD), HEAD)
            keys, values = (
                jnp.concatenate([ref[pl.ds(start, block), lanes] for ref in (both3, both2, both1, both0)], axis=0)
                for start in (0, block)
            )
            scores = lax.dot_general(q_ref[:, lanes], keys, NT, preferred_element_type=f32) * scale + bias[...]
            top = jnp.max(scores, axis=1, keepdims=True)
            expo = jnp.exp(scores - top)
            denom = jnp.sum(expo, axis=1, keepdims=True)
            probs = expo * (1.0 / denom)
            prob_grad = lax.dot_general(do_ref[:, lanes], values, NT, preferred_element_type=f32)
            delta = jnp.sum(probs.astype(jnp.bfloat16).astype(f32) * prob_grad, axis=1, keepdims=True)
            score_grad = (probs * (prob_grad - delta)).astype(jnp.bfloat16)
            out = jnp.dot(score_grad, keys, preferred_element_type=f32) * scale
            out_ref[:, lanes] = out.astype(out_ref.dtype)
            both = jnp.where(lane == head, top + jnp.log(denom), both)
            both = jnp.where(lane == heads + head, delta, both)
        columns[...] = both

    stats_ref[...] = columns[...].T[: stats_ref.shape[0]]


def query_side(device, queries, out_grad, blocks, scale):
    block, width = queries.shape
    heads = width // HEAD
    return pl.pallas_call(
        functools.partial(query_kernel, scale),
        in_specs=[pl.BlockSpec(memory_space=pltpu.SMEM)] + [INSIDE] * 6,
        out_specs=[INSIDE] * 2,
        out_shape=[
            jax.ShapeDtypeStruct((block, width), jnp.bfloat16),
            jax.ShapeDtypeStruct((2 * heads, block), jnp.float32),
        ],
        scratch_shapes=[
            pltpu.VMEM((block, 4 * block), jnp.float32),
            pltpu.VMEM((block, HEAD), jnp.float32),
        ],
        compiler_params=pltpu.CompilerParams(vmem_limit_bytes=VMEM_BYTES),
        cost_estimate=pl.CostEstimate(
            flops=40 * block * block * width, bytes_accessed=24 * block * width, transcendentals=4 * block * block * heads
        ),
    )(device, queries, out_grad, *blocks)


def key_kernel(scale, last, idx_ref, both_ref, q0, q1, q2, q3, d0, d1, d2, d3, s0, s1, s2, s3, dk_ref, dv_ref, bias, lse, delta):
    block = q0.shape[0]
    heads = lse.shape[0]
    f32 = jnp.float32
    rows = lax.broadcasted_iota(jnp.int32, bias.shape, 0)
    cols = lax.broadcasted_iota(jnp.int32, bias.shape, 1)
    bias[...] = jnp.where(cols >= rows, 0.0, -jnp.inf)
    parts = [s0[...]]
    for hop, ref in enumerate((s1, s2, s3), 1):
        part = ref[...]
        row = lax.broadcasted_iota(jnp.int32, part.shape, 0)
        parts.append(jnp.where((idx_ref[0] + hop > last) & (row < heads), BIG, part))
    stats = jnp.concatenate(parts, axis=1)
    for one in range(heads):
        lse[one] = stats[one : one + 1]
        delta[one] = stats[heads + one : heads + one + 1]
    edge = bias.shape[1]

    @pl.loop(0, heads // GROUP)
    def _(step):
        for group in range(GROUP):
            head = GROUP * step + group
            lanes = pl.ds(pl.multiple_of(head * HEAD, HEAD), HEAD)
            queries = jnp.concatenate([ref[:, lanes] for ref in (q0, q1, q2, q3)], axis=0)
            dos = jnp.concatenate([ref[:, lanes] for ref in (d0, d1, d2, d3)], axis=0)
            scores = lax.dot_general(both_ref[pl.ds(0, block), lanes], queries, NT, preferred_element_type=f32) * scale - lse[head]
            scores = jnp.concatenate([scores[:, :edge] + bias[...], scores[:, edge:]], axis=1)
            probs = jnp.exp(scores)
            prob_grad = lax.dot_general(both_ref[pl.ds(block, block), lanes], dos, NT, preferred_element_type=f32)
            score_grad = (probs * (prob_grad - delta[head])).astype(jnp.bfloat16)
            dk_ref[:, lanes] = (jnp.dot(score_grad, queries, preferred_element_type=f32) * scale).astype(dk_ref.dtype)
            dv_ref[:, lanes] = jnp.dot(probs.astype(jnp.bfloat16), dos, preferred_element_type=f32).astype(dv_ref.dtype)


def key_side(device, both, queries, out_grads, stats, scale, last):
    block, width = queries[0].shape
    heads = width // HEAD
    shape = jax.ShapeDtypeStruct((block, width), jnp.bfloat16)
    return pl.pallas_call(
        functools.partial(key_kernel, scale, last),
        in_specs=[pl.BlockSpec(memory_space=pltpu.SMEM)] + [INSIDE] * 13,
        out_specs=[INSIDE] * 2,
        out_shape=[shape, shape],
        scratch_shapes=[
            pltpu.VMEM((block, 256), jnp.float32),
            pltpu.VMEM((heads, 1, 4 * block), jnp.float32),
            pltpu.VMEM((heads, 1, 4 * block), jnp.float32),
        ],
        compiler_params=pltpu.CompilerParams(vmem_limit_bytes=VMEM_BYTES),
        cost_estimate=pl.CostEstimate(
            flops=40 * block * block * width, bytes_accessed=24 * block * width, transcendentals=4 * block * block * heads
        ),
    )(device, both, *queries, *out_grads, *stats)


def per_device(queries, keys, values, stream_grad, conv_input, conv_weight, out_weight):
    block = queries.shape[0]
    last = lax.axis_size(CTX) - 1
    scale = 1.0 / math.sqrt(HEAD)
    device = lax.axis_index(CTX).astype(jnp.int32).reshape(1)
    tp = lax.axis_index("tp")

    kv0, inside, across = pack(device, keys, values, conv_input, stream_grad)
    inside, across = swapped(inside, 0), swapped(across, 1)
    kv1, q1 = rotated(kv0, 1), rotated(queries, -1)
    q2 = rotated(q1, -1)
    q3 = rotated(q2, -1)

    grad_stream, tap_rows = conv(device, stream_grad, conv_input, inside, across, conv_weight, last)
    near_rows = lax.all_gather(tap_rows, "near", axis=0)
    other = lax.ppermute(grad_stream, "tp", [(0, 1), (1, 0)])
    other, sent = lax.optimization_barrier((other, kv1))
    kv2 = rotated(sent, 1)
    out_grad = project(tp, grad_stream, other, out_weight)
    (sent,) = after((kv2,), (out_grad, q1))
    kv3 = rotated(sent, 1)
    (sent,) = after((out_grad,), (q1,))
    d1 = rotated(sent, -1)
    (sent,) = after((d1,), (kv2, q2))
    d2 = rotated(sent, -1)
    d3 = rotated(d2, -1)

    (near_rows,) = after((near_rows,), (kv3, d2, q2))
    all_rows = lax.all_gather(jnp.sum(near_rows, axis=0), "z", axis=0)
    query_grad, stats = query_side(device, queries, out_grad, (kv3, kv2, kv1, kv0), scale)
    all_stats = [stats] + [rotated(stats, -hop) for hop in (1, 2, 3)]
    key_grad, value_grad = key_side(device, kv0, (queries, q1, q2, q3), (out_grad, d1, d2, d3), all_stats, scale, last)
    tap_rows = jnp.sum(all_rows, axis=0)[: conv_weight.shape[0]]
    kernel_grad = tap_rows / math.sqrt(block * (last + 1))
    return (query_grad, key_grad, value_grad, grad_stream, kernel_grad)


def solution(mesh):
    count, pair = mesh.devices.shape
    far = 8
    split = Mesh(mesh.devices.reshape(far, count // far, pair), CTX + ("tp",))
    frames = P(CTX, "tp")
    return jax.shard_map(
        per_device,
        mesh=split,
        in_specs=(frames,) * 5 + (P(None, "tp"), P("tp", None)),
        out_specs=(frames,) * 4 + (P(None, "tp"),),
        check_vma=False,
    )
```

time: 116 us -> 130 us (1.12)
  the two profiles are of different devices: /device:TPU:1 before, /device:TPU:4 now
where the time goes in v7:
time: 130 us
  waiting for transfers between devices  58.6 us (45%)
  starting transfers between devices  26.7 us (21%)
  Pallas kernels  17.9 us (14%)
  between operations  14.2 us (11%)
  other arithmetic  4.33 us (3%)
  matrix products  4.06 us (3%)
  local copies, waits for them, and re-layouts  3.93 us (3%)
    all_gather x1, waiting for transfers between devices, per_device(): all_rows = lax.all_gather(jnp.sum(near_rows, axis=0), 'z', axis=0)  22.3 us
    ppermute x12, starting transfers between devices, rotated(): lax.ppermute(part, CTX, [(i, (i + by) % count) for i in range(count)])  20.8 us
    ppermute x12, waiting for transfers between devices, rotated(): lax.ppermute(part, CTX, [(i, (i + by) % count) for i in range(count)])  17.9 us
    ppermute x1, waiting for transfers between devices, per_device(): other = lax.ppermute(grad_stream, 'tp', [(0, 1), (1, 0)])  9.38 us
    all_gather x1, waiting for transfers between devices, per_device(): near_rows = lax.all_gather(tap_rows, 'near', axis=0)  5.76 us
    pallas_call x1, Pallas kernels, query_side(): pl.pallas_call(functools.partial(query_kernel, scale), in_specs=[pl.Block...  5.73 us
    pallas_call x1, Pallas kernels, key_side(): pl.pallas_call(functools.partial(key_kernel, scale, last), in_specs=[pl.B...  5.38 us
    pallas_call x1, Pallas kernels, conv(): pl.pallas_call(functools.partial(conv_kernel, last), in_specs=[pl.BlockSp...  4.57 us
  transfers between devices with their start and end apart: 17, of which 9 were waited for; matrix products, arithmetic and copies ran while one was open for 3% of the time, Pallas kernels for 9%

profile of v7, /device:TPU:4, one launch (start us, length us, event | category | flops | bytes accessed | tf_op | source)
XLA Modules:
  0.0 129.6 jit_solution(6001256680816005276)
XLA Ops:
  7.3 2.2 %shard_map.110 = (bf16[384,1024]{1,0:T(8,128)(2,1)}, bf16[32,1024]{1,0:T(8,128)(2,1)}, bf16[32,1024]{1,0:T(8,128)(2,1)}) custom-call(s32[1]{0:T(128)} %bitcast.idx_ref, bf16[192,1024]{1,0:T(8,128)(2,1)} %k_ref.1, bf16[192,1024]{1,0:T(8,128)(2,1)} %v_ref.1, bf16[192,1024]{1,0:T(8,128)(2,1)} %input_ref.3, bf16[192,1024]{1,0:T(8,128)(2,1)} %grad_ref.3), custom_call_target="tpu_custom_call" | custom-call | tf_op jit(solution)/shard_map/pallas_call | solution.py:55
  9.5 2.5 %collective-permute-start.1 = (bf16[32,1024]{1,0:T(8,128)(2,1)}, bf16[32,1024]{1,0:T(8,128)(2,1)S(1)}, u32[]{:S(2)}, u32[]{:S(2)}) collective-permute-start(bf16[32,1024]{1,0:T(8,128)(2,1)} %get-tuple-element.21), channel_id=1, source_target_pairs={{0,0},{2,4},{4,2},{6,8},{8,6},{10,12},{12,10},{14,16},{16,14},{18,... | collective-permute-start | bytes 196616 | tf_op jit(solution)/shard_map/ppermute | solution.py:30
  12.1 3.2 %collective-permute-done.1.across_ref = bf16[32,1024]{1,0:T(8,128)(2,1)S(1)} collective-permute-done((bf16[32,1024]{1,0:T(8,128)(2,1)}, bf16[32,1024]{1,0:T(8,128)(2,1)S(1)}, u32[]{:S(2)}, u32[]{:S(2)}) %collective-permute-start.1) | collective-permute-done | bytes 65568 | tf_op jit(solution)/shard_map/ppermute | solution.py:30
  15.3 4.6 %shard_map.111 = (bf16[192,1024]{1,0:T(8,128)(2,1)}, f32[32,1024]{1,0:T(8,128)}) custom-call(s32[1]{0:T(128)} %bitcast.idx_ref, bf16[192,1024]{1,0:T(8,128)(2,1)S(1)} %copy-done, bf16[192,1024]{1,0:T(8,128)(2,1)S(1)} %copy-done.1, bf16[32,1024]{1,0:T(8,128)(2,1)S(1)} %collective-permute-done.inside_ref, ...), custom_call_target="tpu_custom_call" | custom-call | flops 196608 | bytes 12288 | tf_op jit(solution)/shard_map/pallas_call | solution.py:104
  20.0 0.6 collective-permute-start.3
  20.6 3.2 %collective-permute-start.2 = (bf16[192,1024]{1,0:T(8,128)(2,1)}, bf16[192,1024]{1,0:T(8,128)(2,1)S(1)}, u32[]{:S(2)}, u32[]{:S(2)}) collective-permute-start(bf16[192,1024]{1,0:T(8,128)(2,1)} %get-tuple-element.18), channel_id=1, source_target_pairs={{0,1},{1,0},{2,3},{3,2},{4,5},{5,4},{6,7},{7,6},{8,9},{9,8},{10,11... | collective-permute-start | bytes 1179656 | tf_op jit(solution)/shard_map/ppermute | solution.py:256
  23.8 1.0 collective-permute-start.5
  24.7 9.4 %collective-permute-done.2 = bf16[192,1024]{1,0:T(8,128)(2,1)S(1)} collective-permute-done((bf16[192,1024]{1,0:T(8,128)(2,1)}, bf16[192,1024]{1,0:T(8,128)(2,1)S(1)}, u32[]{:S(2)}, u32[]{:S(2)}) %collective-permute-start.2) | collective-permute-done | bytes 393248 | tf_op jit(solution)/shard_map/ppermute | solution.py:256
  34.1 1.7 %collective-permute-start.7 = (bf16[192,1024]{1,0:T(8,128)(2,1)}, bf16[192,1024]{1,0:T(8,128)(2,1)S(1)}, u32[]{:S(2)}, u32[]{:S(2)}) collective-permute-start(bf16[192,1024]{1,0:T(8,128)(2,1)} %collective-permute-done.5.q1), channel_id=1, source_target_pairs={{0,254},{2,0},{4,2},{6,4},{8,6},{10,8},{12,10},{14,12},{16,14},{18... | collective-permute-start | bytes 1179656 | tf_op jit(solution)/shard_map/ppermute | solution.py:24
  35.9 4.1 %convolution_convert_fusion.do_ref.d0 = bf16[192,1024]{1,0:T(8,128)(2,1)S(1)} fusion(bf16[1024,2048]{1,0:T(8,128)(2,1)} %param.13, bf16[192,1024]{1,0:T(8,128)(2,1)S(1)} %collective-permute-done.2, bf16[192,1024]{1,0:T(8,128)(2,1)} %get-tuple-element.18, pred[]{:T(512)S(6)} %eq.3), kind=kOutput, calls=%fused_computation | convolution fusion | flops 809041920 | bytes 5373953 | tf_op jit(solution)/shard_map/dot_general | solution.py:123
  40.1 0.7 copy-done.7
  40.8 10.8 %collective-permute-done.4.both2 = bf16[384,1024]{1,0:T(8,128)(2,1)S(1)} collective-permute-done((bf16[384,1024]{1,0:T(8,128)(2,1)S(1)}, bf16[384,1024]{1,0:T(8,128)(2,1)S(1)}, u32[]{:S(2)}, u32[]{:S(2)}) %collective-permute-start.4) | collective-permute-done | bytes 786464 | tf_op jit(solution)/shard_map/ppermute | solution.py:24
  51.6 6.6 %collective-permute-start.6 = (bf16[384,1024]{1,0:T(8,128)(2,1)S(1)}, bf16[384,1024]{1,0:T(8,128)(2,1)S(1)}, u32[]{:S(2)}, u32[]{:S(2)}) collective-permute-start(bf16[384,1024]{1,0:T(8,128)(2,1)S(1)} %collective-permute-done.4.both2), channel_id=1, source_target_pairs={{0,2},{2,4},{4,6},{6,8},{8,10},{10,12},{12,14},{14,16},{16,18},{18... | collective-permute-start | bytes 2359304 | tf_op jit(solution)/shard_map/ppermute | solution.py:24
  58.4 0.6 copy-done.5
  59.0 0.8 copy-done.9
  59.8 3.9 %collective-permute-done.10.d2 = bf16[192,1024]{1,0:T(8,128)(2,1)S(1)} collective-permute-done((bf16[192,1024]{1,0:T(8,128)(2,1)S(1)}, bf16[192,1024]{1,0:T(8,128)(2,1)S(1)}, u32[]{:S(2)}, u32[]{:S(2)}) %collective-permute-start.10) | collective-permute-done | bytes 393248 | tf_op jit(solution)/shard_map/ppermute | solution.py:24
  63.6 0.7 copy-done.11
  64.4 5.8 %all-gather.5.cloned.1.call-done = f32[512,1024]{1,0:T(8,128)} async-done(((f32[32,1024]{1,0:T(8,128)}), f32[512,1024]{1,0:T(8,128)}) %all-gather.5.cloned.1.call-update) | async-done | bytes 2097168 | tf_op jit(solution)/shard_map/all_gather | solution.py:255
  70.2 2.4 %reduce_sum.18 = f32[32,1024]{1,0:T(8,128)} reduce(f32[16,32,1024]{2,1,0:T(8,128)} %bitcast.4, f32[]{:T(128)} %constant.21.clone.1), dimensions={0}, to_apply=%region_0.1 | reduce | flops 491520 | bytes 2228228 | tf_op jit(solution)/shard_map/reduce_sum | solution.py:269
  72.6 1.1 collective-permute-start.8
  73.6 2.2 %collective-permute-start.11 = (bf16[192,1024]{1,0:T(8,128)(2,1)}, bf16[192,1024]{1,0:T(8,128)(2,1)S(1)}, u32[]{:S(2)}, u32[]{:S(2)}) collective-permute-start(bf16[192,1024]{1,0:T(8,128)(2,1)} %copy-done.11), channel_id=1, source_target_pairs={{0,254},{2,0},{4,2},{6,4},{8,6},{10,8},{12,10},{14,12},{16,14},{18... | collective-permute-start | bytes 1179656 | tf_op jit(solution)/shard_map/ppermute | solution.py:24
  75.8 1.0 copy-done.8
  76.8 5.7 %shard_map.112 = (bf16[192,1024]{1,0:T(8,128)(2,1)}, f32[16,192]{1,0:T(8,128)S(1)}) custom-call(s32[1]{0:T(128)} %bitcast.idx_ref, bf16[192,1024]{1,0:T(8,128)(2,1)S(1)} %copy-done.4, bf16[192,1024]{1,0:T(8,128)(2,1)S(1)} %copy-done.8, bf16[384,1024]{1,0:T(8,128)(2,1)S(1)} %collective-permute-done.6.both3, ...), custom_call_target="tpu_custom_call" | custom-call | flops 1509949440 | bytes 4718592 | tf_op jit(solution)/shard_map/pallas_call | solution.py:167
  82.6 6.3 %collective-permute-start.12 = (f32[16,192]{1,0:T(8,128)S(1)}, f32[16,192]{1,0:T(8,128)S(1)}, u32[]{:S(2)}, u32[]{:S(2)}) collective-permute-start(f32[16,192]{1,0:T(8,128)S(1)} %get-tuple-element.30.s0), channel_id=1, source_target_pairs={{0,254},{2,0},{4,2},{6,4},{8,6},{10,8},{12,10},{14,12},{16,14},{18... | collective-permute-start | bytes 36872 | tf_op jit(solution)/shard_map/ppermute | solution.py:24
  88.9 1.1 collective-permute-start.13
  90.0 0.4 collective-permute-done.12.s1
  90.4 2.3 %collective-permute-done.13.s2 = f32[16,192]{1,0:T(8,128)S(1)} collective-permute-done((f32[16,192]{1,0:T(8,128)S(1)}, f32[16,192]{1,0:T(8,128)S(1)}, u32[]{:S(2)}, u32[]{:S(2)}) %collective-permute-start.13) | collective-permute-done | bytes 12320 | tf_op jit(solution)/shard_map/ppermute | solution.py:24
  92.6 0.5 collective-permute-done.14.s3
  93.2 5.4 %shard_map.113 = (bf16[192,1024]{1,0:T(8,128)(2,1)}, bf16[192,1024]{1,0:T(8,128)(2,1)}) custom-call(s32[1]{0:T(128)} %bitcast.idx_ref, bf16[384,1024]{1,0:T(8,128)(2,1)S(1)} %copy-done.3, bf16[192,1024]{1,0:T(8,128)(2,1)S(1)} %copy-done.4, bf16[192,1024]{1,0:T(8,128)(2,1)} %collective-permute-done.5.q1, bf16[192,1024]{1,0:T(8,128)(2,1)S(1)} %copy-done.6, ...), custom_call_target="tpu_custom_call" | custom-call | flops 1509949440 | bytes 4718592 | tf_op jit(solution)/shard_map/pallas_call | solution.py:224
  98.5 22.3 %all-gather.7.cloned.1.call-done = f32[256,1024]{1,0:T(8,128)} async-done(((f32[32,1024]{1,0:T(8,128)}), f32[256,1024]{1,0:T(8,128)}) %all-gather.7.cloned.1.call-update) | async-done | bytes 1048592 | tf_op jit(solution)/shard_map/all_gather | solution.py:269
  120.8 1.3 reduce_sum.19
  122.1 0.7 slice_multiply_fusion
  (38 shorter events, 0.4 us)
Async XLA Ops:
  7.2 8.2 %copy-start = (bf16[192,1024]{1,0:T(8,128)(2,1)S(1)}, bf16[192,1024]{1,0:T(8,128)(2,1)}, u32[]{:S(2)}) copy-start(bf16[192,1024]{1,0:T(8,128)(2,1)} %grad_ref.3) | copy-start | bytes 1179652
  7.2 8.2 %copy-start.1 = (bf16[192,1024]{1,0:T(8,128)(2,1)S(1)}, bf16[192,1024]{1,0:T(8,128)(2,1)}, u32[]{:S(2)}) copy-start(bf16[192,1024]{1,0:T(8,128)(2,1)} %input_ref.3) | copy-start | bytes 1179652
  7.2 8.2 %copy-start.2 = (bf16[31,1024]{1,0:T(8,128)(2,1)S(1)}, bf16[31,1024]{1,0:T(8,128)(2,1)}, u32[]{:S(2)}) copy-start(bf16[31,1024]{1,0:T(8,128)(2,1)} %taps_ref.1) | copy-start | bytes 190468
  7.2 16.6 %copy-start.4 = (bf16[192,1024]{1,0:T(8,128)(2,1)S(1)}, bf16[192,1024]{1,0:T(8,128)(2,1)}, u32[]{:S(2)}) copy-start(bf16[192,1024]{1,0:T(8,128)(2,1)} %q0.1) | copy-start | bytes 1179652
  7.2 62.9 %all-gather.5.cloned.1.call-start = ((), (), s32[]{:S(2)}) async-start(), calls=%async_computation | async-start | bytes 2228224 | tf_op jit(solution)/shard_map/all_gather | solution.py:255
  9.4 2.6 %collective-permute-start = (bf16[32,1024]{1,0:T(8,128)(2,1)}, bf16[32,1024]{1,0:T(8,128)(2,1)S(1)}, u32[]{:S(2)}, u32[]{:S(2)}) collective-permute-start(bf16[32,1024]{1,0:T(8,128)(2,1)} %get-tuple-element.20), channel_id=1, source_target_pairs={{0,2},{2,0},{4,6},{6,4},{8,10},{10,8},{12,14},{14,12},{16,18},{18,... | collective-permute-start | bytes 196616 | tf_op jit(solution)/shard_map/ppermute | solution.py:30
  9.5 5.8 %collective-permute-start.1 = (bf16[32,1024]{1,0:T(8,128)(2,1)}, bf16[32,1024]{1,0:T(8,128)(2,1)S(1)}, u32[]{:S(2)}, u32[]{:S(2)}) collective-permute-start(bf16[32,1024]{1,0:T(8,128)(2,1)} %get-tuple-element.21), channel_id=1, source_target_pairs={{0,0},{2,4},{4,2},{6,8},{8,6},{10,12},{12,10},{14,16},{16,14},{18,... | collective-permute-start | bytes 196616 | tf_op jit(solution)/shard_map/ppermute | solution.py:30
  19.9 100.9 %all-gather.7.cloned.1.call-start = ((), (), s32[]{:S(2)}) async-start(), calls=%async_computation.1 | async-start | bytes 1179648 | tf_op jit(solution)/shard_map/all_gather | solution.py:269
  20.0 14.1 %collective-permute-start.3 = (bf16[384,1024]{1,0:T(8,128)(2,1)}, bf16[384,1024]{1,0:T(8,128)(2,1)S(1)}, u32[]{:S(2)}, u32[]{:S(2)}) collective-permute-start(bf16[384,1024]{1,0:T(8,128)(2,1)} %get-tuple-element.23.both0.both_ref), channel_id=1, source_target_pairs={{0,2},{2,4},{4,6},{6,8},{8,10},{10,12},{12,14},{14,16},{16,18},{18... | collective-permute-start | bytes 2359304 | tf_op jit(solution)/shard_map/ppermute | solution.py:24
  20.6 13.6 %collective-permute-start.2 = (bf16[192,1024]{1,0:T(8,128)(2,1)}, bf16[192,1024]{1,0:T(8,128)(2,1)S(1)}, u32[]{:S(2)}, u32[]{:S(2)}) collective-permute-start(bf16[192,1024]{1,0:T(8,128)(2,1)} %get-tuple-element.18), channel_id=1, source_target_pairs={{0,1},{1,0},{2,3},{3,2},{4,5},{5,4},{6,7},{7,6},{8,9},{9,8},{10,11... | collective-permute-start | bytes 1179656 | tf_op jit(solution)/shard_map/ppermute | solution.py:256
  23.8 10.4 %collective-permute-start.5 = (bf16[192,1024]{1,0:T(8,128)(2,1)S(1)}, bf16[192,1024]{1,0:T(8,128)(2,1)}, u32[]{:S(2)}, u32[]{:S(2)}) collective-permute-start(bf16[192,1024]{1,0:T(8,128)(2,1)S(1)} %copy-done.4), channel_id=1, source_target_pairs={{0,254},{2,0},{4,2},{6,4},{8,6},{10,8},{12,10},{14,12},{16,14},{18... | collective-permute-start | bytes 1179656 | tf_op jit(solution)/shard_map/ppermute | solution.py:24
  34.1 17.5 %collective-permute-start.4 = (bf16[384,1024]{1,0:T(8,128)(2,1)S(1)}, bf16[384,1024]{1,0:T(8,128)(2,1)S(1)}, u32[]{:S(2)}, u32[]{:S(2)}) collective-permute-start(bf16[384,1024]{1,0:T(8,128)(2,1)S(1)} %collective-permute-done.3.both1), channel_id=1, source_target_pairs={{0,2},{2,4},{4,6},{6,8},{8,10},{10,12},{12,14},{14,16},{16,18},{18... | collective-permute-start | bytes 2359304 | tf_op jit(solution)/shard_map/ppermute | solution.py:24
  34.1 24.1 %collective-permute-start.7 = (bf16[192,1024]{1,0:T(8,128)(2,1)}, bf16[192,1024]{1,0:T(8,128)(2,1)S(1)}, u32[]{:S(2)}, u32[]{:S(2)}) collective-permute-start(bf16[192,1024]{1,0:T(8,128)(2,1)} %collective-permute-done.5.q1), channel_id=1, source_target_pairs={{0,254},{2,0},{4,2},{6,4},{8,6},{10,8},{12,10},{14,12},{16,14},{18... | collective-permute-start | bytes 1179656 | tf_op jit(solution)/shard_map/ppermute | solution.py:24
  39.9 35.9 %copy-start.3 = (bf16[384,1024]{1,0:T(8,128)(2,1)S(1)}, bf16[384,1024]{1,0:T(8,128)(2,1)}, u32[]{:S(2)}) copy-start(bf16[384,1024]{1,0:T(8,128)(2,1)} %get-tuple-element.23.both0.both_ref) | copy-start | bytes 2359300
  39.9 18.3 %collective-permute-start.9 = (bf16[192,1024]{1,0:T(8,128)(2,1)S(1)}, bf16[192,1024]{1,0:T(8,128)(2,1)S(1)}, u32[]{:S(2)}, u32[]{:S(2)}) collective-permute-start(bf16[192,1024]{1,0:T(8,128)(2,1)S(1)} %convolution_convert_fusion.do_ref.d0), channel_id=1, source_target_pairs={{0,254},{2,0},{4,2},{6,4},{8,6},{10,8},{12,10},{14,12},{16,14},{18... | collective-permute-start | bytes 1179656 | tf_op jit(solution)/shard_map/ppermute | solution.py:24
  40.0 0.7 copy-start.7
  51.6 12.8 %collective-permute-start.6 = (bf16[384,1024]{1,0:T(8,128)(2,1)S(1)}, bf16[384,1024]{1,0:T(8,128)(2,1)S(1)}, u32[]{:S(2)}, u32[]{:S(2)}) collective-permute-start(bf16[384,1024]{1,0:T(8,128)(2,1)S(1)} %collective-permute-done.4.both2), channel_id=1, source_target_pairs={{0,2},{2,4},{4,6},{6,8},{8,10},{10,12},{12,14},{14,16},{16,18},{18... | collective-permute-start | bytes 2359304 | tf_op jit(solution)/shard_map/ppermute | solution.py:24
  58.3 0.7 copy-start.5
  58.3 5.4 %collective-permute-start.10 = (bf16[192,1024]{1,0:T(8,128)(2,1)S(1)}, bf16[192,1024]{1,0:T(8,128)(2,1)S(1)}, u32[]{:S(2)}, u32[]{:S(2)}) collective-permute-start(bf16[192,1024]{1,0:T(8,128)(2,1)S(1)} %collective-permute-done.9.d1), channel_id=1, source_target_pairs={{0,254},{2,0},{4,2},{6,4},{8,6},{10,8},{12,10},{14,12},{16,14},{18... | collective-permute-start | bytes 1179656 | tf_op jit(solution)/shard_map/ppermute | solution.py:24
  59.0 0.8 copy-start.9
  63.6 0.7 copy-start.11
  72.5 20.6 %copy-start.6 = (bf16[192,1024]{1,0:T(8,128)(2,1)S(1)}, bf16[192,1024]{1,0:T(8,128)(2,1)}, u32[]{:S(2)}) copy-start(bf16[192,1024]{1,0:T(8,128)(2,1)} %copy-done.5) | copy-start | bytes 1179652
  72.6 17.4 %collective-permute-start.8 = (bf16[192,1024]{1,0:T(8,128)(2,1)}, bf16[192,1024]{1,0:T(8,128)(2,1)S(1)}, u32[]{:S(2)}, u32[]{:S(2)}) collective-permute-start(bf16[192,1024]{1,0:T(8,128)(2,1)} %copy-done.5), channel_id=1, source_target_pairs={{0,254},{2,0},{4,2},{6,4},{8,6},{10,8},{12,10},{14,12},{16,14},{18... | collective-permute-start | bytes 1179656 | tf_op jit(solution)/shard_map/ppermute | solution.py:24
  73.6 16.4 %collective-permute-start.11 = (bf16[192,1024]{1,0:T(8,128)(2,1)}, bf16[192,1024]{1,0:T(8,128)(2,1)S(1)}, u32[]{:S(2)}, u32[]{:S(2)}) collective-permute-start(bf16[192,1024]{1,0:T(8,128)(2,1)} %copy-done.11), channel_id=1, source_target_pairs={{0,254},{2,0},{4,2},{6,4},{8,6},{10,8},{12,10},{14,12},{16,14},{18... | collective-permute-start | bytes 1179656 | tf_op jit(solution)/shard_map/ppermute | solution.py:24
  75.8 1.0 copy-start.8
  76.8 16.3 %copy-start.10 = (bf16[192,1024]{1,0:T(8,128)(2,1)S(1)}, bf16[192,1024]{1,0:T(8,128)(2,1)}, u32[]{:S(2)}) copy-start(bf16[192,1024]{1,0:T(8,128)(2,1)} %copy-done.9) | copy-start | bytes 1179652
  76.8 16.3 %copy-start.12 = (bf16[192,1024]{1,0:T(8,128)(2,1)S(1)}, bf16[192,1024]{1,0:T(8,128)(2,1)}, u32[]{:S(2)}) copy-start(bf16[192,1024]{1,0:T(8,128)(2,1)} %copy-done.11) | copy-start | bytes 1179652
  82.6 7.8 %collective-permute-start.12 = (f32[16,192]{1,0:T(8,128)S(1)}, f32[16,192]{1,0:T(8,128)S(1)}, u32[]{:S(2)}, u32[]{:S(2)}) collective-permute-start(f32[16,192]{1,0:T(8,128)S(1)} %get-tuple-element.30.s0), channel_id=1, source_target_pairs={{0,254},{2,0},{4,2},{6,4},{8,6},{10,8},{12,10},{14,12},{16,14},{18... | collective-permute-start | bytes 36872 | tf_op jit(solution)/shard_map/ppermute | solution.py:24
  88.9 3.7 %collective-permute-start.13 = (f32[16,192]{1,0:T(8,128)S(1)}, f32[16,192]{1,0:T(8,128)S(1)}, u32[]{:S(2)}, u32[]{:S(2)}) collective-permute-start(f32[16,192]{1,0:T(8,128)S(1)} %get-tuple-element.30.s0), channel_id=1, source_target_pairs={{0,252},{2,254},{4,0},{6,2},{8,4},{10,6},{12,8},{14,10},{16,12},{1... | collective-permute-start | bytes 36872 | tf_op jit(solution)/shard_map/ppermute | solution.py:24
  90.0 3.2 %collective-permute-start.14 = (f32[16,192]{1,0:T(8,128)S(1)}, f32[16,192]{1,0:T(8,128)S(1)}, u32[]{:S(2)}, u32[]{:S(2)}) collective-permute-start(f32[16,192]{1,0:T(8,128)S(1)} %get-tuple-element.30.s0), channel_id=1, source_target_pairs={{0,250},{2,252},{4,254},{6,0},{8,2},{10,4},{12,6},{14,8},{16,10},{... | collective-permute-start | bytes 36872 | tf_op jit(solution)/shard_map/ppermute | solution.py:24
Sparse Core Ops, SparseCore 0:
  20.1 50.0 all-gather.4
  72.7 48.1 all-gather.6

commit v8 on v7

--- a/solution.py
+++ b/solution.py
@@ -62,21 +62,27 @@
     )(device, keys, values, inputs, grad)
 
 
+def conv_back(padded, grad, taps):
+    block = grad.shape[0]
+    taps_count = taps.shape[0]
+    total = grad
+    for tap in range(taps_count):
+        total = total + taps[tap : tap + 1] * padded[pl.ds(EDGE + taps_count // 2 - tap, block), :]
+    return total
+
+
 def conv_kernel(last, idx_ref, grad_ref, input_ref, inside_ref, across_ref, taps_ref, out_ref, rows_ref, gpad, cpad):
     block = grad_ref.shape[0]
-    width = grad_ref.shape[1]
     taps_count = taps_ref.shape[0]
-    reach = taps_count // 2
     device = idx_ref[0]
+    even = lax.rem(device, 2) == 0
     f32 = jnp.float32
-    columns = width // HEAD
-
-    @pl.loop(0, columns)
+
+    @pl.loop(0, grad_ref.shape[1] // HEAD)
     def _(column):
         lanes = pl.ds(pl.multiple_of(column * HEAD, HEAD), HEAD)
         inside = inside_ref[:, lanes].astype(f32)
         across = across_ref[:, lanes].astype(f32)
-        even = lax.rem(device, 2) == 0
         low = jnp.where(device > 0, jnp.where(even, across, inside), 0.0)
         high = jnp.where(device < last, jnp.where(even, inside, across), 0.0)
         grad = grad_ref[:, lanes].astype(f32)
@@ -86,16 +92,12 @@
         gpad[EDGE : EDGE + block] = grad
         cpad[EDGE + block :] = high[:EDGE]
         gpad[EDGE + block :] = high[EDGE:]
-        taps = taps_ref[:, lanes].astype(f32)
-        total = grad
-        for tap in range(taps_count):
-            total = total + taps[tap : tap + 1] * gpad[pl.ds(EDGE + reach - tap, block), :]
-        out_ref[:, lanes] = total.astype(out_ref.dtype)
+        out_ref[:, lanes] = conv_back(gpad, grad, taps_ref[:, lanes].astype(f32)).astype(out_ref.dtype)
         grad = gpad[EDGE : EDGE + block]
         for tap in range(taps_count):
-            prod = grad * cpad[pl.ds(EDGE - reach + tap, block), :]
-            rows_ref[tap : tap + 1, lanes] = jnp.sum(prod, axis=0, keepdims=True)
-        rows_ref[taps_count:, lanes] = jnp.zeros_like(rows_ref[taps_count:, lanes])
+            prod = grad * cpad[pl.ds(EDGE - taps_count // 2 + tap, block), :]
+            rows_ref[column, tap : tap + 1, :] = jnp.sum(prod, axis=0, keepdims=True)
+        rows_ref[column, taps_count:, :] = jnp.zeros_like(rows_ref[column, taps_count:, :])
 
 
 def conv(device, grad, inputs, inside, across, taps, last):
@@ -107,15 +109,43 @@
         out_specs=[INSIDE] * 2,
         out_shape=[
             jax.ShapeDtypeStruct((block, width), jnp.bfloat16),
-            jax.ShapeDtypeStruct((8 * pl.cdiv(count, 8), width), jnp.float32),
+            jax.ShapeDtypeStruct((width // HEAD, 8 * pl.cdiv(count, 8), HEAD), jnp.float32),
         ],
-        scratch_shapes=[
-            pltpu.VMEM((block + 2 * EDGE, HEAD), jnp.float32),
-            pltpu.VMEM((block + 2 * EDGE, HEAD), jnp.float32),
-        ],
+        scratch_shapes=[pltpu.VMEM((block + 2 * EDGE, HEAD), jnp.float32)] * 2,
         compiler_params=pltpu.CompilerParams(vmem_limit_bytes=VMEM_BYTES),
         cost_estimate=pl.CostEstimate(flops=block * width, bytes_accessed=block * width // 16, transcendentals=0),
     )(device, grad, inputs, inside, across, taps)
+
+
+def other_kernel(last, count, idx_ref, grad_ref, edges_ref, out_ref, gpad):
+    block = grad_ref.shape[0]
+    device = idx_ref[0]
+    even = lax.rem(device, 2) == 0
+    f32 = jnp.float32
+
+    @pl.loop(0, grad_ref.shape[1] // HEAD)
+    def _(column):
+        lanes = pl.ds(pl.multiple_of(column * HEAD, HEAD), HEAD)
+        edges = edges_ref[:, lanes].astype(f32)
+        inside, across = edges[:EDGE], edges[EDGE : 2 * EDGE]
+        grad = grad_ref[:, lanes].astype(f32)
+        gpad[:EDGE] = jnp.where(device > 0, jnp.where(even, across, inside), 0.0)
+        gpad[EDGE : EDGE + block] = grad
+        gpad[EDGE + block :] = jnp.where(device < last, jnp.where(even, inside, across), 0.0)
+        out_ref[:, lanes] = conv_back(gpad, grad, edges[2 * EDGE : 2 * EDGE + count]).astype(out_ref.dtype)
+
+
+def conv_other(device, grad, edges, count, last):
+    block, width = grad.shape
+    return pl.pallas_call(
+        functools.partial(other_kernel, last, count),
+        in_specs=[pl.BlockSpec(memory_space=pltpu.SMEM)] + [INSIDE] * 2,
+        out_specs=INSIDE,
+        out_shape=jax.ShapeDtypeStruct((block, width), jnp.bfloat16),
+        scratch_shapes=[pltpu.VMEM((block + 2 * EDGE, HEAD), jnp.float32)],
+        compiler_params=pltpu.CompilerParams(vmem_limit_bytes=VMEM_BYTES),
+        cost_estimate=pl.CostEstimate(flops=block * width, bytes_accessed=block * width // 16, transcendentals=0),
+    )(device, grad, edges)
 
 
 def project(tp, own, other, weight):
@@ -245,33 +275,45 @@
     device = lax.axis_index(CTX).astype(jnp.int32).reshape(1)
     tp = lax.axis_index("tp")
 
+    pair = [(0, 1), (1, 0)]
     kv0, inside, across = pack(device, keys, values, conv_input, stream_grad)
     inside, across = swapped(inside, 0), swapped(across, 1)
-    kv1, q1 = rotated(kv0, 1), rotated(queries, -1)
+    other = lax.ppermute(stream_grad, "tp", pair)
+    (sent,) = after((kv0,), (across,))
+    kv1, q1 = rotated(sent, 1), rotated(queries, -1)
     q2 = rotated(q1, -1)
     q3 = rotated(q2, -1)
 
+    taps_count = conv_weight.shape[0]
+    padding = jnp.zeros((2 * EDGE - taps_count, conv_weight.shape[1]), conv_weight.dtype)
+    edges = lax.ppermute(jnp.concatenate([inside[EDGE:], across[EDGE:], conv_weight, padding], axis=0), "tp", pair)
     grad_stream, tap_rows = conv(device, stream_grad, conv_input, inside, across, conv_weight, last)
-    near_rows = lax.all_gather(tap_rows, "near", axis=0)
-    other = lax.ppermute(grad_stream, "tp", [(0, 1), (1, 0)])
-    other, sent = lax.optimization_barrier((other, kv1))
+    other, edges, sent = after((other, edges, kv1), (q1, grad_stream))
     kv2 = rotated(sent, 1)
-    out_grad = project(tp, grad_stream, other, out_weight)
+    out_grad = project(tp, grad_stream, conv_other(device, other, edges, taps_count, last), out_weight)
     (sent,) = after((kv2,), (out_grad, q1))
     kv3 = rotated(sent, 1)
-    (sent,) = after((out_grad,), (q1,))
-    d1 = rotated(sent, -1)
-    (sent,) = after((d1,), (kv2, q2))
+
+    (tap_rows,) = after((tap_rows,), (kv1,))
+    tap_sums = jnp.sum(lax.all_to_all(tap_rows, "z", 0, 0, tiled=True), axis=0)
+    d1 = rotated(out_grad, -1)
+    (sent,) = after((d1,), (kv2, q2, tap_sums))
     d2 = rotated(sent, -1)
-    d3 = rotated(d2, -1)
-
-    (near_rows,) = after((near_rows,), (kv3, d2, q2))
-    all_rows = lax.all_gather(jnp.sum(near_rows, axis=0), "z", axis=0)
-    query_grad, stats = query_side(device, queries, out_grad, (kv3, kv2, kv1, kv0), scale)
+    copies = jnp.broadcast_to(tap_sums, (lax.axis_size("near"),) + tap_sums.shape)
+    (copies,) = after((copies,), (d1,))
+    tap_sums = jnp.sum(lax.all_to_all(copies, "near", 0, 0, tiled=True), axis=0)
+    (sent,) = after((d2,), (kv3, q3))
+    d3 = rotated(sent, -1)
+
+    (near,) = after((queries,), (tap_sums,))
+    query_grad, stats = query_side(device, near, out_grad, (kv3, kv2, kv1, kv0), scale)
     all_stats = [stats] + [rotated(stats, -hop) for hop in (1, 2, 3)]
+    copies = jnp.broadcast_to(tap_sums, (lax.axis_size("z"),) + tap_sums.shape)
+    (copies,) = after((copies,), (*all_stats[1:], d3))
+    tap_sums = lax.all_to_all(copies, "z", 0, 0, tiled=True)
     key_grad, value_grad = key_side(device, kv0, (queries, q1, q2, q3), (out_grad, d1, d2, d3), all_stats, scale, last)
-    tap_rows = jnp.sum(all_rows, axis=0)[: conv_weight.shape[0]]
-    kernel_grad = tap_rows / math.sqrt(block * (last + 1))
+    rows = jnp.transpose(tap_sums, (1, 0, 2)).reshape(tap_sums.shape[1], -1)[:taps_count]
+    kernel_grad = rows / math.sqrt(block * (last + 1))
     return (query_grad, key_grad, value_grad, grad_stream, kernel_grad)
 
 

time: 130 us -> 122 us (0.938)
  the two profiles are of different devices: /device:TPU:4 before, /device:TPU:1 now
where the time goes in v8:
time: 122 us; the launch traced here: 121 us
  starting transfers between devices  55.9 us (46%)
  waiting for transfers between devices  32.4 us (27%)
  Pallas kernels  21.3 us (17%)
  matrix products  4.03 us (3%)
  local copies, waits for them, and re-layouts  4.01 us (3%)
  other arithmetic  2.6 us (2%)
    ppermute x12, starting transfers between devices, rotated(): lax.ppermute(part, CTX, [(i, (i + by) % count) for i in range(count)])  26.9 us
    ppermute x1, waiting for transfers between devices, per_device(): lax.ppermute(jnp.concatenate([inside[EDGE:], across[EDGE:], conv_weight,...  13.8 us
    all_to_all x1, starting transfers between devices, per_device(): tap_sums = jnp.sum(lax.all_to_all(tap_rows, 'z', 0, 0, tiled=True), axis=0)  11.3 us
    pallas_call x1, Pallas kernels, query_side(): pl.pallas_call(functools.partial(query_kernel, scale), in_specs=[pl.Block...  6.91 us
    all_to_all x1, waiting for transfers between devices, per_device(): tap_sums = jnp.sum(lax.all_to_all(copies, 'near', 0, 0, tiled=True), axis=0)  6.7 us
    all_to_all x1, starting transfers between devices, per_device(): tap_sums = jnp.sum(lax.all_to_all(copies, 'near', 0, 0, tiled=True), axis=0)  6.21 us
    pallas_call x1, Pallas kernels, key_side(): pl.pallas_call(functools.partial(key_kernel, scale, last), in_specs=[pl.B...  5.72 us
    pallas_call x1, Pallas kernels, conv(): pl.pallas_call(functools.partial(conv_kernel, last), in_specs=[pl.BlockSp...  4.57 us
  transfers between devices with their start and end apart: 19, of which 6 were waited for; matrix products, arithmetic and copies ran while one was open for 6% of the time, Pallas kernels for 16%

profile of v8, /device:TPU:1, one launch (start us, length us, event | category | flops | bytes accessed | tf_op | source)
XLA Modules:
  0.0 121.1 jit_solution(16286720519206027872)
XLA Ops:
  0.7 2.2 %shard_map.110 = (bf16[384,1024]{1,0:T(8,128)(2,1)}, bf16[32,1024]{1,0:T(8,128)(2,1)}, bf16[32,1024]{1,0:T(8,128)(2,1)}) custom-call(s32[1]{0:T(128)} %bitcast.idx_ref, bf16[192,1024]{1,0:T(8,128)(2,1)} %k_ref.1, bf16[192,1024]{1,0:T(8,128)(2,1)} %v_ref.1, bf16[192,1024]{1,0:T(8,128)(2,1)} %input_ref.3, bf16[192,1024]{1,0:T(8,128)(2,1)} %grad_ref.3), custom_call_target="tpu_custom_call" | custom-call | tf_op jit(solution)/shard_map/pallas_call | solution.py:55
  2.9 4.5 %collective-permute-start.1 = (bf16[32,1024]{1,0:T(8,128)(2,1)}, bf16[32,1024]{1,0:T(8,128)(2,1)S(1)}, u32[]{:S(2)}, u32[]{:S(2)}) collective-permute-start(bf16[32,1024]{1,0:T(8,128)(2,1)} %get-tuple-element.26), channel_id=1, source_target_pairs={{0,0},{2,4},{4,2},{6,8},{8,6},{10,12},{12,10},{14,16},{16,14},{18,... | collective-permute-start | bytes 196616 | tf_op jit(solution)/shard_map/ppermute | solution.py:30
  7.4 2.1 %collective-permute-done.1.across_ref = bf16[32,1024]{1,0:T(8,128)(2,1)S(1)} collective-permute-done((bf16[32,1024]{1,0:T(8,128)(2,1)}, bf16[32,1024]{1,0:T(8,128)(2,1)S(1)}, u32[]{:S(2)}, u32[]{:S(2)}) %collective-permute-start.1) | collective-permute-done | bytes 65568 | tf_op jit(solution)/shard_map/ppermute | solution.py:30
  9.5 1.7 %collective-permute-start.2 = (bf16[384,1024]{1,0:T(8,128)(2,1)}, bf16[384,1024]{1,0:T(8,128)(2,1)S(1)}, u32[]{:S(2)}, u32[]{:S(2)}) collective-permute-start(bf16[384,1024]{1,0:T(8,128)(2,1)} %get-tuple-element.29.both0.both_ref), channel_id=1, source_target_pairs={{0,2},{2,4},{4,6},{6,8},{8,10},{10,12},{12,14},{14,16},{16,18},{18... | collective-permute-start | bytes 2359304 | tf_op jit(solution)/shard_map/ppermute | solution.py:24
  11.3 2.9 %collective-permute-start.3 = (bf16[192,1024]{1,0:T(8,128)(2,1)S(1)}, bf16[192,1024]{1,0:T(8,128)(2,1)S(1)}, u32[]{:S(2)}, u32[]{:S(2)}) collective-permute-start(bf16[192,1024]{1,0:T(8,128)(2,1)S(1)} %copy-done.1), channel_id=1, source_target_pairs={{0,1},{1,0},{2,3},{3,2},{4,5},{5,4},{6,7},{7,6},{8,9},{9,8},{10,11... | collective-permute-start | bytes 1179656 | tf_op jit(solution)/shard_map/ppermute | solution.py:281
  14.2 0.8 collective-permute-start.5
  15.8 4.6 %shard_map.111 = (bf16[192,1024]{1,0:T(8,128)(2,1)}, f32[8,32,128]{2,1,0:T(8,128)}) custom-call(s32[1]{0:T(128)} %bitcast.idx_ref, bf16[192,1024]{1,0:T(8,128)(2,1)S(1)} %copy-done.1, bf16[192,1024]{1,0:T(8,128)(2,1)S(1)} %copy-done, bf16[32,1024]{1,0:T(8,128)(2,1)S(1)} %collective-permute-done.inside_ref, ...), custom_call_target="tpu_custom_call" | custom-call | flops 196608 | bytes 12288 | tf_op jit(solution)/shard_map/pallas_call | solution.py:106
  20.4 13.8 %collective-permute-done.4.edges_ref = bf16[64,1024]{1,0:T(8,128)(2,1)S(1)} collective-permute-done((bf16[64,1024]{1,0:T(8,128)(2,1)S(1)}, bf16[64,1024]{1,0:T(8,128)(2,1)S(1)}, u32[]{:S(2)}, u32[]{:S(2)}) %collective-permute-start.4) | collective-permute-done | bytes 131104 | tf_op jit(solution)/shard_map/ppermute | solution.py:289
  34.2 0.7 copy-done.5
  35.0 1.4 %collective-permute-start.9 = (bf16[192,1024]{1,0:T(8,128)(2,1)}, bf16[192,1024]{1,0:T(8,128)(2,1)}, u32[]{:S(2)}, u32[]{:S(2)}) collective-permute-start(bf16[192,1024]{1,0:T(8,128)(2,1)} %copy-done.5), channel_id=1, source_target_pairs={{0,254},{2,0},{4,2},{6,4},{8,6},{10,8},{12,10},{14,12},{16,14},{18... | collective-permute-start | bytes 1179656 | tf_op jit(solution)/shard_map/ppermute | solution.py:24
  36.3 1.9 %shard_map.112 = bf16[192,1024]{1,0:T(8,128)(2,1)S(1)} custom-call(s32[1]{0:T(128)} %bitcast.idx_ref, bf16[192,1024]{1,0:T(8,128)(2,1)S(1)} %collective-permute-done.3.grad_ref, bf16[64,1024]{1,0:T(8,128)(2,1)S(1)} %collective-permute-done.4.edges_ref), custom_call_target="tpu_custom_call" | custom-call | flops 196608 | bytes 12288 | tf_op jit(solution)/shard_map/pallas_call | solution.py:140
  38.2 4.0 %convolution_convert_fusion.do_ref.d0 = bf16[192,1024]{1,0:T(8,128)(2,1)S(1)} fusion(bf16[1024,2048]{1,0:T(8,128)(2,1)} %param.13, bf16[192,1024]{1,0:T(8,128)(2,1)S(1)} %shard_map.112, bf16[192,1024]{1,0:T(8,128)(2,1)} %get-tuple-element.23, pred[]{:T(512)S(6)} %eq.3), kind=kOutput, calls=%fused_computation | convolution fusion | flops 809041920 | bytes 5373953 | tf_op jit(solution)/shard_map/dot_general | solution.py:153
  42.3 6.0 %collective-permute-start.6 = (bf16[192,1024]{1,0:T(8,128)(2,1)S(1)}, bf16[192,1024]{1,0:T(8,128)(2,1)S(1)}, u32[]{:S(2)}, u32[]{:S(2)}) collective-permute-start(bf16[192,1024]{1,0:T(8,128)(2,1)S(1)} %convolution_convert_fusion.do_ref.d0), channel_id=1, source_target_pairs={{0,254},{2,0},{4,2},{6,4},{8,6},{10,8},{12,10},{14,12},{16,14},{18... | collective-permute-start | bytes 1179656 | tf_op jit(solution)/shard_map/ppermute | solution.py:24
  48.3 11.3 %all-to-all-start = ((f32[8,32,128]{2,1,0:T(8,128)}), f32[8,32,128]{2,1,0:T(8,128)}, u32[]{:S(2)}, u32[]{:S(2)}) async-start(f32[8,32,128]{2,1,0:T(8,128)} %get-tuple-element.30), calls=%async_computation | async-start | bytes 262144 | tf_op jit(solution)/shard_map/all_to_all | solution.py:298
  59.7 4.0 %collective-permute-start.10 = (bf16[192,1024]{1,0:T(8,128)(2,1)}, bf16[192,1024]{1,0:T(8,128)(2,1)}, u32[]{:S(2)}, u32[]{:S(2)}) collective-permute-start(bf16[192,1024]{1,0:T(8,128)(2,1)} %collective-permute-done.9.q2), channel_id=1, source_target_pairs={{0,254},{2,0},{4,2},{6,4},{8,6},{10,8},{12,10},{14,12},{16,14},{18... | collective-permute-start | bytes 1179656 | tf_op jit(solution)/shard_map/ppermute | solution.py:24
  63.6 4.3 %all-to-all-done = f32[8,32,128]{2,1,0:T(8,128)} async-done(((f32[8,32,128]{2,1,0:T(8,128)}), f32[8,32,128]{2,1,0:T(8,128)}, u32[]{:S(2)}, u32[]{:S(2)}) %all-to-all-start) | async-done | bytes 131104 | tf_op jit(solution)/shard_map/all_to_all | solution.py:298
  68.0 0.9 reduce_sum.18
  68.9 4.8 %collective-permute-start.11 = (bf16[192,1024]{1,0:T(8,128)(2,1)S(1)}, bf16[192,1024]{1,0:T(8,128)(2,1)}, u32[]{:S(2)}, u32[]{:S(2)}) collective-permute-start(bf16[192,1024]{1,0:T(8,128)(2,1)S(1)} %collective-permute-done.6.d1), channel_id=1, source_target_pairs={{0,254},{2,0},{4,2},{6,4},{8,6},{10,8},{12,10},{14,12},{16,14},{18... | collective-permute-start | bytes 1179656 | tf_op jit(solution)/shard_map/ppermute | solution.py:24
  73.8 0.7 broadcast_in_dim.9
  74.5 6.2 %all-to-all-start.1 = ((f32[16,32,128]{2,1,0:T(8,128)}), f32[16,32,128]{2,1,0:T(8,128)}, u32[]{:S(2)}, u32[]{:S(2)}) async-start(f32[16,32,128]{2,1,0:T(8,128)} %broadcast_in_dim.9), calls=%async_computation.1 | async-start | bytes 524288 | tf_op jit(solution)/shard_map/all_to_all | solution.py:304
  81.3 6.7 %all-to-all-done.1 = f32[16,32,128]{2,1,0:T(8,128)} async-done(((f32[16,32,128]{2,1,0:T(8,128)}), f32[16,32,128]{2,1,0:T(8,128)}, u32[]{:S(2)}, u32[]{:S(2)}) %all-to-all-start.1) | async-done | bytes 262176 | tf_op jit(solution)/shard_map/all_to_all | solution.py:304
  88.0 1.6 %reduce_sum.19 = f32[32,128]{1,0:T(8,128)} reduce(f32[16,32,128]{2,1,0:T(8,128)} %all-to-all-done.1, f32[]{:T(128)} %constant.21.clone.1), dimensions={0}, to_apply=%region_1.2 | reduce | flops 61440 | bytes 278532 | tf_op jit(solution)/shard_map/reduce_sum | solution.py:304
  89.6 6.9 %shard_map.113 = (bf16[192,1024]{1,0:T(8,128)(2,1)}, f32[16,192]{1,0:T(8,128)S(1)}) custom-call(s32[1]{0:T(128)} %bitcast.idx_ref, bf16[192,1024]{1,0:T(8,128)(2,1)S(1)} %copy-done.4, bf16[192,1024]{1,0:T(8,128)(2,1)S(1)} %convolution_convert_fusion.do_ref.d0, bf16[384,1024]{1,0:T(8,128)(2,1)} %collective-permute-done.8.both3, ...), custom_call_target="tpu_custom_call" | custom-call | flops 1509949440 | bytes 4718592 | tf_op jit(solution)/shard_map/pallas_call | solution.py:197
  96.5 1.1 collective-permute-start.13
  97.6 4.6 %collective-permute-start.14 = (f32[16,192]{1,0:T(8,128)S(1)}, f32[16,192]{1,0:T(8,128)S(1)}, u32[]{:S(2)}, u32[]{:S(2)}) collective-permute-start(f32[16,192]{1,0:T(8,128)S(1)} %get-tuple-element.41.s0), channel_id=1, source_target_pairs={{0,252},{2,254},{4,0},{6,2},{8,4},{10,6},{12,8},{14,10},{16,12},{1... | collective-permute-start | bytes 36872 | tf_op jit(solution)/shard_map/ppermute | solution.py:24
  102.3 1.8 %collective-permute-start.15 = (f32[16,192]{1,0:T(8,128)S(1)}, f32[16,192]{1,0:T(8,128)S(1)}, u32[]{:S(2)}, u32[]{:S(2)}) collective-permute-start(f32[16,192]{1,0:T(8,128)S(1)} %get-tuple-element.41.s0), channel_id=1, source_target_pairs={{0,250},{2,252},{4,254},{6,0},{8,2},{10,4},{12,6},{14,8},{16,10},{... | collective-permute-start | bytes 36872 | tf_op jit(solution)/shard_map/ppermute | solution.py:24
  104.1 2.9 %collective-permute-done.15.s3 = f32[16,192]{1,0:T(8,128)S(1)} collective-permute-done((f32[16,192]{1,0:T(8,128)S(1)}, f32[16,192]{1,0:T(8,128)S(1)}, u32[]{:S(2)}, u32[]{:S(2)}) %collective-permute-start.15) | collective-permute-done | bytes 12320 | tf_op jit(solution)/shard_map/ppermute | solution.py:24
  107.6 3.4 %all-to-all-start.2 = ((f32[8,32,128]{2,1,0:T(8,128)}), f32[8,32,128]{2,1,0:T(8,128)S(1)}, u32[]{:S(2)}, u32[]{:S(2)}) async-start(f32[8,32,128]{2,1,0:T(8,128)} %broadcast_in_dim.11), calls=%async_computation.2 | async-start | bytes 262144 | tf_op jit(solution)/shard_map/all_to_all | solution.py:313
  111.0 1.0 copy-done.8
  112.0 5.7 %shard_map.114 = (bf16[192,1024]{1,0:T(8,128)(2,1)}, bf16[192,1024]{1,0:T(8,128)(2,1)}) custom-call(s32[1]{0:T(128)} %bitcast.idx_ref, bf16[384,1024]{1,0:T(8,128)(2,1)S(1)} %copy-done.3, bf16[192,1024]{1,0:T(8,128)(2,1)S(1)} %copy-done.4, bf16[192,1024]{1,0:T(8,128)(2,1)S(1)} %copy-done.6, bf16[192,1024]{1,0:T(8,128)(2,1)} %collective-permute-done.9.q2, ...), custom_call_target="tpu_custom_call" | custom-call | flops 1509949440 | bytes 4718592 | tf_op jit(solution)/shard_map/pallas_call | solution.py:254
  117.7 2.5 %all-to-all-done.2 = f32[8,32,128]{2,1,0:T(8,128)S(1)} async-done(((f32[8,32,128]{2,1,0:T(8,128)}), f32[8,32,128]{2,1,0:T(8,128)S(1)}, u32[]{:S(2)}, u32[]{:S(2)}) %all-to-all-start.2) | async-done | bytes 131104 | tf_op jit(solution)/shard_map/all_to_all | solution.py:313
  120.4 0.7 copy.15
  (44 shorter events, 2.3 us)
Async XLA Ops:
  0.6 10.7 %copy-start.1 = (bf16[192,1024]{1,0:T(8,128)(2,1)S(1)}, bf16[192,1024]{1,0:T(8,128)(2,1)}, u32[]{:S(2)}) copy-start(bf16[192,1024]{1,0:T(8,128)(2,1)} %grad_ref.3) | copy-start | bytes 1179652
  0.6 15.2 %copy-start = (bf16[192,1024]{1,0:T(8,128)(2,1)S(1)}, bf16[192,1024]{1,0:T(8,128)(2,1)}, u32[]{:S(2)}) copy-start(bf16[192,1024]{1,0:T(8,128)(2,1)} %input_ref.3) | copy-start | bytes 1179652
  0.7 13.5 %copy-start.4 = (bf16[192,1024]{1,0:T(8,128)(2,1)S(1)}, bf16[192,1024]{1,0:T(8,128)(2,1)}, u32[]{:S(2)}) copy-start(bf16[192,1024]{1,0:T(8,128)(2,1)} %q0.1) | copy-start | bytes 1179652
  0.7 14.4 %copy-start.2 = (bf16[31,1024]{1,0:T(8,128)(2,1)S(1)}, bf16[31,1024]{1,0:T(8,128)(2,1)}, u32[]{:S(2)}) copy-start(bf16[31,1024]{1,0:T(8,128)(2,1)} %taps_ref.1) | copy-start | bytes 190468
  2.9 6.7 %collective-permute-start.1 = (bf16[32,1024]{1,0:T(8,128)(2,1)}, bf16[32,1024]{1,0:T(8,128)(2,1)S(1)}, u32[]{:S(2)}, u32[]{:S(2)}) collective-permute-start(bf16[32,1024]{1,0:T(8,128)(2,1)} %get-tuple-element.26), channel_id=1, source_target_pairs={{0,0},{2,4},{4,2},{6,8},{8,6},{10,12},{12,10},{14,16},{16,14},{18,... | collective-permute-start | bytes 196616 | tf_op jit(solution)/shard_map/ppermute | solution.py:30
  9.5 24.7 %collective-permute-start.2 = (bf16[384,1024]{1,0:T(8,128)(2,1)}, bf16[384,1024]{1,0:T(8,128)(2,1)S(1)}, u32[]{:S(2)}, u32[]{:S(2)}) collective-permute-start(bf16[384,1024]{1,0:T(8,128)(2,1)} %get-tuple-element.29.both0.both_ref), channel_id=1, source_target_pairs={{0,2},{2,4},{4,6},{6,8},{8,10},{10,12},{12,14},{14,16},{16,18},{18... | collective-permute-start | bytes 2359304 | tf_op jit(solution)/shard_map/ppermute | solution.py:24
  11.3 3.8 %collective-permute-start = (bf16[32,1024]{1,0:T(8,128)(2,1)}, bf16[32,1024]{1,0:T(8,128)(2,1)S(1)}, u32[]{:S(2)}, u32[]{:S(2)}) collective-permute-start(bf16[32,1024]{1,0:T(8,128)(2,1)} %get-tuple-element.25), channel_id=1, source_target_pairs={{0,2},{2,0},{4,6},{6,4},{8,10},{10,8},{12,14},{14,12},{16,18},{18,... | collective-permute-start | bytes 196616 | tf_op jit(solution)/shard_map/ppermute | solution.py:30
  11.3 22.9 %collective-permute-start.3 = (bf16[192,1024]{1,0:T(8,128)(2,1)S(1)}, bf16[192,1024]{1,0:T(8,128)(2,1)S(1)}, u32[]{:S(2)}, u32[]{:S(2)}) collective-permute-start(bf16[192,1024]{1,0:T(8,128)(2,1)S(1)} %copy-done.1), channel_id=1, source_target_pairs={{0,1},{1,0},{2,3},{3,2},{4,5},{5,4},{6,7},{7,6},{8,9},{9,8},{10,11... | collective-permute-start | bytes 1179656 | tf_op jit(solution)/shard_map/ppermute | solution.py:281
  14.2 20.0 %collective-permute-start.5 = (bf16[192,1024]{1,0:T(8,128)(2,1)S(1)}, bf16[192,1024]{1,0:T(8,128)(2,1)S(1)}, u32[]{:S(2)}, u32[]{:S(2)}) collective-permute-start(bf16[192,1024]{1,0:T(8,128)(2,1)S(1)} %copy-done.4), channel_id=1, source_target_pairs={{0,254},{2,0},{4,2},{6,4},{8,6},{10,8},{12,10},{14,12},{16,14},{18... | collective-permute-start | bytes 1179656 | tf_op jit(solution)/shard_map/ppermute | solution.py:24
  15.2 19.0 %collective-permute-start.4 = (bf16[64,1024]{1,0:T(8,128)(2,1)S(1)}, bf16[64,1024]{1,0:T(8,128)(2,1)S(1)}, u32[]{:S(2)}, u32[]{:S(2)}) collective-permute-start(bf16[64,1024]{1,0:T(8,128)(2,1)S(1)} %maximum_maximum_fusion), channel_id=1, source_target_pairs={{0,1},{1,0},{2,3},{3,2},{4,5},{5,4},{6,7},{7,6},{8,9},{9,8},{10,11... | collective-permute-start | bytes 393224 | tf_op jit(solution)/shard_map/ppermute | solution.py:289
  34.2 0.7 copy-start.5
  34.9 13.4 %collective-permute-start.7 = (bf16[384,1024]{1,0:T(8,128)(2,1)S(1)}, bf16[384,1024]{1,0:T(8,128)(2,1)S(1)}, u32[]{:S(2)}, u32[]{:S(2)}) collective-permute-start(bf16[384,1024]{1,0:T(8,128)(2,1)S(1)} %collective-permute-done.2.both1), channel_id=1, source_target_pairs={{0,2},{2,4},{4,6},{6,8},{8,10},{10,12},{12,14},{14,16},{16,18},{18... | collective-permute-start | bytes 2359304 | tf_op jit(solution)/shard_map/ppermute | solution.py:24
  35.0 24.7 %collective-permute-start.9 = (bf16[192,1024]{1,0:T(8,128)(2,1)}, bf16[192,1024]{1,0:T(8,128)(2,1)}, u32[]{:S(2)}, u32[]{:S(2)}) collective-permute-start(bf16[192,1024]{1,0:T(8,128)(2,1)} %copy-done.5), channel_id=1, source_target_pairs={{0,254},{2,0},{4,2},{6,4},{8,6},{10,8},{12,10},{14,12},{16,14},{18... | collective-permute-start | bytes 1179656 | tf_op jit(solution)/shard_map/ppermute | solution.py:24
  38.2 51.4 %copy-start.3 = (bf16[384,1024]{1,0:T(8,128)(2,1)S(1)}, bf16[384,1024]{1,0:T(8,128)(2,1)}, u32[]{:S(2)}) copy-start(bf16[384,1024]{1,0:T(8,128)(2,1)} %get-tuple-element.29.both0.both_ref) | copy-start | bytes 2359300
  42.3 26.6 %collective-permute-start.6 = (bf16[192,1024]{1,0:T(8,128)(2,1)S(1)}, bf16[192,1024]{1,0:T(8,128)(2,1)S(1)}, u32[]{:S(2)}, u32[]{:S(2)}) collective-permute-start(bf16[192,1024]{1,0:T(8,128)(2,1)S(1)} %convolution_convert_fusion.do_ref.d0), channel_id=1, source_target_pairs={{0,254},{2,0},{4,2},{6,4},{8,6},{10,8},{12,10},{14,12},{16,14},{18... | collective-permute-start | bytes 1179656 | tf_op jit(solution)/shard_map/ppermute | solution.py:24
  48.3 32.4 %collective-permute-start.8 = (bf16[384,1024]{1,0:T(8,128)(2,1)S(1)}, bf16[384,1024]{1,0:T(8,128)(2,1)}, u32[]{:S(2)}, u32[]{:S(2)}) collective-permute-start(bf16[384,1024]{1,0:T(8,128)(2,1)S(1)} %collective-permute-done.7.both2), channel_id=1, source_target_pairs={{0,2},{2,4},{4,6},{6,8},{8,10},{10,12},{12,14},{14,16},{16,18},{18... | collective-permute-start | bytes 2359304 | tf_op jit(solution)/shard_map/ppermute | solution.py:24
  48.3 19.7 %all-to-all-start = ((f32[8,32,128]{2,1,0:T(8,128)}), f32[8,32,128]{2,1,0:T(8,128)}, u32[]{:S(2)}, u32[]{:S(2)}) async-start(f32[8,32,128]{2,1,0:T(8,128)} %get-tuple-element.30), calls=%async_computation | async-start | bytes 262144 | tf_op jit(solution)/shard_map/all_to_all | solution.py:298
  59.7 21.0 %collective-permute-start.10 = (bf16[192,1024]{1,0:T(8,128)(2,1)}, bf16[192,1024]{1,0:T(8,128)(2,1)}, u32[]{:S(2)}, u32[]{:S(2)}) collective-permute-start(bf16[192,1024]{1,0:T(8,128)(2,1)} %collective-permute-done.9.q2), channel_id=1, source_target_pairs={{0,254},{2,0},{4,2},{6,4},{8,6},{10,8},{12,10},{14,12},{16,14},{18... | collective-permute-start | bytes 1179656 | tf_op jit(solution)/shard_map/ppermute | solution.py:24
  68.9 19.1 %copy-start.7 = (bf16[192,1024]{1,0:T(8,128)(2,1)}, bf16[192,1024]{1,0:T(8,128)(2,1)S(1)}, u32[]{:S(2)}) copy-start(bf16[192,1024]{1,0:T(8,128)(2,1)S(1)} %collective-permute-done.6.d1) | copy-start | bytes 1179652
  68.9 11.8 %collective-permute-start.11 = (bf16[192,1024]{1,0:T(8,128)(2,1)S(1)}, bf16[192,1024]{1,0:T(8,128)(2,1)}, u32[]{:S(2)}, u32[]{:S(2)}) collective-permute-start(bf16[192,1024]{1,0:T(8,128)(2,1)S(1)} %collective-permute-done.6.d1), channel_id=1, source_target_pairs={{0,254},{2,0},{4,2},{6,4},{8,6},{10,8},{12,10},{14,12},{16,14},{18... | collective-permute-start | bytes 1179656 | tf_op jit(solution)/shard_map/ppermute | solution.py:24
  74.5 13.6 %all-to-all-start.1 = ((f32[16,32,128]{2,1,0:T(8,128)}), f32[16,32,128]{2,1,0:T(8,128)}, u32[]{:S(2)}, u32[]{:S(2)}) async-start(f32[16,32,128]{2,1,0:T(8,128)} %broadcast_in_dim.9), calls=%async_computation.1 | async-start | bytes 524288 | tf_op jit(solution)/shard_map/all_to_all | solution.py:304
  80.7 26.2 %collective-permute-start.12 = (bf16[192,1024]{1,0:T(8,128)(2,1)}, bf16[192,1024]{1,0:T(8,128)(2,1)}, u32[]{:S(2)}, u32[]{:S(2)}) collective-permute-start(bf16[192,1024]{1,0:T(8,128)(2,1)} %collective-permute-done.11.d2), channel_id=1, source_target_pairs={{0,254},{2,0},{4,2},{6,4},{8,6},{10,8},{12,10},{14,12},{16,14},{18... | collective-permute-start | bytes 1179656 | tf_op jit(solution)/shard_map/ppermute | solution.py:24
  89.6 17.3 %copy-start.9 = (f32[32,128]{1,0:T(8,128)S(1)}, f32[32,128]{1,0:T(8,128)}, u32[]{:S(2)}) copy-start(f32[32,128]{1,0:T(8,128)} %reduce_sum.19) | copy-start | bytes 49156
  89.6 21.4 %copy-start.6 = (bf16[192,1024]{1,0:T(8,128)(2,1)S(1)}, bf16[192,1024]{1,0:T(8,128)(2,1)}, u32[]{:S(2)}) copy-start(bf16[192,1024]{1,0:T(8,128)(2,1)} %copy-done.5) | copy-start | bytes 1179652
  96.5 7.5 %collective-permute-start.13 = (f32[16,192]{1,0:T(8,128)S(1)}, f32[16,192]{1,0:T(8,128)S(1)}, u32[]{:S(2)}, u32[]{:S(2)}) collective-permute-start(f32[16,192]{1,0:T(8,128)S(1)} %get-tuple-element.41.s0), channel_id=1, source_target_pairs={{0,254},{2,0},{4,2},{6,4},{8,6},{10,8},{12,10},{14,12},{16,14},{18... | collective-permute-start | bytes 36872 | tf_op jit(solution)/shard_map/ppermute | solution.py:24
  97.6 6.4 %collective-permute-start.14 = (f32[16,192]{1,0:T(8,128)S(1)}, f32[16,192]{1,0:T(8,128)S(1)}, u32[]{:S(2)}, u32[]{:S(2)}) collective-permute-start(f32[16,192]{1,0:T(8,128)S(1)} %get-tuple-element.41.s0), channel_id=1, source_target_pairs={{0,252},{2,254},{4,0},{6,2},{8,4},{10,6},{12,8},{14,10},{16,12},{1... | collective-permute-start | bytes 36872 | tf_op jit(solution)/shard_map/ppermute | solution.py:24
  102.3 4.7 %collective-permute-start.15 = (f32[16,192]{1,0:T(8,128)S(1)}, f32[16,192]{1,0:T(8,128)S(1)}, u32[]{:S(2)}, u32[]{:S(2)}) collective-permute-start(f32[16,192]{1,0:T(8,128)S(1)} %get-tuple-element.41.s0), channel_id=1, source_target_pairs={{0,250},{2,252},{4,254},{6,0},{8,2},{10,4},{12,6},{14,8},{16,10},{... | collective-permute-start | bytes 36872 | tf_op jit(solution)/shard_map/ppermute | solution.py:24
  107.6 12.6 %all-to-all-start.2 = ((f32[8,32,128]{2,1,0:T(8,128)}), f32[8,32,128]{2,1,0:T(8,128)S(1)}, u32[]{:S(2)}, u32[]{:S(2)}) async-start(f32[8,32,128]{2,1,0:T(8,128)} %broadcast_in_dim.11), calls=%async_computation.2 | async-start | bytes 262144 | tf_op jit(solution)/shard_map/all_to_all | solution.py:313
  111.0 1.0 copy-start.8

commit v9 on v8

--- a/solution.py
+++ b/solution.py
@@ -22,6 +22,11 @@
 def rotated(part, by):
     count = lax.axis_size(CTX)
     return lax.ppermute(part, CTX, [(i, (i + by) % count) for i in range(count)])
+
+
+def exchanged(part, by):
+    count = lax.axis_size(CTX)
+    return part + lax.ppermute(part, CTX, [(i, i ^ by) for i in range(count)])
 
 
 def swapped(part, first):
@@ -96,8 +101,8 @@
         grad = gpad[EDGE : EDGE + block]
         for tap in range(taps_count):
             prod = grad * cpad[pl.ds(EDGE - taps_count // 2 + tap, block), :]
-            rows_ref[column, tap : tap + 1, :] = jnp.sum(prod, axis=0, keepdims=True)
-        rows_ref[column, taps_count:, :] = jnp.zeros_like(rows_ref[column, taps_count:, :])
+            rows_ref[tap : tap + 1, lanes] = jnp.sum(prod, axis=0, keepdims=True)
+        rows_ref[taps_count:, lanes] = jnp.zeros_like(rows_ref[taps_count:, lanes])
 
 
 def conv(device, grad, inputs, inside, across, taps, last):
@@ -109,7 +114,7 @@
         out_specs=[INSIDE] * 2,
         out_shape=[
             jax.ShapeDtypeStruct((block, width), jnp.bfloat16),
-            jax.ShapeDtypeStruct((width // HEAD, 8 * pl.cdiv(count, 8), HEAD), jnp.float32),
+            jax.ShapeDtypeStruct((8 * pl.cdiv(count, 8), width), jnp.float32),
         ],
         scratch_shapes=[pltpu.VMEM((block + 2 * EDGE, HEAD), jnp.float32)] * 2,
         compiler_params=pltpu.CompilerParams(vmem_limit_bytes=VMEM_BYTES),
@@ -150,6 +155,7 @@
 
 def project(tp, own, other, weight):
     full = jnp.where(tp == 0, jnp.concatenate([own, other], axis=1), jnp.concatenate([other, own], axis=1))
+    full = lax.optimization_barrier(full)
     return lax.dot_general(full, weight, NT, preferred_element_type=jnp.float32).astype(jnp.bfloat16)
 
 
@@ -286,34 +292,35 @@
 
     taps_count = conv_weight.shape[0]
     padding = jnp.zeros((2 * EDGE - taps_count, conv_weight.shape[1]), conv_weight.dtype)
-    edges = lax.ppermute(jnp.concatenate([inside[EDGE:], across[EDGE:], conv_weight, padding], axis=0), "tp", pair)
+    edges = jnp.concatenate([inside[EDGE:], across[EDGE:], conv_weight, padding], axis=0)
+    (edges,) = after((edges,), (other,))
+    edges = lax.ppermute(edges, "tp", pair)
     grad_stream, tap_rows = conv(device, stream_grad, conv_input, inside, across, conv_weight, last)
-    other, edges, sent = after((other, edges, kv1), (q1, grad_stream))
+    tap_rows = exchanged(exchanged(tap_rows, 1), 2)
+    other, edges, sent = after((other, edges, kv1), (q1, tap_rows))
     kv2 = rotated(sent, 1)
+    tap_rows = exchanged(tap_rows, 4)
     out_grad = project(tp, grad_stream, conv_other(device, other, edges, taps_count, last), out_weight)
     (sent,) = after((kv2,), (out_grad, q1))
     kv3 = rotated(sent, 1)
 
-    (tap_rows,) = after((tap_rows,), (kv1,))
-    tap_sums = jnp.sum(lax.all_to_all(tap_rows, "z", 0, 0, tiled=True), axis=0)
-    d1 = rotated(out_grad, -1)
-    (sent,) = after((d1,), (kv2, q2, tap_sums))
+    (sent,) = after((out_grad,), (tap_rows,))
+    d1 = rotated(sent, -1)
+    tap_rows = exchanged(tap_rows, 8)
+    (sent,) = after((d1,), (kv2, q2, tap_rows))
     d2 = rotated(sent, -1)
-    copies = jnp.broadcast_to(tap_sums, (lax.axis_size("near"),) + tap_sums.shape)
-    (copies,) = after((copies,), (d1,))
-    tap_sums = jnp.sum(lax.all_to_all(copies, "near", 0, 0, tiled=True), axis=0)
-    (sent,) = after((d2,), (kv3, q3))
+    tap_rows = exchanged(tap_rows, 16)
+    (sent,) = after((d2,), (q3, tap_rows))
     d3 = rotated(sent, -1)
-
-    (near,) = after((queries,), (tap_sums,))
-    query_grad, stats = query_side(device, near, out_grad, (kv3, kv2, kv1, kv0), scale)
+    tap_rows = exchanged(tap_rows, 32)
+
+    query_grad, stats = query_side(device, queries, out_grad, (kv3, kv2, kv1, kv0), scale)
+    (stats,) = after((stats,), (tap_rows,))
     all_stats = [stats] + [rotated(stats, -hop) for hop in (1, 2, 3)]
-    copies = jnp.broadcast_to(tap_sums, (lax.axis_size("z"),) + tap_sums.shape)
-    (copies,) = after((copies,), (*all_stats[1:], d3))
-    tap_sums = lax.all_to_all(copies, "z", 0, 0, tiled=True)
+    (tap_rows,) = after((tap_rows,), (*all_stats[1:], d3))
+    tap_rows = exchanged(tap_rows, 64)
     key_grad, value_grad = key_side(device, kv0, (queries, q1, q2, q3), (out_grad, d1, d2, d3), all_stats, scale, last)
-    rows = jnp.transpose(tap_sums, (1, 0, 2)).reshape(tap_sums.shape[1], -1)[:taps_count]
-    kernel_grad = rows / math.sqrt(block * (last + 1))
+    kernel_grad = tap_rows[:taps_count] / math.sqrt(block * (last + 1))
     return (query_grad, key_grad, value_grad, grad_stream, kernel_grad)
 
 

time: 122 us -> 120 us (0.984)
  starting transfers between devices: 55.9 us -> 62.5 us
  local copies, waits for them, and re-layouts: 4.01 us -> 0.11 us
  Pallas kernels: 21.3 us -> 18.6 us
  other arithmetic: 2.6 us -> 1.13 us
    all_to_all x3 -> x0, starting transfers between devices: 20.9 us -> none  [the longest x1 11.3 us: per_device(): tap_sums = jnp.sum(lax.all_to_all(tap_rows, 'z', 0, 0, tiled=True), axis=0)]
    ppermute x1 -> x8, starting transfers between devices: 0.66 us -> 19.9 us  [the longest x7 16.9 us: exchanged(): return part + lax.ppermute(part, CTX, [(i, i ^ by) for i in range(count)])]
    all_to_all x3 -> x0, waiting for transfers between devices: 13.6 us -> none  [the longest x1 6.7 us: per_device(): tap_sums = jnp.sum(lax.all_to_all(copies, 'near', 0, 0, tiled=True), axis=0)]
    ppermute x1 -> x8, waiting for transfers between devices: 13.8 us -> 23.3 us  [the longest x7 23 us: exchanged(): return part + lax.ppermute(part, CTX, [(i, i ^ by) for i in range(count)])]
    ppermute x12, starting transfers between devices: 26.9 us -> 35.2 us  [rotated(): lax.ppermute(part, CTX, [(i, (i + by) % count) for i in range(count)])]
    ppermute x12, waiting for transfers between devices: 2.89 us -> 6.04 us  [rotated(): lax.ppermute(part, CTX, [(i, (i + by) % count) for i in range(count)])]
    reduce_sum x2 -> x0, other arithmetic: 2.5 us -> none  [the longest x1 1.58 us: per_device(): tap_sums = jnp.sum(lax.all_to_all(copies, 'near', 0, 0, tiled=True), axis=0)]
    unnamed x22 -> x12, local copies, waits for them, and re-layouts: 2.45 us -> 0.02 us
  transfers between devices with their start and end apart: 19 -> 23, of which waited for: 6 -> 13; matrix products, arithmetic and copies ran while one was open for 6% -> 4% of each run, Pallas kernels for 16% -> 14%
where the time goes in v9:
time: 120 us
  starting transfers between devices  62.5 us (52%)
  waiting for transfers between devices  33 us (28%)
  Pallas kernels  18.6 us (16%)
  matrix products  3.82 us (3%)
    ppermute x12, starting transfers between devices, rotated(): lax.ppermute(part, CTX, [(i, (i + by) % count) for i in range(count)])  35.2 us
    ppermute x7, waiting for transfers between devices, exchanged(): return part + lax.ppermute(part, CTX, [(i, i ^ by) for i in range(count)])  23 us
    ppermute x7, starting transfers between devices, exchanged(): return part + lax.ppermute(part, CTX, [(i, i ^ by) for i in range(count)])  16.9 us
    ppermute x12, waiting for transfers between devices, rotated(): lax.ppermute(part, CTX, [(i, (i + by) % count) for i in range(count)])  6.04 us
    pallas_call x1, Pallas kernels, query_side(): pl.pallas_call(functools.partial(query_kernel, scale), in_specs=[pl.Block...  5.72 us
    ppermute x2, starting transfers between devices, swapped(): lax.ppermute(part, CTX, [(i, partner(i) if 0 <= partner(i) < count and i...  4.51 us
    pallas_call x1, Pallas kernels, conv(): pl.pallas_call(functools.partial(conv_kernel, last), in_specs=[pl.BlockSp...  4.42 us
    pallas_call x1, Pallas kernels, key_side(): pl.pallas_call(functools.partial(key_kernel, scale, last), in_specs=[pl.B...  4.37 us
  transfers between devices with their start and end apart: 23, of which 13 were waited for; matrix products, arithmetic and copies ran while one was open for 4% of the time, Pallas kernels for 14%

profile of v9, /device:TPU:1, one launch (start us, length us, event | category | flops | bytes accessed | tf_op | source)
XLA Modules:
  0.0 119.9 jit_solution(14097257409635405854)
XLA Ops:
  0.7 2.2 %shard_map.110 = (bf16[384,1024]{1,0:T(8,128)(2,1)}, bf16[32,1024]{1,0:T(8,128)(2,1)}, bf16[32,1024]{1,0:T(8,128)(2,1)}) custom-call(s32[1]{0:T(128)} %bitcast.idx_ref, bf16[192,1024]{1,0:T(8,128)(2,1)} %k_ref.1, bf16[192,1024]{1,0:T(8,128)(2,1)} %v_ref.1, bf16[192,1024]{1,0:T(8,128)(2,1)} %input_ref.3, bf16[192,1024]{1,0:T(8,128)(2,1)} %grad_ref.3), custom_call_target="tpu_custom_call" | custom-call | tf_op jit(solution)/shard_map/pallas_call | solution.py:60
  2.9 4.5 %collective-permute-start.1 = (bf16[32,1024]{1,0:T(8,128)(2,1)}, bf16[32,1024]{1,0:T(8,128)(2,1)S(1)}, u32[]{:S(2)}, u32[]{:S(2)}) collective-permute-start(bf16[32,1024]{1,0:T(8,128)(2,1)} %get-tuple-element.26), channel_id=1, source_target_pairs={{0,0},{2,4},{4,2},{6,8},{8,6},{10,12},{12,10},{14,16},{16,14},{18,... | collective-permute-start | bytes 196616 | tf_op jit(solution)/shard_map/ppermute | solution.py:35
  7.4 2.1 %collective-permute-done.1.across_ref = bf16[32,1024]{1,0:T(8,128)(2,1)S(1)} collective-permute-done((bf16[32,1024]{1,0:T(8,128)(2,1)}, bf16[32,1024]{1,0:T(8,128)(2,1)S(1)}, u32[]{:S(2)}, u32[]{:S(2)}) %collective-permute-start.1) | collective-permute-done | bytes 65568 | tf_op jit(solution)/shard_map/ppermute | solution.py:35
  9.5 1.7 %collective-permute-start.4 = (bf16[384,1024]{1,0:T(8,128)(2,1)}, bf16[384,1024]{1,0:T(8,128)(2,1)S(1)}, u32[]{:S(2)}, u32[]{:S(2)}) collective-permute-start(bf16[384,1024]{1,0:T(8,128)(2,1)} %get-tuple-element.30.both0.both_ref), channel_id=1, source_target_pairs={{0,2},{2,4},{4,6},{6,8},{8,10},{10,12},{12,14},{14,16},{16,18},{18... | collective-permute-start | bytes 2359304 | tf_op jit(solution)/shard_map/ppermute | solution.py:24
  11.3 2.9 %collective-permute-start.2 = (bf16[192,1024]{1,0:T(8,128)(2,1)S(1)}, bf16[192,1024]{1,0:T(8,128)(2,1)S(1)}, u32[]{:S(2)}, u32[]{:S(2)}) collective-permute-start(bf16[192,1024]{1,0:T(8,128)(2,1)S(1)} %copy-done.1), channel_id=1, source_target_pairs={{0,1},{1,0},{2,3},{3,2},{4,5},{5,4},{6,7},{7,6},{8,9},{9,8},{10,11... | collective-permute-start | bytes 1179656 | tf_op jit(solution)/shard_map/ppermute | solution.py:287
  14.2 4.4 %shard_map.111 = (bf16[192,1024]{1,0:T(8,128)(2,1)}, f32[32,1024]{1,0:T(8,128)S(1)}) custom-call(s32[1]{0:T(128)} %bitcast.idx_ref, bf16[192,1024]{1,0:T(8,128)(2,1)S(1)} %copy-done.1, bf16[192,1024]{1,0:T(8,128)(2,1)S(1)} %copy-done, bf16[32,1024]{1,0:T(8,128)(2,1)S(1)} %collective-permute-done.inside_ref, ...), custom_call_target="tpu_custom_call" | custom-call | flops 196608 | bytes 12288 | tf_op jit(solution)/shard_map/pallas_call | solution.py:111
  20.4 1.3 %collective-permute-start.7 = (f32[32,1024]{1,0:T(8,128)S(1)}, f32[32,1024]{1,0:T(8,128)S(1)}, u32[]{:S(2)}, u32[]{:S(2)}) collective-permute-start(f32[32,1024]{1,0:T(8,128)S(1)} %add.25), channel_id=1, source_target_pairs={{0,4},{2,6},{4,0},{6,2},{8,12},{10,14},{12,8},{14,10},{16,20},{18,... | collective-permute-start | bytes 393224 | tf_op jit(solution)/shard_map/ppermute | solution.py:29
  21.8 4.1 %collective-permute-done.7 = f32[32,1024]{1,0:T(8,128)S(1)} collective-permute-done((f32[32,1024]{1,0:T(8,128)S(1)}, f32[32,1024]{1,0:T(8,128)S(1)}, u32[]{:S(2)}, u32[]{:S(2)}) %collective-permute-start.7) | collective-permute-done | bytes 131104 | tf_op jit(solution)/shard_map/ppermute | solution.py:29
  26.0 3.9 %collective-permute-start.12 = (f32[32,1024]{1,0:T(8,128)S(1)}, f32[32,1024]{1,0:T(8,128)S(1)}, u32[]{:S(2)}, u32[]{:S(2)}) collective-permute-start(f32[32,1024]{1,0:T(8,128)S(1)} %add.26), channel_id=1, source_target_pairs={{0,8},{2,10},{4,12},{6,14},{8,0},{10,2},{12,4},{14,6},{16,24},{18,... | collective-permute-start | bytes 393224 | tf_op jit(solution)/shard_map/ppermute | solution.py:29
  29.8 1.5 %collective-permute-done.2.grad_ref = bf16[192,1024]{1,0:T(8,128)(2,1)S(1)} collective-permute-done((bf16[192,1024]{1,0:T(8,128)(2,1)S(1)}, bf16[192,1024]{1,0:T(8,128)(2,1)S(1)}, u32[]{:S(2)}, u32[]{:S(2)}) %collective-permute-start.2) | collective-permute-done | bytes 393248 | tf_op jit(solution)/shard_map/ppermute | solution.py:287
  31.4 2.9 %collective-permute-start.3 = (bf16[64,1024]{1,0:T(8,128)(2,1)S(1)}, bf16[64,1024]{1,0:T(8,128)(2,1)S(1)}, u32[]{:S(2)}, u32[]{:S(2)}) collective-permute-start(bf16[64,1024]{1,0:T(8,128)(2,1)S(1)} %maximum_maximum_fusion), channel_id=1, source_target_pairs={{0,1},{1,0},{2,3},{3,2},{4,5},{5,4},{6,7},{7,6},{8,9},{9,8},{10,11... | collective-permute-start | bytes 393224 | tf_op jit(solution)/shard_map/ppermute | solution.py:297
  34.3 2.4 %collective-permute-start.10 = (bf16[192,1024]{1,0:T(8,128)(2,1)S(1)}, bf16[192,1024]{1,0:T(8,128)(2,1)S(1)}, u32[]{:S(2)}, u32[]{:S(2)}) collective-permute-start(bf16[192,1024]{1,0:T(8,128)(2,1)S(1)} %collective-permute-done.5.q1), channel_id=1, source_target_pairs={{0,254},{2,0},{4,2},{6,4},{8,6},{10,8},{12,10},{14,12},{16,14},{18... | collective-permute-start | bytes 1179656 | tf_op jit(solution)/shard_map/ppermute | solution.py:24
  37.0 3.5 %collective-permute-start.8 = (bf16[384,1024]{1,0:T(8,128)(2,1)S(1)}, bf16[384,1024]{1,0:T(8,128)(2,1)S(1)}, u32[]{:S(2)}, u32[]{:S(2)}) collective-permute-start(bf16[384,1024]{1,0:T(8,128)(2,1)S(1)} %collective-permute-done.4.both1), channel_id=1, source_target_pairs={{0,2},{2,4},{4,6},{6,8},{8,10},{10,12},{12,14},{14,16},{16,18},{18... | collective-permute-start | bytes 2359304 | tf_op jit(solution)/shard_map/ppermute | solution.py:24
  40.5 1.9 %shard_map.112 = bf16[192,1024]{1,0:T(8,128)(2,1)S(1)} custom-call(s32[1]{0:T(128)} %bitcast.idx_ref, bf16[192,1024]{1,0:T(8,128)(2,1)S(1)} %collective-permute-done.2.grad_ref, bf16[64,1024]{1,0:T(8,128)(2,1)S(1)} %collective-permute-done.3.edges_ref), custom_call_target="tpu_custom_call" | custom-call | flops 196608 | bytes 12288 | tf_op jit(solution)/shard_map/pallas_call | solution.py:145
  42.7 3.8 %convolution_convert_fusion.do_ref.d0 = bf16[192,1024]{1,0:T(8,128)(2,1)S(1)} fusion(bf16[192,2048]{1,0:T(8,128)(2,1)S(1)} %maximum_select_fusion, bf16[1024,2048]{1,0:T(8,128)(2,1)} %param.13), kind=kOutput, calls=%fused_computation | convolution fusion | flops 805502976 | bytes 5373952 | tf_op jit(solution)/shard_map/dot_general | solution.py:159
  46.6 1.5 %collective-permute-start.13 = (bf16[192,1024]{1,0:T(8,128)(2,1)S(1)}, bf16[192,1024]{1,0:T(8,128)(2,1)S(1)}, u32[]{:S(2)}, u32[]{:S(2)}) collective-permute-start(bf16[192,1024]{1,0:T(8,128)(2,1)S(1)} %convolution_convert_fusion.do_ref.d0), channel_id=1, source_target_pairs={{0,254},{2,0},{4,2},{6,4},{8,6},{10,8},{12,10},{14,12},{16,14},{18... | collective-permute-start | bytes 1179656 | tf_op jit(solution)/shard_map/ppermute | solution.py:24
  48.1 1.4 %collective-permute-done.8.both2 = bf16[384,1024]{1,0:T(8,128)(2,1)S(1)} collective-permute-done((bf16[384,1024]{1,0:T(8,128)(2,1)S(1)}, bf16[384,1024]{1,0:T(8,128)(2,1)S(1)}, u32[]{:S(2)}, u32[]{:S(2)}) %collective-permute-start.8) | collective-permute-done | bytes 786464 | tf_op jit(solution)/shard_map/ppermute | solution.py:24
  49.5 2.5 %collective-permute-start.9 = (bf16[384,1024]{1,0:T(8,128)(2,1)S(1)}, bf16[384,1024]{1,0:T(8,128)(2,1)S(1)}, u32[]{:S(2)}, u32[]{:S(2)}) collective-permute-start(bf16[384,1024]{1,0:T(8,128)(2,1)S(1)} %collective-permute-done.8.both2), channel_id=1, source_target_pairs={{0,2},{2,4},{4,6},{6,8},{8,10},{10,12},{12,14},{14,16},{16,18},{18... | collective-permute-start | bytes 2359304 | tf_op jit(solution)/shard_map/ppermute | solution.py:24
  51.9 2.1 %collective-permute-start.14 = (f32[32,1024]{1,0:T(8,128)S(1)}, f32[32,1024]{1,0:T(8,128)S(1)}, u32[]{:S(2)}, u32[]{:S(2)}) collective-permute-start(f32[32,1024]{1,0:T(8,128)S(1)} %add.27), channel_id=1, source_target_pairs={{0,16},{2,18},{4,20},{6,22},{8,24},{10,26},{12,28},{14,30},{16,0},... | collective-permute-start | bytes 393224 | tf_op jit(solution)/shard_map/ppermute | solution.py:29
  54.0 4.3 %collective-permute-done.14 = f32[32,1024]{1,0:T(8,128)S(1)} collective-permute-done((f32[32,1024]{1,0:T(8,128)S(1)}, f32[32,1024]{1,0:T(8,128)S(1)}, u32[]{:S(2)}, u32[]{:S(2)}) %collective-permute-start.14) | collective-permute-done | bytes 131104 | tf_op jit(solution)/shard_map/ppermute | solution.py:29
  58.4 4.4 %collective-permute-start.11 = (bf16[192,1024]{1,0:T(8,128)(2,1)S(1)}, bf16[192,1024]{1,0:T(8,128)(2,1)S(1)}, u32[]{:S(2)}, u32[]{:S(2)}) collective-permute-start(bf16[192,1024]{1,0:T(8,128)(2,1)S(1)} %collective-permute-done.10.q2), channel_id=1, source_target_pairs={{0,254},{2,0},{4,2},{6,4},{8,6},{10,8},{12,10},{14,12},{16,14},{18... | collective-permute-start | bytes 1179656 | tf_op jit(solution)/shard_map/ppermute | solution.py:24
  62.8 5.9 %collective-permute-start.15 = (bf16[192,1024]{1,0:T(8,128)(2,1)S(1)}, bf16[192,1024]{1,0:T(8,128)(2,1)S(1)}, u32[]{:S(2)}, u32[]{:S(2)}) collective-permute-start(bf16[192,1024]{1,0:T(8,128)(2,1)S(1)} %collective-permute-done.13.d1), channel_id=1, source_target_pairs={{0,254},{2,0},{4,2},{6,4},{8,6},{10,8},{12,10},{14,12},{16,14},{18... | collective-permute-start | bytes 1179656 | tf_op jit(solution)/shard_map/ppermute | solution.py:24
  68.7 5.3 %collective-permute-done.16 = f32[32,1024]{1,0:T(8,128)S(1)} collective-permute-done((f32[32,1024]{1,0:T(8,128)S(1)}, f32[32,1024]{1,0:T(8,128)S(1)}, u32[]{:S(2)}, u32[]{:S(2)}) %collective-permute-start.16) | collective-permute-done | bytes 131104 | tf_op jit(solution)/shard_map/ppermute | solution.py:29
  74.0 6.8 %collective-permute-start.17 = (bf16[192,1024]{1,0:T(8,128)(2,1)S(1)}, bf16[192,1024]{1,0:T(8,128)(2,1)S(1)}, u32[]{:S(2)}, u32[]{:S(2)}) collective-permute-start(bf16[192,1024]{1,0:T(8,128)(2,1)S(1)} %collective-permute-done.15.d2), channel_id=1, source_target_pairs={{0,254},{2,0},{4,2},{6,4},{8,6},{10,8},{12,10},{14,12},{16,14},{18... | collective-permute-start | bytes 1179656 | tf_op jit(solution)/shard_map/ppermute | solution.py:24
  80.8 8.9 %collective-permute-start.18 = (f32[32,1024]{1,0:T(8,128)S(1)}, f32[32,1024]{1,0:T(8,128)S(1)}, u32[]{:S(2)}, u32[]{:S(2)}) collective-permute-start(f32[32,1024]{1,0:T(8,128)S(1)} %add.29), channel_id=1, source_target_pairs={{0,64},{2,66},{4,68},{6,70},{8,72},{10,74},{12,76},{14,78},{16,80}... | collective-permute-start | bytes 393224 | tf_op jit(solution)/shard_map/ppermute | solution.py:29
  89.7 4.1 %collective-permute-done.18 = f32[32,1024]{1,0:T(8,128)S(1)} collective-permute-done((f32[32,1024]{1,0:T(8,128)S(1)}, f32[32,1024]{1,0:T(8,128)S(1)}, u32[]{:S(2)}, u32[]{:S(2)}) %collective-permute-start.18) | collective-permute-done | bytes 131104 | tf_op jit(solution)/shard_map/ppermute | solution.py:29
  93.8 5.7 %shard_map.113 = (bf16[192,1024]{1,0:T(8,128)(2,1)}, f32[16,192]{1,0:T(8,128)S(1)}) custom-call(s32[1]{0:T(128)} %bitcast.idx_ref, bf16[192,1024]{1,0:T(8,128)(2,1)S(1)} %copy-done.4, bf16[192,1024]{1,0:T(8,128)(2,1)S(1)} %convolution_convert_fusion.do_ref.d0, bf16[384,1024]{1,0:T(8,128)(2,1)S(1)} %collective-permute-done.9.both3, ...), custom_call_target="tpu_custom_call" | custom-call | flops 1509949440 | bytes 4718592 | tf_op jit(solution)/shard_map/pallas_call | solution.py:203
  99.5 6.3 %collective-permute-start.19 = (f32[16,192]{1,0:T(8,128)S(1)}, f32[16,192]{1,0:T(8,128)S(1)}, u32[]{:S(2)}, u32[]{:S(2)}) collective-permute-start(f32[16,192]{1,0:T(8,128)S(1)} %get-tuple-element.41.s0), channel_id=1, source_target_pairs={{0,254},{2,0},{4,2},{6,4},{8,6},{10,8},{12,10},{14,12},{16,14},{18... | collective-permute-start | bytes 36872 | tf_op jit(solution)/shard_map/ppermute | solution.py:24
  106.7 1.9 %collective-permute-done.20.s2 = f32[16,192]{1,0:T(8,128)S(1)} collective-permute-done((f32[16,192]{1,0:T(8,128)S(1)}, f32[16,192]{1,0:T(8,128)S(1)}, u32[]{:S(2)}, u32[]{:S(2)}) %collective-permute-start.20) | collective-permute-done | bytes 12320 | tf_op jit(solution)/shard_map/ppermute | solution.py:24
  108.6 2.0 %collective-permute-done.21.s3 = f32[16,192]{1,0:T(8,128)S(1)} collective-permute-done((f32[16,192]{1,0:T(8,128)S(1)}, f32[16,192]{1,0:T(8,128)S(1)}, u32[]{:S(2)}, u32[]{:S(2)}) %collective-permute-start.21) | collective-permute-done | bytes 12320 | tf_op jit(solution)/shard_map/ppermute | solution.py:24
  110.5 4.4 %shard_map.114 = (bf16[192,1024]{1,0:T(8,128)(2,1)}, bf16[192,1024]{1,0:T(8,128)(2,1)}) custom-call(s32[1]{0:T(128)} %bitcast.idx_ref, bf16[384,1024]{1,0:T(8,128)(2,1)S(1)} %copy-done.3, bf16[192,1024]{1,0:T(8,128)(2,1)S(1)} %copy-done.4, bf16[192,1024]{1,0:T(8,128)(2,1)S(1)} %collective-permute-done.5.q1, ...), custom_call_target="tpu_custom_call" | custom-call | flops 1509949440 | bytes 4718592 | tf_op jit(solution)/shard_map/pallas_call | solution.py:260
  114.9 4.4 %collective-permute-done.22 = f32[32,1024]{1,0:T(8,128)S(1)} collective-permute-done((f32[32,1024]{1,0:T(8,128)S(1)}, f32[32,1024]{1,0:T(8,128)S(1)}, u32[]{:S(2)}, u32[]{:S(2)}) %collective-permute-start.22) | collective-permute-done | bytes 131104 | tf_op jit(solution)/shard_map/ppermute | solution.py:29
  (44 shorter events, 4.0 us)
Async XLA Ops:
  0.6 10.6 %copy-start.1 = (bf16[192,1024]{1,0:T(8,128)(2,1)S(1)}, bf16[192,1024]{1,0:T(8,128)(2,1)}, u32[]{:S(2)}) copy-start(bf16[192,1024]{1,0:T(8,128)(2,1)} %grad_ref.3) | copy-start | bytes 1179652
  0.6 13.6 %copy-start = (bf16[192,1024]{1,0:T(8,128)(2,1)S(1)}, bf16[192,1024]{1,0:T(8,128)(2,1)}, u32[]{:S(2)}) copy-start(bf16[192,1024]{1,0:T(8,128)(2,1)} %input_ref.3) | copy-start | bytes 1179652
  0.7 13.5 %copy-start.2 = (bf16[31,1024]{1,0:T(8,128)(2,1)S(1)}, bf16[31,1024]{1,0:T(8,128)(2,1)}, u32[]{:S(2)}) copy-start(bf16[31,1024]{1,0:T(8,128)(2,1)} %taps_ref.1) | copy-start | bytes 190468
  0.7 18.8 %copy-start.4 = (bf16[192,1024]{1,0:T(8,128)(2,1)S(1)}, bf16[192,1024]{1,0:T(8,128)(2,1)}, u32[]{:S(2)}) copy-start(bf16[192,1024]{1,0:T(8,128)(2,1)} %q0.1) | copy-start | bytes 1179652
  2.9 6.7 %collective-permute-start.1 = (bf16[32,1024]{1,0:T(8,128)(2,1)}, bf16[32,1024]{1,0:T(8,128)(2,1)S(1)}, u32[]{:S(2)}, u32[]{:S(2)}) collective-permute-start(bf16[32,1024]{1,0:T(8,128)(2,1)} %get-tuple-element.26), channel_id=1, source_target_pairs={{0,0},{2,4},{4,2},{6,8},{8,6},{10,12},{12,10},{14,16},{16,14},{18,... | collective-permute-start | bytes 196616 | tf_op jit(solution)/shard_map/ppermute | solution.py:35
  9.5 27.5 %collective-permute-start.4 = (bf16[384,1024]{1,0:T(8,128)(2,1)}, bf16[384,1024]{1,0:T(8,128)(2,1)S(1)}, u32[]{:S(2)}, u32[]{:S(2)}) collective-permute-start(bf16[384,1024]{1,0:T(8,128)(2,1)} %get-tuple-element.30.both0.both_ref), channel_id=1, source_target_pairs={{0,2},{2,4},{4,6},{6,8},{8,10},{10,12},{12,14},{14,16},{16,18},{18... | collective-permute-start | bytes 2359304 | tf_op jit(solution)/shard_map/ppermute | solution.py:24
  11.3 2.9 %collective-permute-start = (bf16[32,1024]{1,0:T(8,128)(2,1)}, bf16[32,1024]{1,0:T(8,128)(2,1)S(1)}, u32[]{:S(2)}, u32[]{:S(2)}) collective-permute-start(bf16[32,1024]{1,0:T(8,128)(2,1)} %get-tuple-element.25), channel_id=1, source_target_pairs={{0,2},{2,0},{4,6},{6,4},{8,10},{10,8},{12,14},{14,12},{16,18},{18,... | collective-permute-start | bytes 196616 | tf_op jit(solution)/shard_map/ppermute | solution.py:35
  11.3 20.1 %collective-permute-start.2 = (bf16[192,1024]{1,0:T(8,128)(2,1)S(1)}, bf16[192,1024]{1,0:T(8,128)(2,1)S(1)}, u32[]{:S(2)}, u32[]{:S(2)}) collective-permute-start(bf16[192,1024]{1,0:T(8,128)(2,1)S(1)} %copy-done.1), channel_id=1, source_target_pairs={{0,1},{1,0},{2,3},{3,2},{4,5},{5,4},{6,7},{7,6},{8,9},{9,8},{10,11... | collective-permute-start | bytes 1179656 | tf_op jit(solution)/shard_map/ppermute | solution.py:287
  18.6 23.8 %copy-start.5 = (bf16[192,1024]{1,0:T(8,128)(2,1)S(1)}, bf16[192,1024]{1,0:T(8,128)(2,1)}, u32[]{:S(2)}) copy-start(bf16[192,1024]{1,0:T(8,128)(2,1)} %get-tuple-element.23) | copy-start | bytes 1179652
  18.6 1.8 %collective-permute-start.6 = (f32[32,1024]{1,0:T(8,128)S(1)}, f32[32,1024]{1,0:T(8,128)S(1)}, u32[]{:S(2)}, u32[]{:S(2)}) collective-permute-start(f32[32,1024]{1,0:T(8,128)S(1)} %get-tuple-element.31), channel_id=1, source_target_pairs={{0,2},{2,0},{4,6},{6,4},{8,10},{10,8},{12,14},{14,12},{16,18},{18,... | collective-permute-start | bytes 393224 | tf_op jit(solution)/shard_map/ppermute | solution.py:29
  19.4 14.9 %collective-permute-start.5 = (bf16[192,1024]{1,0:T(8,128)(2,1)S(1)}, bf16[192,1024]{1,0:T(8,128)(2,1)S(1)}, u32[]{:S(2)}, u32[]{:S(2)}) collective-permute-start(bf16[192,1024]{1,0:T(8,128)(2,1)S(1)} %copy-done.4), channel_id=1, source_target_pairs={{0,254},{2,0},{4,2},{6,4},{8,6},{10,8},{12,10},{14,12},{16,14},{18... | collective-permute-start | bytes 1179656 | tf_op jit(solution)/shard_map/ppermute | solution.py:24
  20.4 5.5 %collective-permute-start.7 = (f32[32,1024]{1,0:T(8,128)S(1)}, f32[32,1024]{1,0:T(8,128)S(1)}, u32[]{:S(2)}, u32[]{:S(2)}) collective-permute-start(f32[32,1024]{1,0:T(8,128)S(1)} %add.25), channel_id=1, source_target_pairs={{0,4},{2,6},{4,0},{6,2},{8,12},{10,14},{12,8},{14,10},{16,20},{18,... | collective-permute-start | bytes 393224 | tf_op jit(solution)/shard_map/ppermute | solution.py:29
  26.0 10.7 %collective-permute-start.12 = (f32[32,1024]{1,0:T(8,128)S(1)}, f32[32,1024]{1,0:T(8,128)S(1)}, u32[]{:S(2)}, u32[]{:S(2)}) collective-permute-start(f32[32,1024]{1,0:T(8,128)S(1)} %add.26), channel_id=1, source_target_pairs={{0,8},{2,10},{4,12},{6,14},{8,0},{10,2},{12,4},{14,6},{16,24},{18,... | collective-permute-start | bytes 393224 | tf_op jit(solution)/shard_map/ppermute | solution.py:29
  31.4 5.6 %collective-permute-start.3 = (bf16[64,1024]{1,0:T(8,128)(2,1)S(1)}, bf16[64,1024]{1,0:T(8,128)(2,1)S(1)}, u32[]{:S(2)}, u32[]{:S(2)}) collective-permute-start(bf16[64,1024]{1,0:T(8,128)(2,1)S(1)} %maximum_maximum_fusion), channel_id=1, source_target_pairs={{0,1},{1,0},{2,3},{3,2},{4,5},{5,4},{6,7},{7,6},{8,9},{9,8},{10,11... | collective-permute-start | bytes 393224 | tf_op jit(solution)/shard_map/ppermute | solution.py:297
  34.3 24.1 %collective-permute-start.10 = (bf16[192,1024]{1,0:T(8,128)(2,1)S(1)}, bf16[192,1024]{1,0:T(8,128)(2,1)S(1)}, u32[]{:S(2)}, u32[]{:S(2)}) collective-permute-start(bf16[192,1024]{1,0:T(8,128)(2,1)S(1)} %collective-permute-done.5.q1), channel_id=1, source_target_pairs={{0,254},{2,0},{4,2},{6,4},{8,6},{10,8},{12,10},{14,12},{16,14},{18... | collective-permute-start | bytes 1179656 | tf_op jit(solution)/shard_map/ppermute | solution.py:24
  37.0 12.5 %collective-permute-start.8 = (bf16[384,1024]{1,0:T(8,128)(2,1)S(1)}, bf16[384,1024]{1,0:T(8,128)(2,1)S(1)}, u32[]{:S(2)}, u32[]{:S(2)}) collective-permute-start(bf16[384,1024]{1,0:T(8,128)(2,1)S(1)} %collective-permute-done.4.both1), channel_id=1, source_target_pairs={{0,2},{2,4},{4,6},{6,8},{8,10},{10,12},{12,14},{14,16},{16,18},{18... | collective-permute-start | bytes 2359304 | tf_op jit(solution)/shard_map/ppermute | solution.py:24
  42.7 51.1 %copy-start.3 = (bf16[384,1024]{1,0:T(8,128)(2,1)S(1)}, bf16[384,1024]{1,0:T(8,128)(2,1)}, u32[]{:S(2)}) copy-start(bf16[384,1024]{1,0:T(8,128)(2,1)} %get-tuple-element.30.both0.both_ref) | copy-start | bytes 2359300
  46.6 16.2 %collective-permute-start.13 = (bf16[192,1024]{1,0:T(8,128)(2,1)S(1)}, bf16[192,1024]{1,0:T(8,128)(2,1)S(1)}, u32[]{:S(2)}, u32[]{:S(2)}) collective-permute-start(bf16[192,1024]{1,0:T(8,128)(2,1)S(1)} %convolution_convert_fusion.do_ref.d0), channel_id=1, source_target_pairs={{0,254},{2,0},{4,2},{6,4},{8,6},{10,8},{12,10},{14,12},{16,14},{18... | collective-permute-start | bytes 1179656 | tf_op jit(solution)/shard_map/ppermute | solution.py:24
  49.5 44.3 %collective-permute-start.9 = (bf16[384,1024]{1,0:T(8,128)(2,1)S(1)}, bf16[384,1024]{1,0:T(8,128)(2,1)S(1)}, u32[]{:S(2)}, u32[]{:S(2)}) collective-permute-start(bf16[384,1024]{1,0:T(8,128)(2,1)S(1)} %collective-permute-done.8.both2), channel_id=1, source_target_pairs={{0,2},{2,4},{4,6},{6,8},{8,10},{10,12},{12,14},{14,16},{16,18},{18... | collective-permute-start | bytes 2359304 | tf_op jit(solution)/shard_map/ppermute | solution.py:24
  51.9 6.4 %collective-permute-start.14 = (f32[32,1024]{1,0:T(8,128)S(1)}, f32[32,1024]{1,0:T(8,128)S(1)}, u32[]{:S(2)}, u32[]{:S(2)}) collective-permute-start(f32[32,1024]{1,0:T(8,128)S(1)} %add.27), channel_id=1, source_target_pairs={{0,16},{2,18},{4,20},{6,22},{8,24},{10,26},{12,28},{14,30},{16,0},... | collective-permute-start | bytes 393224 | tf_op jit(solution)/shard_map/ppermute | solution.py:29
  58.4 15.6 %collective-permute-start.11 = (bf16[192,1024]{1,0:T(8,128)(2,1)S(1)}, bf16[192,1024]{1,0:T(8,128)(2,1)S(1)}, u32[]{:S(2)}, u32[]{:S(2)}) collective-permute-start(bf16[192,1024]{1,0:T(8,128)(2,1)S(1)} %collective-permute-done.10.q2), channel_id=1, source_target_pairs={{0,254},{2,0},{4,2},{6,4},{8,6},{10,8},{12,10},{14,12},{16,14},{18... | collective-permute-start | bytes 1179656 | tf_op jit(solution)/shard_map/ppermute | solution.py:24
  62.8 11.2 %collective-permute-start.15 = (bf16[192,1024]{1,0:T(8,128)(2,1)S(1)}, bf16[192,1024]{1,0:T(8,128)(2,1)S(1)}, u32[]{:S(2)}, u32[]{:S(2)}) collective-permute-start(bf16[192,1024]{1,0:T(8,128)(2,1)S(1)} %collective-permute-done.13.d1), channel_id=1, source_target_pairs={{0,254},{2,0},{4,2},{6,4},{8,6},{10,8},{12,10},{14,12},{16,14},{18... | collective-permute-start | bytes 1179656 | tf_op jit(solution)/shard_map/ppermute | solution.py:24
  68.7 5.3 %collective-permute-start.16 = (f32[32,1024]{1,0:T(8,128)S(1)}, f32[32,1024]{1,0:T(8,128)S(1)}, u32[]{:S(2)}, u32[]{:S(2)}) collective-permute-start(f32[32,1024]{1,0:T(8,128)S(1)} %add.28), channel_id=1, source_target_pairs={{0,32},{2,34},{4,36},{6,38},{8,40},{10,42},{12,44},{14,46},{16,48}... | collective-permute-start | bytes 393224 | tf_op jit(solution)/shard_map/ppermute | solution.py:29
  74.0 31.9 %collective-permute-start.17 = (bf16[192,1024]{1,0:T(8,128)(2,1)S(1)}, bf16[192,1024]{1,0:T(8,128)(2,1)S(1)}, u32[]{:S(2)}, u32[]{:S(2)}) collective-permute-start(bf16[192,1024]{1,0:T(8,128)(2,1)S(1)} %collective-permute-done.15.d2), channel_id=1, source_target_pairs={{0,254},{2,0},{4,2},{6,4},{8,6},{10,8},{12,10},{14,12},{16,14},{18... | collective-permute-start | bytes 1179656 | tf_op jit(solution)/shard_map/ppermute | solution.py:24
  80.8 13.0 %collective-permute-start.18 = (f32[32,1024]{1,0:T(8,128)S(1)}, f32[32,1024]{1,0:T(8,128)S(1)}, u32[]{:S(2)}, u32[]{:S(2)}) collective-permute-start(f32[32,1024]{1,0:T(8,128)S(1)} %add.29), channel_id=1, source_target_pairs={{0,64},{2,66},{4,68},{6,70},{8,72},{10,74},{12,76},{14,78},{16,80}... | collective-permute-start | bytes 393224 | tf_op jit(solution)/shard_map/ppermute | solution.py:29
  99.5 7.2 %collective-permute-start.19 = (f32[16,192]{1,0:T(8,128)S(1)}, f32[16,192]{1,0:T(8,128)S(1)}, u32[]{:S(2)}, u32[]{:S(2)}) collective-permute-start(f32[16,192]{1,0:T(8,128)S(1)} %get-tuple-element.41.s0), channel_id=1, source_target_pairs={{0,254},{2,0},{4,2},{6,4},{8,6},{10,8},{12,10},{14,12},{16,14},{18... | collective-permute-start | bytes 36872 | tf_op jit(solution)/shard_map/ppermute | solution.py:24
  105.9 2.7 %collective-permute-start.20 = (f32[16,192]{1,0:T(8,128)S(1)}, f32[16,192]{1,0:T(8,128)S(1)}, u32[]{:S(2)}, u32[]{:S(2)}) collective-permute-start(f32[16,192]{1,0:T(8,128)S(1)} %get-tuple-element.41.s0), channel_id=1, source_target_pairs={{0,252},{2,254},{4,0},{6,2},{8,4},{10,6},{12,8},{14,10},{16,12},{1... | collective-permute-start | bytes 36872 | tf_op jit(solution)/shard_map/ppermute | solution.py:24
  105.9 4.7 %collective-permute-start.21 = (f32[16,192]{1,0:T(8,128)S(1)}, f32[16,192]{1,0:T(8,128)S(1)}, u32[]{:S(2)}, u32[]{:S(2)}) collective-permute-start(f32[16,192]{1,0:T(8,128)S(1)} %get-tuple-element.41.s0), channel_id=1, source_target_pairs={{0,250},{2,252},{4,254},{6,0},{8,2},{10,4},{12,6},{14,8},{16,10},{... | collective-permute-start | bytes 36872 | tf_op jit(solution)/shard_map/ppermute | solution.py:24
  110.5 8.7 %collective-permute-start.22 = (f32[32,1024]{1,0:T(8,128)S(1)}, f32[32,1024]{1,0:T(8,128)S(1)}, u32[]{:S(2)}, u32[]{:S(2)}) collective-permute-start(f32[32,1024]{1,0:T(8,128)S(1)} %add.30), channel_id=1, source_target_pairs={{0,128},{2,130},{4,132},{6,134},{8,136},{10,138},{12,140},{14,142}... | collective-permute-start | bytes 393224 | tf_op jit(solution)/shard_map/ppermute | solution.py:29

commit v10 on v6

--- a/solution.py
+++ b/solution.py
@@ -22,12 +22,6 @@
 def rotated(part, by):
     count = lax.axis_size(CTX)
     return lax.ppermute(part, CTX, [(i, (i + by) % count) for i in range(count)])
-
-
-def exchanged(part, low):
-    count = lax.axis_size(CTX)
-    one, two, three = (lax.ppermute(part, CTX, [(i, i ^ (low * k)) for i in range(count)]) for k in (1, 2, 3))
-    return (part + one) + (two + three)
 
 
 def after(parts, done):
@@ -92,8 +86,8 @@
         grad = gpad[EDGE : EDGE + block]
         for tap in range(taps_count):
             prod = grad * cpad[pl.ds(EDGE - reach + tap, block), :]
-            rows_ref[tap : tap + 1, lanes] = jnp.sum(prod, axis=0, keepdims=True)
-        rows_ref[taps_count:, lanes] = jnp.zeros_like(rows_ref[taps_count:, lanes])
+            rows_ref[column, tap : tap + 1, :] = jnp.sum(prod, axis=0, keepdims=True)
+        rows_ref[column, taps_count:, :] = jnp.zeros_like(rows_ref[column, taps_count:, :])
 
 
 def conv(device, grad, inputs, low, high, taps, last):
@@ -105,7 +99,7 @@
         out_specs=[INSIDE] * 2,
         out_shape=[
             jax.ShapeDtypeStruct((block, width), jnp.bfloat16),
-            jax.ShapeDtypeStruct((8 * pl.cdiv(count, 8), width), jnp.float32),
+            jax.ShapeDtypeStruct((width // HEAD, 8 * pl.cdiv(count, 8), HEAD), jnp.float32),
         ],
         scratch_shapes=[
             pltpu.VMEM((block + 2 * EDGE, HEAD), jnp.float32),
@@ -250,30 +244,34 @@
 
     grad_stream, tap_rows = conv(device, stream_grad, conv_input, k1, q1, conv_weight, last)
     other = lax.ppermute(grad_stream, "tp", [(0, 1), (1, 0)])
-    tap_rows = tap_rows + lax.ppermute(tap_rows, CTX, [(i, i ^ 1) for i in range(last + 1)])
-    tap_rows = exchanged(tap_rows, 2)
-    (other,) = after((other,), (k2, q2))
+    (tap_rows,) = after((tap_rows,), (k2,))
+    tap_sums = jnp.sum(lax.all_to_all(tap_rows, "far", 0, 0, tiled=True), axis=0)
+    (other,) = after((other,), (k2, q2, tap_sums))
     out_grad = project(tp, grad_stream, other, out_weight)
     k3, q3 = rotated(k2, 1), rotated(q2, -1)
     v3 = rotated(v2, 1)
 
     (sent,) = after((out_grad,), (v2,))
     d1 = rotated(sent, -1)
-    (sent,) = after((d1,), (k3, q3, tap_rows))
+    (sent,) = after((d1,), (k3, q3))
     d2 = rotated(sent, -1)
     (sent,) = after((d2,), (v3,))
     d3 = rotated(sent, -1)
 
-    tap_rows = exchanged(tap_rows, 8)
-    query_grad, stats = query_side(device, queries, out_grad, (k3, k2, k1, keys), (v3, v2, v1, values), scale)
-    (stats,) = after((stats,), (tap_rows,))
+    copies = jnp.broadcast_to(tap_sums, (lax.axis_size("near"),) + tap_sums.shape)
+    (copies,) = after((copies,), (v2, out_grad))
+    tap_sums = jnp.sum(lax.all_to_all(copies, "near", 0, 0, tiled=True), axis=0)
+    (near,) = after((queries,), (tap_sums,))
+    query_grad, stats = query_side(device, near, out_grad, (k3, k2, k1, keys), (v3, v2, v1, values), scale)
     all_stats = [stats] + [rotated(stats, -hop) for hop in (1, 2, 3)]
-    (tap_rows,) = after((tap_rows,), (*all_stats[1:], d3))
-    tap_rows = exchanged(tap_rows, 32)
+    copies = jnp.broadcast_to(tap_sums, (lax.axis_size("far"),) + tap_sums.shape)
+    (copies,) = after((copies,), (*all_stats[1:], d3))
+    tap_sums = lax.all_to_all(copies, "far", 0, 0, tiled=True)
     key_grad, value_grad = key_side(
         device, keys, values, (queries, q1, q2, q3), (out_grad, d1, d2, d3), all_stats, scale, last
     )
-    kernel_grad = tap_rows[: conv_weight.shape[0]] / math.sqrt(block * (last + 1))
+    rows = jnp.transpose(tap_sums, (1, 0, 2)).reshape(tap_sums.shape[1], -1)[: conv_weight.shape[0]]
+    kernel_grad = rows / math.sqrt(block * (last + 1))
     return (query_grad, key_grad, value_grad, grad_stream, kernel_grad)
 
 

time: 116 us -> 113 us (0.974)
  waiting for transfers between devices: 34.1 us -> 19 us
  local copies, waits for them, and re-layouts: 0.03 us -> 5.83 us
  starting transfers between devices: 58.1 us -> 61.7 us
  Pallas kernels: 17.7 us -> 19.5 us
    all_to_all x0 -> x3, starting transfers between devices: none -> 20.1 us  [the longest x1 10.2 us: per_device(): tap_sums = jnp.sum(lax.all_to_all(copies, 'near', 0, 0, tiled=True), axis=0)]
    ppermute x10 -> x0, waiting for transfers between devices: 18.5 us -> none  [the longest x9 17.5 us: exchanged(): lax.ppermute(part, CTX, [(i, i ^ low * k) for i in range(count)])]
    ppermute x10 -> x0, starting transfers between devices: 14.9 us -> none  [the longest x9 8.58 us: exchanged(): lax.ppermute(part, CTX, [(i, i ^ low * k) for i in range(count)])]
    all_to_all x0 -> x3, waiting for transfers between devices: none -> 10.3 us  [the longest x1 6.38 us: per_device(): tap_sums = jnp.sum(lax.all_to_all(copies, 'near', 0, 0, tiled=True), axis=0)]
    ppermute x15, waiting for transfers between devices: 13.9 us -> 8.63 us  [rotated(): lax.ppermute(part, CTX, [(i, (i + by) % count) for i in range(count)])]
    unnamed x12 -> x20, local copies, waits for them, and re-layouts: 0.03 us -> 3.45 us
    ppermute x1, waiting for transfers between devices: 1.7 us -> 0.01 us  [per_device(): other = lax.ppermute(grad_stream, 'tp', [(0, 1), (1, 0)])]
    ppermute x15, starting transfers between devices: 40.6 us -> 39 us  [rotated(): lax.ppermute(part, CTX, [(i, (i + by) % count) for i in range(count)])]
  transfers between devices with their start and end apart: 26 -> 19, of which waited for: 11 -> 6; matrix products, arithmetic and copies ran while one was open for 4% -> 5% of each run, Pallas kernels for 13% -> 15%
where the time goes in v10:
time: 113 us; the launch traced here: 112 us
  starting transfers between devices  61.7 us (55%)
  Pallas kernels  19.5 us (17%)
  waiting for transfers between devices  19 us (17%)
  local copies, waits for them, and re-layouts  5.83 us (5%)
  matrix products  4.28 us (4%)
    ppermute x15, starting transfers between devices, rotated(): lax.ppermute(part, CTX, [(i, (i + by) % count) for i in range(count)])  39 us
    all_to_all x1, starting transfers between devices, per_device(): tap_sums = jnp.sum(lax.all_to_all(copies, 'near', 0, 0, tiled=True), axis=0)  10.2 us
    ppermute x15, waiting for transfers between devices, rotated(): lax.ppermute(part, CTX, [(i, (i + by) % count) for i in range(count)])  8.63 us
    pallas_call x1, Pallas kernels, query_side(): pl.pallas_call(functools.partial(query_kernel, scale), in_specs=[pl.Block...  7.1 us
    all_to_all x1, waiting for transfers between devices, per_device(): tap_sums = jnp.sum(lax.all_to_all(copies, 'near', 0, 0, tiled=True), axis=0)  6.38 us
    all_to_all x1, starting transfers between devices, per_device(): lax.all_to_all(tap_rows, 'far', 0, 0, tiled=True)  5.92 us
    pallas_call x1, Pallas kernels, key_side(): pl.pallas_call(functools.partial(key_kernel, scale, last), in_specs=[pl.B...  5.61 us
    pallas_call x1, Pallas kernels, conv(): pl.pallas_call(functools.partial(conv_kernel, last), in_specs=[pl.BlockSp...  4.57 us
  transfers between devices with their start and end apart: 19, of which 6 were waited for; matrix products, arithmetic and copies ran while one was open for 5% of the time, Pallas kernels for 15%

profile of v10, /device:TPU:1, one launch (start us, length us, event | category | flops | bytes accessed | tf_op | source)
XLA Modules:
  0.0 112.1 jit_solution(2667216761033381648)
XLA Ops:
  0.7 2.2 %shard_map.110 = (bf16[224,1024]{1,0:T(8,128)(2,1)}, bf16[224,1024]{1,0:T(8,128)(2,1)}) custom-call(bf16[192,1024]{1,0:T(8,128)(2,1)} %k_ref.3, bf16[192,1024]{1,0:T(8,128)(2,1)} %q0.1, bf16[192,1024]{1,0:T(8,128)(2,1)} %input_ref.3, bf16[192,1024]{1,0:T(8,128)(2,1)} %grad_ref.3), custom_call_target="tpu_custom_call" | custom-call | tf_op jit(solution)/shard_map/pallas_call | solution.py:50
  2.9 2.7 %collective-permute-start = (bf16[224,1024]{1,0:T(8,128)(2,1)}, bf16[224,1024]{1,0:T(8,128)(2,1)S(1)}, u32[]{:S(2)}, u32[]{:S(2)}) collective-permute-start(bf16[224,1024]{1,0:T(8,128)(2,1)} %get-tuple-element.22), channel_id=1, source_target_pairs={{0,2},{2,4},{4,6},{6,8},{8,10},{10,12},{12,14},{14,16},{16,18},{18... | collective-permute-start | bytes 1376264 | tf_op jit(solution)/shard_map/ppermute | solution.py:24
  5.6 0.7 collective-permute-start.1
  6.3 5.0 %collective-permute-done.low_ref.k1 = bf16[224,1024]{1,0:T(8,128)(2,1)S(1)} collective-permute-done((bf16[224,1024]{1,0:T(8,128)(2,1)}, bf16[224,1024]{1,0:T(8,128)(2,1)S(1)}, u32[]{:S(2)}, u32[]{:S(2)}) %collective-permute-start) | collective-permute-done | bytes 458784 | tf_op jit(solution)/shard_map/ppermute | solution.py:24
  11.3 2.4 %collective-permute-start.2 = (bf16[224,1024]{1,0:T(8,128)(2,1)S(1)}, bf16[224,1024]{1,0:T(8,128)(2,1)S(1)}, u32[]{:S(2)}, u32[]{:S(2)}) collective-permute-start(bf16[224,1024]{1,0:T(8,128)(2,1)S(1)} %collective-permute-done.low_ref.k1), channel_id=1, source_target_pairs={{0,2},{2,4},{4,6},{6,8},{8,10},{10,12},{12,14},{14,16},{16,18},{18... | collective-permute-start | bytes 1376264 | tf_op jit(solution)/shard_map/ppermute | solution.py:24
  13.7 5.7 %collective-permute-start.6 = (bf16[224,1024]{1,0:T(8,128)(2,1)S(1)}, bf16[224,1024]{1,0:T(8,128)(2,1)S(1)}, u32[]{:S(2)}, u32[]{:S(2)}) collective-permute-start(bf16[224,1024]{1,0:T(8,128)(2,1)S(1)} %collective-permute-done.1.high_ref.q1), channel_id=1, source_target_pairs={{0,254},{2,0},{4,2},{6,4},{8,6},{10,8},{12,10},{14,12},{16,14},{18... | collective-permute-start | bytes 1376264 | tf_op jit(solution)/shard_map/ppermute | solution.py:24
  19.4 4.6 %shard_map.111 = (bf16[192,1024]{1,0:T(8,128)(2,1)}, f32[8,32,128]{2,1,0:T(8,128)}) custom-call(s32[1]{0:T(128)} %bitcast.idx_ref, bf16[192,1024]{1,0:T(8,128)(2,1)S(1)} %copy-done, bf16[192,1024]{1,0:T(8,128)(2,1)S(1)} %copy-done.1, bf16[224,1024]{1,0:T(8,128)(2,1)S(1)} %collective-permute-done.low_ref.k1, ...), custom_call_target="tpu_custom_call" | custom-call | flops 48758784 | bytes 786432 | tf_op jit(solution)/shard_map/pallas_call | solution.py:96
  24.0 2.6 %collective-permute-start.5 = (bf16[192,1024]{1,0:T(8,128)(2,1)}, bf16[192,1024]{1,0:T(8,128)(2,1)}, u32[]{:S(2)}, u32[]{:S(2)}) collective-permute-start(bf16[192,1024]{1,0:T(8,128)(2,1)} %get-tuple-element.20), channel_id=1, source_target_pairs={{0,1},{1,0},{2,3},{3,2},{4,5},{5,4},{6,7},{7,6},{8,9},{9,8},{10,11... | collective-permute-start | bytes 1179656 | tf_op jit(solution)/shard_map/ppermute | solution.py:246
  26.6 5.9 %all-to-all-start = ((f32[8,32,128]{2,1,0:T(8,128)}), f32[8,32,128]{2,1,0:T(8,128)S(1)}, u32[]{:S(2)}, u32[]{:S(2)}) async-start(f32[8,32,128]{2,1,0:T(8,128)} %get-tuple-element.25), calls=%async_computation | async-start | bytes 262144 | tf_op jit(solution)/shard_map/all_to_all | solution.py:248
  32.8 6.5 %collective-permute-start.9 = (bf16[224,1024]{1,0:T(8,128)(2,1)S(1)}, bf16[224,1024]{1,0:T(8,128)(2,1)S(1)}, u32[]{:S(2)}, u32[]{:S(2)}) collective-permute-start(bf16[224,1024]{1,0:T(8,128)(2,1)S(1)} %collective-permute-done.6.q2), channel_id=1, source_target_pairs={{0,254},{2,0},{4,2},{6,4},{8,6},{10,8},{12,10},{14,12},{16,14},{18... | collective-permute-start | bytes 1376264 | tf_op jit(solution)/shard_map/ppermute | solution.py:24
  39.3 1.1 %all-to-all-done = f32[8,32,128]{2,1,0:T(8,128)S(1)} async-done(((f32[8,32,128]{2,1,0:T(8,128)}), f32[8,32,128]{2,1,0:T(8,128)S(1)}, u32[]{:S(2)}, u32[]{:S(2)}) %all-to-all-start) | async-done | bytes 131104 | tf_op jit(solution)/shard_map/all_to_all | solution.py:248
  40.5 4.3 %convolution_convert_fusion.do_ref.d0 = bf16[192,1024]{1,0:T(8,128)(2,1)S(1)} fusion(bf16[1024,2048]{1,0:T(8,128)(2,1)} %param.13, bf16[192,1024]{1,0:T(8,128)(2,1)} %collective-permute-done.5, bf16[192,1024]{1,0:T(8,128)(2,1)} %get-tuple-element.20, pred[]{:T(512)S(6)} %eq.3), kind=kOutput, calls=%fused_computation | convolution fusion | flops 809041920 | bytes 5373953 | tf_op jit(solution)/shard_map/dot_general | solution.py:115
  44.8 7.7 %collective-permute-start.10 = (bf16[192,1024]{1,0:T(8,128)(2,1)S(1)}, bf16[192,1024]{1,0:T(8,128)(2,1)}, u32[]{:S(2)}, u32[]{:S(2)}) collective-permute-start(bf16[192,1024]{1,0:T(8,128)(2,1)S(1)} %convolution_convert_fusion.do_ref.d0), channel_id=1, source_target_pairs={{0,254},{2,0},{4,2},{6,4},{8,6},{10,8},{12,10},{14,12},{16,14},{18... | collective-permute-start | bytes 1179656 | tf_op jit(solution)/shard_map/ppermute | solution.py:24
  52.5 0.7 copy-done.6
  53.3 0.7 collective-permute-done.10.d1
  54.0 4.6 %collective-permute-start.11 = (bf16[192,1024]{1,0:T(8,128)(2,1)}, bf16[192,1024]{1,0:T(8,128)(2,1)}, u32[]{:S(2)}, u32[]{:S(2)}) collective-permute-start(bf16[192,1024]{1,0:T(8,128)(2,1)} %collective-permute-done.10.d1), channel_id=1, source_target_pairs={{0,254},{2,0},{4,2},{6,4},{8,6},{10,8},{12,10},{14,12},{16,14},{18... | collective-permute-start | bytes 1179656 | tf_op jit(solution)/shard_map/ppermute | solution.py:24
  58.6 0.7 broadcast_in_dim.6
  59.4 10.2 %all-to-all-start.1 = ((f32[16,32,128]{2,1,0:T(8,128)}), f32[16,32,128]{2,1,0:T(8,128)}, u32[]{:S(2)}, u32[]{:S(2)}) async-start(f32[16,32,128]{2,1,0:T(8,128)} %broadcast_in_dim.6), calls=%async_computation.1 | async-start | bytes 524288 | tf_op jit(solution)/shard_map/all_to_all | solution.py:263
  69.5 0.9 collective-permute-start.12
  70.5 6.4 %all-to-all-done.1 = f32[16,32,128]{2,1,0:T(8,128)} async-done(((f32[16,32,128]{2,1,0:T(8,128)}), f32[16,32,128]{2,1,0:T(8,128)}, u32[]{:S(2)}, u32[]{:S(2)}) %all-to-all-start.1) | async-done | bytes 262176 | tf_op jit(solution)/shard_map/all_to_all | solution.py:263
  76.9 1.0 reduce_sum.19
  77.9 1.0 copy-done.7
  78.9 7.1 %shard_map.112 = (bf16[192,1024]{1,0:T(8,128)(2,1)}, f32[16,192]{1,0:T(8,128)S(1)}) custom-call(s32[1]{0:T(128)} %bitcast.idx_ref, bf16[192,1024]{1,0:T(8,128)(2,1)S(1)} %copy-done.2, bf16[192,1024]{1,0:T(8,128)(2,1)S(1)} %copy-done.7, bf16[224,1024]{1,0:T(8,128)(2,1)} %collective-permute-done.7.k3, bf16[224,1024]{1,0:T(8,128)(2,1)S(1)} %collective-permute-done.2.k2, ...), custom_call_target="tpu_custom_call" | custom-call | flops 1509949440 | bytes 4718592 | tf_op jit(solution)/shard_map/pallas_call | solution.py:157
  86.0 1.0 collective-permute-start.13
  86.9 4.6 %collective-permute-start.14 = (f32[16,192]{1,0:T(8,128)S(1)}, f32[16,192]{1,0:T(8,128)S(1)}, u32[]{:S(2)}, u32[]{:S(2)}) collective-permute-start(f32[16,192]{1,0:T(8,128)S(1)} %get-tuple-element.35.s0), channel_id=1, source_target_pairs={{0,252},{2,254},{4,0},{6,2},{8,4},{10,6},{12,8},{14,10},{16,12},{1... | collective-permute-start | bytes 36872 | tf_op jit(solution)/shard_map/ppermute | solution.py:24
  91.6 1.8 %collective-permute-start.15 = (f32[16,192]{1,0:T(8,128)S(1)}, f32[16,192]{1,0:T(8,128)S(1)}, u32[]{:S(2)}, u32[]{:S(2)}) collective-permute-start(f32[16,192]{1,0:T(8,128)S(1)} %get-tuple-element.35.s0), channel_id=1, source_target_pairs={{0,250},{2,252},{4,254},{6,0},{8,2},{10,4},{12,6},{14,8},{16,10},{... | collective-permute-start | bytes 36872 | tf_op jit(solution)/shard_map/ppermute | solution.py:24
  93.4 2.9 %collective-permute-done.15.s3 = f32[16,192]{1,0:T(8,128)S(1)} collective-permute-done((f32[16,192]{1,0:T(8,128)S(1)}, f32[16,192]{1,0:T(8,128)S(1)}, u32[]{:S(2)}, u32[]{:S(2)}) %collective-permute-start.15) | collective-permute-done | bytes 12320 | tf_op jit(solution)/shard_map/ppermute | solution.py:24
  96.9 4.0 %all-to-all-start.2 = ((f32[8,32,128]{2,1,0:T(8,128)}), f32[8,32,128]{2,1,0:T(8,128)}, u32[]{:S(2)}, u32[]{:S(2)}) async-start(f32[8,32,128]{2,1,0:T(8,128)} %broadcast_in_dim.7), calls=%async_computation.2 | async-start | bytes 262144 | tf_op jit(solution)/shard_map/all_to_all | solution.py:269
  101.0 1.0 copy-done.8
  101.9 5.6 %shard_map.113 = (bf16[192,1024]{1,0:T(8,128)(2,1)}, bf16[192,1024]{1,0:T(8,128)(2,1)}) custom-call(s32[1]{0:T(128)} %bitcast.idx_ref, bf16[192,1024]{1,0:T(8,128)(2,1)S(1)} %copy-done.3, bf16[192,1024]{1,0:T(8,128)(2,1)S(1)} %copy-done.5, bf16[192,1024]{1,0:T(8,128)(2,1)S(1)} %copy-done.2, bf16[224,1024]{1,0:T(8,128)(2,1)S(1)} %collective-permute-done.1.high_ref.q1, ...), custom_call_target="tpu_custom_call" | custom-call | flops 1509949440 | bytes 4718592 | tf_op jit(solution)/shard_map/pallas_call | solution.py:214
  107.6 2.8 %all-to-all-done.2 = f32[8,32,128]{2,1,0:T(8,128)} async-done(((f32[8,32,128]{2,1,0:T(8,128)}), f32[8,32,128]{2,1,0:T(8,128)}, u32[]{:S(2)}, u32[]{:S(2)}) %all-to-all-start.2) | async-done | bytes 131104 | tf_op jit(solution)/shard_map/all_to_all | solution.py:269
  110.4 1.0 copy.17
  (37 shorter events, 1.7 us)
Async XLA Ops:
  0.6 18.7 %copy-start = (bf16[192,1024]{1,0:T(8,128)(2,1)S(1)}, bf16[192,1024]{1,0:T(8,128)(2,1)}, u32[]{:S(2)}) copy-start(bf16[192,1024]{1,0:T(8,128)(2,1)} %grad_ref.3) | copy-start | bytes 1179652
  0.6 18.7 %copy-start.1 = (bf16[192,1024]{1,0:T(8,128)(2,1)S(1)}, bf16[192,1024]{1,0:T(8,128)(2,1)}, u32[]{:S(2)}) copy-start(bf16[192,1024]{1,0:T(8,128)(2,1)} %input_ref.3) | copy-start | bytes 1179652
  0.7 18.7 %copy-start.5 = (bf16[192,1024]{1,0:T(8,128)(2,1)S(1)}, bf16[192,1024]{1,0:T(8,128)(2,1)}, u32[]{:S(2)}) copy-start(bf16[192,1024]{1,0:T(8,128)(2,1)} %v_ref.1) | copy-start | bytes 1179652
  0.7 18.7 %copy-start.4 = (bf16[31,1024]{1,0:T(8,128)(2,1)S(1)}, bf16[31,1024]{1,0:T(8,128)(2,1)}, u32[]{:S(2)}) copy-start(bf16[31,1024]{1,0:T(8,128)(2,1)} %taps_ref.1) | copy-start | bytes 190468
  2.9 8.4 %collective-permute-start = (bf16[224,1024]{1,0:T(8,128)(2,1)}, bf16[224,1024]{1,0:T(8,128)(2,1)S(1)}, u32[]{:S(2)}, u32[]{:S(2)}) collective-permute-start(bf16[224,1024]{1,0:T(8,128)(2,1)} %get-tuple-element.22), channel_id=1, source_target_pairs={{0,2},{2,4},{4,6},{6,8},{8,10},{10,12},{12,14},{14,16},{16,18},{18... | collective-permute-start | bytes 1376264 | tf_op jit(solution)/shard_map/ppermute | solution.py:24
  5.6 8.1 %collective-permute-start.1 = (bf16[224,1024]{1,0:T(8,128)(2,1)}, bf16[224,1024]{1,0:T(8,128)(2,1)S(1)}, u32[]{:S(2)}, u32[]{:S(2)}) collective-permute-start(bf16[224,1024]{1,0:T(8,128)(2,1)} %get-tuple-element.23), channel_id=1, source_target_pairs={{0,254},{2,0},{4,2},{6,4},{8,6},{10,8},{12,10},{14,12},{16,14},{18... | collective-permute-start | bytes 1376264 | tf_op jit(solution)/shard_map/ppermute | solution.py:24
  11.3 15.3 %collective-permute-start.2 = (bf16[224,1024]{1,0:T(8,128)(2,1)S(1)}, bf16[224,1024]{1,0:T(8,128)(2,1)S(1)}, u32[]{:S(2)}, u32[]{:S(2)}) collective-permute-start(bf16[224,1024]{1,0:T(8,128)(2,1)S(1)} %collective-permute-done.low_ref.k1), channel_id=1, source_target_pairs={{0,2},{2,4},{4,6},{6,8},{8,10},{10,12},{12,14},{14,16},{16,18},{18... | collective-permute-start | bytes 1376264 | tf_op jit(solution)/shard_map/ppermute | solution.py:24
  13.7 19.1 %collective-permute-start.6 = (bf16[224,1024]{1,0:T(8,128)(2,1)S(1)}, bf16[224,1024]{1,0:T(8,128)(2,1)S(1)}, u32[]{:S(2)}, u32[]{:S(2)}) collective-permute-start(bf16[224,1024]{1,0:T(8,128)(2,1)S(1)} %collective-permute-done.1.high_ref.q1), channel_id=1, source_target_pairs={{0,254},{2,0},{4,2},{6,4},{8,6},{10,8},{12,10},{14,12},{16,14},{18... | collective-permute-start | bytes 1376264 | tf_op jit(solution)/shard_map/ppermute | solution.py:24
  19.4 13.1 %collective-permute-start.3 = (bf16[192,1024]{1,0:T(8,128)(2,1)S(1)}, bf16[192,1024]{1,0:T(8,128)(2,1)}, u32[]{:S(2)}, u32[]{:S(2)}) collective-permute-start(bf16[192,1024]{1,0:T(8,128)(2,1)S(1)} %copy-done.5), channel_id=1, source_target_pairs={{0,2},{2,4},{4,6},{6,8},{8,10},{10,12},{12,14},{14,16},{16,18},{18... | collective-permute-start | bytes 1179656 | tf_op jit(solution)/shard_map/ppermute | solution.py:24
  24.0 16.5 %collective-permute-start.5 = (bf16[192,1024]{1,0:T(8,128)(2,1)}, bf16[192,1024]{1,0:T(8,128)(2,1)}, u32[]{:S(2)}, u32[]{:S(2)}) collective-permute-start(bf16[192,1024]{1,0:T(8,128)(2,1)} %get-tuple-element.20), channel_id=1, source_target_pairs={{0,1},{1,0},{2,3},{3,2},{4,5},{5,4},{6,7},{7,6},{8,9},{9,8},{10,11... | collective-permute-start | bytes 1179656 | tf_op jit(solution)/shard_map/ppermute | solution.py:246
  26.6 13.8 %all-to-all-start = ((f32[8,32,128]{2,1,0:T(8,128)}), f32[8,32,128]{2,1,0:T(8,128)S(1)}, u32[]{:S(2)}, u32[]{:S(2)}) async-start(f32[8,32,128]{2,1,0:T(8,128)} %get-tuple-element.25), calls=%async_computation | async-start | bytes 262144 | tf_op jit(solution)/shard_map/all_to_all | solution.py:248
  32.5 12.3 %collective-permute-start.4 = (bf16[192,1024]{1,0:T(8,128)(2,1)}, bf16[192,1024]{1,0:T(8,128)(2,1)}, u32[]{:S(2)}, u32[]{:S(2)}) collective-permute-start(bf16[192,1024]{1,0:T(8,128)(2,1)} %collective-permute-done.3.v1), channel_id=1, source_target_pairs={{0,2},{2,4},{4,6},{6,8},{8,10},{10,12},{12,14},{14,16},{16,18},{18... | collective-permute-start | bytes 1179656 | tf_op jit(solution)/shard_map/ppermute | solution.py:24
  32.6 20.7 %collective-permute-start.7 = (bf16[224,1024]{1,0:T(8,128)(2,1)S(1)}, bf16[224,1024]{1,0:T(8,128)(2,1)}, u32[]{:S(2)}, u32[]{:S(2)}) collective-permute-start(bf16[224,1024]{1,0:T(8,128)(2,1)S(1)} %collective-permute-done.2.k2), channel_id=1, source_target_pairs={{0,2},{2,4},{4,6},{6,8},{8,10},{10,12},{12,14},{14,16},{16,18},{18... | collective-permute-start | bytes 1376264 | tf_op jit(solution)/shard_map/ppermute | solution.py:24
  32.8 20.5 %collective-permute-start.9 = (bf16[224,1024]{1,0:T(8,128)(2,1)S(1)}, bf16[224,1024]{1,0:T(8,128)(2,1)S(1)}, u32[]{:S(2)}, u32[]{:S(2)}) collective-permute-start(bf16[224,1024]{1,0:T(8,128)(2,1)S(1)} %collective-permute-done.6.q2), channel_id=1, source_target_pairs={{0,254},{2,0},{4,2},{6,4},{8,6},{10,8},{12,10},{14,12},{16,14},{18... | collective-permute-start | bytes 1376264 | tf_op jit(solution)/shard_map/ppermute | solution.py:24
  40.5 37.4 %copy-start.2 = (bf16[192,1024]{1,0:T(8,128)(2,1)S(1)}, bf16[192,1024]{1,0:T(8,128)(2,1)}, u32[]{:S(2)}) copy-start(bf16[192,1024]{1,0:T(8,128)(2,1)} %q0.1) | copy-start | bytes 1179652
  40.5 37.4 %copy-start.3 = (bf16[192,1024]{1,0:T(8,128)(2,1)S(1)}, bf16[192,1024]{1,0:T(8,128)(2,1)}, u32[]{:S(2)}) copy-start(bf16[192,1024]{1,0:T(8,128)(2,1)} %k_ref.3) | copy-start | bytes 1179652
  44.8 9.2 %collective-permute-start.10 = (bf16[192,1024]{1,0:T(8,128)(2,1)S(1)}, bf16[192,1024]{1,0:T(8,128)(2,1)}, u32[]{:S(2)}, u32[]{:S(2)}) collective-permute-start(bf16[192,1024]{1,0:T(8,128)(2,1)S(1)} %convolution_convert_fusion.do_ref.d0), channel_id=1, source_target_pairs={{0,254},{2,0},{4,2},{6,4},{8,6},{10,8},{12,10},{14,12},{16,14},{18... | collective-permute-start | bytes 1179656 | tf_op jit(solution)/shard_map/ppermute | solution.py:24
  52.5 0.7 copy-start.6
  53.3 16.2 %collective-permute-start.8 = (bf16[192,1024]{1,0:T(8,128)(2,1)}, bf16[192,1024]{1,0:T(8,128)(2,1)}, u32[]{:S(2)}, u32[]{:S(2)}) collective-permute-start(bf16[192,1024]{1,0:T(8,128)(2,1)} %collective-permute-done.4.v2), channel_id=1, source_target_pairs={{0,2},{2,4},{4,6},{6,8},{8,10},{10,12},{12,14},{14,16},{16,18},{18... | collective-permute-start | bytes 1179656 | tf_op jit(solution)/shard_map/ppermute | solution.py:24
  54.0 15.5 %collective-permute-start.11 = (bf16[192,1024]{1,0:T(8,128)(2,1)}, bf16[192,1024]{1,0:T(8,128)(2,1)}, u32[]{:S(2)}, u32[]{:S(2)}) collective-permute-start(bf16[192,1024]{1,0:T(8,128)(2,1)} %collective-permute-done.10.d1), channel_id=1, source_target_pairs={{0,254},{2,0},{4,2},{6,4},{8,6},{10,8},{12,10},{14,12},{16,14},{18... | collective-permute-start | bytes 1179656 | tf_op jit(solution)/shard_map/ppermute | solution.py:24
  59.4 17.5 %all-to-all-start.1 = ((f32[16,32,128]{2,1,0:T(8,128)}), f32[16,32,128]{2,1,0:T(8,128)}, u32[]{:S(2)}, u32[]{:S(2)}) async-start(f32[16,32,128]{2,1,0:T(8,128)} %broadcast_in_dim.6), calls=%async_computation.1 | async-start | bytes 524288 | tf_op jit(solution)/shard_map/all_to_all | solution.py:263
  69.5 26.7 %collective-permute-start.12 = (bf16[192,1024]{1,0:T(8,128)(2,1)}, bf16[192,1024]{1,0:T(8,128)(2,1)}, u32[]{:S(2)}, u32[]{:S(2)}) collective-permute-start(bf16[192,1024]{1,0:T(8,128)(2,1)} %collective-permute-done.11.d2), channel_id=1, source_target_pairs={{0,254},{2,0},{4,2},{6,4},{8,6},{10,8},{12,10},{14,12},{16,14},{18... | collective-permute-start | bytes 1179656 | tf_op jit(solution)/shard_map/ppermute | solution.py:24
  77.9 1.0 copy-start.7
  86.0 7.4 %collective-permute-start.13 = (f32[16,192]{1,0:T(8,128)S(1)}, f32[16,192]{1,0:T(8,128)S(1)}, u32[]{:S(2)}, u32[]{:S(2)}) collective-permute-start(f32[16,192]{1,0:T(8,128)S(1)} %get-tuple-element.35.s0), channel_id=1, source_target_pairs={{0,254},{2,0},{4,2},{6,4},{8,6},{10,8},{12,10},{14,12},{16,14},{18... | collective-permute-start | bytes 36872 | tf_op jit(solution)/shard_map/ppermute | solution.py:24
  86.9 6.5 %collective-permute-start.14 = (f32[16,192]{1,0:T(8,128)S(1)}, f32[16,192]{1,0:T(8,128)S(1)}, u32[]{:S(2)}, u32[]{:S(2)}) collective-permute-start(f32[16,192]{1,0:T(8,128)S(1)} %get-tuple-element.35.s0), channel_id=1, source_target_pairs={{0,252},{2,254},{4,0},{6,2},{8,4},{10,6},{12,8},{14,10},{16,12},{1... | collective-permute-start | bytes 36872 | tf_op jit(solution)/shard_map/ppermute | solution.py:24
  91.6 4.7 %collective-permute-start.15 = (f32[16,192]{1,0:T(8,128)S(1)}, f32[16,192]{1,0:T(8,128)S(1)}, u32[]{:S(2)}, u32[]{:S(2)}) collective-permute-start(f32[16,192]{1,0:T(8,128)S(1)} %get-tuple-element.35.s0), channel_id=1, source_target_pairs={{0,250},{2,252},{4,254},{6,0},{8,2},{10,4},{12,6},{14,8},{16,10},{... | collective-permute-start | bytes 36872 | tf_op jit(solution)/shard_map/ppermute | solution.py:24
  96.9 13.4 %all-to-all-start.2 = ((f32[8,32,128]{2,1,0:T(8,128)}), f32[8,32,128]{2,1,0:T(8,128)}, u32[]{:S(2)}, u32[]{:S(2)}) async-start(f32[8,32,128]{2,1,0:T(8,128)} %broadcast_in_dim.7), calls=%async_computation.2 | async-start | bytes 262144 | tf_op jit(solution)/shard_map/all_to_all | solution.py:269
  100.9 1.0 copy-start.8

commit v11 on v8

--- a/solution.py
+++ b/solution.py
@@ -150,6 +150,7 @@
 
 def project(tp, own, other, weight):
     full = jnp.where(tp == 0, jnp.concatenate([own, other], axis=1), jnp.concatenate([other, own], axis=1))
+    full = lax.optimization_barrier(full)
     return lax.dot_general(full, weight, NT, preferred_element_type=jnp.float32).astype(jnp.bfloat16)
 
 
@@ -279,7 +280,7 @@
     kv0, inside, across = pack(device, keys, values, conv_input, stream_grad)
     inside, across = swapped(inside, 0), swapped(across, 1)
     other = lax.ppermute(stream_grad, "tp", pair)
-    (sent,) = after((kv0,), (across,))
+    (sent,) = after((kv0,), (across, other))
     kv1, q1 = rotated(sent, 1), rotated(queries, -1)
     q2 = rotated(q1, -1)
     q3 = rotated(q2, -1)
@@ -288,25 +289,22 @@
     padding = jnp.zeros((2 * EDGE - taps_count, conv_weight.shape[1]), conv_weight.dtype)
     edges = lax.ppermute(jnp.concatenate([inside[EDGE:], across[EDGE:], conv_weight, padding], axis=0), "tp", pair)
     grad_stream, tap_rows = conv(device, stream_grad, conv_input, inside, across, conv_weight, last)
-    other, edges, sent = after((other, edges, kv1), (q1, grad_stream))
+    out_grad = project(tp, grad_stream, conv_other(device, other, edges, taps_count, last), out_weight)
+    (sent,) = after((kv1,), (q1, out_grad))
     kv2 = rotated(sent, 1)
-    out_grad = project(tp, grad_stream, conv_other(device, other, edges, taps_count, last), out_weight)
-    (sent,) = after((kv2,), (out_grad, q1))
-    kv3 = rotated(sent, 1)
-
-    (tap_rows,) = after((tap_rows,), (kv1,))
+    kv3 = rotated(kv2, 1)
+    d1 = rotated(out_grad, -1)
+    (sent,) = after((d1,), (kv2, q2))
+    d2 = rotated(sent, -1)
+    (sent,) = after((d2,), (q3,))
+    d3 = rotated(sent, -1)
+
+    (tap_rows,) = after((tap_rows,), (kv1, d1))
     tap_sums = jnp.sum(lax.all_to_all(tap_rows, "z", 0, 0, tiled=True), axis=0)
-    d1 = rotated(out_grad, -1)
-    (sent,) = after((d1,), (kv2, q2, tap_sums))
-    d2 = rotated(sent, -1)
     copies = jnp.broadcast_to(tap_sums, (lax.axis_size("near"),) + tap_sums.shape)
-    (copies,) = after((copies,), (d1,))
+    (copies,) = after((copies,), (kv3,))
     tap_sums = jnp.sum(lax.all_to_all(copies, "near", 0, 0, tiled=True), axis=0)
-    (sent,) = after((d2,), (kv3, q3))
-    d3 = rotated(sent, -1)
-
-    (near,) = after((queries,), (tap_sums,))
-    query_grad, stats = query_side(device, near, out_grad, (kv3, kv2, kv1, kv0), scale)
+    query_grad, stats = query_side(device, queries, out_grad, (kv3, kv2, kv1, kv0), scale)
     all_stats = [stats] + [rotated(stats, -hop) for hop in (1, 2, 3)]
     copies = jnp.broadcast_to(tap_sums, (lax.axis_size("z"),) + tap_sums.shape)
     (copies,) = after((copies,), (*all_stats[1:], d3))

time: 122 us -> 121 us (level)
  starting transfers between devices: 55.9 us -> 61.1 us
  waiting for transfers between devices: 32.4 us -> 27.2 us
  local copies, waits for them, and re-layouts: 4.01 us -> 2.27 us
    all_to_all x1, waiting for transfers between devices: 6.7 us -> 0.01 us  [per_device(): tap_sums = jnp.sum(lax.all_to_all(copies, 'near', 0, 0, tiled=True), axis=0)]
    ppermute x1, waiting for transfers between devices: 13.8 us -> 7.67 us  [per_device(): lax.ppermute(jnp.concatenate([inside[EDGE:], across[EDGE:], conv_weight,...]
    all_to_all x1, starting transfers between devices: 3.37 us -> 7.87 us  [per_device(): tap_sums = lax.all_to_all(copies, 'z', 0, 0, tiled=True)]
    all_to_all x1, waiting for transfers between devices: 4.35 us -> 7.92 us  [per_device(): tap_sums = jnp.sum(lax.all_to_all(tap_rows, 'z', 0, 0, tiled=True), axis=0)]
    ppermute x12, waiting for transfers between devices: 2.89 us -> 5.49 us  [rotated(): lax.ppermute(part, CTX, [(i, (i + by) % count) for i in range(count)])]
    ppermute x1, starting transfers between devices: 0.66 us -> 3 us  [per_device(): lax.ppermute(jnp.concatenate([inside[EDGE:], across[EDGE:], conv_weight,...]
    all_to_all x1, starting transfers between devices: 11.3 us -> 9.19 us  [per_device(): tap_sums = jnp.sum(lax.all_to_all(tap_rows, 'z', 0, 0, tiled=True), axis=0)]
    unnamed x22 -> x12, local copies, waits for them, and re-layouts: 2.45 us -> 0.71 us
  transfers between devices with their start and end apart: 19 -> 19, of which waited for: 6 -> 6; matrix products, arithmetic and copies ran while one was open for 6% -> 7% of each run, Pallas kernels for 16% -> 18%
where the time goes in v11:
time: 121 us; the launch traced here: 120 us
  starting transfers between devices  61.1 us (50%)
  waiting for transfers between devices  27.2 us (22%)
  Pallas kernels  21.3 us (18%)
  matrix products  3.79 us (3%)
  other arithmetic  3.51 us (3%)
  local copies, waits for them, and re-layouts  2.27 us (2%)
    ppermute x12, starting transfers between devices, rotated(): lax.ppermute(part, CTX, [(i, (i + by) % count) for i in range(count)])  27.7 us
    all_to_all x1, starting transfers between devices, per_device(): tap_sums = jnp.sum(lax.all_to_all(tap_rows, 'z', 0, 0, tiled=True), axis=0)  9.19 us
    all_to_all x1, waiting for transfers between devices, per_device(): tap_sums = jnp.sum(lax.all_to_all(tap_rows, 'z', 0, 0, tiled=True), axis=0)  7.92 us
    all_to_all x1, starting transfers between devices, per_device(): tap_sums = lax.all_to_all(copies, 'z', 0, 0, tiled=True)  7.87 us
    ppermute x1, waiting for transfers between devices, per_device(): lax.ppermute(jnp.concatenate([inside[EDGE:], across[EDGE:], conv_weight,...  7.67 us
    pallas_call x1, Pallas kernels, query_side(): pl.pallas_call(functools.partial(query_kernel, scale), in_specs=[pl.Block...  6.87 us
    pallas_call x1, Pallas kernels, key_side(): pl.pallas_call(functools.partial(key_kernel, scale, last), in_specs=[pl.B...  5.83 us
    all_to_all x1, starting transfers between devices, per_device(): tap_sums = jnp.sum(lax.all_to_all(copies, 'near', 0, 0, tiled=True), axis=0)  5.49 us
  transfers between devices with their start and end apart: 19, of which 6 were waited for; matrix products, arithmetic and copies ran while one was open for 7% of the time, Pallas kernels for 18%

profile of v11, /device:TPU:1, one launch (start us, length us, event | category | flops | bytes accessed | tf_op | source)
XLA Modules:
  0.0 119.9 jit_solution(9026224981960708487)
XLA Ops:
  0.7 3.8 %collective-permute-start.2 = (bf16[192,1024]{1,0:T(8,128)(2,1)}, bf16[192,1024]{1,0:T(8,128)(2,1)S(1)}, u32[]{:S(2)}, u32[]{:S(2)}) collective-permute-start(bf16[192,1024]{1,0:T(8,128)(2,1)} %grad_ref.3), channel_id=1, source_target_pairs={{0,1},{1,0},{2,3},{3,2},{4,5},{5,4},{6,7},{7,6},{8,9},{9,8},{10,11... | collective-permute-start | bytes 1179656 | tf_op jit(solution)/shard_map/ppermute | solution.py:282
  4.5 2.1 %shard_map.110 = (bf16[384,1024]{1,0:T(8,128)(2,1)}, bf16[32,1024]{1,0:T(8,128)(2,1)}, bf16[32,1024]{1,0:T(8,128)(2,1)}) custom-call(s32[1]{0:T(128)} %bitcast.idx_ref, bf16[192,1024]{1,0:T(8,128)(2,1)} %k_ref.1, bf16[192,1024]{1,0:T(8,128)(2,1)} %v_ref.1, bf16[192,1024]{1,0:T(8,128)(2,1)} %input_ref.3, bf16[192,1024]{1,0:T(8,128)(2,1)} %grad_ref.3), custom_call_target="tpu_custom_call" | custom-call | tf_op jit(solution)/shard_map/pallas_call | solution.py:55
  6.6 4.0 %collective-permute-start.1 = (bf16[32,1024]{1,0:T(8,128)(2,1)}, bf16[32,1024]{1,0:T(8,128)(2,1)S(1)}, u32[]{:S(2)}, u32[]{:S(2)}) collective-permute-start(bf16[32,1024]{1,0:T(8,128)(2,1)} %get-tuple-element.22), channel_id=1, source_target_pairs={{0,0},{2,4},{4,2},{6,8},{8,6},{10,12},{12,10},{14,16},{16,14},{18,... | collective-permute-start | bytes 196616 | tf_op jit(solution)/shard_map/ppermute | solution.py:30
  10.7 2.3 %collective-permute-done.1.across_ref = bf16[32,1024]{1,0:T(8,128)(2,1)S(1)} collective-permute-done((bf16[32,1024]{1,0:T(8,128)(2,1)}, bf16[32,1024]{1,0:T(8,128)(2,1)S(1)}, u32[]{:S(2)}, u32[]{:S(2)}) %collective-permute-start.1) | collective-permute-done | bytes 65568 | tf_op jit(solution)/shard_map/ppermute | solution.py:30
  13.0 2.9 %collective-permute-start.4 = (bf16[384,1024]{1,0:T(8,128)(2,1)}, bf16[384,1024]{1,0:T(8,128)(2,1)S(1)}, u32[]{:S(2)}, u32[]{:S(2)}) collective-permute-start(bf16[384,1024]{1,0:T(8,128)(2,1)} %get-tuple-element.25.both0.both_ref), channel_id=1, source_target_pairs={{0,2},{2,4},{4,6},{6,8},{8,10},{10,12},{12,14},{14,16},{16,18},{18... | collective-permute-start | bytes 2359304 | tf_op jit(solution)/shard_map/ppermute | solution.py:24
  16.0 3.0 %collective-permute-start.3 = (bf16[64,1024]{1,0:T(8,128)(2,1)S(1)}, bf16[64,1024]{1,0:T(8,128)(2,1)S(1)}, u32[]{:S(2)}, u32[]{:S(2)}) collective-permute-start(bf16[64,1024]{1,0:T(8,128)(2,1)S(1)} %maximum_maximum_fusion), channel_id=1, source_target_pairs={{0,1},{1,0},{2,3},{3,2},{4,5},{5,4},{6,7},{7,6},{8,9},{9,8},{10,11... | collective-permute-start | bytes 393224 | tf_op jit(solution)/shard_map/ppermute | solution.py:290
  19.0 4.6 %shard_map.111 = (bf16[192,1024]{1,0:T(8,128)(2,1)}, f32[8,32,128]{2,1,0:T(8,128)}) custom-call(s32[1]{0:T(128)} %bitcast.idx_ref, bf16[192,1024]{1,0:T(8,128)(2,1)S(1)} %copy-done, bf16[192,1024]{1,0:T(8,128)(2,1)S(1)} %copy-done.1, bf16[32,1024]{1,0:T(8,128)(2,1)S(1)} %collective-permute-done.inside_ref, ...), custom_call_target="tpu_custom_call" | custom-call | flops 196608 | bytes 12288 | tf_op jit(solution)/shard_map/pallas_call | solution.py:106
  23.6 7.7 %collective-permute-done.3.edges_ref = bf16[64,1024]{1,0:T(8,128)(2,1)S(1)} collective-permute-done((bf16[64,1024]{1,0:T(8,128)(2,1)S(1)}, bf16[64,1024]{1,0:T(8,128)(2,1)S(1)}, u32[]{:S(2)}, u32[]{:S(2)}) %collective-permute-start.3) | collective-permute-done | bytes 131104 | tf_op jit(solution)/shard_map/ppermute | solution.py:290
  31.3 1.9 %shard_map.112 = bf16[192,1024]{1,0:T(8,128)(2,1)S(1)} custom-call(s32[1]{0:T(128)} %bitcast.idx_ref, bf16[192,1024]{1,0:T(8,128)(2,1)S(1)} %collective-permute-done.2.grad_ref, bf16[64,1024]{1,0:T(8,128)(2,1)S(1)} %collective-permute-done.3.edges_ref), custom_call_target="tpu_custom_call" | custom-call | flops 196608 | bytes 12288 | tf_op jit(solution)/shard_map/pallas_call | solution.py:140
  33.2 1.5 %maximum_select_fusion = bf16[192,2048]{1,0:T(8,128)(2,1)S(1)} fusion(bf16[192,1024]{1,0:T(8,128)(2,1)S(1)} %shard_map.112, bf16[192,1024]{1,0:T(8,128)(2,1)} %get-tuple-element.19, pred[]{:T(512)S(6)} %eq.3), kind=kLoop, calls=%fused_computation.1 | loop fusion | flops 3538944 | bytes 1572865 | tf_op jit(solution)/shard_map/jit(_where)/select_n | solution.py:152
  34.7 3.8 %convolution_convert_fusion.do_ref.d0 = bf16[192,1024]{1,0:T(8,128)(2,1)S(1)} fusion(bf16[192,2048]{1,0:T(8,128)(2,1)S(1)} %maximum_select_fusion, bf16[1024,2048]{1,0:T(8,128)(2,1)} %param.13), kind=kOutput, calls=%fused_computation | convolution fusion | flops 805502976 | bytes 5373952 | tf_op jit(solution)/shard_map/dot_general | solution.py:154
  39.1 5.6 %collective-permute-start.10 = (bf16[192,1024]{1,0:T(8,128)(2,1)S(1)}, bf16[192,1024]{1,0:T(8,128)(2,1)}, u32[]{:S(2)}, u32[]{:S(2)}) collective-permute-start(bf16[192,1024]{1,0:T(8,128)(2,1)S(1)} %convolution_convert_fusion.do_ref.d0), channel_id=1, source_target_pairs={{0,254},{2,0},{4,2},{6,4},{8,6},{10,8},{12,10},{14,12},{16,14},{18... | collective-permute-start | bytes 1179656 | tf_op jit(solution)/shard_map/ppermute | solution.py:24
  44.7 2.8 %collective-permute-done.6.both2 = bf16[384,1024]{1,0:T(8,128)(2,1)S(1)} collective-permute-done((bf16[384,1024]{1,0:T(8,128)(2,1)S(1)}, bf16[384,1024]{1,0:T(8,128)(2,1)S(1)}, u32[]{:S(2)}, u32[]{:S(2)}) %collective-permute-start.6) | collective-permute-done | bytes 786464 | tf_op jit(solution)/shard_map/ppermute | solution.py:24
  47.6 2.5 %collective-permute-start.7 = (bf16[384,1024]{1,0:T(8,128)(2,1)S(1)}, bf16[384,1024]{1,0:T(8,128)(2,1)}, u32[]{:S(2)}, u32[]{:S(2)}) collective-permute-start(bf16[384,1024]{1,0:T(8,128)(2,1)S(1)} %collective-permute-done.6.both2), channel_id=1, source_target_pairs={{0,2},{2,4},{4,6},{6,8},{8,10},{10,12},{12,14},{14,16},{16,18},{18... | collective-permute-start | bytes 2359304 | tf_op jit(solution)/shard_map/ppermute | solution.py:24
  50.1 4.4 %collective-permute-start.9 = (bf16[192,1024]{1,0:T(8,128)(2,1)}, bf16[192,1024]{1,0:T(8,128)(2,1)}, u32[]{:S(2)}, u32[]{:S(2)}) collective-permute-start(bf16[192,1024]{1,0:T(8,128)(2,1)} %collective-permute-done.8.q2), channel_id=1, source_target_pairs={{0,254},{2,0},{4,2},{6,4},{8,6},{10,8},{12,10},{14,12},{16,14},{18... | collective-permute-start | bytes 1179656 | tf_op jit(solution)/shard_map/ppermute | solution.py:24
  54.4 6.0 %collective-permute-start.11 = (bf16[192,1024]{1,0:T(8,128)(2,1)}, bf16[192,1024]{1,0:T(8,128)(2,1)}, u32[]{:S(2)}, u32[]{:S(2)}) collective-permute-start(bf16[192,1024]{1,0:T(8,128)(2,1)} %collective-permute-done.10.d1), channel_id=1, source_target_pairs={{0,254},{2,0},{4,2},{6,4},{8,6},{10,8},{12,10},{14,12},{16,14},{18... | collective-permute-start | bytes 1179656 | tf_op jit(solution)/shard_map/ppermute | solution.py:24
  60.4 9.2 %all-to-all-start = ((f32[8,32,128]{2,1,0:T(8,128)}), f32[8,32,128]{2,1,0:T(8,128)}, u32[]{:S(2)}, u32[]{:S(2)}) async-start(f32[8,32,128]{2,1,0:T(8,128)} %get-tuple-element.34), calls=%async_computation | async-start | bytes 262144 | tf_op jit(solution)/shard_map/all_to_all | solution.py:303
  69.6 0.6 collective-permute-start.12
  70.2 7.9 %all-to-all-done = f32[8,32,128]{2,1,0:T(8,128)} async-done(((f32[8,32,128]{2,1,0:T(8,128)}), f32[8,32,128]{2,1,0:T(8,128)}, u32[]{:S(2)}, u32[]{:S(2)}) %all-to-all-start) | async-done | bytes 131104 | tf_op jit(solution)/shard_map/all_to_all | solution.py:303
  78.1 0.9 reduce_sum.18
  79.1 0.7 broadcast_in_dim.10
  79.8 5.5 %all-to-all-start.1 = ((f32[16,32,128]{2,1,0:T(8,128)}), f32[16,32,128]{2,1,0:T(8,128)}, u32[]{:S(2)}, u32[]{:S(2)}) async-start(f32[16,32,128]{2,1,0:T(8,128)} %broadcast_in_dim.10), calls=%async_computation.1 | async-start | bytes 524288 | tf_op jit(solution)/shard_map/all_to_all | solution.py:306
  85.3 6.9 %shard_map.113 = (bf16[192,1024]{1,0:T(8,128)(2,1)}, f32[16,192]{1,0:T(8,128)S(1)}) custom-call(s32[1]{0:T(128)} %bitcast.idx_ref, bf16[192,1024]{1,0:T(8,128)(2,1)S(1)} %copy-done.4, bf16[192,1024]{1,0:T(8,128)(2,1)S(1)} %convolution_convert_fusion.do_ref.d0, bf16[384,1024]{1,0:T(8,128)(2,1)} %collective-permute-done.7.both3, ...), custom_call_target="tpu_custom_call" | custom-call | flops 1509949440 | bytes 4718592 | tf_op jit(solution)/shard_map/pallas_call | solution.py:198
  92.6 3.7 %collective-permute-start.14 = (f32[16,192]{1,0:T(8,128)S(1)}, f32[16,192]{1,0:T(8,128)S(1)}, u32[]{:S(2)}, u32[]{:S(2)}) collective-permute-start(f32[16,192]{1,0:T(8,128)S(1)} %get-tuple-element.30.s0), channel_id=1, source_target_pairs={{0,252},{2,254},{4,0},{6,2},{8,4},{10,6},{12,8},{14,10},{16,12},{1... | collective-permute-start | bytes 36872 | tf_op jit(solution)/shard_map/ppermute | solution.py:24
  96.3 1.0 collective-permute-start.15
  97.4 1.0 reduce_sum.19
  98.4 2.6 %collective-permute-done.15.s3 = f32[16,192]{1,0:T(8,128)S(1)} collective-permute-done((f32[16,192]{1,0:T(8,128)S(1)}, f32[16,192]{1,0:T(8,128)S(1)}, u32[]{:S(2)}, u32[]{:S(2)}) %collective-permute-start.15) | collective-permute-done | bytes 12320 | tf_op jit(solution)/shard_map/ppermute | solution.py:24
  101.0 0.7 broadcast_in_dim.11
  101.6 7.9 %all-to-all-start.2 = ((f32[8,32,128]{2,1,0:T(8,128)}), f32[8,32,128]{2,1,0:T(8,128)S(1)}, u32[]{:S(2)}, u32[]{:S(2)}) async-start(f32[8,32,128]{2,1,0:T(8,128)} %broadcast_in_dim.11), calls=%async_computation.2 | async-start | bytes 262144 | tf_op jit(solution)/shard_map/all_to_all | solution.py:311
  109.5 5.8 %shard_map.114 = (bf16[192,1024]{1,0:T(8,128)(2,1)}, bf16[192,1024]{1,0:T(8,128)(2,1)}) custom-call(s32[1]{0:T(128)} %bitcast.idx_ref, bf16[384,1024]{1,0:T(8,128)(2,1)S(1)} %copy-done.3, bf16[192,1024]{1,0:T(8,128)(2,1)S(1)} %copy-done.4, bf16[192,1024]{1,0:T(8,128)(2,1)S(1)} %collective-permute-done.5.q1, bf16[192,1024]{1,0:T(8,128)(2,1)} %collective-permute-done.8.q2, ...), custom_call_target="tpu_custom_call" | custom-call | flops 1509949440 | bytes 4718592 | tf_op jit(solution)/shard_map/pallas_call | solution.py:255
  115.3 3.8 %all-to-all-done.2 = f32[8,32,128]{2,1,0:T(8,128)S(1)} async-done(((f32[8,32,128]{2,1,0:T(8,128)}), f32[8,32,128]{2,1,0:T(8,128)S(1)}, u32[]{:S(2)}, u32[]{:S(2)}) %all-to-all-start.2) | async-done | bytes 131104 | tf_op jit(solution)/shard_map/all_to_all | solution.py:311
  119.3 0.7 copy.15
  (35 shorter events, 1.5 us)
Async XLA Ops:
  0.6 18.4 %copy-start = (bf16[192,1024]{1,0:T(8,128)(2,1)S(1)}, bf16[192,1024]{1,0:T(8,128)(2,1)}, u32[]{:S(2)}) copy-start(bf16[192,1024]{1,0:T(8,128)(2,1)} %grad_ref.3) | copy-start | bytes 1179652
  0.6 18.4 %copy-start.1 = (bf16[192,1024]{1,0:T(8,128)(2,1)S(1)}, bf16[192,1024]{1,0:T(8,128)(2,1)}, u32[]{:S(2)}) copy-start(bf16[192,1024]{1,0:T(8,128)(2,1)} %input_ref.3) | copy-start | bytes 1179652
  0.7 15.3 %copy-start.2 = (bf16[31,1024]{1,0:T(8,128)(2,1)S(1)}, bf16[31,1024]{1,0:T(8,128)(2,1)}, u32[]{:S(2)}) copy-start(bf16[31,1024]{1,0:T(8,128)(2,1)} %taps_ref.1) | copy-start | bytes 190468
  0.7 18.4 %copy-start.4 = (bf16[192,1024]{1,0:T(8,128)(2,1)S(1)}, bf16[192,1024]{1,0:T(8,128)(2,1)}, u32[]{:S(2)}) copy-start(bf16[192,1024]{1,0:T(8,128)(2,1)} %q0.1) | copy-start | bytes 1179652
  0.7 12.3 %collective-permute-start.2 = (bf16[192,1024]{1,0:T(8,128)(2,1)}, bf16[192,1024]{1,0:T(8,128)(2,1)S(1)}, u32[]{:S(2)}, u32[]{:S(2)}) collective-permute-start(bf16[192,1024]{1,0:T(8,128)(2,1)} %grad_ref.3), channel_id=1, source_target_pairs={{0,1},{1,0},{2,3},{3,2},{4,5},{5,4},{6,7},{7,6},{8,9},{9,8},{10,11... | collective-permute-start | bytes 1179656 | tf_op jit(solution)/shard_map/ppermute | solution.py:282
  6.6 6.4 %collective-permute-start.1 = (bf16[32,1024]{1,0:T(8,128)(2,1)}, bf16[32,1024]{1,0:T(8,128)(2,1)S(1)}, u32[]{:S(2)}, u32[]{:S(2)}) collective-permute-start(bf16[32,1024]{1,0:T(8,128)(2,1)} %get-tuple-element.22), channel_id=1, source_target_pairs={{0,0},{2,4},{4,2},{6,8},{8,6},{10,12},{12,10},{14,16},{16,14},{18,... | collective-permute-start | bytes 196616 | tf_op jit(solution)/shard_map/ppermute | solution.py:30
  10.6 2.4 %collective-permute-start = (bf16[32,1024]{1,0:T(8,128)(2,1)}, bf16[32,1024]{1,0:T(8,128)(2,1)S(1)}, u32[]{:S(2)}, u32[]{:S(2)}) collective-permute-start(bf16[32,1024]{1,0:T(8,128)(2,1)} %get-tuple-element.21), channel_id=1, source_target_pairs={{0,2},{2,0},{4,6},{6,4},{8,10},{10,8},{12,14},{14,12},{16,18},{18,... | collective-permute-start | bytes 196616 | tf_op jit(solution)/shard_map/ppermute | solution.py:30
  13.0 25.5 %collective-permute-start.4 = (bf16[384,1024]{1,0:T(8,128)(2,1)}, bf16[384,1024]{1,0:T(8,128)(2,1)S(1)}, u32[]{:S(2)}, u32[]{:S(2)}) collective-permute-start(bf16[384,1024]{1,0:T(8,128)(2,1)} %get-tuple-element.25.both0.both_ref), channel_id=1, source_target_pairs={{0,2},{2,4},{4,6},{6,8},{8,10},{10,12},{12,14},{14,16},{16,18},{18... | collective-permute-start | bytes 2359304 | tf_op jit(solution)/shard_map/ppermute | solution.py:24
  16.0 15.3 %collective-permute-start.3 = (bf16[64,1024]{1,0:T(8,128)(2,1)S(1)}, bf16[64,1024]{1,0:T(8,128)(2,1)S(1)}, u32[]{:S(2)}, u32[]{:S(2)}) collective-permute-start(bf16[64,1024]{1,0:T(8,128)(2,1)S(1)} %maximum_maximum_fusion), channel_id=1, source_target_pairs={{0,1},{1,0},{2,3},{3,2},{4,5},{5,4},{6,7},{7,6},{8,9},{9,8},{10,11... | collective-permute-start | bytes 393224 | tf_op jit(solution)/shard_map/ppermute | solution.py:290
  19.0 19.5 %collective-permute-start.5 = (bf16[192,1024]{1,0:T(8,128)(2,1)S(1)}, bf16[192,1024]{1,0:T(8,128)(2,1)S(1)}, u32[]{:S(2)}, u32[]{:S(2)}) collective-permute-start(bf16[192,1024]{1,0:T(8,128)(2,1)S(1)} %copy-done.4), channel_id=1, source_target_pairs={{0,254},{2,0},{4,2},{6,4},{8,6},{10,8},{12,10},{14,12},{16,14},{18... | collective-permute-start | bytes 1179656 | tf_op jit(solution)/shard_map/ppermute | solution.py:24
  34.7 50.5 %copy-start.3 = (bf16[384,1024]{1,0:T(8,128)(2,1)S(1)}, bf16[384,1024]{1,0:T(8,128)(2,1)}, u32[]{:S(2)}) copy-start(bf16[384,1024]{1,0:T(8,128)(2,1)} %get-tuple-element.25.both0.both_ref) | copy-start | bytes 2359300
  38.6 9.0 %collective-permute-start.6 = (bf16[384,1024]{1,0:T(8,128)(2,1)S(1)}, bf16[384,1024]{1,0:T(8,128)(2,1)S(1)}, u32[]{:S(2)}, u32[]{:S(2)}) collective-permute-start(bf16[384,1024]{1,0:T(8,128)(2,1)S(1)} %collective-permute-done.4.both1), channel_id=1, source_target_pairs={{0,2},{2,4},{4,6},{6,8},{8,10},{10,12},{12,14},{14,16},{16,18},{18... | collective-permute-start | bytes 2359304 | tf_op jit(solution)/shard_map/ppermute | solution.py:24
  38.7 11.4 %collective-permute-start.8 = (bf16[192,1024]{1,0:T(8,128)(2,1)S(1)}, bf16[192,1024]{1,0:T(8,128)(2,1)}, u32[]{:S(2)}, u32[]{:S(2)}) collective-permute-start(bf16[192,1024]{1,0:T(8,128)(2,1)S(1)} %collective-permute-done.5.q1), channel_id=1, source_target_pairs={{0,254},{2,0},{4,2},{6,4},{8,6},{10,8},{12,10},{14,12},{16,14},{18... | collective-permute-start | bytes 1179656 | tf_op jit(solution)/shard_map/ppermute | solution.py:24
  39.1 15.3 %collective-permute-start.10 = (bf16[192,1024]{1,0:T(8,128)(2,1)S(1)}, bf16[192,1024]{1,0:T(8,128)(2,1)}, u32[]{:S(2)}, u32[]{:S(2)}) collective-permute-start(bf16[192,1024]{1,0:T(8,128)(2,1)S(1)} %convolution_convert_fusion.do_ref.d0), channel_id=1, source_target_pairs={{0,254},{2,0},{4,2},{6,4},{8,6},{10,8},{12,10},{14,12},{16,14},{18... | collective-permute-start | bytes 1179656 | tf_op jit(solution)/shard_map/ppermute | solution.py:24
  47.6 31.5 %collective-permute-start.7 = (bf16[384,1024]{1,0:T(8,128)(2,1)S(1)}, bf16[384,1024]{1,0:T(8,128)(2,1)}, u32[]{:S(2)}, u32[]{:S(2)}) collective-permute-start(bf16[384,1024]{1,0:T(8,128)(2,1)S(1)} %collective-permute-done.6.both2), channel_id=1, source_target_pairs={{0,2},{2,4},{4,6},{6,8},{8,10},{10,12},{12,14},{14,16},{16,18},{18... | collective-permute-start | bytes 2359304 | tf_op jit(solution)/shard_map/ppermute | solution.py:24
  50.1 19.5 %collective-permute-start.9 = (bf16[192,1024]{1,0:T(8,128)(2,1)}, bf16[192,1024]{1,0:T(8,128)(2,1)}, u32[]{:S(2)}, u32[]{:S(2)}) collective-permute-start(bf16[192,1024]{1,0:T(8,128)(2,1)} %collective-permute-done.8.q2), channel_id=1, source_target_pairs={{0,254},{2,0},{4,2},{6,4},{8,6},{10,8},{12,10},{14,12},{16,14},{18... | collective-permute-start | bytes 1179656 | tf_op jit(solution)/shard_map/ppermute | solution.py:24
  54.4 15.2 %collective-permute-start.11 = (bf16[192,1024]{1,0:T(8,128)(2,1)}, bf16[192,1024]{1,0:T(8,128)(2,1)}, u32[]{:S(2)}, u32[]{:S(2)}) collective-permute-start(bf16[192,1024]{1,0:T(8,128)(2,1)} %collective-permute-done.10.d1), channel_id=1, source_target_pairs={{0,254},{2,0},{4,2},{6,4},{8,6},{10,8},{12,10},{14,12},{16,14},{18... | collective-permute-start | bytes 1179656 | tf_op jit(solution)/shard_map/ppermute | solution.py:24
  60.4 17.7 %all-to-all-start = ((f32[8,32,128]{2,1,0:T(8,128)}), f32[8,32,128]{2,1,0:T(8,128)}, u32[]{:S(2)}, u32[]{:S(2)}) async-start(f32[8,32,128]{2,1,0:T(8,128)} %get-tuple-element.34), calls=%async_computation | async-start | bytes 262144 | tf_op jit(solution)/shard_map/all_to_all | solution.py:303
  69.6 28.7 %collective-permute-start.12 = (bf16[192,1024]{1,0:T(8,128)(2,1)}, bf16[192,1024]{1,0:T(8,128)(2,1)}, u32[]{:S(2)}, u32[]{:S(2)}) collective-permute-start(bf16[192,1024]{1,0:T(8,128)(2,1)} %collective-permute-done.11.d2), channel_id=1, source_target_pairs={{0,254},{2,0},{4,2},{6,4},{8,6},{10,8},{12,10},{14,12},{16,14},{18... | collective-permute-start | bytes 1179656 | tf_op jit(solution)/shard_map/ppermute | solution.py:24
  79.8 17.6 %all-to-all-start.1 = ((f32[16,32,128]{2,1,0:T(8,128)}), f32[16,32,128]{2,1,0:T(8,128)}, u32[]{:S(2)}, u32[]{:S(2)}) async-start(f32[16,32,128]{2,1,0:T(8,128)} %broadcast_in_dim.10), calls=%async_computation.1 | async-start | bytes 524288 | tf_op jit(solution)/shard_map/all_to_all | solution.py:306
  92.2 6.2 %collective-permute-start.13 = (f32[16,192]{1,0:T(8,128)S(1)}, f32[16,192]{1,0:T(8,128)S(1)}, u32[]{:S(2)}, u32[]{:S(2)}) collective-permute-start(f32[16,192]{1,0:T(8,128)S(1)} %get-tuple-element.30.s0), channel_id=1, source_target_pairs={{0,254},{2,0},{4,2},{6,4},{8,6},{10,8},{12,10},{14,12},{16,14},{18... | collective-permute-start | bytes 36872 | tf_op jit(solution)/shard_map/ppermute | solution.py:24
  92.6 5.7 %collective-permute-start.14 = (f32[16,192]{1,0:T(8,128)S(1)}, f32[16,192]{1,0:T(8,128)S(1)}, u32[]{:S(2)}, u32[]{:S(2)}) collective-permute-start(f32[16,192]{1,0:T(8,128)S(1)} %get-tuple-element.30.s0), channel_id=1, source_target_pairs={{0,252},{2,254},{4,0},{6,2},{8,4},{10,6},{12,8},{14,10},{16,12},{1... | collective-permute-start | bytes 36872 | tf_op jit(solution)/shard_map/ppermute | solution.py:24
  96.3 4.7 %collective-permute-start.15 = (f32[16,192]{1,0:T(8,128)S(1)}, f32[16,192]{1,0:T(8,128)S(1)}, u32[]{:S(2)}, u32[]{:S(2)}) collective-permute-start(f32[16,192]{1,0:T(8,128)S(1)} %get-tuple-element.30.s0), channel_id=1, source_target_pairs={{0,250},{2,252},{4,254},{6,0},{8,2},{10,4},{12,6},{14,8},{16,10},{... | collective-permute-start | bytes 36872 | tf_op jit(solution)/shard_map/ppermute | solution.py:24
  101.6 17.5 %all-to-all-start.2 = ((f32[8,32,128]{2,1,0:T(8,128)}), f32[8,32,128]{2,1,0:T(8,128)S(1)}, u32[]{:S(2)}, u32[]{:S(2)}) async-start(f32[8,32,128]{2,1,0:T(8,128)} %broadcast_in_dim.11), calls=%async_computation.2 | async-start | bytes 262144 | tf_op jit(solution)/shard_map/all_to_all | solution.py:311

commit v12 on v11

--- a/solution.py
+++ b/solution.py
@@ -21,7 +21,7 @@
 
 def rotated(part, by):
     count = lax.axis_size(CTX)
-    return lax.ppermute(part, CTX, [(i, (i + by) % count) for i in range(count)])
+    return lax.ppermute(part, CTX, [(i, i + by) for i in range(count) if 0 <= i + by < count])
 
 
 def swapped(part, first):

time: 121 us -> 134 us (1.11)
  starting transfers between devices: 61.1 us -> 74 us
    all_to_all x1, starting transfers between devices: 9.19 us -> 20.3 us  [per_device(): tap_sums = jnp.sum(lax.all_to_all(tap_rows, 'z', 0, 0, tiled=True), axis=0)]
    ppermute x12, waiting for transfers between devices: 5.49 us -> 9.7 us  [rotated(): lax.ppermute(part, CTX, [(i, i + by) for i in range(count) if 0 <= i + by...]
    ppermute x1, waiting for transfers between devices: 7.67 us -> 4.88 us  [per_device(): lax.ppermute(jnp.concatenate([inside[EDGE:], across[EDGE:], conv_weight,...]
    all_to_all x1, waiting for transfers between devices: 7.92 us -> 6.39 us  [per_device(): tap_sums = jnp.sum(lax.all_to_all(tap_rows, 'z', 0, 0, tiled=True), axis=0)]
  transfers between devices with their start and end apart: 19 -> 19, of which waited for: 6 -> 7; matrix products, arithmetic and copies ran while one was open for 7% -> 6% of each run, Pallas kernels for 18% -> 16%
where the time goes in v12:
time: 134 us; the launch traced here: 133 us
  starting transfers between devices  74 us (55%)
  waiting for transfers between devices  27 us (20%)
  Pallas kernels  21.3 us (16%)
  matrix products  3.79 us (3%)
  other arithmetic  3.51 us (3%)
  local copies, waits for them, and re-layouts  2.27 us (2%)
    ppermute x12, starting transfers between devices, rotated(): lax.ppermute(part, CTX, [(i, i + by) for i in range(count) if 0 <= i + by...  28.2 us
    all_to_all x1, starting transfers between devices, per_device(): tap_sums = jnp.sum(lax.all_to_all(tap_rows, 'z', 0, 0, tiled=True), axis=0)  20.3 us
    ppermute x12, waiting for transfers between devices, rotated(): lax.ppermute(part, CTX, [(i, i + by) for i in range(count) if 0 <= i + by...  9.7 us
    all_to_all x1, starting transfers between devices, per_device(): tap_sums = lax.all_to_all(copies, 'z', 0, 0, tiled=True)  9.15 us
    pallas_call x1, Pallas kernels, query_side(): pl.pallas_call(functools.partial(query_kernel, scale), in_specs=[pl.Block...  6.86 us
    all_to_all x1, waiting for transfers between devices, per_device(): tap_sums = jnp.sum(lax.all_to_all(tap_rows, 'z', 0, 0, tiled=True), axis=0)  6.39 us
    pallas_call x1, Pallas kernels, key_side(): pl.pallas_call(functools.partial(key_kernel, scale, last), in_specs=[pl.B...  5.83 us
    all_to_all x1, starting transfers between devices, per_device(): tap_sums = jnp.sum(lax.all_to_all(copies, 'near', 0, 0, tiled=True), axis=0)  5.43 us
  transfers between devices with their start and end apart: 19, of which 7 were waited for; matrix products, arithmetic and copies ran while one was open for 6% of the time, Pallas kernels for 16%

profile of v12, /device:TPU:1, one launch (start us, length us, event | category | flops | bytes accessed | tf_op | source)
XLA Modules:
  0.0 132.8 jit_solution(15582812992653075333)
XLA Ops:
  0.7 3.8 %collective-permute-start.2 = (bf16[192,1024]{1,0:T(8,128)(2,1)}, bf16[192,1024]{1,0:T(8,128)(2,1)S(1)}, u32[]{:S(2)}, u32[]{:S(2)}) collective-permute-start(bf16[192,1024]{1,0:T(8,128)(2,1)} %grad_ref.3), channel_id=1, source_target_pairs={{0,1},{1,0},{2,3},{3,2},{4,5},{5,4},{6,7},{7,6},{8,9},{9,8},{10,11... | collective-permute-start | bytes 1179656 | tf_op jit(solution)/shard_map/ppermute | solution.py:282
  4.5 2.1 %shard_map.110 = (bf16[384,1024]{1,0:T(8,128)(2,1)}, bf16[32,1024]{1,0:T(8,128)(2,1)}, bf16[32,1024]{1,0:T(8,128)(2,1)}) custom-call(s32[1]{0:T(128)} %bitcast.idx_ref, bf16[192,1024]{1,0:T(8,128)(2,1)} %k_ref.1, bf16[192,1024]{1,0:T(8,128)(2,1)} %v_ref.1, bf16[192,1024]{1,0:T(8,128)(2,1)} %input_ref.3, bf16[192,1024]{1,0:T(8,128)(2,1)} %grad_ref.3), custom_call_target="tpu_custom_call" | custom-call | tf_op jit(solution)/shard_map/pallas_call | solution.py:55
  6.6 4.0 %collective-permute-start.1 = (bf16[32,1024]{1,0:T(8,128)(2,1)}, bf16[32,1024]{1,0:T(8,128)(2,1)S(1)}, u32[]{:S(2)}, u32[]{:S(2)}) collective-permute-start(bf16[32,1024]{1,0:T(8,128)(2,1)} %get-tuple-element.22), channel_id=1, source_target_pairs={{0,0},{2,4},{4,2},{6,8},{8,6},{10,12},{12,10},{14,16},{16,14},{18,... | collective-permute-start | bytes 196616 | tf_op jit(solution)/shard_map/ppermute | solution.py:30
  10.7 2.3 %collective-permute-done.1.across_ref = bf16[32,1024]{1,0:T(8,128)(2,1)S(1)} collective-permute-done((bf16[32,1024]{1,0:T(8,128)(2,1)}, bf16[32,1024]{1,0:T(8,128)(2,1)S(1)}, u32[]{:S(2)}, u32[]{:S(2)}) %collective-permute-start.1) | collective-permute-done | bytes 65568 | tf_op jit(solution)/shard_map/ppermute | solution.py:30
  13.0 4.8 %collective-permute-start.4 = (bf16[384,1024]{1,0:T(8,128)(2,1)}, bf16[384,1024]{1,0:T(8,128)(2,1)S(1)}, u32[]{:S(2)}, u32[]{:S(2)}) collective-permute-start(bf16[384,1024]{1,0:T(8,128)(2,1)} %get-tuple-element.25.both0.both_ref), channel_id=1, source_target_pairs={{0,2},{2,4},{4,6},{6,8},{8,10},{10,12},{12,14},{14,16},{16,18},{18... | collective-permute-start | bytes 2359304 | tf_op jit(solution)/shard_map/ppermute | solution.py:24
  17.9 3.0 %collective-permute-start.3 = (bf16[64,1024]{1,0:T(8,128)(2,1)S(1)}, bf16[64,1024]{1,0:T(8,128)(2,1)S(1)}, u32[]{:S(2)}, u32[]{:S(2)}) collective-permute-start(bf16[64,1024]{1,0:T(8,128)(2,1)S(1)} %maximum_maximum_fusion), channel_id=1, source_target_pairs={{0,1},{1,0},{2,3},{3,2},{4,5},{5,4},{6,7},{7,6},{8,9},{9,8},{10,11... | collective-permute-start | bytes 393224 | tf_op jit(solution)/shard_map/ppermute | solution.py:290
  20.9 1.9 %collective-permute-start.5 = (bf16[192,1024]{1,0:T(8,128)(2,1)S(1)}, bf16[192,1024]{1,0:T(8,128)(2,1)S(1)}, u32[]{:S(2)}, u32[]{:S(2)}) collective-permute-start(bf16[192,1024]{1,0:T(8,128)(2,1)S(1)} %copy-done.4), channel_id=1, source_target_pairs={{2,0},{4,2},{6,4},{8,6},{10,8},{12,10},{14,12},{16,14},{18,16},{20... | collective-permute-start | bytes 1179656 | tf_op jit(solution)/shard_map/ppermute | solution.py:24
  22.9 4.6 %shard_map.111 = (bf16[192,1024]{1,0:T(8,128)(2,1)}, f32[8,32,128]{2,1,0:T(8,128)}) custom-call(s32[1]{0:T(128)} %bitcast.idx_ref, bf16[192,1024]{1,0:T(8,128)(2,1)S(1)} %copy-done, bf16[192,1024]{1,0:T(8,128)(2,1)S(1)} %copy-done.1, bf16[32,1024]{1,0:T(8,128)(2,1)S(1)} %collective-permute-done.inside_ref, ...), custom_call_target="tpu_custom_call" | custom-call | flops 196608 | bytes 12288 | tf_op jit(solution)/shard_map/pallas_call | solution.py:106
  27.5 4.9 %collective-permute-done.3.edges_ref = bf16[64,1024]{1,0:T(8,128)(2,1)S(1)} collective-permute-done((bf16[64,1024]{1,0:T(8,128)(2,1)S(1)}, bf16[64,1024]{1,0:T(8,128)(2,1)S(1)}, u32[]{:S(2)}, u32[]{:S(2)}) %collective-permute-start.3) | collective-permute-done | bytes 131104 | tf_op jit(solution)/shard_map/ppermute | solution.py:290
  32.3 1.9 %shard_map.112 = bf16[192,1024]{1,0:T(8,128)(2,1)S(1)} custom-call(s32[1]{0:T(128)} %bitcast.idx_ref, bf16[192,1024]{1,0:T(8,128)(2,1)S(1)} %collective-permute-done.2.grad_ref, bf16[64,1024]{1,0:T(8,128)(2,1)S(1)} %collective-permute-done.3.edges_ref), custom_call_target="tpu_custom_call" | custom-call | flops 196608 | bytes 12288 | tf_op jit(solution)/shard_map/pallas_call | solution.py:140
  34.3 1.5 %maximum_select_fusion = bf16[192,2048]{1,0:T(8,128)(2,1)S(1)} fusion(bf16[192,1024]{1,0:T(8,128)(2,1)S(1)} %shard_map.112, bf16[192,1024]{1,0:T(8,128)(2,1)} %get-tuple-element.19, pred[]{:T(512)S(6)} %eq.3), kind=kLoop, calls=%fused_computation.1 | loop fusion | flops 3538944 | bytes 1572865 | tf_op jit(solution)/shard_map/jit(_where)/select_n | solution.py:152
  35.8 3.8 %convolution_convert_fusion.do_ref.d0 = bf16[192,1024]{1,0:T(8,128)(2,1)S(1)} fusion(bf16[192,2048]{1,0:T(8,128)(2,1)S(1)} %maximum_select_fusion, bf16[1024,2048]{1,0:T(8,128)(2,1)} %param.13), kind=kOutput, calls=%fused_computation | convolution fusion | flops 805502976 | bytes 5373952 | tf_op jit(solution)/shard_map/dot_general | solution.py:154
  39.6 1.9 %collective-permute-start.6 = (bf16[384,1024]{1,0:T(8,128)(2,1)S(1)}, bf16[384,1024]{1,0:T(8,128)(2,1)S(1)}, u32[]{:S(2)}, u32[]{:S(2)}) collective-permute-start(bf16[384,1024]{1,0:T(8,128)(2,1)S(1)} %collective-permute-done.4.both1), channel_id=1, source_target_pairs={{0,2},{2,4},{4,6},{6,8},{8,10},{10,12},{12,14},{14,16},{16,18},{18... | collective-permute-start | bytes 2359304 | tf_op jit(solution)/shard_map/ppermute | solution.py:24
  41.5 2.5 %collective-permute-start.8 = (bf16[192,1024]{1,0:T(8,128)(2,1)S(1)}, bf16[192,1024]{1,0:T(8,128)(2,1)}, u32[]{:S(2)}, u32[]{:S(2)}) collective-permute-start(bf16[192,1024]{1,0:T(8,128)(2,1)S(1)} %collective-permute-done.5.q1), channel_id=1, source_target_pairs={{2,0},{4,2},{6,4},{8,6},{10,8},{12,10},{14,12},{16,14},{18,16},{20... | collective-permute-start | bytes 1179656 | tf_op jit(solution)/shard_map/ppermute | solution.py:24
  44.0 1.9 %collective-permute-start.10 = (bf16[192,1024]{1,0:T(8,128)(2,1)S(1)}, bf16[192,1024]{1,0:T(8,128)(2,1)}, u32[]{:S(2)}, u32[]{:S(2)}) collective-permute-start(bf16[192,1024]{1,0:T(8,128)(2,1)S(1)} %convolution_convert_fusion.do_ref.d0), channel_id=1, source_target_pairs={{2,0},{4,2},{6,4},{8,6},{10,8},{12,10},{14,12},{16,14},{18,16},{20... | collective-permute-start | bytes 1179656 | tf_op jit(solution)/shard_map/ppermute | solution.py:24
  45.9 4.5 %collective-permute-done.6.both2 = bf16[384,1024]{1,0:T(8,128)(2,1)S(1)} collective-permute-done((bf16[384,1024]{1,0:T(8,128)(2,1)S(1)}, bf16[384,1024]{1,0:T(8,128)(2,1)S(1)}, u32[]{:S(2)}, u32[]{:S(2)}) %collective-permute-start.6) | collective-permute-done | bytes 786464 | tf_op jit(solution)/shard_map/ppermute | solution.py:24
  50.4 4.4 %collective-permute-start.7 = (bf16[384,1024]{1,0:T(8,128)(2,1)S(1)}, bf16[384,1024]{1,0:T(8,128)(2,1)}, u32[]{:S(2)}, u32[]{:S(2)}) collective-permute-start(bf16[384,1024]{1,0:T(8,128)(2,1)S(1)} %collective-permute-done.6.both2), channel_id=1, source_target_pairs={{0,2},{2,4},{4,6},{6,8},{8,10},{10,12},{12,14},{14,16},{16,18},{18... | collective-permute-start | bytes 2359304 | tf_op jit(solution)/shard_map/ppermute | solution.py:24
  54.8 1.9 %collective-permute-start.9 = (bf16[192,1024]{1,0:T(8,128)(2,1)}, bf16[192,1024]{1,0:T(8,128)(2,1)}, u32[]{:S(2)}, u32[]{:S(2)}) collective-permute-start(bf16[192,1024]{1,0:T(8,128)(2,1)} %collective-permute-done.8.q2), channel_id=1, source_target_pairs={{2,0},{4,2},{6,4},{8,6},{10,8},{12,10},{14,12},{16,14},{18,16},{20... | collective-permute-start | bytes 1179656 | tf_op jit(solution)/shard_map/ppermute | solution.py:24
  56.8 1.9 %collective-permute-start.11 = (bf16[192,1024]{1,0:T(8,128)(2,1)}, bf16[192,1024]{1,0:T(8,128)(2,1)}, u32[]{:S(2)}, u32[]{:S(2)}) collective-permute-start(bf16[192,1024]{1,0:T(8,128)(2,1)} %collective-permute-done.10.d1), channel_id=1, source_target_pairs={{2,0},{4,2},{6,4},{8,6},{10,8},{12,10},{14,12},{16,14},{18,16},{20... | collective-permute-start | bytes 1179656 | tf_op jit(solution)/shard_map/ppermute | solution.py:24
  58.7 20.3 %all-to-all-start = ((f32[8,32,128]{2,1,0:T(8,128)}), f32[8,32,128]{2,1,0:T(8,128)}, u32[]{:S(2)}, u32[]{:S(2)}) async-start(f32[8,32,128]{2,1,0:T(8,128)} %get-tuple-element.34), calls=%async_computation | async-start | bytes 262144 | tf_op jit(solution)/shard_map/all_to_all | solution.py:303
  79.0 2.2 %collective-permute-start.12 = (bf16[192,1024]{1,0:T(8,128)(2,1)}, bf16[192,1024]{1,0:T(8,128)(2,1)}, u32[]{:S(2)}, u32[]{:S(2)}) collective-permute-start(bf16[192,1024]{1,0:T(8,128)(2,1)} %collective-permute-done.11.d2), channel_id=1, source_target_pairs={{2,0},{4,2},{6,4},{8,6},{10,8},{12,10},{14,12},{16,14},{18,16},{20... | collective-permute-start | bytes 1179656 | tf_op jit(solution)/shard_map/ppermute | solution.py:24
  81.2 6.4 %all-to-all-done = f32[8,32,128]{2,1,0:T(8,128)} async-done(((f32[8,32,128]{2,1,0:T(8,128)}), f32[8,32,128]{2,1,0:T(8,128)}, u32[]{:S(2)}, u32[]{:S(2)}) %all-to-all-start) | async-done | bytes 131104 | tf_op jit(solution)/shard_map/all_to_all | solution.py:303
  89.3 5.4 %all-to-all-start.1 = ((f32[16,32,128]{2,1,0:T(8,128)}), f32[16,32,128]{2,1,0:T(8,128)}, u32[]{:S(2)}, u32[]{:S(2)}) async-start(f32[16,32,128]{2,1,0:T(8,128)} %broadcast_in_dim.10), calls=%async_computation.1 | async-start | bytes 524288 | tf_op jit(solution)/shard_map/all_to_all | solution.py:306
  94.7 6.9 %shard_map.113 = (bf16[192,1024]{1,0:T(8,128)(2,1)}, f32[16,192]{1,0:T(8,128)S(1)}) custom-call(s32[1]{0:T(128)} %bitcast.idx_ref, bf16[192,1024]{1,0:T(8,128)(2,1)S(1)} %copy-done.4, bf16[192,1024]{1,0:T(8,128)(2,1)S(1)} %convolution_convert_fusion.do_ref.d0, bf16[384,1024]{1,0:T(8,128)(2,1)} %collective-permute-done.7.both3, ...), custom_call_target="tpu_custom_call" | custom-call | flops 1509949440 | bytes 4718592 | tf_op jit(solution)/shard_map/pallas_call | solution.py:198
  101.6 2.2 %collective-permute-start.13 = (f32[16,192]{1,0:T(8,128)S(1)}, f32[16,192]{1,0:T(8,128)S(1)}, u32[]{:S(2)}, u32[]{:S(2)}) collective-permute-start(f32[16,192]{1,0:T(8,128)S(1)} %get-tuple-element.30.s0), channel_id=1, source_target_pairs={{2,0},{4,2},{6,4},{8,6},{10,8},{12,10},{14,12},{16,14},{18,16},{20... | collective-permute-start | bytes 36872 | tf_op jit(solution)/shard_map/ppermute | solution.py:24
  103.8 1.3 collective-permute-start.14
  105.1 1.3 collective-permute-start.15
  106.4 1.0 reduce_sum.19
  108.3 4.3 %collective-permute-done.15.s3 = f32[16,192]{1,0:T(8,128)S(1)} collective-permute-done((f32[16,192]{1,0:T(8,128)S(1)}, f32[16,192]{1,0:T(8,128)S(1)}, u32[]{:S(2)}, u32[]{:S(2)}) %collective-permute-start.15) | collective-permute-done | bytes 12320 | tf_op jit(solution)/shard_map/ppermute | solution.py:24
  113.2 9.1 %all-to-all-start.2 = ((f32[8,32,128]{2,1,0:T(8,128)}), f32[8,32,128]{2,1,0:T(8,128)S(1)}, u32[]{:S(2)}, u32[]{:S(2)}) async-start(f32[8,32,128]{2,1,0:T(8,128)} %broadcast_in_dim.11), calls=%async_computation.2 | async-start | bytes 262144 | tf_op jit(solution)/shard_map/all_to_all | solution.py:311
  122.4 5.8 %shard_map.114 = (bf16[192,1024]{1,0:T(8,128)(2,1)}, bf16[192,1024]{1,0:T(8,128)(2,1)}) custom-call(s32[1]{0:T(128)} %bitcast.idx_ref, bf16[384,1024]{1,0:T(8,128)(2,1)S(1)} %copy-done.3, bf16[192,1024]{1,0:T(8,128)(2,1)S(1)} %copy-done.4, bf16[192,1024]{1,0:T(8,128)(2,1)S(1)} %collective-permute-done.5.q1, bf16[192,1024]{1,0:T(8,128)(2,1)} %collective-permute-done.8.q2, ...), custom_call_target="tpu_custom_call" | custom-call | flops 1509949440 | bytes 4718592 | tf_op jit(solution)/shard_map/pallas_call | solution.py:255
  128.2 3.8 %all-to-all-done.2 = f32[8,32,128]{2,1,0:T(8,128)S(1)} async-done(((f32[8,32,128]{2,1,0:T(8,128)}), f32[8,32,128]{2,1,0:T(8,128)S(1)}, u32[]{:S(2)}, u32[]{:S(2)}) %all-to-all-start.2) | async-done | bytes 131104 | tf_op jit(solution)/shard_map/all_to_all | solution.py:311
  (35 shorter events, 4.3 us)
Async XLA Ops:
  0.6 22.2 %copy-start = (bf16[192,1024]{1,0:T(8,128)(2,1)S(1)}, bf16[192,1024]{1,0:T(8,128)(2,1)}, u32[]{:S(2)}) copy-start(bf16[192,1024]{1,0:T(8,128)(2,1)} %grad_ref.3) | copy-start | bytes 1179652
  0.6 22.2 %copy-start.1 = (bf16[192,1024]{1,0:T(8,128)(2,1)S(1)}, bf16[192,1024]{1,0:T(8,128)(2,1)}, u32[]{:S(2)}) copy-start(bf16[192,1024]{1,0:T(8,128)(2,1)} %input_ref.3) | copy-start | bytes 1179652
  0.7 17.2 %copy-start.2 = (bf16[31,1024]{1,0:T(8,128)(2,1)S(1)}, bf16[31,1024]{1,0:T(8,128)(2,1)}, u32[]{:S(2)}) copy-start(bf16[31,1024]{1,0:T(8,128)(2,1)} %taps_ref.1) | copy-start | bytes 190468
  0.7 20.3 %copy-start.4 = (bf16[192,1024]{1,0:T(8,128)(2,1)S(1)}, bf16[192,1024]{1,0:T(8,128)(2,1)}, u32[]{:S(2)}) copy-start(bf16[192,1024]{1,0:T(8,128)(2,1)} %q0.1) | copy-start | bytes 1179652
  0.7 12.3 %collective-permute-start.2 = (bf16[192,1024]{1,0:T(8,128)(2,1)}, bf16[192,1024]{1,0:T(8,128)(2,1)S(1)}, u32[]{:S(2)}, u32[]{:S(2)}) collective-permute-start(bf16[192,1024]{1,0:T(8,128)(2,1)} %grad_ref.3), channel_id=1, source_target_pairs={{0,1},{1,0},{2,3},{3,2},{4,5},{5,4},{6,7},{7,6},{8,9},{9,8},{10,11... | collective-permute-start | bytes 1179656 | tf_op jit(solution)/shard_map/ppermute | solution.py:282
  6.6 6.4 %collective-permute-start.1 = (bf16[32,1024]{1,0:T(8,128)(2,1)}, bf16[32,1024]{1,0:T(8,128)(2,1)S(1)}, u32[]{:S(2)}, u32[]{:S(2)}) collective-permute-start(bf16[32,1024]{1,0:T(8,128)(2,1)} %get-tuple-element.22), channel_id=1, source_target_pairs={{0,0},{2,4},{4,2},{6,8},{8,6},{10,12},{12,10},{14,16},{16,14},{18,... | collective-permute-start | bytes 196616 | tf_op jit(solution)/shard_map/ppermute | solution.py:30
  10.6 2.4 %collective-permute-start = (bf16[32,1024]{1,0:T(8,128)(2,1)}, bf16[32,1024]{1,0:T(8,128)(2,1)S(1)}, u32[]{:S(2)}, u32[]{:S(2)}) collective-permute-start(bf16[32,1024]{1,0:T(8,128)(2,1)} %get-tuple-element.21), channel_id=1, source_target_pairs={{0,2},{2,0},{4,6},{6,4},{8,10},{10,8},{12,14},{14,12},{16,18},{18,... | collective-permute-start | bytes 196616 | tf_op jit(solution)/shard_map/ppermute | solution.py:30
  13.0 26.6 %collective-permute-start.4 = (bf16[384,1024]{1,0:T(8,128)(2,1)}, bf16[384,1024]{1,0:T(8,128)(2,1)S(1)}, u32[]{:S(2)}, u32[]{:S(2)}) collective-permute-start(bf16[384,1024]{1,0:T(8,128)(2,1)} %get-tuple-element.25.both0.both_ref), channel_id=1, source_target_pairs={{0,2},{2,4},{4,6},{6,8},{8,10},{10,12},{12,14},{14,16},{16,18},{18... | collective-permute-start | bytes 2359304 | tf_op jit(solution)/shard_map/ppermute | solution.py:24
  17.9 14.4 %collective-permute-start.3 = (bf16[64,1024]{1,0:T(8,128)(2,1)S(1)}, bf16[64,1024]{1,0:T(8,128)(2,1)S(1)}, u32[]{:S(2)}, u32[]{:S(2)}) collective-permute-start(bf16[64,1024]{1,0:T(8,128)(2,1)S(1)} %maximum_maximum_fusion), channel_id=1, source_target_pairs={{0,1},{1,0},{2,3},{3,2},{4,5},{5,4},{6,7},{7,6},{8,9},{9,8},{10,11... | collective-permute-start | bytes 393224 | tf_op jit(solution)/shard_map/ppermute | solution.py:290
  20.9 18.6 %collective-permute-start.5 = (bf16[192,1024]{1,0:T(8,128)(2,1)S(1)}, bf16[192,1024]{1,0:T(8,128)(2,1)S(1)}, u32[]{:S(2)}, u32[]{:S(2)}) collective-permute-start(bf16[192,1024]{1,0:T(8,128)(2,1)S(1)} %copy-done.4), channel_id=1, source_target_pairs={{2,0},{4,2},{6,4},{8,6},{10,8},{12,10},{14,12},{16,14},{18,16},{20... | collective-permute-start | bytes 1179656 | tf_op jit(solution)/shard_map/ppermute | solution.py:24
  35.8 58.9 %copy-start.3 = (bf16[384,1024]{1,0:T(8,128)(2,1)S(1)}, bf16[384,1024]{1,0:T(8,128)(2,1)}, u32[]{:S(2)}) copy-start(bf16[384,1024]{1,0:T(8,128)(2,1)} %get-tuple-element.25.both0.both_ref) | copy-start | bytes 2359300
  39.6 10.8 %collective-permute-start.6 = (bf16[384,1024]{1,0:T(8,128)(2,1)S(1)}, bf16[384,1024]{1,0:T(8,128)(2,1)S(1)}, u32[]{:S(2)}, u32[]{:S(2)}) collective-permute-start(bf16[384,1024]{1,0:T(8,128)(2,1)S(1)} %collective-permute-done.4.both1), channel_id=1, source_target_pairs={{0,2},{2,4},{4,6},{6,8},{8,10},{10,12},{12,14},{14,16},{16,18},{18... | collective-permute-start | bytes 2359304 | tf_op jit(solution)/shard_map/ppermute | solution.py:24
  41.5 13.3 %collective-permute-start.8 = (bf16[192,1024]{1,0:T(8,128)(2,1)S(1)}, bf16[192,1024]{1,0:T(8,128)(2,1)}, u32[]{:S(2)}, u32[]{:S(2)}) collective-permute-start(bf16[192,1024]{1,0:T(8,128)(2,1)S(1)} %collective-permute-done.5.q1), channel_id=1, source_target_pairs={{2,0},{4,2},{6,4},{8,6},{10,8},{12,10},{14,12},{16,14},{18,16},{20... | collective-permute-start | bytes 1179656 | tf_op jit(solution)/shard_map/ppermute | solution.py:24
  44.0 12.8 %collective-permute-start.10 = (bf16[192,1024]{1,0:T(8,128)(2,1)S(1)}, bf16[192,1024]{1,0:T(8,128)(2,1)}, u32[]{:S(2)}, u32[]{:S(2)}) collective-permute-start(bf16[192,1024]{1,0:T(8,128)(2,1)S(1)} %convolution_convert_fusion.do_ref.d0), channel_id=1, source_target_pairs={{2,0},{4,2},{6,4},{8,6},{10,8},{12,10},{14,12},{16,14},{18,16},{20... | collective-permute-start | bytes 1179656 | tf_op jit(solution)/shard_map/ppermute | solution.py:24
  50.4 38.1 %collective-permute-start.7 = (bf16[384,1024]{1,0:T(8,128)(2,1)S(1)}, bf16[384,1024]{1,0:T(8,128)(2,1)}, u32[]{:S(2)}, u32[]{:S(2)}) collective-permute-start(bf16[384,1024]{1,0:T(8,128)(2,1)S(1)} %collective-permute-done.6.both2), channel_id=1, source_target_pairs={{0,2},{2,4},{4,6},{6,8},{8,10},{10,12},{12,14},{14,16},{16,18},{18... | collective-permute-start | bytes 2359304 | tf_op jit(solution)/shard_map/ppermute | solution.py:24
  54.8 24.2 %collective-permute-start.9 = (bf16[192,1024]{1,0:T(8,128)(2,1)}, bf16[192,1024]{1,0:T(8,128)(2,1)}, u32[]{:S(2)}, u32[]{:S(2)}) collective-permute-start(bf16[192,1024]{1,0:T(8,128)(2,1)} %collective-permute-done.8.q2), channel_id=1, source_target_pairs={{2,0},{4,2},{6,4},{8,6},{10,8},{12,10},{14,12},{16,14},{18,16},{20... | collective-permute-start | bytes 1179656 | tf_op jit(solution)/shard_map/ppermute | solution.py:24
  56.8 22.2 %collective-permute-start.11 = (bf16[192,1024]{1,0:T(8,128)(2,1)}, bf16[192,1024]{1,0:T(8,128)(2,1)}, u32[]{:S(2)}, u32[]{:S(2)}) collective-permute-start(bf16[192,1024]{1,0:T(8,128)(2,1)} %collective-permute-done.10.d1), channel_id=1, source_target_pairs={{2,0},{4,2},{6,4},{8,6},{10,8},{12,10},{14,12},{16,14},{18,16},{20... | collective-permute-start | bytes 1179656 | tf_op jit(solution)/shard_map/ppermute | solution.py:24
  58.7 28.9 %all-to-all-start = ((f32[8,32,128]{2,1,0:T(8,128)}), f32[8,32,128]{2,1,0:T(8,128)}, u32[]{:S(2)}, u32[]{:S(2)}) async-start(f32[8,32,128]{2,1,0:T(8,128)} %get-tuple-element.34), calls=%async_computation | async-start | bytes 262144 | tf_op jit(solution)/shard_map/all_to_all | solution.py:303
  79.0 28.3 %collective-permute-start.12 = (bf16[192,1024]{1,0:T(8,128)(2,1)}, bf16[192,1024]{1,0:T(8,128)(2,1)}, u32[]{:S(2)}, u32[]{:S(2)}) collective-permute-start(bf16[192,1024]{1,0:T(8,128)(2,1)} %collective-permute-done.11.d2), channel_id=1, source_target_pairs={{2,0},{4,2},{6,4},{8,6},{10,8},{12,10},{14,12},{16,14},{18,16},{20... | collective-permute-start | bytes 1179656 | tf_op jit(solution)/shard_map/ppermute | solution.py:24
  89.3 17.1 %all-to-all-start.1 = ((f32[16,32,128]{2,1,0:T(8,128)}), f32[16,32,128]{2,1,0:T(8,128)}, u32[]{:S(2)}, u32[]{:S(2)}) async-start(f32[16,32,128]{2,1,0:T(8,128)} %broadcast_in_dim.10), calls=%async_computation.1 | async-start | bytes 524288 | tf_op jit(solution)/shard_map/all_to_all | solution.py:306
  101.6 5.8 %collective-permute-start.13 = (f32[16,192]{1,0:T(8,128)S(1)}, f32[16,192]{1,0:T(8,128)S(1)}, u32[]{:S(2)}, u32[]{:S(2)}) collective-permute-start(f32[16,192]{1,0:T(8,128)S(1)} %get-tuple-element.30.s0), channel_id=1, source_target_pairs={{2,0},{4,2},{6,4},{8,6},{10,8},{12,10},{14,12},{16,14},{18,16},{20... | collective-permute-start | bytes 36872 | tf_op jit(solution)/shard_map/ppermute | solution.py:24
  103.8 4.5 %collective-permute-start.14 = (f32[16,192]{1,0:T(8,128)S(1)}, f32[16,192]{1,0:T(8,128)S(1)}, u32[]{:S(2)}, u32[]{:S(2)}) collective-permute-start(f32[16,192]{1,0:T(8,128)S(1)} %get-tuple-element.30.s0), channel_id=1, source_target_pairs={{4,0},{6,2},{8,4},{10,6},{12,8},{14,10},{16,12},{18,14},{20,16},{2... | collective-permute-start | bytes 36872 | tf_op jit(solution)/shard_map/ppermute | solution.py:24
  105.1 7.5 %collective-permute-start.15 = (f32[16,192]{1,0:T(8,128)S(1)}, f32[16,192]{1,0:T(8,128)S(1)}, u32[]{:S(2)}, u32[]{:S(2)}) collective-permute-start(f32[16,192]{1,0:T(8,128)S(1)} %get-tuple-element.30.s0), channel_id=1, source_target_pairs={{6,0},{8,2},{10,4},{12,6},{14,8},{16,10},{18,12},{20,14},{22,16},{... | collective-permute-start | bytes 36872 | tf_op jit(solution)/shard_map/ppermute | solution.py:24
  113.2 18.8 %all-to-all-start.2 = ((f32[8,32,128]{2,1,0:T(8,128)}), f32[8,32,128]{2,1,0:T(8,128)S(1)}, u32[]{:S(2)}, u32[]{:S(2)}) async-start(f32[8,32,128]{2,1,0:T(8,128)} %broadcast_in_dim.11), calls=%async_computation.2 | async-start | bytes 262144 | tf_op jit(solution)/shard_map/all_to_all | solution.py:311

commit v13 on v11

--- a/solution.py
+++ b/solution.py
@@ -292,19 +292,21 @@
     out_grad = project(tp, grad_stream, conv_other(device, other, edges, taps_count, last), out_weight)
     (sent,) = after((kv1,), (q1, out_grad))
     kv2 = rotated(sent, 1)
-    kv3 = rotated(kv2, 1)
     d1 = rotated(out_grad, -1)
+    (tap_rows,) = after((tap_rows,), (out_grad, q1))
+    tap_sums = jnp.sum(lax.all_to_all(tap_rows, "z", 0, 0, tiled=True), axis=0)
+    (sent,) = after((kv2,), (tap_sums,))
+    kv3 = rotated(sent, 1)
     (sent,) = after((d1,), (kv2, q2))
     d2 = rotated(sent, -1)
-    (sent,) = after((d2,), (q3,))
+
+    copies = jnp.broadcast_to(tap_sums, (lax.axis_size("near"),) + tap_sums.shape)
+    (copies,) = after((copies,), (kv2, d1, q2))
+    tap_sums = jnp.sum(lax.all_to_all(copies, "near", 0, 0, tiled=True), axis=0)
+    (near,) = after((queries,), (tap_sums,))
+    query_grad, stats = query_side(device, near, out_grad, (kv3, kv2, kv1, kv0), scale)
+    (sent,) = after((d2,), (stats,))
     d3 = rotated(sent, -1)
-
-    (tap_rows,) = after((tap_rows,), (kv1, d1))
-    tap_sums = jnp.sum(lax.all_to_all(tap_rows, "z", 0, 0, tiled=True), axis=0)
-    copies = jnp.broadcast_to(tap_sums, (lax.axis_size("near"),) + tap_sums.shape)
-    (copies,) = after((copies,), (kv3,))
-    tap_sums = jnp.sum(lax.all_to_all(copies, "near", 0, 0, tiled=True), axis=0)
-    query_grad, stats = query_side(device, queries, out_grad, (kv3, kv2, kv1, kv0), scale)
     all_stats = [stats] + [rotated(stats, -hop) for hop in (1, 2, 3)]
     copies = jnp.broadcast_to(tap_sums, (lax.axis_size("z"),) + tap_sums.shape)
     (copies,) = after((copies,), (*all_stats[1:], d3))

time: 121 us -> 130 us (1.074)
  the two profiles are of different devices: /device:TPU:1 before, /device:TPU:14 now
where the time goes in v13:
time: 130 us; the launch traced here: 129 us
  starting transfers between devices  38.1 us (29%)
  blocking collectives  34.1 us (26%)
  waiting for transfers between devices  26.7 us (21%)
  Pallas kernels  20.9 us (16%)
  matrix products  3.82 us (3%)
  local copies, waits for them, and re-layouts  3.29 us (3%)
  other arithmetic  1.65 us (1%)
    ppermute x12, waiting for transfers between devices, rotated(): lax.ppermute(part, CTX, [(i, (i + by) % count) for i in range(count)])  20.2 us
    ppermute x12, starting transfers between devices, rotated(): lax.ppermute(part, CTX, [(i, (i + by) % count) for i in range(count)])  18.4 us
    all_to_all x1, blocking collectives, per_device(): tap_sums = jnp.sum(lax.all_to_all(tap_rows, 'z', 0, 0, tiled=True), axis=0)  17.7 us
    all_to_all x1, blocking collectives, per_device(): tap_sums = jnp.sum(lax.all_to_all(copies, 'near', 0, 0, tiled=True), axis=0)  16.4 us
    all_to_all x1, starting transfers between devices, per_device(): tap_sums = lax.all_to_all(copies, 'z', 0, 0, tiled=True)  10.2 us
    pallas_call x1, Pallas kernels, query_side(): pl.pallas_call(functools.partial(query_kernel, scale), in_specs=[pl.Block...  6.87 us
    pallas_call x1, Pallas kernels, key_side(): pl.pallas_call(functools.partial(key_kernel, scale, last), in_specs=[pl.B...  5.6 us
    ppermute x2, starting transfers between devices, swapped(): lax.ppermute(part, CTX, [(i, partner(i) if 0 <= partner(i) < count and i...  4.73 us
  transfers between devices with their start and end apart: 17, of which 7 were waited for; matrix products, arithmetic and copies ran while one was open for 5% of the time, Pallas kernels for 16%

profile of v13, /device:TPU:14, one launch (start us, length us, event | category | flops | bytes accessed | tf_op | source)
XLA Modules:
  0.0 129.4 jit_solution(9859924875099864196)
XLA Ops:
  0.7 2.4 %collective-permute-start.2 = (bf16[192,1024]{1,0:T(8,128)(2,1)}, bf16[192,1024]{1,0:T(8,128)(2,1)S(1)}, u32[]{:S(2)}, u32[]{:S(2)}) collective-permute-start(bf16[192,1024]{1,0:T(8,128)(2,1)} %grad_ref.3), channel_id=1, source_target_pairs={{0,1},{1,0},{2,3},{3,2},{4,5},{5,4},{6,7},{7,6},{8,9},{9,8},{10,11... | collective-permute-start | bytes 1179656 | tf_op jit(solution)/shard_map/ppermute | solution.py:282
  3.1 2.1 %shard_map.110 = (bf16[384,1024]{1,0:T(8,128)(2,1)}, bf16[32,1024]{1,0:T(8,128)(2,1)}, bf16[32,1024]{1,0:T(8,128)(2,1)}) custom-call(s32[1]{0:T(128)} %bitcast.idx_ref, bf16[192,1024]{1,0:T(8,128)(2,1)} %k_ref.1, bf16[192,1024]{1,0:T(8,128)(2,1)} %v_ref.1, bf16[192,1024]{1,0:T(8,128)(2,1)} %input_ref.3, bf16[192,1024]{1,0:T(8,128)(2,1)} %grad_ref.3), custom_call_target="tpu_custom_call" | custom-call | tf_op jit(solution)/shard_map/pallas_call | solution.py:55
  5.1 1.9 %collective-permute-start.1 = (bf16[32,1024]{1,0:T(8,128)(2,1)}, bf16[32,1024]{1,0:T(8,128)(2,1)S(1)}, u32[]{:S(2)}, u32[]{:S(2)}) collective-permute-start(bf16[32,1024]{1,0:T(8,128)(2,1)} %get-tuple-element.24), channel_id=1, source_target_pairs={{0,0},{2,4},{4,2},{6,8},{8,6},{10,12},{12,10},{14,16},{16,14},{18,... | collective-permute-start | bytes 196616 | tf_op jit(solution)/shard_map/ppermute | solution.py:30
  7.1 2.8 %collective-permute-start = (bf16[32,1024]{1,0:T(8,128)(2,1)}, bf16[32,1024]{1,0:T(8,128)(2,1)S(1)}, u32[]{:S(2)}, u32[]{:S(2)}) collective-permute-start(bf16[32,1024]{1,0:T(8,128)(2,1)} %get-tuple-element.23), channel_id=1, source_target_pairs={{0,2},{2,0},{4,6},{6,4},{8,10},{10,8},{12,14},{14,12},{16,18},{18,... | collective-permute-start | bytes 196616 | tf_op jit(solution)/shard_map/ppermute | solution.py:30
  10.0 1.0 collective-permute-done.1.across_ref
  11.0 3.0 %collective-permute-done.2.grad_ref = bf16[192,1024]{1,0:T(8,128)(2,1)S(1)} collective-permute-done((bf16[192,1024]{1,0:T(8,128)(2,1)}, bf16[192,1024]{1,0:T(8,128)(2,1)S(1)}, u32[]{:S(2)}, u32[]{:S(2)}) %collective-permute-start.2) | collective-permute-done | bytes 393248 | tf_op jit(solution)/shard_map/ppermute | solution.py:282
  14.1 2.4 %collective-permute-start.3 = (bf16[64,1024]{1,0:T(8,128)(2,1)S(1)}, bf16[64,1024]{1,0:T(8,128)(2,1)S(1)}, u32[]{:S(2)}, u32[]{:S(2)}) collective-permute-start(bf16[64,1024]{1,0:T(8,128)(2,1)S(1)} %maximum_maximum_fusion), channel_id=1, source_target_pairs={{0,1},{1,0},{2,3},{3,2},{4,5},{5,4},{6,7},{7,6},{8,9},{9,8},{10,11... | collective-permute-start | bytes 393224 | tf_op jit(solution)/shard_map/ppermute | solution.py:290
  16.5 1.5 %collective-permute-start.4 = (bf16[192,1024]{1,0:T(8,128)(2,1)S(1)}, bf16[192,1024]{1,0:T(8,128)(2,1)S(1)}, u32[]{:S(2)}, u32[]{:S(2)}) collective-permute-start(bf16[192,1024]{1,0:T(8,128)(2,1)S(1)} %copy-done.4), channel_id=1, source_target_pairs={{0,254},{2,0},{4,2},{6,4},{8,6},{10,8},{12,10},{14,12},{16,14},{18... | collective-permute-start | bytes 1179656 | tf_op jit(solution)/shard_map/ppermute | solution.py:24
  18.0 4.4 %shard_map.111 = (bf16[192,1024]{1,0:T(8,128)(2,1)}, f32[8,32,128]{2,1,0:T(8,128)S(1)}) custom-call(s32[1]{0:T(128)} %bitcast.idx_ref, bf16[192,1024]{1,0:T(8,128)(2,1)S(1)} %copy-done, bf16[192,1024]{1,0:T(8,128)(2,1)S(1)} %copy-done.1, bf16[32,1024]{1,0:T(8,128)(2,1)S(1)} %collective-permute-done.inside_ref, ...), custom_call_target="tpu_custom_call" | custom-call | flops 196608 | bytes 12288 | tf_op jit(solution)/shard_map/pallas_call | solution.py:106
  22.4 1.9 %shard_map.112 = bf16[192,1024]{1,0:T(8,128)(2,1)S(1)} custom-call(s32[1]{0:T(128)} %bitcast.idx_ref, bf16[192,1024]{1,0:T(8,128)(2,1)S(1)} %collective-permute-done.2.grad_ref, bf16[64,1024]{1,0:T(8,128)(2,1)S(1)} %collective-permute-done.3.edges_ref), custom_call_target="tpu_custom_call" | custom-call | flops 196608 | bytes 12288 | tf_op jit(solution)/shard_map/pallas_call | solution.py:140
  24.3 1.5 %maximum_select_fusion = bf16[192,2048]{1,0:T(8,128)(2,1)S(1)} fusion(bf16[192,1024]{1,0:T(8,128)(2,1)S(1)} %shard_map.112, bf16[192,1024]{1,0:T(8,128)(2,1)} %get-tuple-element.21, pred[]{:T(512)S(6)} %eq.3), kind=kLoop, calls=%fused_computation.1 | loop fusion | flops 3538944 | bytes 1572865 | tf_op jit(solution)/shard_map/jit(_where)/select_n | solution.py:152
  25.9 3.8 %convolution_convert_fusion.do_ref.d0 = bf16[192,1024]{1,0:T(8,128)(2,1)S(1)} fusion(bf16[192,2048]{1,0:T(8,128)(2,1)S(1)} %maximum_select_fusion, bf16[1024,2048]{1,0:T(8,128)(2,1)} %param.13), kind=kOutput, calls=%fused_computation | convolution fusion | flops 805502976 | bytes 5373952 | tf_op jit(solution)/shard_map/dot_general | solution.py:154
  29.7 0.7 copy-done.5
  30.4 4.1 %collective-permute-start.6 = (bf16[384,1024]{1,0:T(8,128)(2,1)S(1)}, bf16[384,1024]{1,0:T(8,128)(2,1)S(1)}, u32[]{:S(2)}, u32[]{:S(2)}) collective-permute-start(bf16[384,1024]{1,0:T(8,128)(2,1)S(1)} %collective-permute-done.5.both1), channel_id=1, source_target_pairs={{0,2},{2,4},{4,6},{6,8},{8,10},{10,12},{12,14},{14,16},{16,18},{18... | collective-permute-start | bytes 2359304 | tf_op jit(solution)/shard_map/ppermute | solution.py:24
  34.5 17.7 %all_to_all.15 = f32[8,32,128]{2,1,0:T(8,128)S(1)} all-to-all(f32[8,32,128]{2,1,0:T(8,128)S(1)} %get-tuple-element.27), channel_id=1, replica_groups=mesh['z'=8,'near'=16,'tp'=2] {'z'}, dimensions={0} | all-to-all | bytes 262144 | tf_op jit(solution)/shard_map/all_to_all | solution.py:297
  52.3 5.6 %collective-permute-start.9 = (bf16[384,1024]{1,0:T(8,128)(2,1)S(1)}, bf16[384,1024]{1,0:T(8,128)(2,1)}, u32[]{:S(2)}, u32[]{:S(2)}) collective-permute-start(bf16[384,1024]{1,0:T(8,128)(2,1)S(1)} %collective-permute-done.6.both2), channel_id=1, source_target_pairs={{0,2},{2,4},{4,6},{6,8},{8,10},{10,12},{12,14},{14,16},{16,18},{18... | collective-permute-start | bytes 2359304 | tf_op jit(solution)/shard_map/ppermute | solution.py:24
  57.9 5.3 %collective-permute-done.7.d1 = bf16[192,1024]{1,0:T(8,128)(2,1)} collective-permute-done((bf16[192,1024]{1,0:T(8,128)(2,1)S(1)}, bf16[192,1024]{1,0:T(8,128)(2,1)}, u32[]{:S(2)}, u32[]{:S(2)}) %collective-permute-start.7) | collective-permute-done | bytes 393248 | tf_op jit(solution)/shard_map/ppermute | solution.py:24
  63.2 4.3 %collective-permute-done.8.q2 = bf16[192,1024]{1,0:T(8,128)(2,1)} collective-permute-done((bf16[192,1024]{1,0:T(8,128)(2,1)}, bf16[192,1024]{1,0:T(8,128)(2,1)}, u32[]{:S(2)}, u32[]{:S(2)}) %collective-permute-start.8) | collective-permute-done | bytes 393248 | tf_op jit(solution)/shard_map/ppermute | solution.py:24
  67.5 1.9 %collective-permute-start.11 = (bf16[192,1024]{1,0:T(8,128)(2,1)}, bf16[192,1024]{1,0:T(8,128)(2,1)}, u32[]{:S(2)}, u32[]{:S(2)}) collective-permute-start(bf16[192,1024]{1,0:T(8,128)(2,1)} %collective-permute-done.7.d1), channel_id=1, source_target_pairs={{0,254},{2,0},{4,2},{6,4},{8,6},{10,8},{12,10},{14,12},{16,14},{18... | collective-permute-start | bytes 1179656 | tf_op jit(solution)/shard_map/ppermute | solution.py:24
  69.5 16.4 %all_to_all.16 = f32[16,32,128]{2,1,0:T(8,128)S(1)} all-to-all(f32[16,32,128]{2,1,0:T(8,128)S(1)} %broadcast_in_dim.10), channel_id=1, replica_groups=mesh['z'=8,'near'=16,'tp'=2] {'near'}, dimensions={0} | all-to-all | bytes 524288 | tf_op jit(solution)/shard_map/all_to_all | solution.py:305
  85.9 6.9 %shard_map.113 = (bf16[192,1024]{1,0:T(8,128)(2,1)}, f32[16,192]{1,0:T(8,128)S(1)}) custom-call(s32[1]{0:T(128)} %bitcast.idx_ref, bf16[192,1024]{1,0:T(8,128)(2,1)S(1)} %copy-done.4, bf16[192,1024]{1,0:T(8,128)(2,1)S(1)} %convolution_convert_fusion.do_ref.d0, bf16[384,1024]{1,0:T(8,128)(2,1)} %collective-permute-done.9.both3, ...), custom_call_target="tpu_custom_call" | custom-call | flops 1509949440 | bytes 4718592 | tf_op jit(solution)/shard_map/pallas_call | solution.py:198
  93.6 1.2 collective-permute-start.13
  94.8 1.4 %collective-permute-start.14 = (f32[16,192]{1,0:T(8,128)S(1)}, f32[16,192]{1,0:T(8,128)S(1)}, u32[]{:S(2)}, u32[]{:S(2)}) collective-permute-start(f32[16,192]{1,0:T(8,128)S(1)} %get-tuple-element.36.s0), channel_id=1, source_target_pairs={{0,252},{2,254},{4,0},{6,2},{8,4},{10,6},{12,8},{14,10},{16,12},{1... | collective-permute-start | bytes 36872 | tf_op jit(solution)/shard_map/ppermute | solution.py:24
  96.2 1.9 %collective-permute-start.15 = (f32[16,192]{1,0:T(8,128)S(1)}, f32[16,192]{1,0:T(8,128)S(1)}, u32[]{:S(2)}, u32[]{:S(2)}) collective-permute-start(f32[16,192]{1,0:T(8,128)S(1)} %get-tuple-element.36.s0), channel_id=1, source_target_pairs={{0,250},{2,252},{4,254},{6,0},{8,2},{10,4},{12,6},{14,8},{16,10},{... | collective-permute-start | bytes 36872 | tf_op jit(solution)/shard_map/ppermute | solution.py:24
  98.1 5.5 %collective-permute-done.13.s1 = f32[16,192]{1,0:T(8,128)S(1)} collective-permute-done((f32[16,192]{1,0:T(8,128)S(1)}, f32[16,192]{1,0:T(8,128)S(1)}, u32[]{:S(2)}, u32[]{:S(2)}) %collective-permute-start.13) | collective-permute-done | bytes 12320 | tf_op jit(solution)/shard_map/ppermute | solution.py:24
  103.6 5.0 %collective-permute-done.14.s2 = f32[16,192]{1,0:T(8,128)S(1)} collective-permute-done((f32[16,192]{1,0:T(8,128)S(1)}, f32[16,192]{1,0:T(8,128)S(1)}, u32[]{:S(2)}, u32[]{:S(2)}) %collective-permute-start.14) | collective-permute-done | bytes 12320 | tf_op jit(solution)/shard_map/ppermute | solution.py:24
  108.6 0.7 broadcast_in_dim.11
  109.3 10.2 %all-to-all-start.2 = ((f32[8,32,128]{2,1,0:T(8,128)}), f32[8,32,128]{2,1,0:T(8,128)S(1)}, u32[]{:S(2)}, u32[]{:S(2)}) async-start(f32[8,32,128]{2,1,0:T(8,128)} %broadcast_in_dim.11), calls=%async_computation.2 | async-start | bytes 262144 | tf_op jit(solution)/shard_map/all_to_all | solution.py:313
  119.5 1.0 copy-done.6
  120.5 5.6 %shard_map.114 = (bf16[192,1024]{1,0:T(8,128)(2,1)}, bf16[192,1024]{1,0:T(8,128)(2,1)}) custom-call(s32[1]{0:T(128)} %bitcast.idx_ref, bf16[384,1024]{1,0:T(8,128)(2,1)S(1)} %copy-done.3, bf16[192,1024]{1,0:T(8,128)(2,1)S(1)} %copy-done.4, bf16[192,1024]{1,0:T(8,128)(2,1)S(1)} %copy-done.6, bf16[192,1024]{1,0:T(8,128)(2,1)} %collective-permute-done.8.q2, ...), custom_call_target="tpu_custom_call" | custom-call | flops 1509949440 | bytes 4718592 | tf_op jit(solution)/shard_map/pallas_call | solution.py:255
  126.1 2.5 %all-to-all-done.2 = f32[8,32,128]{2,1,0:T(8,128)S(1)} async-done(((f32[8,32,128]{2,1,0:T(8,128)}), f32[8,32,128]{2,1,0:T(8,128)S(1)}, u32[]{:S(2)}, u32[]{:S(2)}) %all-to-all-start.2) | async-done | bytes 131104 | tf_op jit(solution)/shard_map/all_to_all | solution.py:313
  128.7 0.7 copy.15
  (37 shorter events, 1.3 us)
Async XLA Ops:
  0.6 17.3 %copy-start = (bf16[192,1024]{1,0:T(8,128)(2,1)S(1)}, bf16[192,1024]{1,0:T(8,128)(2,1)}, u32[]{:S(2)}) copy-start(bf16[192,1024]{1,0:T(8,128)(2,1)} %grad_ref.3) | copy-start | bytes 1179652
  0.6 17.3 %copy-start.1 = (bf16[192,1024]{1,0:T(8,128)(2,1)S(1)}, bf16[192,1024]{1,0:T(8,128)(2,1)}, u32[]{:S(2)}) copy-start(bf16[192,1024]{1,0:T(8,128)(2,1)} %input_ref.3) | copy-start | bytes 1179652
  0.7 13.4 %copy-start.2 = (bf16[31,1024]{1,0:T(8,128)(2,1)S(1)}, bf16[31,1024]{1,0:T(8,128)(2,1)}, u32[]{:S(2)}) copy-start(bf16[31,1024]{1,0:T(8,128)(2,1)} %taps_ref.1) | copy-start | bytes 190468
  0.7 15.9 %copy-start.4 = (bf16[192,1024]{1,0:T(8,128)(2,1)S(1)}, bf16[192,1024]{1,0:T(8,128)(2,1)}, u32[]{:S(2)}) copy-start(bf16[192,1024]{1,0:T(8,128)(2,1)} %q0.1) | copy-start | bytes 1179652
  0.7 13.4 %collective-permute-start.2 = (bf16[192,1024]{1,0:T(8,128)(2,1)}, bf16[192,1024]{1,0:T(8,128)(2,1)S(1)}, u32[]{:S(2)}, u32[]{:S(2)}) collective-permute-start(bf16[192,1024]{1,0:T(8,128)(2,1)} %grad_ref.3), channel_id=1, source_target_pairs={{0,1},{1,0},{2,3},{3,2},{4,5},{5,4},{6,7},{7,6},{8,9},{9,8},{10,11... | collective-permute-start | bytes 1179656 | tf_op jit(solution)/shard_map/ppermute | solution.py:282
  5.1 5.8 %collective-permute-start.1 = (bf16[32,1024]{1,0:T(8,128)(2,1)}, bf16[32,1024]{1,0:T(8,128)(2,1)S(1)}, u32[]{:S(2)}, u32[]{:S(2)}) collective-permute-start(bf16[32,1024]{1,0:T(8,128)(2,1)} %get-tuple-element.24), channel_id=1, source_target_pairs={{0,0},{2,4},{4,2},{6,8},{8,6},{10,12},{12,10},{14,16},{16,14},{18,... | collective-permute-start | bytes 196616 | tf_op jit(solution)/shard_map/ppermute | solution.py:30
  7.1 3.9 %collective-permute-start = (bf16[32,1024]{1,0:T(8,128)(2,1)}, bf16[32,1024]{1,0:T(8,128)(2,1)S(1)}, u32[]{:S(2)}, u32[]{:S(2)}) collective-permute-start(bf16[32,1024]{1,0:T(8,128)(2,1)} %get-tuple-element.23), channel_id=1, source_target_pairs={{0,2},{2,0},{4,6},{6,4},{8,10},{10,8},{12,14},{14,12},{16,18},{18,... | collective-permute-start | bytes 196616 | tf_op jit(solution)/shard_map/ppermute | solution.py:30
  14.0 16.4 %collective-permute-start.5 = (bf16[384,1024]{1,0:T(8,128)(2,1)}, bf16[384,1024]{1,0:T(8,128)(2,1)S(1)}, u32[]{:S(2)}, u32[]{:S(2)}) collective-permute-start(bf16[384,1024]{1,0:T(8,128)(2,1)} %get-tuple-element.29.both0.both_ref), channel_id=1, source_target_pairs={{0,2},{2,4},{4,6},{6,8},{8,10},{10,12},{12,14},{14,16},{16,18},{18... | collective-permute-start | bytes 2359304 | tf_op jit(solution)/shard_map/ppermute | solution.py:24
  14.1 8.3 %collective-permute-start.3 = (bf16[64,1024]{1,0:T(8,128)(2,1)S(1)}, bf16[64,1024]{1,0:T(8,128)(2,1)S(1)}, u32[]{:S(2)}, u32[]{:S(2)}) collective-permute-start(bf16[64,1024]{1,0:T(8,128)(2,1)S(1)} %maximum_maximum_fusion), channel_id=1, source_target_pairs={{0,1},{1,0},{2,3},{3,2},{4,5},{5,4},{6,7},{7,6},{8,9},{9,8},{10,11... | collective-permute-start | bytes 393224 | tf_op jit(solution)/shard_map/ppermute | solution.py:290
  16.5 13.2 %collective-permute-start.4 = (bf16[192,1024]{1,0:T(8,128)(2,1)S(1)}, bf16[192,1024]{1,0:T(8,128)(2,1)S(1)}, u32[]{:S(2)}, u32[]{:S(2)}) collective-permute-start(bf16[192,1024]{1,0:T(8,128)(2,1)S(1)} %copy-done.4), channel_id=1, source_target_pairs={{0,254},{2,0},{4,2},{6,4},{8,6},{10,8},{12,10},{14,12},{16,14},{18... | collective-permute-start | bytes 1179656 | tf_op jit(solution)/shard_map/ppermute | solution.py:24
  25.8 60.0 %copy-start.3 = (bf16[384,1024]{1,0:T(8,128)(2,1)S(1)}, bf16[384,1024]{1,0:T(8,128)(2,1)}, u32[]{:S(2)}) copy-start(bf16[384,1024]{1,0:T(8,128)(2,1)} %get-tuple-element.29.both0.both_ref) | copy-start | bytes 2359300
  29.7 0.7 copy-start.5
  30.4 21.8 %collective-permute-start.6 = (bf16[384,1024]{1,0:T(8,128)(2,1)S(1)}, bf16[384,1024]{1,0:T(8,128)(2,1)S(1)}, u32[]{:S(2)}, u32[]{:S(2)}) collective-permute-start(bf16[384,1024]{1,0:T(8,128)(2,1)S(1)} %collective-permute-done.5.both1), channel_id=1, source_target_pairs={{0,2},{2,4},{4,6},{6,8},{8,10},{10,12},{12,14},{14,16},{16,18},{18... | collective-permute-start | bytes 2359304 | tf_op jit(solution)/shard_map/ppermute | solution.py:24
  52.3 33.6 %collective-permute-start.9 = (bf16[384,1024]{1,0:T(8,128)(2,1)S(1)}, bf16[384,1024]{1,0:T(8,128)(2,1)}, u32[]{:S(2)}, u32[]{:S(2)}) collective-permute-start(bf16[384,1024]{1,0:T(8,128)(2,1)S(1)} %collective-permute-done.6.both2), channel_id=1, source_target_pairs={{0,2},{2,4},{4,6},{6,8},{8,10},{10,12},{12,14},{14,16},{16,18},{18... | collective-permute-start | bytes 2359304 | tf_op jit(solution)/shard_map/ppermute | solution.py:24
  57.9 5.3 %collective-permute-start.7 = (bf16[192,1024]{1,0:T(8,128)(2,1)S(1)}, bf16[192,1024]{1,0:T(8,128)(2,1)}, u32[]{:S(2)}, u32[]{:S(2)}) collective-permute-start(bf16[192,1024]{1,0:T(8,128)(2,1)S(1)} %convolution_convert_fusion.do_ref.d0), channel_id=1, source_target_pairs={{0,254},{2,0},{4,2},{6,4},{8,6},{10,8},{12,10},{14,12},{16,14},{18... | collective-permute-start | bytes 1179656 | tf_op jit(solution)/shard_map/ppermute | solution.py:24
  57.9 9.6 %collective-permute-start.8 = (bf16[192,1024]{1,0:T(8,128)(2,1)}, bf16[192,1024]{1,0:T(8,128)(2,1)}, u32[]{:S(2)}, u32[]{:S(2)}) collective-permute-start(bf16[192,1024]{1,0:T(8,128)(2,1)} %copy-done.5), channel_id=1, source_target_pairs={{0,254},{2,0},{4,2},{6,4},{8,6},{10,8},{12,10},{14,12},{16,14},{18... | collective-permute-start | bytes 1179656 | tf_op jit(solution)/shard_map/ppermute | solution.py:24
  67.5 25.2 %collective-permute-start.11 = (bf16[192,1024]{1,0:T(8,128)(2,1)}, bf16[192,1024]{1,0:T(8,128)(2,1)}, u32[]{:S(2)}, u32[]{:S(2)}) collective-permute-start(bf16[192,1024]{1,0:T(8,128)(2,1)} %collective-permute-done.7.d1), channel_id=1, source_target_pairs={{0,254},{2,0},{4,2},{6,4},{8,6},{10,8},{12,10},{14,12},{16,14},{18... | collective-permute-start | bytes 1179656 | tf_op jit(solution)/shard_map/ppermute | solution.py:24
  92.8 15.9 %collective-permute-start.12 = (bf16[192,1024]{1,0:T(8,128)(2,1)}, bf16[192,1024]{1,0:T(8,128)(2,1)S(1)}, u32[]{:S(2)}, u32[]{:S(2)}) collective-permute-start(bf16[192,1024]{1,0:T(8,128)(2,1)} %collective-permute-done.11.d2), channel_id=1, source_target_pairs={{0,254},{2,0},{4,2},{6,4},{8,6},{10,8},{12,10},{14,12},{16,14},{18... | collective-permute-start | bytes 1179656 | tf_op jit(solution)/shard_map/ppermute | solution.py:24
  93.4 26.1 %collective-permute-start.10 = (bf16[192,1024]{1,0:T(8,128)(2,1)}, bf16[192,1024]{1,0:T(8,128)(2,1)S(1)}, u32[]{:S(2)}, u32[]{:S(2)}) collective-permute-start(bf16[192,1024]{1,0:T(8,128)(2,1)} %collective-permute-done.8.q2), channel_id=1, source_target_pairs={{0,254},{2,0},{4,2},{6,4},{8,6},{10,8},{12,10},{14,12},{16,14},{18... | collective-permute-start | bytes 1179656 | tf_op jit(solution)/shard_map/ppermute | solution.py:24
  93.6 10.0 %collective-permute-start.13 = (f32[16,192]{1,0:T(8,128)S(1)}, f32[16,192]{1,0:T(8,128)S(1)}, u32[]{:S(2)}, u32[]{:S(2)}) collective-permute-start(f32[16,192]{1,0:T(8,128)S(1)} %get-tuple-element.36.s0), channel_id=1, source_target_pairs={{0,254},{2,0},{4,2},{6,4},{8,6},{10,8},{12,10},{14,12},{16,14},{18... | collective-permute-start | bytes 36872 | tf_op jit(solution)/shard_map/ppermute | solution.py:24
  94.8 13.9 %collective-permute-start.14 = (f32[16,192]{1,0:T(8,128)S(1)}, f32[16,192]{1,0:T(8,128)S(1)}, u32[]{:S(2)}, u32[]{:S(2)}) collective-permute-start(f32[16,192]{1,0:T(8,128)S(1)} %get-tuple-element.36.s0), channel_id=1, source_target_pairs={{0,252},{2,254},{4,0},{6,2},{8,4},{10,6},{12,8},{14,10},{16,12},{1... | collective-permute-start | bytes 36872 | tf_op jit(solution)/shard_map/ppermute | solution.py:24
  96.2 12.4 %collective-permute-start.15 = (f32[16,192]{1,0:T(8,128)S(1)}, f32[16,192]{1,0:T(8,128)S(1)}, u32[]{:S(2)}, u32[]{:S(2)}) collective-permute-start(f32[16,192]{1,0:T(8,128)S(1)} %get-tuple-element.36.s0), channel_id=1, source_target_pairs={{0,250},{2,252},{4,254},{6,0},{8,2},{10,4},{12,6},{14,8},{16,10},{... | collective-permute-start | bytes 36872 | tf_op jit(solution)/shard_map/ppermute | solution.py:24
  109.3 19.2 %all-to-all-start.2 = ((f32[8,32,128]{2,1,0:T(8,128)}), f32[8,32,128]{2,1,0:T(8,128)S(1)}, u32[]{:S(2)}, u32[]{:S(2)}) async-start(f32[8,32,128]{2,1,0:T(8,128)} %broadcast_in_dim.11), calls=%async_computation.2 | async-start | bytes 262144 | tf_op jit(solution)/shard_map/all_to_all | solution.py:313
  119.5 1.0 copy-start.6

commit v14 on v10

--- a/solution.py
+++ b/solution.py
@@ -253,16 +253,15 @@
 
     (sent,) = after((out_grad,), (v2,))
     d1 = rotated(sent, -1)
-    (sent,) = after((d1,), (k3, q3))
-    d2 = rotated(sent, -1)
-    (sent,) = after((d2,), (v3,))
-    d3 = rotated(sent, -1)
-
     copies = jnp.broadcast_to(tap_sums, (lax.axis_size("near"),) + tap_sums.shape)
     (copies,) = after((copies,), (v2, out_grad))
     tap_sums = jnp.sum(lax.all_to_all(copies, "near", 0, 0, tiled=True), axis=0)
+    (sent,) = after((d1,), (k3, q3, tap_sums))
+    d2 = rotated(sent, -1)
     (near,) = after((queries,), (tap_sums,))
     query_grad, stats = query_side(device, near, out_grad, (k3, k2, k1, keys), (v3, v2, v1, values), scale)
+    (sent,) = after((d2,), (stats,))
+    d3 = rotated(sent, -1)
     all_stats = [stats] + [rotated(stats, -hop) for hop in (1, 2, 3)]
     copies = jnp.broadcast_to(tap_sums, (lax.axis_size("far"),) + tap_sums.shape)
     (copies,) = after((copies,), (*all_stats[1:], d3))

time: 113 us -> 110 us (0.973); the launches traced: 112 us -> 108 us
  starting transfers between devices: 61.7 us -> 59.5 us
  waiting for transfers between devices: 19 us -> 17 us
    all_to_all x1, starting transfers between devices: 10.2 us -> 4.74 us  [per_device(): tap_sums = jnp.sum(lax.all_to_all(copies, 'near', 0, 0, tiled=True), axis=0)]
    ppermute x15, starting transfers between devices: 39 us -> 42.3 us  [rotated(): lax.ppermute(part, CTX, [(i, (i + by) % count) for i in range(count)])]
    all_to_all x1, waiting for transfers between devices: 2.83 us -> 1.29 us  [per_device(): tap_sums = lax.all_to_all(copies, 'far', 0, 0, tiled=True)]
    unnamed x20 -> x18, local copies, waits for them, and re-layouts: 3.45 us -> 2.46 us
  transfers between devices with their start and end apart: 19 -> 19, of which waited for: 6 -> 6; matrix products, arithmetic and copies ran while one was open for 5% -> 6% of each run, Pallas kernels for 15% -> 16%
where the time goes in v14:
time: 110 us; the launch traced here: 108 us
  starting transfers between devices  59.5 us (54%)
  Pallas kernels  19.5 us (18%)
  waiting for transfers between devices  17 us (15%)
  matrix products  5.05 us (5%)
  local copies, waits for them, and re-layouts  4.83 us (4%)
    ppermute x15, starting transfers between devices, rotated(): lax.ppermute(part, CTX, [(i, (i + by) % count) for i in range(count)])  42.3 us
    ppermute x15, waiting for transfers between devices, rotated(): lax.ppermute(part, CTX, [(i, (i + by) % count) for i in range(count)])  8.89 us
    pallas_call x1, Pallas kernels, query_side(): pl.pallas_call(functools.partial(query_kernel, scale), in_specs=[pl.Block...  7.22 us
    all_to_all x1, starting transfers between devices, per_device(): lax.all_to_all(tap_rows, 'far', 0, 0, tiled=True)  5.92 us
    all_to_all x1, waiting for transfers between devices, per_device(): tap_sums = jnp.sum(lax.all_to_all(copies, 'near', 0, 0, tiled=True), axis=0)  5.71 us
    pallas_call x1, Pallas kernels, key_side(): pl.pallas_call(functools.partial(key_kernel, scale, last), in_specs=[pl.B...  5.47 us
    dot_general x1, matrix products, project(): lax.dot_general(full, weight, NT, preferred_element_type=jnp.float32)  5.05 us
    all_to_all x1, starting transfers between devices, per_device(): tap_sums = jnp.sum(lax.all_to_all(copies, 'near', 0, 0, tiled=True), axis=0)  4.74 us
  transfers between devices with their start and end apart: 19, of which 6 were waited for; matrix products, arithmetic and copies ran while one was open for 6% of the time, Pallas kernels for 16%

profile of v14, /device:TPU:1, one launch (start us, length us, event | category | flops | bytes accessed | tf_op | source)
XLA Modules:
  0.0 107.7 jit_solution(24115902695907861)
XLA Ops:
  0.7 2.2 %shard_map.110 = (bf16[224,1024]{1,0:T(8,128)(2,1)}, bf16[224,1024]{1,0:T(8,128)(2,1)}) custom-call(bf16[192,1024]{1,0:T(8,128)(2,1)} %k_ref.3, bf16[192,1024]{1,0:T(8,128)(2,1)} %q0.1, bf16[192,1024]{1,0:T(8,128)(2,1)} %input_ref.3, bf16[192,1024]{1,0:T(8,128)(2,1)} %grad_ref.3), custom_call_target="tpu_custom_call" | custom-call | tf_op jit(solution)/shard_map/pallas_call | solution.py:50
  2.9 2.7 %collective-permute-start = (bf16[224,1024]{1,0:T(8,128)(2,1)}, bf16[224,1024]{1,0:T(8,128)(2,1)S(1)}, u32[]{:S(2)}, u32[]{:S(2)}) collective-permute-start(bf16[224,1024]{1,0:T(8,128)(2,1)} %get-tuple-element.22), channel_id=1, source_target_pairs={{0,2},{2,4},{4,6},{6,8},{8,10},{10,12},{12,14},{14,16},{16,18},{18... | collective-permute-start | bytes 1376264 | tf_op jit(solution)/shard_map/ppermute | solution.py:24
  5.6 0.7 collective-permute-start.1
  6.3 5.0 %collective-permute-done.low_ref.k1 = bf16[224,1024]{1,0:T(8,128)(2,1)S(1)} collective-permute-done((bf16[224,1024]{1,0:T(8,128)(2,1)}, bf16[224,1024]{1,0:T(8,128)(2,1)S(1)}, u32[]{:S(2)}, u32[]{:S(2)}) %collective-permute-start) | collective-permute-done | bytes 458784 | tf_op jit(solution)/shard_map/ppermute | solution.py:24
  11.3 2.4 %collective-permute-start.2 = (bf16[224,1024]{1,0:T(8,128)(2,1)S(1)}, bf16[224,1024]{1,0:T(8,128)(2,1)S(1)}, u32[]{:S(2)}, u32[]{:S(2)}) collective-permute-start(bf16[224,1024]{1,0:T(8,128)(2,1)S(1)} %collective-permute-done.low_ref.k1), channel_id=1, source_target_pairs={{0,2},{2,4},{4,6},{6,8},{8,10},{10,12},{12,14},{14,16},{16,18},{18... | collective-permute-start | bytes 1376264 | tf_op jit(solution)/shard_map/ppermute | solution.py:24
  13.7 5.7 %collective-permute-start.6 = (bf16[224,1024]{1,0:T(8,128)(2,1)S(1)}, bf16[224,1024]{1,0:T(8,128)(2,1)S(1)}, u32[]{:S(2)}, u32[]{:S(2)}) collective-permute-start(bf16[224,1024]{1,0:T(8,128)(2,1)S(1)} %collective-permute-done.1.high_ref.q1), channel_id=1, source_target_pairs={{0,254},{2,0},{4,2},{6,4},{8,6},{10,8},{12,10},{14,12},{16,14},{18... | collective-permute-start | bytes 1376264 | tf_op jit(solution)/shard_map/ppermute | solution.py:24
  19.4 4.6 %shard_map.111 = (bf16[192,1024]{1,0:T(8,128)(2,1)}, f32[8,32,128]{2,1,0:T(8,128)}) custom-call(s32[1]{0:T(128)} %bitcast.idx_ref, bf16[192,1024]{1,0:T(8,128)(2,1)S(1)} %copy-done, bf16[192,1024]{1,0:T(8,128)(2,1)S(1)} %copy-done.1, bf16[224,1024]{1,0:T(8,128)(2,1)S(1)} %collective-permute-done.low_ref.k1, ...), custom_call_target="tpu_custom_call" | custom-call | flops 48758784 | bytes 786432 | tf_op jit(solution)/shard_map/pallas_call | solution.py:96
  24.0 2.6 %collective-permute-start.5 = (bf16[192,1024]{1,0:T(8,128)(2,1)}, bf16[192,1024]{1,0:T(8,128)(2,1)}, u32[]{:S(2)}, u32[]{:S(2)}) collective-permute-start(bf16[192,1024]{1,0:T(8,128)(2,1)} %get-tuple-element.20), channel_id=1, source_target_pairs={{0,1},{1,0},{2,3},{3,2},{4,5},{5,4},{6,7},{7,6},{8,9},{9,8},{10,11... | collective-permute-start | bytes 1179656 | tf_op jit(solution)/shard_map/ppermute | solution.py:246
  26.6 5.9 %all-to-all-start = ((f32[8,32,128]{2,1,0:T(8,128)}), f32[8,32,128]{2,1,0:T(8,128)S(1)}, u32[]{:S(2)}, u32[]{:S(2)}) async-start(f32[8,32,128]{2,1,0:T(8,128)} %get-tuple-element.25), calls=%async_computation | async-start | bytes 262144 | tf_op jit(solution)/shard_map/all_to_all | solution.py:248
  32.8 6.5 %collective-permute-start.9 = (bf16[224,1024]{1,0:T(8,128)(2,1)S(1)}, bf16[224,1024]{1,0:T(8,128)(2,1)S(1)}, u32[]{:S(2)}, u32[]{:S(2)}) collective-permute-start(bf16[224,1024]{1,0:T(8,128)(2,1)S(1)} %collective-permute-done.6.q2), channel_id=1, source_target_pairs={{0,254},{2,0},{4,2},{6,4},{8,6},{10,8},{12,10},{14,12},{16,14},{18... | collective-permute-start | bytes 1376264 | tf_op jit(solution)/shard_map/ppermute | solution.py:24
  39.3 1.1 %all-to-all-done = f32[8,32,128]{2,1,0:T(8,128)S(1)} async-done(((f32[8,32,128]{2,1,0:T(8,128)}), f32[8,32,128]{2,1,0:T(8,128)S(1)}, u32[]{:S(2)}, u32[]{:S(2)}) %all-to-all-start) | async-done | bytes 131104 | tf_op jit(solution)/shard_map/all_to_all | solution.py:248
  40.5 5.0 %convolution_convert_fusion.do_ref.d0 = bf16[192,1024]{1,0:T(8,128)(2,1)} fusion(bf16[1024,2048]{1,0:T(8,128)(2,1)} %param.13, bf16[192,1024]{1,0:T(8,128)(2,1)} %collective-permute-done.5, bf16[192,1024]{1,0:T(8,128)(2,1)} %get-tuple-element.20, pred[]{:T(512)S(6)} %eq.3), kind=kOutput, calls=%fused_computation | convolution fusion | flops 809041920 | bytes 5373953 | tf_op jit(solution)/shard_map/dot_general | solution.py:115
  45.6 7.7 %collective-permute-start.10 = (bf16[192,1024]{1,0:T(8,128)(2,1)}, bf16[192,1024]{1,0:T(8,128)(2,1)}, u32[]{:S(2)}, u32[]{:S(2)}) collective-permute-start(bf16[192,1024]{1,0:T(8,128)(2,1)} %convolution_convert_fusion.do_ref.d0), channel_id=1, source_target_pairs={{0,254},{2,0},{4,2},{6,4},{8,6},{10,8},{12,10},{14,12},{16,14},{18... | collective-permute-start | bytes 1179656 | tf_op jit(solution)/shard_map/ppermute | solution.py:24
  53.2 0.7 broadcast_in_dim.6
  54.0 4.7 %all-to-all-start.1 = ((f32[16,32,128]{2,1,0:T(8,128)}), f32[16,32,128]{2,1,0:T(8,128)}, u32[]{:S(2)}, u32[]{:S(2)}) async-start(f32[16,32,128]{2,1,0:T(8,128)} %broadcast_in_dim.6), calls=%async_computation.1 | async-start | bytes 524288 | tf_op jit(solution)/shard_map/all_to_all | solution.py:258
  58.7 1.6 %collective-permute-start.8 = (bf16[192,1024]{1,0:T(8,128)(2,1)}, bf16[192,1024]{1,0:T(8,128)(2,1)}, u32[]{:S(2)}, u32[]{:S(2)}) collective-permute-start(bf16[192,1024]{1,0:T(8,128)(2,1)} %collective-permute-done.4.v2), channel_id=1, source_target_pairs={{0,2},{2,4},{4,6},{6,8},{8,10},{10,12},{12,14},{14,16},{16,18},{18... | collective-permute-start | bytes 1179656 | tf_op jit(solution)/shard_map/ppermute | solution.py:24
  60.3 5.7 %all-to-all-done.1 = f32[16,32,128]{2,1,0:T(8,128)} async-done(((f32[16,32,128]{2,1,0:T(8,128)}), f32[16,32,128]{2,1,0:T(8,128)}, u32[]{:S(2)}, u32[]{:S(2)}) %all-to-all-start.1) | async-done | bytes 262176 | tf_op jit(solution)/shard_map/all_to_all | solution.py:258
  66.0 1.0 reduce_sum.19
  67.1 1.1 collective-permute-start.11
  68.1 7.2 %shard_map.112 = (bf16[192,1024]{1,0:T(8,128)(2,1)}, f32[16,192]{1,0:T(8,128)S(1)}) custom-call(s32[1]{0:T(128)} %bitcast.idx_ref, bf16[192,1024]{1,0:T(8,128)(2,1)S(1)} %copy-done.2, bf16[192,1024]{1,0:T(8,128)(2,1)} %convolution_convert_fusion.do_ref.d0, bf16[224,1024]{1,0:T(8,128)(2,1)} %collective-permute-done.7.k3, ...), custom_call_target="tpu_custom_call" | custom-call | flops 1509949440 | bytes 4718592 | tf_op jit(solution)/shard_map/pallas_call | solution.py:157
  75.4 8.4 %collective-permute-start.12 = (bf16[192,1024]{1,0:T(8,128)(2,1)S(1)}, bf16[192,1024]{1,0:T(8,128)(2,1)S(1)}, u32[]{:S(2)}, u32[]{:S(2)}) collective-permute-start(bf16[192,1024]{1,0:T(8,128)(2,1)S(1)} %collective-permute-done.11.d2), channel_id=1, source_target_pairs={{0,254},{2,0},{4,2},{6,4},{8,6},{10,8},{12,10},{14,12},{16,14},{18... | collective-permute-start | bytes 1179656 | tf_op jit(solution)/shard_map/ppermute | solution.py:24
  83.8 0.7 copy-done.6
  84.5 4.4 %collective-permute-start.13 = (f32[16,192]{1,0:T(8,128)S(1)}, f32[16,192]{1,0:T(8,128)S(1)}, u32[]{:S(2)}, u32[]{:S(2)}) collective-permute-start(f32[16,192]{1,0:T(8,128)S(1)} %get-tuple-element.34.s0), channel_id=1, source_target_pairs={{0,254},{2,0},{4,2},{6,4},{8,6},{10,8},{12,10},{14,12},{16,14},{18... | collective-permute-start | bytes 36872 | tf_op jit(solution)/shard_map/ppermute | solution.py:24
  88.9 0.8 collective-permute-start.15
  89.8 1.8 %collective-permute-done.14.s2 = f32[16,192]{1,0:T(8,128)S(1)} collective-permute-done((f32[16,192]{1,0:T(8,128)S(1)}, f32[16,192]{1,0:T(8,128)S(1)}, u32[]{:S(2)}, u32[]{:S(2)}) %collective-permute-start.14) | collective-permute-done | bytes 12320 | tf_op jit(solution)/shard_map/ppermute | solution.py:24
  91.5 2.1 %collective-permute-done.15.s3 = f32[16,192]{1,0:T(8,128)S(1)} collective-permute-done((f32[16,192]{1,0:T(8,128)S(1)}, f32[16,192]{1,0:T(8,128)S(1)}, u32[]{:S(2)}, u32[]{:S(2)}) %collective-permute-start.15) | collective-permute-done | bytes 12320 | tf_op jit(solution)/shard_map/ppermute | solution.py:24
  94.3 4.0 %all-to-all-start.2 = ((f32[8,32,128]{2,1,0:T(8,128)}), f32[8,32,128]{2,1,0:T(8,128)}, u32[]{:S(2)}, u32[]{:S(2)}) async-start(f32[8,32,128]{2,1,0:T(8,128)} %broadcast_in_dim.7), calls=%async_computation.2 | async-start | bytes 262144 | tf_op jit(solution)/shard_map/all_to_all | solution.py:268
  98.3 1.0 copy-done.7
  99.3 5.5 %shard_map.113 = (bf16[192,1024]{1,0:T(8,128)(2,1)}, bf16[192,1024]{1,0:T(8,128)(2,1)}) custom-call(s32[1]{0:T(128)} %bitcast.idx_ref, bf16[192,1024]{1,0:T(8,128)(2,1)S(1)} %copy-done.3, bf16[192,1024]{1,0:T(8,128)(2,1)S(1)} %copy-done.5, bf16[192,1024]{1,0:T(8,128)(2,1)S(1)} %copy-done.2, bf16[224,1024]{1,0:T(8,128)(2,1)S(1)} %collective-permute-done.1.high_ref.q1, ...), custom_call_target="tpu_custom_call" | custom-call | flops 1509949440 | bytes 4718592 | tf_op jit(solution)/shard_map/pallas_call | solution.py:214
  104.7 1.3 %all-to-all-done.2 = f32[8,32,128]{2,1,0:T(8,128)} async-done(((f32[8,32,128]{2,1,0:T(8,128)}), f32[8,32,128]{2,1,0:T(8,128)}, u32[]{:S(2)}, u32[]{:S(2)}) %all-to-all-start.2) | async-done | bytes 131104 | tf_op jit(solution)/shard_map/all_to_all | solution.py:268
  106.0 1.0 copy.17
  107.0 0.7 copy.15
  (35 shorter events, 1.1 us)
Async XLA Ops:
  0.6 18.8 %copy-start = (bf16[192,1024]{1,0:T(8,128)(2,1)S(1)}, bf16[192,1024]{1,0:T(8,128)(2,1)}, u32[]{:S(2)}) copy-start(bf16[192,1024]{1,0:T(8,128)(2,1)} %grad_ref.3) | copy-start | bytes 1179652
  0.6 18.8 %copy-start.1 = (bf16[192,1024]{1,0:T(8,128)(2,1)S(1)}, bf16[192,1024]{1,0:T(8,128)(2,1)}, u32[]{:S(2)}) copy-start(bf16[192,1024]{1,0:T(8,128)(2,1)} %input_ref.3) | copy-start | bytes 1179652
  0.7 18.7 %copy-start.5 = (bf16[192,1024]{1,0:T(8,128)(2,1)S(1)}, bf16[192,1024]{1,0:T(8,128)(2,1)}, u32[]{:S(2)}) copy-start(bf16[192,1024]{1,0:T(8,128)(2,1)} %v_ref.1) | copy-start | bytes 1179652
  0.7 18.8 %copy-start.4 = (bf16[31,1024]{1,0:T(8,128)(2,1)S(1)}, bf16[31,1024]{1,0:T(8,128)(2,1)}, u32[]{:S(2)}) copy-start(bf16[31,1024]{1,0:T(8,128)(2,1)} %taps_ref.1) | copy-start | bytes 190468
  2.9 8.4 %collective-permute-start = (bf16[224,1024]{1,0:T(8,128)(2,1)}, bf16[224,1024]{1,0:T(8,128)(2,1)S(1)}, u32[]{:S(2)}, u32[]{:S(2)}) collective-permute-start(bf16[224,1024]{1,0:T(8,128)(2,1)} %get-tuple-element.22), channel_id=1, source_target_pairs={{0,2},{2,4},{4,6},{6,8},{8,10},{10,12},{12,14},{14,16},{16,18},{18... | collective-permute-start | bytes 1376264 | tf_op jit(solution)/shard_map/ppermute | solution.py:24
  5.6 8.1 %collective-permute-start.1 = (bf16[224,1024]{1,0:T(8,128)(2,1)}, bf16[224,1024]{1,0:T(8,128)(2,1)S(1)}, u32[]{:S(2)}, u32[]{:S(2)}) collective-permute-start(bf16[224,1024]{1,0:T(8,128)(2,1)} %get-tuple-element.23), channel_id=1, source_target_pairs={{0,254},{2,0},{4,2},{6,4},{8,6},{10,8},{12,10},{14,12},{16,14},{18... | collective-permute-start | bytes 1376264 | tf_op jit(solution)/shard_map/ppermute | solution.py:24
  11.3 15.3 %collective-permute-start.2 = (bf16[224,1024]{1,0:T(8,128)(2,1)S(1)}, bf16[224,1024]{1,0:T(8,128)(2,1)S(1)}, u32[]{:S(2)}, u32[]{:S(2)}) collective-permute-start(bf16[224,1024]{1,0:T(8,128)(2,1)S(1)} %collective-permute-done.low_ref.k1), channel_id=1, source_target_pairs={{0,2},{2,4},{4,6},{6,8},{8,10},{10,12},{12,14},{14,16},{16,18},{18... | collective-permute-start | bytes 1376264 | tf_op jit(solution)/shard_map/ppermute | solution.py:24
  13.7 19.1 %collective-permute-start.6 = (bf16[224,1024]{1,0:T(8,128)(2,1)S(1)}, bf16[224,1024]{1,0:T(8,128)(2,1)S(1)}, u32[]{:S(2)}, u32[]{:S(2)}) collective-permute-start(bf16[224,1024]{1,0:T(8,128)(2,1)S(1)} %collective-permute-done.1.high_ref.q1), channel_id=1, source_target_pairs={{0,254},{2,0},{4,2},{6,4},{8,6},{10,8},{12,10},{14,12},{16,14},{18... | collective-permute-start | bytes 1376264 | tf_op jit(solution)/shard_map/ppermute | solution.py:24
  19.4 13.1 %collective-permute-start.3 = (bf16[192,1024]{1,0:T(8,128)(2,1)S(1)}, bf16[192,1024]{1,0:T(8,128)(2,1)}, u32[]{:S(2)}, u32[]{:S(2)}) collective-permute-start(bf16[192,1024]{1,0:T(8,128)(2,1)S(1)} %copy-done.5), channel_id=1, source_target_pairs={{0,2},{2,4},{4,6},{6,8},{8,10},{10,12},{12,14},{14,16},{16,18},{18... | collective-permute-start | bytes 1179656 | tf_op jit(solution)/shard_map/ppermute | solution.py:24
  24.0 16.5 %collective-permute-start.5 = (bf16[192,1024]{1,0:T(8,128)(2,1)}, bf16[192,1024]{1,0:T(8,128)(2,1)}, u32[]{:S(2)}, u32[]{:S(2)}) collective-permute-start(bf16[192,1024]{1,0:T(8,128)(2,1)} %get-tuple-element.20), channel_id=1, source_target_pairs={{0,1},{1,0},{2,3},{3,2},{4,5},{5,4},{6,7},{7,6},{8,9},{9,8},{10,11... | collective-permute-start | bytes 1179656 | tf_op jit(solution)/shard_map/ppermute | solution.py:246
  26.6 13.8 %all-to-all-start = ((f32[8,32,128]{2,1,0:T(8,128)}), f32[8,32,128]{2,1,0:T(8,128)S(1)}, u32[]{:S(2)}, u32[]{:S(2)}) async-start(f32[8,32,128]{2,1,0:T(8,128)} %get-tuple-element.25), calls=%async_computation | async-start | bytes 262144 | tf_op jit(solution)/shard_map/all_to_all | solution.py:248
  32.5 13.0 %collective-permute-start.4 = (bf16[192,1024]{1,0:T(8,128)(2,1)}, bf16[192,1024]{1,0:T(8,128)(2,1)}, u32[]{:S(2)}, u32[]{:S(2)}) collective-permute-start(bf16[192,1024]{1,0:T(8,128)(2,1)} %collective-permute-done.3.v1), channel_id=1, source_target_pairs={{0,2},{2,4},{4,6},{6,8},{8,10},{10,12},{12,14},{14,16},{16,18},{18... | collective-permute-start | bytes 1179656 | tf_op jit(solution)/shard_map/ppermute | solution.py:24
  32.6 34.4 %collective-permute-start.7 = (bf16[224,1024]{1,0:T(8,128)(2,1)S(1)}, bf16[224,1024]{1,0:T(8,128)(2,1)}, u32[]{:S(2)}, u32[]{:S(2)}) collective-permute-start(bf16[224,1024]{1,0:T(8,128)(2,1)S(1)} %collective-permute-done.2.k2), channel_id=1, source_target_pairs={{0,2},{2,4},{4,6},{6,8},{8,10},{10,12},{12,14},{14,16},{16,18},{18... | collective-permute-start | bytes 1376264 | tf_op jit(solution)/shard_map/ppermute | solution.py:24
  32.8 34.2 %collective-permute-start.9 = (bf16[224,1024]{1,0:T(8,128)(2,1)S(1)}, bf16[224,1024]{1,0:T(8,128)(2,1)S(1)}, u32[]{:S(2)}, u32[]{:S(2)}) collective-permute-start(bf16[224,1024]{1,0:T(8,128)(2,1)S(1)} %collective-permute-done.6.q2), channel_id=1, source_target_pairs={{0,254},{2,0},{4,2},{6,4},{8,6},{10,8},{12,10},{14,12},{16,14},{18... | collective-permute-start | bytes 1376264 | tf_op jit(solution)/shard_map/ppermute | solution.py:24
  40.5 27.7 %copy-start.2 = (bf16[192,1024]{1,0:T(8,128)(2,1)S(1)}, bf16[192,1024]{1,0:T(8,128)(2,1)}, u32[]{:S(2)}) copy-start(bf16[192,1024]{1,0:T(8,128)(2,1)} %q0.1) | copy-start | bytes 1179652
  40.5 27.6 %copy-start.3 = (bf16[192,1024]{1,0:T(8,128)(2,1)S(1)}, bf16[192,1024]{1,0:T(8,128)(2,1)}, u32[]{:S(2)}) copy-start(bf16[192,1024]{1,0:T(8,128)(2,1)} %k_ref.3) | copy-start | bytes 1179652
  45.6 21.5 %collective-permute-start.10 = (bf16[192,1024]{1,0:T(8,128)(2,1)}, bf16[192,1024]{1,0:T(8,128)(2,1)}, u32[]{:S(2)}, u32[]{:S(2)}) collective-permute-start(bf16[192,1024]{1,0:T(8,128)(2,1)} %convolution_convert_fusion.do_ref.d0), channel_id=1, source_target_pairs={{0,254},{2,0},{4,2},{6,4},{8,6},{10,8},{12,10},{14,12},{16,14},{18... | collective-permute-start | bytes 1179656 | tf_op jit(solution)/shard_map/ppermute | solution.py:24
  54.0 12.1 %all-to-all-start.1 = ((f32[16,32,128]{2,1,0:T(8,128)}), f32[16,32,128]{2,1,0:T(8,128)}, u32[]{:S(2)}, u32[]{:S(2)}) async-start(f32[16,32,128]{2,1,0:T(8,128)} %broadcast_in_dim.6), calls=%async_computation.1 | async-start | bytes 524288 | tf_op jit(solution)/shard_map/all_to_all | solution.py:258
  58.7 9.4 %collective-permute-start.8 = (bf16[192,1024]{1,0:T(8,128)(2,1)}, bf16[192,1024]{1,0:T(8,128)(2,1)}, u32[]{:S(2)}, u32[]{:S(2)}) collective-permute-start(bf16[192,1024]{1,0:T(8,128)(2,1)} %collective-permute-done.4.v2), channel_id=1, source_target_pairs={{0,2},{2,4},{4,6},{6,8},{8,10},{10,12},{12,14},{14,16},{16,18},{18... | collective-permute-start | bytes 1179656 | tf_op jit(solution)/shard_map/ppermute | solution.py:24
  67.1 8.3 %collective-permute-start.11 = (bf16[192,1024]{1,0:T(8,128)(2,1)}, bf16[192,1024]{1,0:T(8,128)(2,1)S(1)}, u32[]{:S(2)}, u32[]{:S(2)}) collective-permute-start(bf16[192,1024]{1,0:T(8,128)(2,1)} %collective-permute-done.10.d1), channel_id=1, source_target_pairs={{0,254},{2,0},{4,2},{6,4},{8,6},{10,8},{12,10},{14,12},{16,14},{18... | collective-permute-start | bytes 1179656 | tf_op jit(solution)/shard_map/ppermute | solution.py:24
  75.4 18.2 %collective-permute-start.12 = (bf16[192,1024]{1,0:T(8,128)(2,1)S(1)}, bf16[192,1024]{1,0:T(8,128)(2,1)S(1)}, u32[]{:S(2)}, u32[]{:S(2)}) collective-permute-start(bf16[192,1024]{1,0:T(8,128)(2,1)S(1)} %collective-permute-done.11.d2), channel_id=1, source_target_pairs={{0,254},{2,0},{4,2},{6,4},{8,6},{10,8},{12,10},{14,12},{16,14},{18... | collective-permute-start | bytes 1179656 | tf_op jit(solution)/shard_map/ppermute | solution.py:24
  83.8 0.7 copy-start.6
  84.5 5.2 %collective-permute-start.13 = (f32[16,192]{1,0:T(8,128)S(1)}, f32[16,192]{1,0:T(8,128)S(1)}, u32[]{:S(2)}, u32[]{:S(2)}) collective-permute-start(f32[16,192]{1,0:T(8,128)S(1)} %get-tuple-element.34.s0), channel_id=1, source_target_pairs={{0,254},{2,0},{4,2},{6,4},{8,6},{10,8},{12,10},{14,12},{16,14},{18... | collective-permute-start | bytes 36872 | tf_op jit(solution)/shard_map/ppermute | solution.py:24
  88.9 2.6 %collective-permute-start.14 = (f32[16,192]{1,0:T(8,128)S(1)}, f32[16,192]{1,0:T(8,128)S(1)}, u32[]{:S(2)}, u32[]{:S(2)}) collective-permute-start(f32[16,192]{1,0:T(8,128)S(1)} %get-tuple-element.34.s0), channel_id=1, source_target_pairs={{0,252},{2,254},{4,0},{6,2},{8,4},{10,6},{12,8},{14,10},{16,12},{1... | collective-permute-start | bytes 36872 | tf_op jit(solution)/shard_map/ppermute | solution.py:24
  88.9 4.7 %collective-permute-start.15 = (f32[16,192]{1,0:T(8,128)S(1)}, f32[16,192]{1,0:T(8,128)S(1)}, u32[]{:S(2)}, u32[]{:S(2)}) collective-permute-start(f32[16,192]{1,0:T(8,128)S(1)} %get-tuple-element.34.s0), channel_id=1, source_target_pairs={{0,250},{2,252},{4,254},{6,0},{8,2},{10,4},{12,6},{14,8},{16,10},{... | collective-permute-start | bytes 36872 | tf_op jit(solution)/shard_map/ppermute | solution.py:24
  94.3 11.8 %all-to-all-start.2 = ((f32[8,32,128]{2,1,0:T(8,128)}), f32[8,32,128]{2,1,0:T(8,128)}, u32[]{:S(2)}, u32[]{:S(2)}) async-start(f32[8,32,128]{2,1,0:T(8,128)} %broadcast_in_dim.7), calls=%async_computation.2 | async-start | bytes 262144 | tf_op jit(solution)/shard_map/all_to_all | solution.py:268
  98.3 1.0 copy-start.7

commit v15 on v14

--- a/solution.py
+++ b/solution.py
@@ -262,10 +262,11 @@
     query_grad, stats = query_side(device, near, out_grad, (k3, k2, k1, keys), (v3, v2, v1, values), scale)
     (sent,) = after((d2,), (stats,))
     d3 = rotated(sent, -1)
+    copies = jnp.broadcast_to(tap_sums, (lax.axis_size("far"),) + tap_sums.shape)
+    (copies,) = after((copies,), (d1,))
+    tap_sums = lax.all_to_all(copies, "far", 0, 0, tiled=True)
+    (stats,) = after((stats,), (tap_sums,))
     all_stats = [stats] + [rotated(stats, -hop) for hop in (1, 2, 3)]
-    copies = jnp.broadcast_to(tap_sums, (lax.axis_size("far"),) + tap_sums.shape)
-    (copies,) = after((copies,), (*all_stats[1:], d3))
-    tap_sums = lax.all_to_all(copies, "far", 0, 0, tiled=True)
     key_grad, value_grad = key_side(
         device, keys, values, (queries, q1, q2, q3), (out_grad, d1, d2, d3), all_stats, scale, last
     )

time: 110 us -> 103 us (0.936); the launches traced: 108 us -> 102 us
  waiting for transfers between devices: 17 us -> 12.8 us
  local copies, waits for them, and re-layouts: 4.83 us -> 3.1 us
    all_to_all x1, starting transfers between devices: 4 us -> 12.2 us  [per_device(): tap_sums = lax.all_to_all(copies, 'far', 0, 0, tiled=True)]
    ppermute x15, starting transfers between devices: 42.3 us -> 34.4 us  [rotated(): lax.ppermute(part, CTX, [(i, (i + by) % count) for i in range(count)])]
    ppermute x15, waiting for transfers between devices: 8.89 us -> 5.05 us  [rotated(): lax.ppermute(part, CTX, [(i, (i + by) % count) for i in range(count)])]
    unnamed x18 -> x14, local copies, waits for them, and re-layouts: 2.46 us -> 0.72 us
  transfers between devices with their start and end apart: 19 -> 19, of which waited for: 6 -> 4; matrix products, arithmetic and copies ran while one was open for 6% -> 9% of each run, Pallas kernels for 16% -> 12%
where the time goes in v15:
time: 103 us; the launch traced here: 102 us
  starting transfers between devices  59.8 us (58%)
  Pallas kernels  19.6 us (19%)
  waiting for transfers between devices  12.8 us (12%)
  matrix products  5.04 us (5%)
  local copies, waits for them, and re-layouts  3.1 us (3%)
    ppermute x15, starting transfers between devices, rotated(): lax.ppermute(part, CTX, [(i, (i + by) % count) for i in range(count)])  34.4 us
    all_to_all x1, starting transfers between devices, per_device(): tap_sums = lax.all_to_all(copies, 'far', 0, 0, tiled=True)  12.2 us
    pallas_call x1, Pallas kernels, query_side(): pl.pallas_call(functools.partial(query_kernel, scale), in_specs=[pl.Block...  7.22 us
    all_to_all x1, starting transfers between devices, per_device(): lax.all_to_all(tap_rows, 'far', 0, 0, tiled=True)  5.92 us
    all_to_all x1, waiting for transfers between devices, per_device(): tap_sums = jnp.sum(lax.all_to_all(copies, 'near', 0, 0, tiled=True), axis=0)  5.71 us
    pallas_call x1, Pallas kernels, key_side(): pl.pallas_call(functools.partial(key_kernel, scale, last), in_specs=[pl.B...  5.61 us
    ppermute x15, waiting for transfers between devices, rotated(): lax.ppermute(part, CTX, [(i, (i + by) % count) for i in range(count)])  5.05 us
    dot_general x1, matrix products, project(): lax.dot_general(full, weight, NT, preferred_element_type=jnp.float32)  5.04 us
  transfers between devices with their start and end apart: 19, of which 4 were waited for; matrix products, arithmetic and copies ran while one was open for 9% of the time, Pallas kernels for 12%

profile of v15, /device:TPU:1, one launch (start us, length us, event | category | flops | bytes accessed | tf_op | source)
XLA Modules:
  0.0 102.2 jit_solution(242783755757332900)
XLA Ops:
  0.7 2.2 %shard_map.110 = (bf16[224,1024]{1,0:T(8,128)(2,1)}, bf16[224,1024]{1,0:T(8,128)(2,1)}) custom-call(bf16[192,1024]{1,0:T(8,128)(2,1)} %k_ref.3, bf16[192,1024]{1,0:T(8,128)(2,1)} %q0.1, bf16[192,1024]{1,0:T(8,128)(2,1)} %input_ref.3, bf16[192,1024]{1,0:T(8,128)(2,1)} %grad_ref.3), custom_call_target="tpu_custom_call" | custom-call | tf_op jit(solution)/shard_map/pallas_call | solution.py:50
  2.9 2.7 %collective-permute-start = (bf16[224,1024]{1,0:T(8,128)(2,1)}, bf16[224,1024]{1,0:T(8,128)(2,1)S(1)}, u32[]{:S(2)}, u32[]{:S(2)}) collective-permute-start(bf16[224,1024]{1,0:T(8,128)(2,1)} %get-tuple-element.23), channel_id=1, source_target_pairs={{0,2},{2,4},{4,6},{6,8},{8,10},{10,12},{12,14},{14,16},{16,18},{18... | collective-permute-start | bytes 1376264 | tf_op jit(solution)/shard_map/ppermute | solution.py:24
  5.6 0.7 collective-permute-start.1
  6.3 5.0 %collective-permute-done.low_ref.k1 = bf16[224,1024]{1,0:T(8,128)(2,1)S(1)} collective-permute-done((bf16[224,1024]{1,0:T(8,128)(2,1)}, bf16[224,1024]{1,0:T(8,128)(2,1)S(1)}, u32[]{:S(2)}, u32[]{:S(2)}) %collective-permute-start) | collective-permute-done | bytes 458784 | tf_op jit(solution)/shard_map/ppermute | solution.py:24
  11.3 2.4 %collective-permute-start.2 = (bf16[224,1024]{1,0:T(8,128)(2,1)S(1)}, bf16[224,1024]{1,0:T(8,128)(2,1)S(1)}, u32[]{:S(2)}, u32[]{:S(2)}) collective-permute-start(bf16[224,1024]{1,0:T(8,128)(2,1)S(1)} %collective-permute-done.low_ref.k1), channel_id=1, source_target_pairs={{0,2},{2,4},{4,6},{6,8},{8,10},{10,12},{12,14},{14,16},{16,18},{18... | collective-permute-start | bytes 1376264 | tf_op jit(solution)/shard_map/ppermute | solution.py:24
  13.7 5.7 %collective-permute-start.6 = (bf16[224,1024]{1,0:T(8,128)(2,1)S(1)}, bf16[224,1024]{1,0:T(8,128)(2,1)S(1)}, u32[]{:S(2)}, u32[]{:S(2)}) collective-permute-start(bf16[224,1024]{1,0:T(8,128)(2,1)S(1)} %collective-permute-done.1.high_ref.q1), channel_id=1, source_target_pairs={{0,254},{2,0},{4,2},{6,4},{8,6},{10,8},{12,10},{14,12},{16,14},{18... | collective-permute-start | bytes 1376264 | tf_op jit(solution)/shard_map/ppermute | solution.py:24
  19.4 4.6 %shard_map.111 = (bf16[192,1024]{1,0:T(8,128)(2,1)}, f32[8,32,128]{2,1,0:T(8,128)}) custom-call(s32[1]{0:T(128)} %bitcast.idx_ref, bf16[192,1024]{1,0:T(8,128)(2,1)S(1)} %copy-done, bf16[192,1024]{1,0:T(8,128)(2,1)S(1)} %copy-done.1, bf16[224,1024]{1,0:T(8,128)(2,1)S(1)} %collective-permute-done.low_ref.k1, ...), custom_call_target="tpu_custom_call" | custom-call | flops 48758784 | bytes 786432 | tf_op jit(solution)/shard_map/pallas_call | solution.py:96
  24.0 2.6 %collective-permute-start.5 = (bf16[192,1024]{1,0:T(8,128)(2,1)}, bf16[192,1024]{1,0:T(8,128)(2,1)}, u32[]{:S(2)}, u32[]{:S(2)}) collective-permute-start(bf16[192,1024]{1,0:T(8,128)(2,1)} %get-tuple-element.21), channel_id=1, source_target_pairs={{0,1},{1,0},{2,3},{3,2},{4,5},{5,4},{6,7},{7,6},{8,9},{9,8},{10,11... | collective-permute-start | bytes 1179656 | tf_op jit(solution)/shard_map/ppermute | solution.py:246
  26.6 5.9 %all-to-all-start = ((f32[8,32,128]{2,1,0:T(8,128)}), f32[8,32,128]{2,1,0:T(8,128)S(1)}, u32[]{:S(2)}, u32[]{:S(2)}) async-start(f32[8,32,128]{2,1,0:T(8,128)} %get-tuple-element.26), calls=%async_computation | async-start | bytes 262144 | tf_op jit(solution)/shard_map/all_to_all | solution.py:248
  32.5 0.1 collective-permute-start.4
  32.6 0.2 collective-permute-start.7
  32.8 6.5 %collective-permute-start.9 = (bf16[224,1024]{1,0:T(8,128)(2,1)S(1)}, bf16[224,1024]{1,0:T(8,128)(2,1)S(1)}, u32[]{:S(2)}, u32[]{:S(2)}) collective-permute-start(bf16[224,1024]{1,0:T(8,128)(2,1)S(1)} %collective-permute-done.6.q2), channel_id=1, source_target_pairs={{0,254},{2,0},{4,2},{6,4},{8,6},{10,8},{12,10},{14,12},{16,14},{18... | collective-permute-start | bytes 1376264 | tf_op jit(solution)/shard_map/ppermute | solution.py:24
  39.3 1.1 %all-to-all-done = f32[8,32,128]{2,1,0:T(8,128)S(1)} async-done(((f32[8,32,128]{2,1,0:T(8,128)}), f32[8,32,128]{2,1,0:T(8,128)S(1)}, u32[]{:S(2)}, u32[]{:S(2)}) %all-to-all-start) | async-done | bytes 131104 | tf_op jit(solution)/shard_map/all_to_all | solution.py:248
  40.5 0.0 copy-start.2
  40.5 5.0 %convolution_convert_fusion.do_ref.d0 = bf16[192,1024]{1,0:T(8,128)(2,1)} fusion(bf16[1024,2048]{1,0:T(8,128)(2,1)} %param.13, bf16[192,1024]{1,0:T(8,128)(2,1)} %collective-permute-done.5, bf16[192,1024]{1,0:T(8,128)(2,1)} %get-tuple-element.21, pred[]{:T(512)S(6)} %eq.3), kind=kOutput, calls=%fused_computation | convolution fusion | flops 809041920 | bytes 5373953 | tf_op jit(solution)/shard_map/dot_general | solution.py:115
  45.6 7.7 %collective-permute-start.10 = (bf16[192,1024]{1,0:T(8,128)(2,1)}, bf16[192,1024]{1,0:T(8,128)(2,1)}, u32[]{:S(2)}, u32[]{:S(2)}) collective-permute-start(bf16[192,1024]{1,0:T(8,128)(2,1)} %convolution_convert_fusion.do_ref.d0), channel_id=1, source_target_pairs={{0,254},{2,0},{4,2},{6,4},{8,6},{10,8},{12,10},{14,12},{16,14},{18... | collective-permute-start | bytes 1179656 | tf_op jit(solution)/shard_map/ppermute | solution.py:24
  53.2 0.7 broadcast_in_dim.6
  54.0 4.7 %all-to-all-start.1 = ((f32[16,32,128]{2,1,0:T(8,128)}), f32[16,32,128]{2,1,0:T(8,128)}, u32[]{:S(2)}, u32[]{:S(2)}) async-start(f32[16,32,128]{2,1,0:T(8,128)} %broadcast_in_dim.6), calls=%async_computation.1 | async-start | bytes 524288 | tf_op jit(solution)/shard_map/all_to_all | solution.py:258
  58.7 1.6 %collective-permute-start.8 = (bf16[192,1024]{1,0:T(8,128)(2,1)}, bf16[192,1024]{1,0:T(8,128)(2,1)}, u32[]{:S(2)}, u32[]{:S(2)}) collective-permute-start(bf16[192,1024]{1,0:T(8,128)(2,1)} %collective-permute-done.4.v2), channel_id=1, source_target_pairs={{0,2},{2,4},{4,6},{6,8},{8,10},{10,12},{12,14},{14,16},{16,18},{18... | collective-permute-start | bytes 1179656 | tf_op jit(solution)/shard_map/ppermute | solution.py:24
  60.3 5.7 %all-to-all-done.1 = f32[16,32,128]{2,1,0:T(8,128)} async-done(((f32[16,32,128]{2,1,0:T(8,128)}), f32[16,32,128]{2,1,0:T(8,128)}, u32[]{:S(2)}, u32[]{:S(2)}) %all-to-all-start.1) | async-done | bytes 262176 | tf_op jit(solution)/shard_map/all_to_all | solution.py:258
  66.0 1.0 reduce_sum.19
  67.0 0.9 collective-permute-start.11
  67.9 0.7 broadcast_in_dim.7
  68.6 12.2 %all-to-all-start.2 = ((f32[8,32,128]{2,1,0:T(8,128)}), f32[8,32,128]{2,1,0:T(8,128)}, u32[]{:S(2)}, u32[]{:S(2)}) async-start(f32[8,32,128]{2,1,0:T(8,128)} %broadcast_in_dim.7), calls=%async_computation.2 | async-start | bytes 262144 | tf_op jit(solution)/shard_map/all_to_all | solution.py:267
  80.8 7.2 %shard_map.112 = (bf16[192,1024]{1,0:T(8,128)(2,1)}, f32[16,192]{1,0:T(8,128)S(1)}) custom-call(s32[1]{0:T(128)} %bitcast.idx_ref, bf16[192,1024]{1,0:T(8,128)(2,1)S(1)} %copy-done.2, bf16[192,1024]{1,0:T(8,128)(2,1)} %convolution_convert_fusion.do_ref.d0, bf16[224,1024]{1,0:T(8,128)(2,1)} %collective-permute-done.7.k3, ...), custom_call_target="tpu_custom_call" | custom-call | flops 1509949440 | bytes 4718592 | tf_op jit(solution)/shard_map/pallas_call | solution.py:157
  88.0 0.4 collective-permute-start.12
  88.4 0.9 all-to-all-done.2
  89.4 1.5 %collective-permute-start.13 = (f32[16,192]{1,0:T(8,128)S(1)}, f32[16,192]{1,0:T(8,128)S(1)}, u32[]{:S(2)}, u32[]{:S(2)}) collective-permute-start(f32[16,192]{1,0:T(8,128)S(1)} %get-tuple-element.38.s0), channel_id=1, source_target_pairs={{0,254},{2,0},{4,2},{6,4},{8,6},{10,8},{12,10},{14,12},{16,14},{18... | collective-permute-start | bytes 36872 | tf_op jit(solution)/shard_map/ppermute | solution.py:24
  90.9 4.0 %collective-permute-start.15 = (f32[16,192]{1,0:T(8,128)S(1)}, f32[16,192]{1,0:T(8,128)S(1)}, u32[]{:S(2)}, u32[]{:S(2)}) collective-permute-start(f32[16,192]{1,0:T(8,128)S(1)} %get-tuple-element.38.s0), channel_id=1, source_target_pairs={{0,250},{2,252},{4,254},{6,0},{8,2},{10,4},{12,6},{14,8},{16,10},{... | collective-permute-start | bytes 36872 | tf_op jit(solution)/shard_map/ppermute | solution.py:24
  94.9 1.0 copy.17
  95.9 0.7 copy.15
  96.6 5.6 %shard_map.113 = (bf16[192,1024]{1,0:T(8,128)(2,1)}, bf16[192,1024]{1,0:T(8,128)(2,1)}) custom-call(s32[1]{0:T(128)} %bitcast.idx_ref, bf16[192,1024]{1,0:T(8,128)(2,1)S(1)} %copy-done.3, bf16[192,1024]{1,0:T(8,128)(2,1)S(1)} %copy-done.5, bf16[192,1024]{1,0:T(8,128)(2,1)S(1)} %copy-done.2, bf16[224,1024]{1,0:T(8,128)(2,1)S(1)} %collective-permute-done.1.high_ref.q1, ...), custom_call_target="tpu_custom_call" | custom-call | flops 1509949440 | bytes 4718592 | tf_op jit(solution)/shard_map/pallas_call | solution.py:214
  (31 shorter events, 0.1 us)
Async XLA Ops:
  0.6 18.8 %copy-start = (bf16[192,1024]{1,0:T(8,128)(2,1)S(1)}, bf16[192,1024]{1,0:T(8,128)(2,1)}, u32[]{:S(2)}) copy-start(bf16[192,1024]{1,0:T(8,128)(2,1)} %grad_ref.3) | copy-start | bytes 1179652
  0.6 18.8 %copy-start.1 = (bf16[192,1024]{1,0:T(8,128)(2,1)S(1)}, bf16[192,1024]{1,0:T(8,128)(2,1)}, u32[]{:S(2)}) copy-start(bf16[192,1024]{1,0:T(8,128)(2,1)} %input_ref.3) | copy-start | bytes 1179652
  0.7 18.7 %copy-start.5 = (bf16[192,1024]{1,0:T(8,128)(2,1)S(1)}, bf16[192,1024]{1,0:T(8,128)(2,1)}, u32[]{:S(2)}) copy-start(bf16[192,1024]{1,0:T(8,128)(2,1)} %v_ref.1) | copy-start | bytes 1179652
  0.7 18.7 %copy-start.4 = (bf16[31,1024]{1,0:T(8,128)(2,1)S(1)}, bf16[31,1024]{1,0:T(8,128)(2,1)}, u32[]{:S(2)}) copy-start(bf16[31,1024]{1,0:T(8,128)(2,1)} %taps_ref.1) | copy-start | bytes 190468
  2.9 8.4 %collective-permute-start = (bf16[224,1024]{1,0:T(8,128)(2,1)}, bf16[224,1024]{1,0:T(8,128)(2,1)S(1)}, u32[]{:S(2)}, u32[]{:S(2)}) collective-permute-start(bf16[224,1024]{1,0:T(8,128)(2,1)} %get-tuple-element.23), channel_id=1, source_target_pairs={{0,2},{2,4},{4,6},{6,8},{8,10},{10,12},{12,14},{14,16},{16,18},{18... | collective-permute-start | bytes 1376264 | tf_op jit(solution)/shard_map/ppermute | solution.py:24
  5.6 8.1 %collective-permute-start.1 = (bf16[224,1024]{1,0:T(8,128)(2,1)}, bf16[224,1024]{1,0:T(8,128)(2,1)S(1)}, u32[]{:S(2)}, u32[]{:S(2)}) collective-permute-start(bf16[224,1024]{1,0:T(8,128)(2,1)} %get-tuple-element.24), channel_id=1, source_target_pairs={{0,254},{2,0},{4,2},{6,4},{8,6},{10,8},{12,10},{14,12},{16,14},{18... | collective-permute-start | bytes 1376264 | tf_op jit(solution)/shard_map/ppermute | solution.py:24
  11.3 15.3 %collective-permute-start.2 = (bf16[224,1024]{1,0:T(8,128)(2,1)S(1)}, bf16[224,1024]{1,0:T(8,128)(2,1)S(1)}, u32[]{:S(2)}, u32[]{:S(2)}) collective-permute-start(bf16[224,1024]{1,0:T(8,128)(2,1)S(1)} %collective-permute-done.low_ref.k1), channel_id=1, source_target_pairs={{0,2},{2,4},{4,6},{6,8},{8,10},{10,12},{12,14},{14,16},{16,18},{18... | collective-permute-start | bytes 1376264 | tf_op jit(solution)/shard_map/ppermute | solution.py:24
  13.7 19.1 %collective-permute-start.6 = (bf16[224,1024]{1,0:T(8,128)(2,1)S(1)}, bf16[224,1024]{1,0:T(8,128)(2,1)S(1)}, u32[]{:S(2)}, u32[]{:S(2)}) collective-permute-start(bf16[224,1024]{1,0:T(8,128)(2,1)S(1)} %collective-permute-done.1.high_ref.q1), channel_id=1, source_target_pairs={{0,254},{2,0},{4,2},{6,4},{8,6},{10,8},{12,10},{14,12},{16,14},{18... | collective-permute-start | bytes 1376264 | tf_op jit(solution)/shard_map/ppermute | solution.py:24
  19.4 13.1 %collective-permute-start.3 = (bf16[192,1024]{1,0:T(8,128)(2,1)S(1)}, bf16[192,1024]{1,0:T(8,128)(2,1)}, u32[]{:S(2)}, u32[]{:S(2)}) collective-permute-start(bf16[192,1024]{1,0:T(8,128)(2,1)S(1)} %copy-done.5), channel_id=1, source_target_pairs={{0,2},{2,4},{4,6},{6,8},{8,10},{10,12},{12,14},{14,16},{16,18},{18... | collective-permute-start | bytes 1179656 | tf_op jit(solution)/shard_map/ppermute | solution.py:24
  24.0 16.5 %collective-permute-start.5 = (bf16[192,1024]{1,0:T(8,128)(2,1)}, bf16[192,1024]{1,0:T(8,128)(2,1)}, u32[]{:S(2)}, u32[]{:S(2)}) collective-permute-start(bf16[192,1024]{1,0:T(8,128)(2,1)} %get-tuple-element.21), channel_id=1, source_target_pairs={{0,1},{1,0},{2,3},{3,2},{4,5},{5,4},{6,7},{7,6},{8,9},{9,8},{10,11... | collective-permute-start | bytes 1179656 | tf_op jit(solution)/shard_map/ppermute | solution.py:246
  26.6 13.8 %all-to-all-start = ((f32[8,32,128]{2,1,0:T(8,128)}), f32[8,32,128]{2,1,0:T(8,128)S(1)}, u32[]{:S(2)}, u32[]{:S(2)}) async-start(f32[8,32,128]{2,1,0:T(8,128)} %get-tuple-element.26), calls=%async_computation | async-start | bytes 262144 | tf_op jit(solution)/shard_map/all_to_all | solution.py:248
  32.5 13.0 %collective-permute-start.4 = (bf16[192,1024]{1,0:T(8,128)(2,1)}, bf16[192,1024]{1,0:T(8,128)(2,1)}, u32[]{:S(2)}, u32[]{:S(2)}) collective-permute-start(bf16[192,1024]{1,0:T(8,128)(2,1)} %collective-permute-done.3.v1), channel_id=1, source_target_pairs={{0,2},{2,4},{4,6},{6,8},{8,10},{10,12},{12,14},{14,16},{16,18},{18... | collective-permute-start | bytes 1179656 | tf_op jit(solution)/shard_map/ppermute | solution.py:24
  32.6 34.4 %collective-permute-start.7 = (bf16[224,1024]{1,0:T(8,128)(2,1)S(1)}, bf16[224,1024]{1,0:T(8,128)(2,1)}, u32[]{:S(2)}, u32[]{:S(2)}) collective-permute-start(bf16[224,1024]{1,0:T(8,128)(2,1)S(1)} %collective-permute-done.2.k2), channel_id=1, source_target_pairs={{0,2},{2,4},{4,6},{6,8},{8,10},{10,12},{12,14},{14,16},{16,18},{18... | collective-permute-start | bytes 1376264 | tf_op jit(solution)/shard_map/ppermute | solution.py:24
  32.8 34.2 %collective-permute-start.9 = (bf16[224,1024]{1,0:T(8,128)(2,1)S(1)}, bf16[224,1024]{1,0:T(8,128)(2,1)S(1)}, u32[]{:S(2)}, u32[]{:S(2)}) collective-permute-start(bf16[224,1024]{1,0:T(8,128)(2,1)S(1)} %collective-permute-done.6.q2), channel_id=1, source_target_pairs={{0,254},{2,0},{4,2},{6,4},{8,6},{10,8},{12,10},{14,12},{16,14},{18... | collective-permute-start | bytes 1376264 | tf_op jit(solution)/shard_map/ppermute | solution.py:24
  40.5 40.3 %copy-start.2 = (bf16[192,1024]{1,0:T(8,128)(2,1)S(1)}, bf16[192,1024]{1,0:T(8,128)(2,1)}, u32[]{:S(2)}) copy-start(bf16[192,1024]{1,0:T(8,128)(2,1)} %q0.1) | copy-start | bytes 1179652
  40.5 40.3 %copy-start.3 = (bf16[192,1024]{1,0:T(8,128)(2,1)S(1)}, bf16[192,1024]{1,0:T(8,128)(2,1)}, u32[]{:S(2)}) copy-start(bf16[192,1024]{1,0:T(8,128)(2,1)} %k_ref.3) | copy-start | bytes 1179652
  45.6 21.5 %collective-permute-start.10 = (bf16[192,1024]{1,0:T(8,128)(2,1)}, bf16[192,1024]{1,0:T(8,128)(2,1)}, u32[]{:S(2)}, u32[]{:S(2)}) collective-permute-start(bf16[192,1024]{1,0:T(8,128)(2,1)} %convolution_convert_fusion.do_ref.d0), channel_id=1, source_target_pairs={{0,254},{2,0},{4,2},{6,4},{8,6},{10,8},{12,10},{14,12},{16,14},{18... | collective-permute-start | bytes 1179656 | tf_op jit(solution)/shard_map/ppermute | solution.py:24
  54.0 12.1 %all-to-all-start.1 = ((f32[16,32,128]{2,1,0:T(8,128)}), f32[16,32,128]{2,1,0:T(8,128)}, u32[]{:S(2)}, u32[]{:S(2)}) async-start(f32[16,32,128]{2,1,0:T(8,128)} %broadcast_in_dim.6), calls=%async_computation.1 | async-start | bytes 524288 | tf_op jit(solution)/shard_map/all_to_all | solution.py:258
  58.7 22.1 %collective-permute-start.8 = (bf16[192,1024]{1,0:T(8,128)(2,1)}, bf16[192,1024]{1,0:T(8,128)(2,1)}, u32[]{:S(2)}, u32[]{:S(2)}) collective-permute-start(bf16[192,1024]{1,0:T(8,128)(2,1)} %collective-permute-done.4.v2), channel_id=1, source_target_pairs={{0,2},{2,4},{4,6},{6,8},{8,10},{10,12},{12,14},{14,16},{16,18},{18... | collective-permute-start | bytes 1179656 | tf_op jit(solution)/shard_map/ppermute | solution.py:24
  67.0 21.0 %collective-permute-start.11 = (bf16[192,1024]{1,0:T(8,128)(2,1)}, bf16[192,1024]{1,0:T(8,128)(2,1)}, u32[]{:S(2)}, u32[]{:S(2)}) collective-permute-start(bf16[192,1024]{1,0:T(8,128)(2,1)} %collective-permute-done.10.d1), channel_id=1, source_target_pairs={{0,254},{2,0},{4,2},{6,4},{8,6},{10,8},{12,10},{14,12},{16,14},{18... | collective-permute-start | bytes 1179656 | tf_op jit(solution)/shard_map/ppermute | solution.py:24
  68.6 20.8 %all-to-all-start.2 = ((f32[8,32,128]{2,1,0:T(8,128)}), f32[8,32,128]{2,1,0:T(8,128)}, u32[]{:S(2)}, u32[]{:S(2)}) async-start(f32[8,32,128]{2,1,0:T(8,128)} %broadcast_in_dim.7), calls=%async_computation.2 | async-start | bytes 262144 | tf_op jit(solution)/shard_map/all_to_all | solution.py:267
  88.0 8.6 %collective-permute-start.12 = (bf16[192,1024]{1,0:T(8,128)(2,1)}, bf16[192,1024]{1,0:T(8,128)(2,1)S(1)}, u32[]{:S(2)}, u32[]{:S(2)}) collective-permute-start(bf16[192,1024]{1,0:T(8,128)(2,1)} %collective-permute-done.11.d2), channel_id=1, source_target_pairs={{0,254},{2,0},{4,2},{6,4},{8,6},{10,8},{12,10},{14,12},{16,14},{18... | collective-permute-start | bytes 1179656 | tf_op jit(solution)/shard_map/ppermute | solution.py:24
  89.4 7.2 %collective-permute-start.13 = (f32[16,192]{1,0:T(8,128)S(1)}, f32[16,192]{1,0:T(8,128)S(1)}, u32[]{:S(2)}, u32[]{:S(2)}) collective-permute-start(f32[16,192]{1,0:T(8,128)S(1)} %get-tuple-element.38.s0), channel_id=1, source_target_pairs={{0,254},{2,0},{4,2},{6,4},{8,6},{10,8},{12,10},{14,12},{16,14},{18... | collective-permute-start | bytes 36872 | tf_op jit(solution)/shard_map/ppermute | solution.py:24
  90.9 5.7 %collective-permute-start.14 = (f32[16,192]{1,0:T(8,128)S(1)}, f32[16,192]{1,0:T(8,128)S(1)}, u32[]{:S(2)}, u32[]{:S(2)}) collective-permute-start(f32[16,192]{1,0:T(8,128)S(1)} %get-tuple-element.38.s0), channel_id=1, source_target_pairs={{0,252},{2,254},{4,0},{6,2},{8,4},{10,6},{12,8},{14,10},{16,12},{1... | collective-permute-start | bytes 36872 | tf_op jit(solution)/shard_map/ppermute | solution.py:24
  90.9 5.7 %collective-permute-start.15 = (f32[16,192]{1,0:T(8,128)S(1)}, f32[16,192]{1,0:T(8,128)S(1)}, u32[]{:S(2)}, u32[]{:S(2)}) collective-permute-start(f32[16,192]{1,0:T(8,128)S(1)} %get-tuple-element.38.s0), channel_id=1, source_target_pairs={{0,250},{2,252},{4,254},{6,0},{8,2},{10,4},{12,6},{14,8},{16,10},{... | collective-permute-start | bytes 36872 | tf_op jit(solution)/shard_map/ppermute | solution.py:24
